TPU v7x, 32 devices: a whole 2x2x4 slice. The times are simulated.
32 devices in a mesh: gx: 8 (over z, y), yz: 4 (over x, core).
Axes of the slice: x: 2, y: 2, z: 4, core: 2. Of those that a mesh axis runs over, the one named last changes fastest.
Arguments:
- field: float32 [512, 512, 1024], P('gx', None, 'yz'), may hold values from -58 to 58, as said below
- start: float32 [512, 128], replicated, may hold values from -6 to 6
Outputs:
- basis: float32 [512, 128], replicated
- gram_y: float32 [1024, 1024], P('yz', 'gx')
Inputs may be any that keep to these rules, and one draw needn't show every extreme that they name: `field`: every cell is a real number at most a few tens in magnitude.
All inputs are finite; a program needn't handle non-finite values.
Results may differ from a plain program's by a relative error of at most 0.00025.
Values sent between devices are 32-bit elements; how exact they have to be, the bound alone decides.
No kernel may reach another device: no remote copies, remote signals or barrier semaphores. Data moves between devices by JAX's collectives and lax.ppermute only.
A program may use at most 192 MiB of HBM per device.

v0:
```python
import jax
import jax.numpy as jnp
from jax import lax
from jax.sharding import PartitionSpec as P

ITERS = 4


def orthonormal_rows(product, cross):
    lower = lax.linalg.cholesky(cross)
    return lax.linalg.triangular_solve(
        lower, product, left_side=False, lower=True, transpose_a=True
    )


def inner_cross(product):
    return jnp.dot(
        product.T, product, precision=lax.Precision.HIGHEST, preferred_element_type=jnp.float32
    )


def on_device(field, start):
    x_block, depth, y_block = field.shape
    width_y = y_block * lax.axis_size("yz")
    fibres = lax.all_to_all(field, "gx", split_axis=1, concat_axis=0, tiled=True)
    width_x = fibres.shape[0]
    z_local = fibres.shape[1]
    y_local = fibres.shape[2]
    flat = fibres.reshape(width_x, z_local * y_local)
    partial_value = jnp.dot(
        flat, flat.T, precision=lax.Precision.HIGHEST, preferred_element_type=jnp.float32
    )
    total = float(width_y * depth)
    basis = start
    gram_x = lax.psum(partial_value, ("gx", "yz")) / total
    for step in range(ITERS):
        product = jnp.dot(
            gram_x, basis, precision=lax.Precision.HIGHEST, preferred_element_type=jnp.float32
        )
        basis = orthonormal_rows(product, inner_cross(product))
    rank = basis.shape[1]
    core = jnp.dot(
        basis.T, flat, precision=lax.Precision.HIGHEST, preferred_element_type=jnp.float32
    )
    core = core.reshape(rank, z_local, y_local)
    scale = float(rank * depth)
    own_rows = core.reshape(rank * z_local, y_local)
    piece = lax.all_gather(core, "yz", axis=2, tiled=True)
    other = piece.reshape(rank * z_local, piece.shape[2])
    block = jnp.dot(
        own_rows.T, other, precision=lax.Precision.HIGHEST, preferred_element_type=jnp.float32
    )
    gram_y = lax.psum_scatter(block / scale, "gx", scatter_dimension=1, tiled=True)
    return (basis, gram_y)


def solution(mesh):
    placed = (P("gx", None, "yz"), P())
    return jax.shard_map(
        on_device, mesh=mesh, in_specs=placed, out_specs=(P(), P("yz", "gx")), check_vma=False
    )
```

profile of v0, /device:TPU:0, one launch (start us, length us, event | category | flops | bytes accessed | tf_op | source)
XLA Modules:
  0.0 1458.1 jit_solution(11713974033717332667)
XLA Ops:
  7.2 0.0 copy-start
  7.2 0.0 all-reduce.2.cloned.1.call-start
  7.2 31.8 %copy.15 = f32[64,512,256]{2,0,1:T(8,128)} copy(f32[64,512,256]{2,1,0:T(8,128)} %param.5) | data formatting | bytes 67108864 | tf_op args[0]
  39.1 729.8 %all_to_all.15 = f32[64,512,256]{2,0,1:T(8,128)S(1)} all-to-all(f32[64,512,256]{2,0,1:T(8,128)} %copy.15), channel_id=1, replica_groups=mesh['gx'=8,'yz'=4] {'gx'}, dimensions={1} | all-to-all | bytes 67108864 | tf_op jit(solution)/shard_map/all_to_all | solution.py:25
  768.9 21.5 %copy.16 = f32[64,8,64,256]{3,2,0,1:T(8,128)} copy(f32[64,8,64,256]{3,0,2,1:T(8,128)S(1)} %bitcast.76) | data formatting | bytes 67108864 | tf_op jit(solution)/shard_map/all_to_all | solution.py:25
  790.4 32.9 %copy.22 = f32[64,8,64,256]{3,1,2,0:T(8,128)} copy(f32[64,8,64,256]{3,2,1,0:T(8,128)} %bitcast.77) | data formatting | bytes 67108864
  823.3 60.5 %fusion.34 = f32[512,512]{1,0:T(8,128)} fusion(f32[512,16384]{1,0:T(8,128)} %bitcast.74), kind=kOutput, calls=%fused_computation.54 | convolution fusion | flops 51539607552 | bytes 34603008 | tf_op jit(solution)/shard_map/dot_general | solution.py:30
  883.8 0.0 all-reduce.2.cloned.1.call-update
  883.9 0.4 all-gather.2.cloned.1.call-start
  884.3 128.5 %all-reduce.2.cloned.1.call-done = f32[512,512]{1,0:T(8,128)} async-done(((f32[512,512]{1,0:T(8,128)}), f32[512,512]{1,0:T(8,128)}) %all-reduce.2.cloned.1.call-update) | async-done | bytes 1048592 | tf_op jit(solution)/shard_map/psum | solution.py:35
  1012.8 0.0 copy-done
  1012.8 2.2 fusion.6
  1015.0 0.6 fusion.35
  1015.6 0.1 copy.17
  1015.7 11.7 custom-call.12
  1027.5 0.6 compare_reduce_fusion.3
  1028.1 0.7 fusion.12
  1028.8 9.8 custom-call.13
  1038.6 0.4 convolution_bitcast_fusion.3
  1039.0 2.2 fusion.4
  1041.3 0.6 fusion.36
  1041.9 0.1 copy.18
  1042.0 11.8 custom-call.14
  1053.9 0.6 compare_reduce_fusion.2
  1054.5 0.7 fusion.13
  1055.2 9.8 custom-call.15
  1065.0 0.4 convolution_bitcast_fusion.2
  1065.4 2.2 fusion.2
  1067.6 0.6 fusion.37
  1068.2 0.1 copy.19
  1068.3 11.7 custom-call.16
  1080.1 0.6 compare_reduce_fusion.1
  1080.7 0.7 fusion.14
  1081.4 9.8 custom-call.17
  1091.2 0.4 convolution_bitcast_fusion.1
  1091.6 2.4 fusion
  1094.0 0.6 fusion.38
  1094.6 0.1 copy.20
  1094.8 11.7 custom-call.18
  1106.5 0.6 compare_reduce_fusion
  1107.1 0.7 fusion.15
  1107.8 9.8 custom-call.19
  1117.6 0.4 convolution_bitcast_fusion
  1118.0 25.1 %fusion.39 = f32[128,16384]{1,0:T(8,128)} fusion(f32[512,128]{0,1:T(8,128)S(1)} %convolution_bitcast_fusion, f32[512,16384]{1,0:T(8,128)} %bitcast.75), kind=kOutput, calls=%fused_computation.59 | convolution fusion | flops 12884901888 | bytes 42205184 | tf_op jit(solution)/shard_map/dot_general | solution.py:42
  1143.1 9.2 copy.23
  1152.3 0.0 all-gather.2.cloned.1.call-update
  1152.3 0.0 reduce-scatter.2.cloned.1.call-start
  1152.4 10.1 reshape_reshape.3
  1162.5 190.5 %all-gather.2.cloned.1.call-done = f32[128,64,1024]{2,1,0:T(8,128)} async-done(((f32[128,64,256]{2,1,0:T(8,128)}), f32[128,64,1024]{2,1,0:T(8,128)}) %all-gather.2.cloned.1.call-update) | async-done | bytes 33554448 | tf_op jit(solution)/shard_map/all_gather | solution.py:48
  1353.0 33.9 %convolution_multiply_fusion = f32[256,1024]{1,0:T(8,128)} fusion(f32[8192,256]{1,0:T(8,128)} %reshape_reshape.3, f32[8192,1024]{1,0:T(8,128)} %bitcast.79), kind=kOutput, calls=%fused_computation | convolution fusion | flops 25770065920 | bytes 42991616 | tf_op jit(solution)/shard_map/dot_general | solution.py:50
  1386.9 0.0 reduce-scatter.2.cloned.1.call-update
  1386.9 0.8 copy.21
  1387.8 63.3 %reduce-scatter.2.cloned.1.call-done = f32[256,128]{1,0:T(8,128)} async-done(((f32[256,1024]{1,0:T(8,128)}), f32[256,128]{1,0:T(8,128)}) %reduce-scatter.2.cloned.1.call-update) | async-done | bytes 131088 | tf_op jit(solution)/shard_map/reduce_scatter | solution.py:53
  (8 shorter events, 0.2 us)
Async XLA Ops:
  7.2 1005.7 %copy-start = (f32[512,128]{1,0:T(8,128)S(1)}, f32[512,128]{1,0:T(8,128)}, u32[]{:S(2)}) copy-start(f32[512,128]{1,0:T(8,128)} %param.6) | copy-start | bytes 786436
  7.2 1005.6 %all-reduce.2.cloned.1.call-start = ((), (), s32[]{:S(2)}) async-start(), calls=%async_computation.2 | async-start | bytes 2097152 | tf_op jit(solution)/shard_map/psum | solution.py:35
  883.9 469.1 %all-gather.2.cloned.1.call-start = ((), (), s32[]{:S(2)}) async-start(), calls=%async_computation.3 | async-start | bytes 41943040 | tf_op jit(solution)/shard_map/all_gather | solution.py:48
  1152.3 298.7 %reduce-scatter.2.cloned.1.call-start = ((), (), s32[]{:S(2)}) async-start(), calls=%async_computation.4 | async-start | bytes 1179648 | tf_op jit(solution)/shard_map/reduce_scatter | solution.py:53
Sparse Core Ops, SparseCore 0:
  884.0 128.7 all-reduce.1
  1152.5 200.4 all-gather.1
  1387.1 63.9 reduce-scatter.1
where the time goes:
time: 1460 us
  blocking collectives  730 us (50%)
  waiting for transfers between devices  382 us (26%)
  matrix products  133 us (9%)
  local copies, waits for them, and re-layouts  107 us (7%)
  other arithmetic  91.6 us (6%)
    all_to_all x1, blocking collectives, on_device(): lax.all_to_all(field, 'gx', split_axis=1, concat_axis=0, tiled=True)  730 us
    all_gather x1, waiting for transfers between devices, on_device(): piece = lax.all_gather(core, 'yz', axis=2, tiled=True)  190 us
    psum x1, waiting for transfers between devices, on_device(): gram_x = lax.psum(partial_value, ('gx', 'yz')) / total  128 us
    unnamed x6, local copies, waits for them, and re-layouts  74.8 us
    reduce_scatter x1, waiting for transfers between devices, on_device(): lax.psum_scatter(block / scale, 'gx', scatter_dimension=1, tiled=True)  63.3 us
    dot_general x1, matrix products, on_device(): jnp.dot(flat, flat.T, precision=lax.Precision.HIGHEST, preferred_element_...  60.5 us
    another operation x12, other arithmetic, orthonormal_rows(): lower = lax.linalg.cholesky(cross)  49.7 us
    another operation x8, other arithmetic, orthonormal_rows(): lax.linalg.triangular_solve(lower, product, left_side=False, lower=True,...  41.9 us
  transfers between devices with their start and end apart: 3, of which 3 were waited for; matrix products, arithmetic and copies ran while one was open for 1% of the time, Pallas kernels for 0%

commit v1 on v0

v1 whole, which is shorter than its diff:
```python
import functools

import jax
import jax.numpy as jnp
from jax import lax
from jax.experimental import pallas as pl
from jax.experimental.pallas import tpu as pltpu
from jax.sharding import PartitionSpec as P

ITERS = 4
CHUNKS = 4
WINDOW = 5
LINE = 4
MIB = 1024 * 1024
F32 = jnp.float32
BF16 = jnp.bfloat16


def halves(value):
    high = value.astype(BF16)
    low = (value - high.astype(F32)).astype(BF16)
    return high, low


def dot_nt(left, right):
    return lax.dot_general(left, right, (((1,), (1,)), ((), ())), preferred_element_type=F32)


def dot_tn(left, right):
    return lax.dot_general(left, right, (((0,), (0,)), ((), ())), preferred_element_type=F32)


def gram_body(steps, slab_ref, before_ref, out_ref, main, cross):
    step = pl.program_id(0)

    @pl.when(step == 0)
    def _():
        main[...] = jnp.zeros_like(main)
        cross[...] = jnp.zeros_like(cross)

    depth = slab_ref.shape[0]
    parts = [halves(slab_ref[z]) for z in range(depth)]
    high = jnp.concatenate([part[0] for part in parts], axis=1)
    low = jnp.concatenate([part[1] for part in parts], axis=1)
    main[...] += dot_nt(high, high)
    cross[...] += dot_nt(high, low)

    @pl.when(step == steps - 1)
    def _():
        mixed = cross[...]
        out_ref[...] = before_ref[...] + main[...] + mixed + mixed.T


def gram_of(slab, before):
    depth, width_x, width_y = slab.shape
    block = 4 if depth % 4 == 0 else 1
    steps = depth // block
    square = pl.BlockSpec((width_x, width_x), lambda i: (0, 0))
    return pl.pallas_call(
        functools.partial(gram_body, steps),
        grid=(steps,),
        in_specs=[pl.BlockSpec((block, width_x, width_y), lambda i: (i, 0, 0)), square],
        out_specs=square,
        out_shape=jax.ShapeDtypeStruct((width_x, width_x), F32),
        scratch_shapes=[pltpu.VMEM((width_x, width_x), F32)] * 2,
        compiler_params=pltpu.CompilerParams(vmem_limit_bytes=32 * MIB),
        cost_estimate=pl.CostEstimate(
            flops=4 * width_x * width_x * depth * width_y,
            bytes_accessed=slab.size * 4,
            transcendentals=0,
        ),
        name="gram_x",
    )(slab, before)


def core_body(steps, field_ref, basis_ref, out_ref, stacked_ref, high_ref, low_ref, main, cross):
    step = pl.program_id(0)
    rank = basis_ref.shape[1]

    @pl.when(step == 0)
    def _():
        main[...] = jnp.zeros_like(main)
        cross[...] = jnp.zeros_like(cross)
        basis_high, basis_low = halves(basis_ref[...].T)
        stacked_ref[:rank] = basis_high
        stacked_ref[rank:] = basis_low

    depth, blocks, _, width = field_ref.shape
    stacked = stacked_ref[...]
    for z in range(depth):
        for b in range(blocks):
            high, low = halves(field_ref[z, b])
            both = jnp.dot(stacked, high, preferred_element_type=F32)
            core = both[:rank] + both[rank:]
            core += jnp.dot(stacked[:rank], low, preferred_element_type=F32)
            core_high, core_low = halves(core)
            high_ref[pl.ds(z * rank, rank), pl.ds(b * width, width)] = core_high
            low_ref[pl.ds(z * rank, rank), pl.ds(b * width, width)] = core_low
    high = high_ref[...]
    main[...] += dot_tn(high, high)
    cross[...] += dot_tn(high, low_ref[...])

    @pl.when(step == steps - 1)
    def _():
        mixed = cross[...]
        out_ref[...] = main[...] + mixed + mixed.T


def core_gram(cells, basis):
    depth, blocks, width_x, width = cells.shape
    rank = basis.shape[1]
    width_y = blocks * width
    block = 2 if depth % 2 == 0 else 1
    steps = depth // block
    return pl.pallas_call(
        functools.partial(core_body, steps),
        grid=(steps,),
        in_specs=[
            pl.BlockSpec((block, blocks, width_x, width), lambda i: (i, 0, 0, 0)),
            pl.BlockSpec((width_x, rank), lambda i: (0, 0)),
        ],
        out_specs=pl.BlockSpec((width_y, width_y), lambda i: (0, 0)),
        out_shape=jax.ShapeDtypeStruct((width_y, width_y), F32),
        scratch_shapes=[
            pltpu.VMEM((2 * rank, width_x), BF16),
            pltpu.VMEM((block * rank, width_y), BF16),
            pltpu.VMEM((block * rank, width_y), BF16),
            pltpu.VMEM((width_y, width_y), F32),
            pltpu.VMEM((width_y, width_y), F32),
        ],
        compiler_params=pltpu.CompilerParams(vmem_limit_bytes=48 * MIB),
        cost_estimate=pl.CostEstimate(
            flops=6 * rank * cells.size + 4 * rank * depth * width_y * width_y,
            bytes_accessed=cells.size * 4,
            transcendentals=0,
        ),
        name="core_gram_y",
    )(cells, basis)


def full_dot(left, right, contract):
    return lax.dot_general(
        left,
        right,
        ((contract[:1], contract[1:]), ((), ())),
        precision=lax.Precision.HIGHEST,
        preferred_element_type=F32,
    )


def inverse_factor(cross):
    size = cross.shape[0]
    tall = 8
    wide = 4
    groups = size // tall
    shape = (tall, size)
    sublane = lax.broadcasted_iota(jnp.int32, shape, 0)
    lane = lax.broadcasted_iota(jnp.int32, shape, 1)
    left = [cross[t * tall : (t + 1) * tall] for t in range(groups)]
    right = [(lane == sublane + t * tall).astype(F32) for t in range(groups)]
    pivots = [jnp.ones(shape, F32) for _ in range(groups)]

    def row(value, s):
        return jnp.broadcast_to(value[s : s + 1, :], shape)

    for first in range(0, size, wide):
        top, s0 = first // tall, first % tall
        below = range(top, groups)
        columns = [
            {t: jnp.broadcast_to(left[t][:, first + k : first + k + 1], shape) for t in below}
            for k in range(wide)
        ]
        rows = [row(left[top], s0 + k) for k in range(wide)]
        eyes = [row(right[top], s0 + k) for k in range(wide)]
        scaled = []
        for i in range(wide):
            pivot = row(columns[i][top], s0 + i)
            inverse = 1.0 / pivot
            scaled.append((rows[i] * inverse, eyes[i] * inverse))
            for k in range(i + 1, wide):
                ratio = row(columns[i][top], s0 + k) * inverse
                for t in below:
                    columns[k][t] = columns[k][t] - ratio * columns[i][t]
                rows[k] = rows[k] - ratio * rows[i]
                eyes[k] = eyes[k] - ratio * eyes[i]
            here = sublane == s0 + i
            pivots[top] = jnp.where(here, pivot, pivots[top])
        rest = sublane >= s0 + wide
        for t in below:
            new_left, new_right = left[t], right[t]
            for i in range(wide):
                new_left = new_left - columns[i][t] * scaled[i][0]
                new_right = new_right - columns[i][t] * scaled[i][1]
            if t == top:
                new_left = jnp.where(rest, new_left, left[t])
                new_right = jnp.where(rest, new_right, right[t])
                for i in range(wide):
                    new_right = jnp.where(sublane == s0 + i, eyes[i], new_right)
            left[t], right[t] = new_left, new_right
    for t in range(groups):
        root = lax.rsqrt(pivots[t])
        root = root * (1.5 - 0.5 * pivots[t] * root * root)
        right[t] = right[t] * root
    return jnp.concatenate(right, axis=0)


def iterate_body(total, gram_ref, start_ref, out_ref, gram):
    gram[...] = gram_ref[...] / total
    out_ref[...] = start_ref[...]

    def step(_, carry):
        product = full_dot(gram[...], out_ref[...], (1, 0))
        inverse = inverse_factor(full_dot(product, product, (0, 0)))
        out_ref[...] = full_dot(product, inverse, (1, 1))
        return carry

    lax.fori_loop(0, ITERS, step, 0)


def iterate(gram_sum, start, total):
    width_x, rank = start.shape
    return pl.pallas_call(
        functools.partial(iterate_body, total),
        in_specs=[pl.BlockSpec(memory_space=pltpu.VMEM)] * 2,
        out_specs=pl.BlockSpec(memory_space=pltpu.VMEM),
        out_shape=jax.ShapeDtypeStruct((width_x, rank), F32),
        scratch_shapes=[pltpu.VMEM((width_x, width_x), F32)],
        compiler_params=pltpu.CompilerParams(vmem_limit_bytes=24 * MIB),
        name="subspace",
    )(gram_sum, start)


class Line:
    def __init__(self):
        self.ends = []

    def tied(self, value):
        if len(self.ends) >= WINDOW:
            value, _ = lax.optimization_barrier((value, self.ends[-WINDOW]))
        return value

    def send(self, value, axis, perm):
        got = lax.ppermute(value, axis, perm)
        self.ends.append(got)
        return got


def on_device(field, start):
    n = lax.axis_size("gx")
    m = lax.axis_size("yz")
    g = lax.axis_index("gx")
    q = lax.axis_index("yz")
    x_block, depth, y_block = field.shape
    width_x, width_y = x_block * n, y_block * m
    rank = start.shape[1]
    slab = depth // n
    chunks = CHUNKS if slab % (CHUNKS * m) == 0 else 1
    zc = slab // chunks
    zs = zc // m
    line = LINE if n % LINE == 0 else 1
    rest = n // line
    far = sorted(range(1, line), key=lambda a: abs(2 * a - line))
    shifts = [(a, b) for b in range(rest) for a in far] + [(0, b) for b in range(1, rest)]
    order = Line()

    def moved(index, a, b, sign):
        return (index // rest + sign * a) % line * rest + (index % rest + sign * b) % rest

    def gx_perm(a, b):
        return [(i, moved(i, a, b, 1)) for i in range(n)]

    state = {"cells": jnp.zeros((chunks * zs, m, width_x, y_block), F32), "cut": None}

    def to_gx(c, a, b, whole):
        source = order.tied(field)
        if len(order.ends) < WINDOW and state["cut"] is not None:
            source, _ = lax.optimization_barrier((field, state["cut"]))
        target = moved(g, a, b, 1)
        cut = lax.dynamic_slice_in_dim(source, target * slab + c * zc, zc, axis=1)
        cut = jnp.swapaxes(cut, 0, 1)
        state["cut"] = cut
        got = order.send(cut, "gx", gx_perm(a, b))
        return lax.dynamic_update_slice_in_dim(whole, got[:, None], moved(g, a, b, -1), axis=1)

    def to_yz(c, d, whole):
        cut = lax.dynamic_slice_in_dim(order.tied(whole), (q + d) % m * zs, zs, axis=0)
        got = order.send(cut, "yz", [(i, (i + d) % m) for i in range(m)])
        place = (c * zs, (q - d) % m, 0, 0)
        state["cells"] = lax.dynamic_update_slice(state["cells"], got[:, None], place)

    def keep_own(c, whole):
        own = lax.dynamic_slice_in_dim(whole, q * zs, zs, axis=0)
        state["cells"] = lax.dynamic_update_slice(state["cells"], own[:, None], (c * zs, q, 0, 0))

    gram_x = jnp.zeros((width_x, width_x), F32)
    before = None
    for c in range(chunks):
        whole = jnp.zeros((zc, n, x_block, y_block), F32)
        waiting = list(range(1, m)) if c else []
        for k, (a, b) in enumerate(shifts):
            whole = to_gx(c, a, b, whole)
            while waiting and (k + 1 == len(shifts) or k - 3 >= m - 1 - len(waiting)):
                to_yz(c - 1, waiting.pop(0), before)
                if k + 1 < len(shifts):
                    break
        own = lax.dynamic_slice_in_dim(field, g * slab + c * zc, zc, axis=1)
        own = jnp.swapaxes(own, 0, 1)[:, None]
        whole = lax.dynamic_update_slice_in_dim(whole, own, g, axis=1)
        before = whole.reshape(zc, width_x, y_block)
        gram_x = gram_of(before, gram_x)
        keep_own(c, before)
    for d in range(1, m):
        to_yz(chunks - 1, d, before)

    gram_x = lax.psum(gram_x, ("gx", "yz"))
    basis = iterate(gram_x, start, float(width_y * depth))
    partial_y = core_gram(state["cells"], basis) / float(rank * depth)
    rows_y = lax.psum_scatter(partial_y, "yz", scatter_dimension=0, tiled=True)
    width = width_y // n

    def block(index):
        return lax.dynamic_slice_in_dim(rows_y, index * width, width, axis=1)

    gram_y = block(g)
    for a, b in shifts:
        gram_y = gram_y + lax.ppermute(block(moved(g, a, b, 1)), "gx", gx_perm(a, b))
    return (basis, gram_y)


def solution(mesh):
    placed = (P("gx", None, "yz"), P())
    return jax.shard_map(
        on_device, mesh=mesh, in_specs=placed, out_specs=(P(), P("yz", "gx")), check_vma=False
    )
```

time: 1460 us -> 1110 us (0.76)
  blocking collectives: 730 us -> 0 us
  waiting for transfers between devices: 382 us -> 742 us
  matrix products: 133 us -> 0 us
  starting transfers between devices: 0.53 us -> 105 us
  other arithmetic: 91.6 us -> 4.44 us
  Pallas kernels: 0 us -> 79.3 us
  local copies, waits for them, and re-layouts: 107 us -> 152 us
    all_to_all x1 -> x0, blocking collectives: 730 us -> none  [on_device(): lax.all_to_all(field, 'gx', split_axis=1, concat_axis=0, tiled=True)]
    ppermute x0 -> x47, waiting for transfers between devices: none -> 577 us  [the longest x40 564 us: send(): got = lax.ppermute(value, axis, perm)]
    all_gather x1 -> x0, waiting for transfers between devices: 190 us -> none  [on_device(): piece = lax.all_gather(core, 'yz', axis=2, tiled=True)]
    dot_general x11 -> x0, matrix products: 131 us -> none  [the longest x1 60.5 us: on_device(): jnp.dot(flat, flat.T, precision=lax.Precision.HIGHEST, preferred_element_...]
    ppermute x0 -> x47, starting transfers between devices: none -> 105 us  [the longest x40 89.8 us: send(): got = lax.ppermute(value, axis, perm)]
    another operation x20 -> x0, other arithmetic: 91.6 us -> none  [the longest x12 49.7 us: orthonormal_rows(): lower = lax.linalg.cholesky(cross)]
    pallas_call x0 -> x6, Pallas kernels: none -> 79.3 us  [the longest x1 33.5 us: iterate(): pl.pallas_call(functools.partial(iterate_body, total), in_specs=[pl.Block...]
    unnamed x6 -> x32, local copies, waits for them, and re-layouts: 74.8 us -> 3.13 us
  transfers between devices with their start and end apart: 3 -> 49, of which waited for: 3 -> 22; matrix products, arithmetic and copies ran while one was open for 1% -> 12% of each run, Pallas kernels for 0% -> 5%
where the time goes in v1:
time: 1110 us; the launch traced here: 1100 us
  waiting for transfers between devices  742 us (67%)
  local copies, waits for them, and re-layouts  152 us (14%)
  starting transfers between devices  105 us (9%)
  Pallas kernels  79.3 us (7%)
  between operations  15.2 us (1%)
    ppermute x40, waiting for transfers between devices, send(): got = lax.ppermute(value, axis, perm)  564 us
    psum x1, waiting for transfers between devices, on_device(): gram_x = lax.psum(gram_x, ('gx', 'yz'))  121 us
    ppermute x40, starting transfers between devices, send(): got = lax.ppermute(value, axis, perm)  89.8 us
    transpose x27, local copies, waits for them, and re-layouts, to_gx(): cut = jnp.swapaxes(cut, 0, 1)  48.4 us
    reduce_scatter x1, waiting for transfers between devices, on_device(): rows_y = lax.psum_scatter(partial_y, 'yz', scatter_dimension=0, tiled=True)  43.5 us
    pallas_call x1, Pallas kernels, iterate(): pl.pallas_call(functools.partial(iterate_body, total), in_specs=[pl.Block...  33.5 us
    dynamic_update_slice x28, local copies, waits for them, and re-layouts, to_gx(): lax.dynamic_update_slice_in_dim(whole, got[:, None], moved(g, a, b, -1),...  32.3 us
    dynamic_update_slice x12, local copies, waits for them, and re-layouts, to_yz(): lax.dynamic_update_slice(state['cells'], got[:, None], place)  25.4 us
  transfers between devices with their start and end apart: 49, of which 22 were waited for; matrix products, arithmetic and copies ran while one was open for 12% of the time, Pallas kernels for 5%

profile of v1, /device:TPU:0, one launch (start us, length us, event | category | flops | bytes accessed | tf_op | source)
XLA Modules:
  0.0 1097.9 jit_solution(16505084071886078412)
XLA Ops:
  7.3 4.5 dynamic-slice_bitcast_fusion
  11.8 2.3 dynamic-slice_bitcast_fusion.30
  14.0 2.3 dynamic-slice_bitcast_fusion.29
  16.3 5.0 collective-permute-start
  21.4 2.3 dynamic-slice_bitcast_fusion.23
  24.0 2.3 dynamic-slice_bitcast_fusion.21
  27.8 2.0 collective-permute-start.10
  31.3 14.1 %collective-permute-done = f32[16,64,256]{2,0,1:T(8,128)} collective-permute-done((f32[16,64,256]{2,0,1:T(8,128)}, f32[16,64,256]{2,0,1:T(8,128)}, u32[]{:S(2)}, u32[]{:S(2)}) %collective-permute-start) | collective-permute-done | bytes 1048608 | tf_op jit(solution)/shard_map/ppermute | solution.py:243
  48.1 132.8 %collective-permute-done.6 = f32[16,64,256]{2,0,1:T(8,128)} collective-permute-done((f32[16,64,256]{2,0,1:T(8,128)}, f32[16,64,256]{2,0,1:T(8,128)}, u32[]{:S(2)}, u32[]{:S(2)}) %collective-permute-start.6) | collective-permute-done | bytes 1048608 | tf_op jit(solution)/shard_map/ppermute | solution.py:243
  183.6 3.8 collective-permute-start.9
  187.5 37.5 %collective-permute-done.10 = f32[16,64,256]{2,0,1:T(8,128)} collective-permute-done((f32[16,64,256]{2,0,1:T(8,128)}, f32[16,64,256]{2,0,1:T(8,128)}, u32[]{:S(2)}, u32[]{:S(2)}) %collective-permute-start.10) | collective-permute-done | bytes 1048608 | tf_op jit(solution)/shard_map/ppermute | solution.py:243
  230.3 1.9 copy_dynamic-update-slice_fusion.24
  234.2 2.0 copy_dynamic-update-slice_fusion.22
  236.2 1.9 copy_dynamic-update-slice_fusion.21
  240.1 7.3 collective-permute-done.1
  247.3 2.3 dynamic-slice_bitcast_fusion.27
  249.6 24.0 %collective-permute-start.2 = (f32[16,64,256]{2,0,1:T(8,128)}, f32[16,64,256]{2,0,1:T(8,128)S(1)}, u32[]{:S(2)}, u32[]{:S(2)}) collective-permute-start(f32[16,64,256]{2,0,1:T(8,128)} %dynamic-slice_bitcast_fusion.27), channel_id=1, source_target_pairs={{0,12},{4,8},{8,20},{12,16},{16,28},{20,24},{24,4},{28,0},{1,13},{... | collective-permute-start | bytes 3145736 | tf_op jit(solution)/shard_map/ppermute | solution.py:243
  273.6 40.9 %collective-permute-done.11 = f32[16,64,256]{2,0,1:T(8,128)S(1)} collective-permute-done((f32[16,64,256]{2,0,1:T(8,128)S(1)}, f32[16,64,256]{2,0,1:T(8,128)S(1)}, u32[]{:S(2)}, u32[]{:S(2)}) %collective-permute-start.11) | collective-permute-done | bytes 1048608 | tf_op jit(solution)/shard_map/ppermute | solution.py:243
  314.5 2.3 dynamic-slice_bitcast_fusion.18
  316.8 2.3 dynamic-slice_bitcast_fusion.17
  319.1 4.2 collective-permute-start.13
  332.2 11.1 %broadcast_in_dim.183 = f32[16,4,512,256]{3,2,1,0:T(8,128)} broadcast(f32[]{:T(128)} %constant.657.clone.1), dimensions={} | broadcast | bytes 33554436 | tf_op jit(solution)/shard_map/broadcast_in_dim | solution.py:272
  344.9 5.7 gram_x.4.before_ref
  352.0 15.4 %collective-permute-done.13 = f32[16,64,256]{2,0,1:T(8,128)S(1)} collective-permute-done((f32[16,64,256]{2,0,1:T(8,128)}, f32[16,64,256]{2,0,1:T(8,128)S(1)}, u32[]{:S(2)}, u32[]{:S(2)}) %collective-permute-start.13) | collective-permute-done | bytes 1048608 | tf_op jit(solution)/shard_map/ppermute | solution.py:243
  375.0 57.0 %collective-permute-done.3 = f32[16,64,256]{2,0,1:T(8,128)S(1)} collective-permute-done((f32[16,64,256]{2,0,1:T(8,128)S(1)}, f32[16,64,256]{2,0,1:T(8,128)S(1)}, u32[]{:S(2)}, u32[]{:S(2)}) %collective-permute-start.3) | collective-permute-done | bytes 1048608 | tf_op jit(solution)/shard_map/ppermute | solution.py:243
  436.5 19.8 %collective-permute-start.4 = (f32[16,64,256]{2,0,1:T(8,128)S(1)}, f32[16,64,256]{2,0,1:T(8,128)S(1)}, u32[]{:S(2)}, u32[]{:S(2)}) collective-permute-start(f32[16,64,256]{2,0,1:T(8,128)S(1)} %dynamic-slice_bitcast_fusion.25), channel_id=1, source_target_pairs={{0,12},{4,8},{8,20},{12,16},{16,28},{20,24},{24,4},{28,0},{1,13},{... | collective-permute-start | bytes 3145736 | tf_op jit(solution)/shard_map/ppermute | solution.py:243
  459.0 3.5 collective-permute-start.23
  465.8 13.6 %collective-permute-done.17 = f32[16,64,256]{2,0,1:T(8,128)S(1)} collective-permute-done((f32[16,64,256]{2,0,1:T(8,128)S(1)}, f32[16,64,256]{2,0,1:T(8,128)S(1)}, u32[]{:S(2)}, u32[]{:S(2)}) %collective-permute-start.17) | collective-permute-done | bytes 1048608 | tf_op jit(solution)/shard_map/ppermute | solution.py:243
  483.4 2.6 dynamic-slice_bitcast_fusion.24
  486.1 18.4 %collective-permute-done.19 = f32[16,64,256]{2,0,1:T(8,128)S(1)} collective-permute-done((f32[16,64,256]{2,0,1:T(8,128)S(1)}, f32[16,64,256]{2,0,1:T(8,128)S(1)}, u32[]{:S(2)}, u32[]{:S(2)}) %collective-permute-start.19) | collective-permute-done | bytes 1048608 | tf_op jit(solution)/shard_map/ppermute | solution.py:243
  507.4 18.1 %collective-permute-done.23 = f32[16,64,256]{2,0,1:T(8,128)S(1)} collective-permute-done((f32[16,64,256]{2,0,1:T(8,128)S(1)}, f32[16,64,256]{2,0,1:T(8,128)S(1)}, u32[]{:S(2)}, u32[]{:S(2)}) %collective-permute-start.23) | collective-permute-done | bytes 1048608 | tf_op jit(solution)/shard_map/ppermute | solution.py:243
  525.6 2.7 dynamic-slice_bitcast_fusion.8
  528.2 3.5 collective-permute-start.24
  531.7 2.3 dynamic-slice_bitcast_fusion.7
  539.3 5.7 gram_x.5.before_ref
  545.0 93.0 %collective-permute-done.26 = f32[16,64,256]{2,0,1:T(8,128)S(1)} collective-permute-done((f32[16,64,256]{2,0,1:T(8,128)}, f32[16,64,256]{2,0,1:T(8,128)S(1)}, u32[]{:S(2)}, u32[]{:S(2)}) %collective-permute-start.26) | collective-permute-done | bytes 1048608 | tf_op jit(solution)/shard_map/ppermute | solution.py:243
  641.1 2.3 dynamic-slice_bitcast_fusion.5
  643.4 2.3 copy_dynamic-update-slice_fusion.6
  647.1 40.2 %collective-permute-done.32 = f32[16,64,256]{2,0,1:T(8,128)S(1)} collective-permute-done((f32[16,64,256]{2,0,1:T(8,128)S(1)}, f32[16,64,256]{2,0,1:T(8,128)S(1)}, u32[]{:S(2)}, u32[]{:S(2)}) %collective-permute-start.32) | collective-permute-done | bytes 1048608 | tf_op jit(solution)/shard_map/ppermute | solution.py:243
  690.2 2.3 dynamic-slice_bitcast_fusion.4
  702.6 37.3 %collective-permute-done.21 = f32[16,64,256]{2,0,1:T(8,128)S(1)} collective-permute-done((f32[16,64,256]{2,0,1:T(8,128)S(1)}, f32[16,64,256]{2,0,1:T(8,128)S(1)}, u32[]{:S(2)}, u32[]{:S(2)}) %collective-permute-start.21) | collective-permute-done | bytes 1048608 | tf_op jit(solution)/shard_map/ppermute | solution.py:243
  740.9 2.0 collective-permute-start.35
  742.9 5.7 gram_x.6.before_ref
  752.6 31.7 %collective-permute-done.28 = f32[16,64,256]{2,0,1:T(8,128)S(1)} collective-permute-done((f32[16,64,256]{2,0,1:T(8,128)S(1)}, f32[16,64,256]{2,0,1:T(8,128)S(1)}, u32[]{:S(2)}, u32[]{:S(2)}) %collective-permute-start.28) | collective-permute-done | bytes 1048608 | tf_op jit(solution)/shard_map/ppermute | solution.py:243
  791.5 4.9 collective-permute-done.34
  799.4 2.0 bitcast_dynamic-update-slice_fusion.12
  809.9 6.7 gram_x.7
  819.9 3.0 bitcast_dynamic-update-slice_fusion.10
  823.0 3.0 bitcast_dynamic-update-slice_fusion.9
  826.0 121.1 %all-reduce.2.cloned.1.call-done.gram_ref = f32[512,512]{1,0:T(8,128)} async-done(((f32[512,512]{1,0:T(8,128)}), f32[512,512]{1,0:T(8,128)}) %all-reduce.2.cloned.1.call-update) | async-done | bytes 1048592 | tf_op jit(solution)/shard_map/psum | solution.py:315
  948.4 33.5 %subspace.1.basis_ref = f32[512,128]{1,0:T(8,128)} custom-call(f32[512,512]{1,0:T(8,128)S(1)} %copy-done.1, f32[512,128]{1,0:T(8,128)S(1)} %copy-done.2), custom_call_target="tpu_custom_call" | custom-call | tf_op jit(solution)/shard_map/subspace/pallas_call | solution.py:222
  981.8 3.2 bitcast_dynamic-update-slice_fusion.1
  985.0 3.1 bitcast_dynamic-update-slice_fusion
  988.1 3.0 bitcast_dynamic-update-slice_fusion.8.field_ref
  991.2 21.9 %core_gram_y.1 = f32[1024,1024]{1,0:T(8,128)S(1)} custom-call(f32[16,4,512,256]{3,2,1,0:T(8,128)} %bitcast_dynamic-update-slice_fusion.8.field_ref, f32[512,128]{1,0:T(8,128)S(1)} %copy-done.3), custom_call_target="tpu_custom_call" | custom-call | flops 15032385536 | bytes 33554432 | tf_op jit(solution)/shard_map/core_gram_y/pallas_call | solution.py:115
  1013.1 2.8 broadcast_multiply_fusion
  1016.0 43.5 %reduce-scatter.2.cloned.1.call-done = f32[256,1024]{1,0:T(8,128)} async-done(((f32[1024,1024]{1,0:T(8,128)}), f32[256,1024]{1,0:T(8,128)}) %reduce-scatter.2.cloned.1.call-update) | async-done | bytes 1048592 | tf_op jit(solution)/shard_map/reduce_scatter | solution.py:318
  1062.3 3.3 collective-permute-start.45
  1065.6 2.0 collective-permute-start.43
  1067.6 2.8 collective-permute-start.42
  1070.9 5.0 collective-permute-start.40
  1075.9 2.9 collective-permute-done.43
  1078.8 4.1 collective-permute-done.41
  1082.9 6.1 collective-permute-done.40
  (171 shorter events, 110.4 us)
Async XLA Ops:
  7.2 940.0 %all-reduce.2.cloned.1.call-start = ((), (), s32[]{:S(2)}) async-start(), calls=%async_computation.1 | async-start | bytes 2097152 | tf_op jit(solution)/shard_map/psum | solution.py:315
  16.3 29.0 %collective-permute-start = (f32[16,64,256]{2,0,1:T(8,128)}, f32[16,64,256]{2,0,1:T(8,128)}, u32[]{:S(2)}, u32[]{:S(2)}) collective-permute-start(f32[16,64,256]{2,0,1:T(8,128)} %dynamic-slice_bitcast_fusion.29), channel_id=1, source_target_pairs={{0,24},{4,28},{8,0},{12,4},{16,8},{20,12},{24,16},{28,20},{1,25},{... | collective-permute-start | bytes 3145736 | tf_op jit(solution)/shard_map/ppermute | solution.py:243
  23.6 157.3 %collective-permute-start.6 = (f32[16,64,256]{2,0,1:T(8,128)}, f32[16,64,256]{2,0,1:T(8,128)}, u32[]{:S(2)}, u32[]{:S(2)}) collective-permute-start(f32[16,64,256]{2,0,1:T(8,128)} %dynamic-slice_bitcast_fusion.23), channel_id=1, source_target_pairs={{0,20},{4,16},{8,28},{12,24},{16,4},{20,0},{24,12},{28,8},{1,21},{... | collective-permute-start | bytes 3145736 | tf_op jit(solution)/shard_map/ppermute | solution.py:243
  26.3 156.0 %collective-permute-start.8 = (f32[16,64,256]{2,0,1:T(8,128)}, f32[16,64,256]{2,0,1:T(8,128)}, u32[]{:S(2)}, u32[]{:S(2)}) collective-permute-start(f32[16,64,256]{2,0,1:T(8,128)} %dynamic-slice_bitcast_fusion.21), channel_id=1, source_target_pairs={{0,12},{4,8},{8,20},{12,16},{16,28},{20,24},{24,4},{28,0},{1,13},{... | collective-permute-start | bytes 3145736 | tf_op jit(solution)/shard_map/ppermute | solution.py:243
  27.8 197.2 %collective-permute-start.10 = (f32[16,64,256]{2,0,1:T(8,128)}, f32[16,64,256]{2,0,1:T(8,128)}, u32[]{:S(2)}, u32[]{:S(2)}) collective-permute-start(f32[16,64,256]{2,0,1:T(8,128)} %get-tuple-element.84), channel_id=1, source_target_pairs={{0,16},{4,20},{8,24},{12,28},{16,0},{20,4},{24,8},{28,12},{1,17},{... | collective-permute-start | bytes 3145736 | tf_op jit(solution)/shard_map/ppermute | solution.py:243
  29.8 196.6 %collective-permute-start.14 = (f32[16,64,256]{2,0,1:T(8,128)}, f32[16,64,256]{2,0,1:T(8,128)}, u32[]{:S(2)}, u32[]{:S(2)}) collective-permute-start(f32[16,64,256]{2,0,1:T(8,128)} %dynamic-slice_bitcast_fusion.30), channel_id=1, source_target_pairs={{0,8},{4,12},{8,16},{12,20},{16,24},{20,28},{24,0},{28,4},{1,9},{5... | collective-permute-start | bytes 3145736 | tf_op jit(solution)/shard_map/ppermute | solution.py:243
  46.6 200.7 %collective-permute-start.1 = (f32[16,64,256]{2,0,1:T(8,128)S(1)}, f32[16,64,256]{2,0,1:T(8,128)S(1)}, u32[]{:S(2)}, u32[]{:S(2)}) collective-permute-start(f32[16,64,256]{2,0,1:T(8,128)S(1)} %dynamic-slice_bitcast_fusion.28), channel_id=1, source_target_pairs={{0,16},{4,20},{8,24},{12,28},{16,0},{20,4},{24,8},{28,12},{1,17},{... | collective-permute-start | bytes 3145736 | tf_op jit(solution)/shard_map/ppermute | solution.py:243
  182.2 145.1 %collective-permute-start.7 = (f32[16,64,256]{2,0,1:T(8,128)S(1)}, f32[16,64,256]{2,0,1:T(8,128)S(1)}, u32[]{:S(2)}, u32[]{:S(2)}) collective-permute-start(f32[16,64,256]{2,0,1:T(8,128)S(1)} %dynamic-slice_bitcast_fusion.22), channel_id=1, source_target_pairs={{0,8},{4,12},{8,16},{12,20},{16,24},{20,28},{24,0},{28,4},{1,9},{5... | collective-permute-start | bytes 3145736 | tf_op jit(solution)/shard_map/ppermute | solution.py:243
  183.6 133.2 %collective-permute-start.9 = (f32[16,64,256]{2,0,1:T(8,128)S(1)}, f32[16,64,256]{2,0,1:T(8,128)S(1)}, u32[]{:S(2)}, u32[]{:S(2)}) collective-permute-start(f32[16,64,256]{2,0,1:T(8,128)S(1)} %dynamic-slice_bitcast_fusion.20), channel_id=1, source_target_pairs={{0,24},{4,28},{8,0},{12,4},{16,8},{20,12},{24,16},{28,20},{1,25},{... | collective-permute-start | bytes 3145736 | tf_op jit(solution)/shard_map/ppermute | solution.py:243
  226.3 88.2 %collective-permute-start.11 = (f32[16,64,256]{2,0,1:T(8,128)S(1)}, f32[16,64,256]{2,0,1:T(8,128)S(1)}, u32[]{:S(2)}, u32[]{:S(2)}) collective-permute-start(f32[16,64,256]{2,0,1:T(8,128)S(1)} %dynamic-slice_bitcast_fusion.19), channel_id=1, source_target_pairs={{0,28},{4,24},{8,4},{12,0},{16,12},{20,8},{24,20},{28,16},{1,29},{... | collective-permute-start | bytes 3145736 | tf_op jit(solution)/shard_map/ppermute | solution.py:243
  227.7 96.3 %collective-permute-start.15 = (f32[16,64,256]{2,0,1:T(8,128)S(1)}, f32[16,64,256]{2,0,1:T(8,128)S(1)}, u32[]{:S(2)}, u32[]{:S(2)}) collective-permute-start(f32[16,64,256]{2,0,1:T(8,128)S(1)} %dynamic-slice_bitcast_fusion.16), channel_id=1, source_target_pairs={{0,4},{4,0},{8,12},{12,8},{16,20},{20,16},{24,28},{28,24},{1,5},{5... | collective-permute-start | bytes 3145736 | tf_op jit(solution)/shard_map/ppermute | solution.py:243
  234.2 90.5 %copy-start.4 = (f32[16,1,64,256]{3,0,2,1:T(8,128)S(1)}, f32[16,1,64,256]{3,0,2,1:T(8,128)}, u32[]{:S(2)}) copy-start(f32[16,1,64,256]{3,0,2,1:T(8,128)} %get-tuple-element.83) | copy-start | bytes 3145732
  249.6 101.0 %collective-permute-start.2 = (f32[16,64,256]{2,0,1:T(8,128)}, f32[16,64,256]{2,0,1:T(8,128)S(1)}, u32[]{:S(2)}, u32[]{:S(2)}) collective-permute-start(f32[16,64,256]{2,0,1:T(8,128)} %dynamic-slice_bitcast_fusion.27), channel_id=1, source_target_pairs={{0,12},{4,8},{8,20},{12,16},{16,28},{20,24},{24,4},{28,0},{1,13},{... | collective-permute-start | bytes 3145736 | tf_op jit(solution)/shard_map/ppermute | solution.py:243
  316.8 52.4 %collective-permute-start.12 = (f32[16,64,256]{2,0,1:T(8,128)}, f32[16,64,256]{2,0,1:T(8,128)S(1)}, u32[]{:S(2)}, u32[]{:S(2)}) collective-permute-start(f32[16,64,256]{2,0,1:T(8,128)} %dynamic-slice_bitcast_fusion.18), channel_id=1, source_target_pairs={{0,20},{4,16},{8,28},{12,24},{16,4},{20,0},{24,12},{28,8},{1,21},{... | collective-permute-start | bytes 3145736 | tf_op jit(solution)/shard_map/ppermute | solution.py:243
  319.1 48.4 %collective-permute-start.13 = (f32[16,64,256]{2,0,1:T(8,128)}, f32[16,64,256]{2,0,1:T(8,128)S(1)}, u32[]{:S(2)}, u32[]{:S(2)}) collective-permute-start(f32[16,64,256]{2,0,1:T(8,128)} %dynamic-slice_bitcast_fusion.17), channel_id=1, source_target_pairs={{0,28},{4,24},{8,4},{12,0},{16,12},{20,8},{24,20},{28,16},{1,29},{... | collective-permute-start | bytes 3145736 | tf_op jit(solution)/shard_map/ppermute | solution.py:243
  326.9 105.2 %collective-permute-start.16 = (f32[4,512,256]{2,1,0:T(8,128)}, f32[4,512,256]{2,1,0:T(8,128)S(1)}, u32[]{:S(2)}, u32[]{:S(2)}) collective-permute-start(f32[4,512,256]{2,1,0:T(8,128)} %constant_dynamic-slice_fusion.18), channel_id=1, source_target_pairs={{0,1},{1,2},{2,3},{3,0},{4,5},{5,6},{6,7},{7,4},{8,9},{9,10},{10,1... | collective-permute-start | bytes 6291464 | tf_op jit(solution)/shard_map/ppermute | solution.py:243
  327.5 128.9 %collective-permute-start.18 = (f32[4,512,256]{2,1,0:T(8,128)S(1)}, f32[4,512,256]{2,1,0:T(8,128)S(1)}, u32[]{:S(2)}, u32[]{:S(2)}) collective-permute-start(f32[4,512,256]{2,1,0:T(8,128)S(1)} %constant_dynamic-slice_fusion.17), channel_id=1, source_target_pairs={{0,2},{1,3},{2,0},{3,1},{4,6},{5,7},{6,4},{7,5},{8,10},{9,11},{10,... | collective-permute-start | bytes 6291464 | tf_op jit(solution)/shard_map/ppermute | solution.py:243
  352.0 80.1 %collective-permute-start.3 = (f32[16,64,256]{2,0,1:T(8,128)S(1)}, f32[16,64,256]{2,0,1:T(8,128)S(1)}, u32[]{:S(2)}, u32[]{:S(2)}) collective-permute-start(f32[16,64,256]{2,0,1:T(8,128)S(1)} %dynamic-slice_bitcast_fusion.26), channel_id=1, source_target_pairs={{0,16},{4,20},{8,24},{12,28},{16,0},{20,4},{24,8},{28,12},{1,17},{... | collective-permute-start | bytes 3145736 | tf_op jit(solution)/shard_map/ppermute | solution.py:243
  367.5 1.8 copy-start.12
  369.1 88.6 %collective-permute-start.22 = (f32[16,64,256]{2,0,1:T(8,128)S(1)}, f32[16,64,256]{2,0,1:T(8,128)S(1)}, u32[]{:S(2)}, u32[]{:S(2)}) collective-permute-start(f32[16,64,256]{2,0,1:T(8,128)S(1)} %dynamic-slice_bitcast_fusion.10), channel_id=1, source_target_pairs={{0,24},{4,28},{8,0},{12,4},{16,8},{20,12},{24,16},{28,20},{1,25},{... | collective-permute-start | bytes 3145736 | tf_op jit(solution)/shard_map/ppermute | solution.py:243
  369.2 1.0 copy-start.11
  370.4 161.4 %collective-permute-start.25 = (f32[4,512,256]{2,1,0:T(8,128)S(1)}, f32[4,512,256]{2,1,0:T(8,128)S(1)}, u32[]{:S(2)}, u32[]{:S(2)}) collective-permute-start(f32[4,512,256]{2,1,0:T(8,128)S(1)} %constant_dynamic-slice_fusion.15), channel_id=1, source_target_pairs={{0,3},{1,0},{2,1},{3,2},{4,7},{5,4},{6,5},{7,6},{8,11},{9,8},{10,9... | collective-permute-start | bytes 6291464 | tf_op jit(solution)/shard_map/ppermute | solution.py:243
  433.3 46.0 %collective-permute-start.17 = (f32[16,64,256]{2,0,1:T(8,128)S(1)}, f32[16,64,256]{2,0,1:T(8,128)S(1)}, u32[]{:S(2)}, u32[]{:S(2)}) collective-permute-start(f32[16,64,256]{2,0,1:T(8,128)S(1)} %dynamic-slice_bitcast_fusion.14), channel_id=1, source_target_pairs={{0,4},{4,0},{8,12},{12,8},{16,20},{20,16},{24,28},{28,24},{1,5},{5... | collective-permute-start | bytes 3145736 | tf_op jit(solution)/shard_map/ppermute | solution.py:243
  436.5 46.9 %collective-permute-start.4 = (f32[16,64,256]{2,0,1:T(8,128)S(1)}, f32[16,64,256]{2,0,1:T(8,128)S(1)}, u32[]{:S(2)}, u32[]{:S(2)}) collective-permute-start(f32[16,64,256]{2,0,1:T(8,128)S(1)} %dynamic-slice_bitcast_fusion.25), channel_id=1, source_target_pairs={{0,12},{4,8},{8,20},{12,16},{16,28},{20,24},{24,4},{28,0},{1,13},{... | collective-permute-start | bytes 3145736 | tf_op jit(solution)/shard_map/ppermute | solution.py:243
  457.6 46.9 %collective-permute-start.19 = (f32[16,64,256]{2,0,1:T(8,128)S(1)}, f32[16,64,256]{2,0,1:T(8,128)S(1)}, u32[]{:S(2)}, u32[]{:S(2)}) collective-permute-start(f32[16,64,256]{2,0,1:T(8,128)S(1)} %dynamic-slice_bitcast_fusion.12), channel_id=1, source_target_pairs={{0,8},{4,12},{8,16},{12,20},{16,24},{20,28},{24,0},{28,4},{1,9},{5... | collective-permute-start | bytes 3145736 | tf_op jit(solution)/shard_map/ppermute | solution.py:243
  459.0 66.5 %collective-permute-start.23 = (f32[16,64,256]{2,0,1:T(8,128)S(1)}, f32[16,64,256]{2,0,1:T(8,128)S(1)}, u32[]{:S(2)}, u32[]{:S(2)}) collective-permute-start(f32[16,64,256]{2,0,1:T(8,128)S(1)} %dynamic-slice_bitcast_fusion.9), channel_id=1, source_target_pairs={{0,28},{4,24},{8,4},{12,0},{16,12},{20,8},{24,20},{28,16},{1,29},{... | collective-permute-start | bytes 3145736 | tf_op jit(solution)/shard_map/ppermute | solution.py:243
  480.9 157.1 %collective-permute-start.31 = (f32[4,512,256]{2,1,0:T(8,128)S(1)}, f32[4,512,256]{2,1,0:T(8,128)S(1)}, u32[]{:S(2)}, u32[]{:S(2)}) collective-permute-start(f32[4,512,256]{2,1,0:T(8,128)S(1)} %constant_dynamic-slice_fusion.13), channel_id=1, source_target_pairs={{0,1},{1,2},{2,3},{3,0},{4,5},{5,6},{6,7},{7,4},{8,9},{9,10},{10,1... | collective-permute-start | bytes 6291464 | tf_op jit(solution)/shard_map/ppermute | solution.py:243
  483.4 21.1 %copy-start.7 = (f32[16,64,256]{2,0,1:T(8,128)}, f32[16,64,256]{2,0,1:T(8,128)S(1)}, u32[]{:S(2)}) copy-start(f32[16,64,256]{2,0,1:T(8,128)S(1)} %collective-permute-done.4) | copy-start | bytes 3145732
  486.1 155.0 %collective-permute-start.5 = (f32[16,64,256]{2,0,1:T(8,128)}, f32[16,64,256]{2,0,1:T(8,128)S(1)}, u32[]{:S(2)}, u32[]{:S(2)}) collective-permute-start(f32[16,64,256]{2,0,1:T(8,128)} %dynamic-slice_bitcast_fusion.24), channel_id=1, source_target_pairs={{0,16},{4,20},{8,24},{12,28},{16,0},{20,4},{24,8},{28,12},{1,17},{... | collective-permute-start | bytes 3145736 | tf_op jit(solution)/shard_map/ppermute | solution.py:243
  505.9 188.3 %collective-permute-start.20 = (f32[4,512,256]{2,1,0:T(8,128)}, f32[4,512,256]{2,1,0:T(8,128)S(1)}, u32[]{:S(2)}, u32[]{:S(2)}) collective-permute-start(f32[4,512,256]{2,1,0:T(8,128)} %constant_dynamic-slice_fusion.16), channel_id=1, source_target_pairs={{0,2},{1,3},{2,0},{3,1},{4,6},{5,7},{6,4},{7,5},{8,10},{9,11},{10,... | collective-permute-start | bytes 6291464 | tf_op jit(solution)/shard_map/ppermute | solution.py:243
  525.6 12.3 %copy-start.9 = (f32[16,64,256]{2,0,1:T(8,128)}, f32[16,64,256]{2,0,1:T(8,128)S(1)}, u32[]{:S(2)}) copy-start(f32[16,64,256]{2,0,1:T(8,128)S(1)} %collective-permute-done.23) | copy-start | bytes 3145732
  528.2 115.1 %collective-permute-start.24 = (f32[16,64,256]{2,0,1:T(8,128)}, f32[16,64,256]{2,0,1:T(8,128)S(1)}, u32[]{:S(2)}, u32[]{:S(2)}) collective-permute-start(f32[16,64,256]{2,0,1:T(8,128)} %dynamic-slice_bitcast_fusion.8), channel_id=1, source_target_pairs={{0,24},{4,28},{8,0},{12,4},{16,8},{20,12},{24,16},{28,20},{1,25},{... | collective-permute-start | bytes 3145736 | tf_op jit(solution)/shard_map/ppermute | solution.py:243
  534.0 104.0 %collective-permute-start.26 = (f32[16,64,256]{2,0,1:T(8,128)}, f32[16,64,256]{2,0,1:T(8,128)S(1)}, u32[]{:S(2)}, u32[]{:S(2)}) collective-permute-start(f32[16,64,256]{2,0,1:T(8,128)} %dynamic-slice_bitcast_fusion.7), channel_id=1, source_target_pairs={{0,20},{4,16},{8,28},{12,24},{16,4},{20,0},{24,12},{28,8},{1,21},{... | collective-permute-start | bytes 3145736 | tf_op jit(solution)/shard_map/ppermute | solution.py:243
  545.0 100.7 %copy-start.8 = (f32[16,64,256]{2,0,1:T(8,128)S(1)}, f32[16,64,256]{2,0,1:T(8,128)}, u32[]{:S(2)}) copy-start(f32[16,64,256]{2,0,1:T(8,128)} %copy-done.7) | copy-start | bytes 3145732
  545.0 101.4 %copy-start.10 = (f32[16,64,256]{2,0,1:T(8,128)S(1)}, f32[16,64,256]{2,0,1:T(8,128)}, u32[]{:S(2)}) copy-start(f32[16,64,256]{2,0,1:T(8,128)} %copy-done.9) | copy-start | bytes 3145732
  638.0 2.0 copy-start.13
  639.7 47.6 %collective-permute-start.32 = (f32[16,64,256]{2,0,1:T(8,128)S(1)}, f32[16,64,256]{2,0,1:T(8,128)S(1)}, u32[]{:S(2)}, u32[]{:S(2)}) collective-permute-start(f32[16,64,256]{2,0,1:T(8,128)S(1)} %dynamic-slice_bitcast_fusion.3), channel_id=1, source_target_pairs={{0,4},{4,0},{8,12},{12,8},{16,20},{20,16},{24,28},{28,24},{1,5},{5... | collective-permute-start | bytes 3145736 | tf_op jit(solution)/shard_map/ppermute | solution.py:243
  640.1 60.6 %collective-permute-start.27 = (f32[4,512,256]{2,1,0:T(8,128)S(1)}, f32[4,512,256]{2,1,0:T(8,128)S(1)}, u32[]{:S(2)}, u32[]{:S(2)}) collective-permute-start(f32[4,512,256]{2,1,0:T(8,128)S(1)} %constant_dynamic-slice_fusion.14), channel_id=1, source_target_pairs={{0,3},{1,0},{2,1},{3,2},{4,7},{5,4},{6,5},{7,6},{8,11},{9,8},{10,9... | collective-permute-start | bytes 6291464 | tf_op jit(solution)/shard_map/ppermute | solution.py:243
  643.4 144.2 %collective-permute-start.29 = (f32[16,64,256]{2,0,1:T(8,128)}, f32[16,64,256]{2,0,1:T(8,128)}, u32[]{:S(2)}, u32[]{:S(2)}) collective-permute-start(f32[16,64,256]{2,0,1:T(8,128)} %dynamic-slice_bitcast_fusion.5), channel_id=1, source_target_pairs={{0,12},{4,8},{8,20},{12,16},{16,28},{20,24},{24,4},{28,0},{1,13},{... | collective-permute-start | bytes 3145736 | tf_op jit(solution)/shard_map/ppermute | solution.py:243
  643.4 45.3 %copy-start.5 = (f32[16,64,256]{2,0,1:T(8,128)}, f32[16,64,256]{2,0,1:T(8,128)S(1)}, u32[]{:S(2)}) copy-start(f32[16,64,256]{2,0,1:T(8,128)S(1)} %collective-permute-done.24) | copy-start | bytes 3145732
  690.2 59.2 %collective-permute-start.33 = (f32[4,512,256]{2,1,0:T(8,128)}, f32[4,512,256]{2,1,0:T(8,128)S(1)}, u32[]{:S(2)}, u32[]{:S(2)}) collective-permute-start(f32[4,512,256]{2,1,0:T(8,128)} %constant_dynamic-slice_fusion.12), channel_id=1, source_target_pairs={{0,1},{1,2},{2,3},{3,0},{4,5},{5,6},{6,7},{7,4},{8,9},{9,10},{10,1... | collective-permute-start | bytes 6291464 | tf_op jit(solution)/shard_map/ppermute | solution.py:243
  692.5 97.0 %collective-permute-start.30 = (f32[16,64,256]{2,0,1:T(8,128)}, f32[16,64,256]{2,0,1:T(8,128)}, u32[]{:S(2)}, u32[]{:S(2)}) collective-permute-start(f32[16,64,256]{2,0,1:T(8,128)} %dynamic-slice_bitcast_fusion.4), channel_id=1, source_target_pairs={{0,28},{4,24},{8,4},{12,0},{16,12},{20,8},{24,20},{28,16},{1,29},{... | collective-permute-start | bytes 3145736 | tf_op jit(solution)/shard_map/ppermute | solution.py:243
  695.5 44.4 %collective-permute-start.21 = (f32[16,64,256]{2,0,1:T(8,128)S(1)}, f32[16,64,256]{2,0,1:T(8,128)S(1)}, u32[]{:S(2)}, u32[]{:S(2)}) collective-permute-start(f32[16,64,256]{2,0,1:T(8,128)S(1)} %dynamic-slice_bitcast_fusion.11), channel_id=1, source_target_pairs={{0,8},{4,12},{8,16},{12,20},{16,24},{20,28},{24,0},{28,4},{1,9},{5... | collective-permute-start | bytes 3145736 | tf_op jit(solution)/shard_map/ppermute | solution.py:243
  702.0 82.3 %collective-permute-start.28 = (f32[16,64,256]{2,0,1:T(8,128)S(1)}, f32[16,64,256]{2,0,1:T(8,128)S(1)}, u32[]{:S(2)}, u32[]{:S(2)}) collective-permute-start(f32[16,64,256]{2,0,1:T(8,128)S(1)} %dynamic-slice_bitcast_fusion.6), channel_id=1, source_target_pairs={{0,20},{4,16},{8,28},{12,24},{16,4},{20,0},{24,12},{28,8},{1,21},{... | collective-permute-start | bytes 3145736 | tf_op jit(solution)/shard_map/ppermute | solution.py:243
  740.9 11.1 %copy-start.6 = (f32[16,64,256]{2,0,1:T(8,128)S(1)}, f32[16,64,256]{2,0,1:T(8,128)}, u32[]{:S(2)}) copy-start(f32[16,64,256]{2,0,1:T(8,128)} %copy-done.5) | copy-start | bytes 3145732
  740.9 60.4 %collective-permute-start.35 = (f32[4,512,256]{2,1,0:T(8,128)S(1)}, f32[4,512,256]{2,1,0:T(8,128)S(1)}, u32[]{:S(2)}, u32[]{:S(2)}) collective-permute-start(f32[4,512,256]{2,1,0:T(8,128)S(1)} %constant_dynamic-slice_fusion.10), channel_id=1, source_target_pairs={{0,2},{1,3},{2,0},{3,1},{4,6},{5,7},{6,4},{7,5},{8,10},{9,11},{10,... | collective-permute-start | bytes 6291464 | tf_op jit(solution)/shard_map/ppermute | solution.py:243
  742.9 5.8 copy-start.15
  750.7 45.7 %collective-permute-start.34 = (f32[16,64,256]{2,0,1:T(8,128)S(1)}, f32[16,64,256]{2,0,1:T(8,128)S(1)}, u32[]{:S(2)}, u32[]{:S(2)}) collective-permute-start(f32[16,64,256]{2,0,1:T(8,128)S(1)} %dynamic-slice_bitcast_fusion.1), channel_id=1, source_target_pairs={{0,4},{4,0},{8,12},{12,8},{16,20},{20,16},{24,28},{28,24},{1,5},{5... | collective-permute-start | bytes 3145736 | tf_op jit(solution)/shard_map/ppermute | solution.py:243
  785.8 34.1 %collective-permute-start.36 = (f32[4,512,256]{2,1,0:T(8,128)}, f32[4,512,256]{2,1,0:T(8,128)}, u32[]{:S(2)}, u32[]{:S(2)}) collective-permute-start(f32[4,512,256]{2,1,0:T(8,128)} %constant_dynamic-slice_fusion.9), channel_id=1, source_target_pairs={{0,3},{1,0},{2,1},{3,2},{4,7},{5,4},{6,5},{7,6},{8,11},{9,8},{10,9... | collective-permute-start | bytes 6291464 | tf_op jit(solution)/shard_map/ppermute | solution.py:243
  797.8 12.1 %copy-start = (f32[16,8,64,256]{3,2,1,0:T(8,128)}, f32[16,8,64,256]{3,2,1,0:T(8,128)S(1)}, u32[]{:S(2)}) copy-start(f32[16,8,64,256]{3,2,1,0:T(8,128)S(1)} %copy_dynamic-update-slice_fusion) | copy-start | bytes 25165828
  799.4 182.5 %collective-permute-start.37 = (f32[4,512,256]{2,1,0:T(8,128)}, f32[4,512,256]{2,1,0:T(8,128)}, u32[]{:S(2)}, u32[]{:S(2)}) collective-permute-start(f32[4,512,256]{2,1,0:T(8,128)} %constant_dynamic-slice_fusion.7), channel_id=1, source_target_pairs={{0,1},{1,2},{2,3},{3,0},{4,5},{5,6},{6,7},{7,4},{8,9},{9,10},{10,1... | collective-permute-start | bytes 6291464 | tf_op jit(solution)/shard_map/ppermute | solution.py:243
  802.9 182.1 %collective-permute-start.38 = (f32[4,512,256]{2,1,0:T(8,128)}, f32[4,512,256]{2,1,0:T(8,128)}, u32[]{:S(2)}, u32[]{:S(2)}) collective-permute-start(f32[4,512,256]{2,1,0:T(8,128)} %constant_dynamic-slice_fusion.6), channel_id=1, source_target_pairs={{0,2},{1,3},{2,0},{3,1},{4,6},{5,7},{6,4},{7,5},{8,10},{9,11},{10,... | collective-permute-start | bytes 6291464 | tf_op jit(solution)/shard_map/ppermute | solution.py:243
  807.2 180.9 %collective-permute-start.39 = (f32[4,512,256]{2,1,0:T(8,128)}, f32[4,512,256]{2,1,0:T(8,128)}, u32[]{:S(2)}, u32[]{:S(2)}) collective-permute-start(f32[4,512,256]{2,1,0:T(8,128)} %constant_dynamic-slice_fusion.5), channel_id=1, source_target_pairs={{0,3},{1,0},{2,1},{3,2},{4,7},{5,4},{6,5},{7,6},{8,11},{9,8},{10,9... | collective-permute-start | bytes 6291464 | tf_op jit(solution)/shard_map/ppermute | solution.py:243
  816.6 130.5 %copy-start.2 = (f32[512,128]{1,0:T(8,128)S(1)}, f32[512,128]{1,0:T(8,128)}, u32[]{:S(2)}) copy-start(f32[512,128]{1,0:T(8,128)} %start_ref.1) | copy-start | bytes 786436
  816.6 242.8 %reduce-scatter.2.cloned.1.call-start = ((), (), s32[]{:S(2)}) async-start(), calls=%async_computation.2 | async-start | bytes 5242880 | tf_op jit(solution)/shard_map/reduce_scatter | solution.py:318
  947.1 1.2 copy-start.1
  981.8 9.3 copy-start.3
  1060.8 9.6 collective-permute-start.46
  1062.3 8.6 collective-permute-start.45
  1065.6 10.3 collective-permute-start.44
  1065.6 13.2 %collective-permute-start.43 = (f32[256,128]{1,0:T(8,128)S(1)}, f32[256,128]{1,0:T(8,128)S(1)}, u32[]{:S(2)}, u32[]{:S(2)}) collective-permute-start(f32[256,128]{1,0:T(8,128)S(1)} %get-tuple-element.89), channel_id=1, source_target_pairs={{0,20},{4,16},{8,28},{12,24},{16,4},{20,0},{24,12},{28,8},{1,21},{... | collective-permute-start | bytes 393224 | tf_op jit(solution)/shard_map/ppermute | solution.py:326
  1067.6 11.2 %collective-permute-start.42 = (f32[256,128]{1,0:T(8,128)S(1)}, f32[256,128]{1,0:T(8,128)S(1)}, u32[]{:S(2)}, u32[]{:S(2)}) collective-permute-start(f32[256,128]{1,0:T(8,128)S(1)} %get-tuple-element.90), channel_id=1, source_target_pairs={{0,24},{4,28},{8,0},{12,4},{16,8},{20,12},{24,16},{28,20},{1,25},{... | collective-permute-start | bytes 393224 | tf_op jit(solution)/shard_map/ppermute | solution.py:326
  1070.4 12.5 %collective-permute-start.41 = (f32[256,128]{1,0:T(8,128)S(1)}, f32[256,128]{1,0:T(8,128)S(1)}, u32[]{:S(2)}, u32[]{:S(2)}) collective-permute-start(f32[256,128]{1,0:T(8,128)S(1)} %get-tuple-element.91), channel_id=1, source_target_pairs={{0,8},{4,12},{8,16},{12,20},{16,24},{20,28},{24,0},{28,4},{1,9},{5... | collective-permute-start | bytes 393224 | tf_op jit(solution)/shard_map/ppermute | solution.py:326
  1070.9 18.0 %collective-permute-start.40 = (f32[256,128]{1,0:T(8,128)S(1)}, f32[256,128]{1,0:T(8,128)S(1)}, u32[]{:S(2)}, u32[]{:S(2)}) collective-permute-start(f32[256,128]{1,0:T(8,128)S(1)} %get-tuple-element.85), channel_id=1, source_target_pairs={{0,16},{4,20},{8,24},{12,28},{16,0},{20,4},{24,8},{28,12},{1,17},{... | collective-permute-start | bytes 393224 | tf_op jit(solution)/shard_map/ppermute | solution.py:326
  (1 other events, 1.0 us)
Sparse Core Ops, SparseCore 0:
  816.7 130.3 all-reduce.1
  1016.1 43.3 reduce-scatter.1

commit v2 on v1

--- a/solution.py
+++ b/solution.py
@@ -73,7 +73,7 @@
     )(slab, before)
 
 
-def core_body(steps, field_ref, basis_ref, out_ref, stacked_ref, high_ref, low_ref, main, cross):
+def core_body(steps, total, field_ref, basis_ref, out_ref, stacked_ref, high_ref, low_ref, main, cross):
     step = pl.program_id(0)
     rank = basis_ref.shape[1]
 
@@ -103,17 +103,17 @@
     @pl.when(step == steps - 1)
     def _():
         mixed = cross[...]
-        out_ref[...] = main[...] + mixed + mixed.T
-
-
-def core_gram(cells, basis):
+        out_ref[...] = (main[...] + mixed + mixed.T) / total
+
+
+def core_gram(cells, basis, total):
     depth, blocks, width_x, width = cells.shape
     rank = basis.shape[1]
     width_y = blocks * width
     block = 2 if depth % 2 == 0 else 1
     steps = depth // block
     return pl.pallas_call(
-        functools.partial(core_body, steps),
+        functools.partial(core_body, steps, total),
         grid=(steps,),
         in_specs=[
             pl.BlockSpec((block, blocks, width_x, width), lambda i: (i, 0, 0, 0)),
@@ -204,8 +204,12 @@
     return jnp.concatenate(right, axis=0)
 
 
-def iterate_body(total, gram_ref, start_ref, out_ref, gram):
-    gram[...] = gram_ref[...] / total
+def iterate_body(total, places_ref, *refs):
+    *piece_refs, start_ref, out_ref, gram = refs
+    height = piece_refs[0].shape[0]
+    for i, piece_ref in enumerate(piece_refs):
+        place = pl.multiple_of(places_ref[i] * height, height)
+        gram[pl.ds(place, height)] = piece_ref[...] / total
     out_ref[...] = start_ref[...]
 
     def step(_, carry):
@@ -217,32 +221,61 @@
     lax.fori_loop(0, ITERS, step, 0)
 
 
-def iterate(gram_sum, start, total):
+def iterate(pieces, places, start, total):
     width_x, rank = start.shape
     return pl.pallas_call(
         functools.partial(iterate_body, total),
-        in_specs=[pl.BlockSpec(memory_space=pltpu.VMEM)] * 2,
+        in_specs=[pl.BlockSpec(memory_space=pltpu.SMEM)]
+        + [pl.BlockSpec(memory_space=pltpu.VMEM)] * (len(pieces) + 1),
         out_specs=pl.BlockSpec(memory_space=pltpu.VMEM),
         out_shape=jax.ShapeDtypeStruct((width_x, rank), F32),
         scratch_shapes=[pltpu.VMEM((width_x, width_x), F32)],
         compiler_params=pltpu.CompilerParams(vmem_limit_bytes=24 * MIB),
         name="subspace",
-    )(gram_sum, start)
+    )(places, *pieces, start)
+
+
+def stack_body(places_ref, *refs):
+    *piece_refs, out_ref = refs
+    for i, piece_ref in enumerate(piece_refs):
+        out_ref[places_ref[i]] = piece_ref[...]
+
+
+def stack(pieces, places):
+    return pl.pallas_call(
+        stack_body,
+        in_specs=[pl.BlockSpec(memory_space=pltpu.SMEM)]
+        + [pl.BlockSpec(memory_space=pltpu.VMEM)] * len(pieces),
+        out_specs=pl.BlockSpec(memory_space=pltpu.VMEM),
+        out_shape=jax.ShapeDtypeStruct((len(pieces),) + pieces[0].shape, F32),
+        compiler_params=pltpu.CompilerParams(vmem_limit_bytes=16 * MIB),
+        name="stack_rows",
+    )(places, *pieces)
+
+
+def tie(value, others):
+    return lax.optimization_barrier((value, *others))[0] if others else value
 
 
 class Line:
     def __init__(self):
         self.ends = []
 
-    def tied(self, value):
-        if len(self.ends) >= WINDOW:
-            value, _ = lax.optimization_barrier((value, self.ends[-WINDOW]))
-        return value
-
-    def send(self, value, axis, perm):
-        got = lax.ppermute(value, axis, perm)
+    def done(self, ahead):
+        last = len(self.ends) - WINDOW + 1 - ahead
+        return self.ends[max(0, last - WINDOW) : max(0, last)]
+
+    def send(self, cut, source, axis, perm):
+        value = cut(tie(source, self.done(2)))
+        got = lax.ppermute(tie(value, self.done(0)), axis, perm)
         self.ends.append(got)
         return got
+
+
+def chunk_depths(units):
+    last = max(1, units // 8)
+    others = min(CHUNKS - 1, units - last)
+    return [(units - last + k) // others for k in reversed(range(others))] + [last]
 
 
 def on_device(field, start):
@@ -254,68 +287,106 @@
     width_x, width_y = x_block * n, y_block * m
     rank = start.shape[1]
     slab = depth // n
-    chunks = CHUNKS if slab % (CHUNKS * m) == 0 else 1
-    zc = slab // chunks
-    zs = zc // m
     line = LINE if n % LINE == 0 else 1
     rest = n // line
+    order = Line()
+
+    def moved(index, a, b, sign=1):
+        return (index // rest + sign * a) % line * rest + (index % rest + sign * b) % rest
+
+    def gx_perm(a, b):
+        return [(i, moved(i, a, b)) for i in range(n)]
+
+    def yz_perm(d):
+        return [(i, (i + d) % m) for i in range(m)]
+
     far = sorted(range(1, line), key=lambda a: abs(2 * a - line))
-    shifts = [(a, b) for b in range(rest) for a in far] + [(0, b) for b in range(1, rest)]
-    order = Line()
-
-    def moved(index, a, b, sign):
-        return (index // rest + sign * a) % line * rest + (index % rest + sign * b) % rest
-
-    def gx_perm(a, b):
-        return [(i, moved(i, a, b, 1)) for i in range(n)]
-
-    state = {"cells": jnp.zeros((chunks * zs, m, width_x, y_block), F32), "cut": None}
-
-    def to_gx(c, a, b, whole):
-        source = order.tied(field)
-        if len(order.ends) < WINDOW and state["cut"] is not None:
-            source, _ = lax.optimization_barrier((field, state["cut"]))
-        target = moved(g, a, b, 1)
-        cut = lax.dynamic_slice_in_dim(source, target * slab + c * zc, zc, axis=1)
-        cut = jnp.swapaxes(cut, 0, 1)
-        state["cut"] = cut
-        got = order.send(cut, "gx", gx_perm(a, b))
+    shifts = [(a, (b + k) % rest) for b in range(rest) for k, a in enumerate(far)]
+    shifts[4:4] = [(0, b) for b in range(1, rest)]
+    turns = sorted(range(1, m), key=lambda d: abs(2 * d - m))
+
+    cells = jnp.zeros((slab // m, m, width_x, y_block), F32)
+
+    def to_gx(first, zc, a, b, whole):
+        def cut(source):
+            place = moved(g, a, b) * slab + first
+            return jnp.swapaxes(lax.dynamic_slice_in_dim(source, place, zc, axis=1), 0, 1)
+
+        got = order.send(cut, field, "gx", gx_perm(a, b))
         return lax.dynamic_update_slice_in_dim(whole, got[:, None], moved(g, a, b, -1), axis=1)
 
-    def to_yz(c, d, whole):
-        cut = lax.dynamic_slice_in_dim(order.tied(whole), (q + d) % m * zs, zs, axis=0)
-        got = order.send(cut, "yz", [(i, (i + d) % m) for i in range(m)])
-        place = (c * zs, (q - d) % m, 0, 0)
-        state["cells"] = lax.dynamic_update_slice(state["cells"], got[:, None], place)
-
-    def keep_own(c, whole):
-        own = lax.dynamic_slice_in_dim(whole, q * zs, zs, axis=0)
-        state["cells"] = lax.dynamic_update_slice(state["cells"], own[:, None], (c * zs, q, 0, 0))
-
-    gram_x = jnp.zeros((width_x, width_x), F32)
-    before = None
-    for c in range(chunks):
+    def to_yz(cells, first, d, whole):
+        zs = whole.shape[0] // m
+
+        def cut(source):
+            return lax.dynamic_slice_in_dim(source, (q + d) % m * zs, zs, axis=0)
+
+        got = order.send(cut, whole, "yz", yz_perm(d))
+        return lax.dynamic_update_slice(cells, got[:, None], (first // m, (q - d) % m, 0, 0))
+
+    gram = jnp.zeros((width_x, width_x), F32)
+    before, start_z, first = None, 0, 0
+    for units in chunk_depths(slab // m):
+        zc = units * m
         whole = jnp.zeros((zc, n, x_block, y_block), F32)
-        waiting = list(range(1, m)) if c else []
+        waiting = list(turns) if before is not None else []
         for k, (a, b) in enumerate(shifts):
-            whole = to_gx(c, a, b, whole)
-            while waiting and (k + 1 == len(shifts) or k - 3 >= m - 1 - len(waiting)):
-                to_yz(c - 1, waiting.pop(0), before)
-                if k + 1 < len(shifts):
-                    break
-        own = lax.dynamic_slice_in_dim(field, g * slab + c * zc, zc, axis=1)
+            whole = to_gx(first, zc, a, b, whole)
+            if k >= WINDOW - 1 and waiting:
+                cells = to_yz(cells, start_z, waiting.pop(0), before)
+        for d in waiting:
+            cells = to_yz(cells, start_z, d, before)
+        own = lax.dynamic_slice_in_dim(field, g * slab + first, zc, axis=1)
         own = jnp.swapaxes(own, 0, 1)[:, None]
         whole = lax.dynamic_update_slice_in_dim(whole, own, g, axis=1)
         before = whole.reshape(zc, width_x, y_block)
-        gram_x = gram_of(before, gram_x)
-        keep_own(c, before)
-    for d in range(1, m):
-        to_yz(chunks - 1, d, before)
-
-    gram_x = lax.psum(gram_x, ("gx", "yz"))
-    basis = iterate(gram_x, start, float(width_y * depth))
-    partial_y = core_gram(state["cells"], basis) / float(rank * depth)
-    rows_y = lax.psum_scatter(partial_y, "yz", scatter_dimension=0, tiled=True)
+        gram = gram_of(before, gram)
+        own = lax.dynamic_slice_in_dim(before, q * units, units, axis=0)
+        cells = lax.dynamic_update_slice(cells, own[:, None], (first // m, q, 0, 0))
+        start_z, first = first, first + zc
+
+    rows = width_x // m
+    slabs = gram.reshape(m, rows, width_x)
+
+    def pick(array, index):
+        return lax.dynamic_index_in_dim(array, index, axis=0, keepdims=False)
+
+    summed = pick(slabs, q)
+    for d in turns:
+        summed = summed + lax.ppermute(pick(slabs, (q + d) % m), "yz", yz_perm(d))
+    before = tie(before, [summed])
+    cells = to_yz(cells, start_z, turns[0], before)
+    strips = summed.reshape(n, rows // n, width_x)
+    summed = pick(strips, g)
+    for a, b in shifts:
+        summed = summed + lax.ppermute(pick(strips, moved(g, a, b)), "gx", gx_perm(a, b))
+    before = tie(before, [summed])
+    for d in turns[1:]:
+        cells = to_yz(cells, start_z, d, before)
+    pieces = [summed] + [lax.ppermute(summed, "gx", gx_perm(a, b)) for a, b in shifts]
+    places = jnp.stack([g] + [moved(g, a, b, -1) for a, b in shifts]).astype(jnp.int32)
+    summed = stack(pieces, places).reshape(rows, width_x)
+    pieces = [summed] + [lax.ppermute(summed, "yz", yz_perm(d)) for d in turns]
+    places = jnp.stack([q] + [(q - d) % m for d in turns]).astype(jnp.int32)
+    basis = iterate(pieces, places, start, float(width_y * depth))
+
+    partial_y = core_gram(cells, basis, float(rank * depth))
+    cores = 2 if m % 2 == 0 else 1
+    chips = m // cores
+    core, chip = q % cores, q // cores
+    blocks = partial_y.reshape(chips, cores, y_block, width_y)
+
+    def of_core(index):
+        return lax.dynamic_index_in_dim(blocks, index, axis=1, keepdims=False)
+
+    blocks_here = of_core(core)
+    for d in range(1, cores):
+        perm = [(i, i // cores * cores + (i + d) % cores) for i in range(m)]
+        blocks_here = blocks_here + lax.ppermute(of_core((core + d) % cores), "yz", perm)
+    rows_y = pick(blocks_here, chip)
+    for d in range(1, chips):
+        perm = [(i, (i + d * cores) % m) for i in range(m)]
+        rows_y = rows_y + lax.ppermute(pick(blocks_here, (chip + d) % chips), "yz", perm)
     width = width_y // n
 
     def block(index):
@@ -323,7 +394,7 @@
 
     gram_y = block(g)
     for a, b in shifts:
-        gram_y = gram_y + lax.ppermute(block(moved(g, a, b, 1)), "gx", gx_perm(a, b))
+        gram_y = gram_y + lax.ppermute(block(moved(g, a, b)), "gx", gx_perm(a, b))
     return (basis, gram_y)
 
 

time: 1110 us -> 1070 us (0.964)
  waiting for transfers between devices: 742 us -> 399 us
  local copies, waits for them, and re-layouts: 152 us -> 363 us
  starting transfers between devices: 105 us -> 210 us
  between operations: 15.2 us -> 2.11 us
    optimization_barrier x0 -> x7, local copies, waits for them, and re-layouts: none -> 223 us  [tie(): return lax.optimization_barrier((value, *others))[0] if others else value]
    ppermute x47 -> x69, waiting for transfers between devices: 577 us -> 399 us  [the longest x40 279 us: send(): got = lax.ppermute(tie(value, self.done(0)), axis, perm)]
    psum x1 -> x0, waiting for transfers between devices: 121 us -> none  [on_device(): gram_x = lax.psum(gram_x, ('gx', 'yz'))]
    ppermute x47 -> x69, starting transfers between devices: 105 us -> 210 us  [the longest x40 172 us: send(): got = lax.ppermute(tie(value, self.done(0)), axis, perm)]
    reduce_scatter x1 -> x0, waiting for transfers between devices: 43.5 us -> none  [on_device(): rows_y = lax.psum_scatter(partial_y, 'yz', scatter_dimension=0, tiled=True)]
    transpose x27 -> x22, local copies, waits for them, and re-layouts: 48.4 us -> 36.1 us  [cut(): jnp.swapaxes(lax.dynamic_slice_in_dim(source, place, zc, axis=1), 0, 1)]
    unnamed x32 -> x25, local copies, waits for them, and re-layouts: 3.13 us -> 15.1 us
    pallas_call x1 -> x2, Pallas kernels: 21.9 us -> 22.5 us  [the longest x1 21.9 us: core_gram(): pl.pallas_call(functools.partial(core_body, steps, total), grid=(steps,),...]
  transfers between devices with their start and end apart: 49 -> 69, of which waited for: 22 -> 29; matrix products, arithmetic and copies ran while one was open for 12% -> 32% of each run, Pallas kernels for 5% -> 5%
where the time goes in v2:
time: 1070 us; the launch traced here: 1060 us
  waiting for transfers between devices  399 us (37%)
  local copies, waits for them, and re-layouts  363 us (34%)
  starting transfers between devices  210 us (20%)
  Pallas kernels  80.2 us (7%)
    ppermute x40, waiting for transfers between devices, send(): got = lax.ppermute(tie(value, self.done(0)), axis, perm)  279 us
    optimization_barrier x7, local copies, waits for them, and re-layouts, tie(): return lax.optimization_barrier((value, *others))[0] if others else value  223 us
    ppermute x40, starting transfers between devices, send(): got = lax.ppermute(tie(value, self.done(0)), axis, perm)  172 us
    ppermute x3, waiting for transfers between devices, on_device(): pieces = [summed] + [lax.ppermute(summed, 'yz', yz_perm(d)) for d in turns]  56.7 us
    transpose x22, local copies, waits for them, and re-layouts, cut(): jnp.swapaxes(lax.dynamic_slice_in_dim(source, place, zc, axis=1), 0, 1)  36.1 us
    pallas_call x1, Pallas kernels, iterate(): pl.pallas_call(functools.partial(iterate_body, total), in_specs=[pl.Block...  34 us
    ppermute x1, waiting for transfers between devices, on_device(): lax.ppermute(pick(blocks_here, (chip + d) % chips), 'yz', perm)  24 us
    pallas_call x4, Pallas kernels, gram_of(): pl.pallas_call(functools.partial(gram_body, steps), grid=(steps,), in_spe...  23.7 us
  transfers between devices with their start and end apart: 69, of which 29 were waited for; matrix products, arithmetic and copies ran while one was open for 32% of the time, Pallas kernels for 5%

profile of v2, /device:TPU:0, one launch (start us, length us, event | category | flops | bytes accessed | tf_op | source)
XLA Modules:
  0.0 1059.5 jit_solution(9142199310073084020)
XLA Ops:
  0.8 9.2 dynamic-slice_bitcast_fusion.1
  11.5 4.0 collective-permute-start
  17.0 2.5 collective-permute-start.1
  28.7 2.3 dynamic-slice_bitcast_fusion.11
  33.2 69.3 %collective-permute-done = f32[20,64,256]{2,1,0:T(8,128)} collective-permute-done((f32[20,64,256]{2,1,0:T(8,128)}, f32[20,64,256]{2,1,0:T(8,128)}, u32[]{:S(2)}, u32[]{:S(2)}) %collective-permute-start) | collective-permute-done | bytes 1310752 | tf_op jit(solution)/shard_map/ppermute | solution.py:270
  102.5 5.9 collective-permute-start.6
  108.4 31.8 %copy.59 = f32[64,512,256]{2,0,1:T(8,128)} copy(f32[64,512,256]{2,1,0:T(8,128)} %param.2) | data formatting | bytes 67108864 | tf_op jit(solution)/shard_map/optimization_barrier | solution.py:257
  141.6 53.7 %collective-permute-start.7 = (f32[20,64,256]{2,1,0:T(8,128)S(1)}, f32[20,64,256]{2,1,0:T(8,128)S(1)}, u32[]{:S(2)}, u32[]{:S(2)}) collective-permute-start(f32[20,64,256]{2,1,0:T(8,128)S(1)} %dynamic-slice_bitcast_fusion.9), channel_id=1, source_target_pairs={{0,16},{4,20},{8,24},{12,28},{16,0},{20,4},{24,8},{28,12},{1,17},{... | collective-permute-start | bytes 3932168 | tf_op jit(solution)/shard_map/ppermute | solution.py:270
  195.3 31.8 %copy.60 = f32[64,512,256]{2,0,1:T(8,128)} copy(f32[64,512,256]{2,1,0:T(8,128)} %param.2) | data formatting | bytes 67108864 | tf_op jit(solution)/shard_map/optimization_barrier | solution.py:257
  228.5 14.9 %collective-permute-done.3 = f32[20,64,256]{2,1,0:T(8,128)} collective-permute-done((f32[20,64,256]{2,1,0:T(8,128)}, f32[20,64,256]{2,1,0:T(8,128)}, u32[]{:S(2)}, u32[]{:S(2)}) %collective-permute-start.3) | collective-permute-done | bytes 1310752 | tf_op jit(solution)/shard_map/ppermute | solution.py:270
  243.4 31.8 %copy.61 = f32[64,512,256]{2,0,1:T(8,128)} copy(f32[64,512,256]{2,1,0:T(8,128)} %param.2) | data formatting | bytes 67108864 | tf_op jit(solution)/shard_map/optimization_barrier | solution.py:257
  276.6 3.7 collective-permute-start.9
  280.3 31.8 %copy.62 = f32[64,512,256]{2,0,1:T(8,128)} copy(f32[64,512,256]{2,1,0:T(8,128)} %param.2) | data formatting | bytes 67108864 | tf_op jit(solution)/shard_map/optimization_barrier | solution.py:257
  319.1 2.5 dynamic-slice_bitcast_fusion.6
  321.6 31.8 %copy.63 = f32[64,512,256]{2,0,1:T(8,128)} copy(f32[64,512,256]{2,1,0:T(8,128)} %param.2) | data formatting | bytes 67108864 | tf_op jit(solution)/shard_map/optimization_barrier | solution.py:257
  353.4 2.6 dynamic-slice_bitcast_fusion.5
  363.5 32.2 %copy.64 = f32[64,512,256]{2,0,1:T(8,128)} copy(f32[64,512,256]{2,1,0:T(8,128)} %param.2) | data formatting | bytes 67108864 | tf_op jit(solution)/shard_map/optimization_barrier | solution.py:257
  395.7 2.5 dynamic-slice_bitcast_fusion.4
  402.7 31.8 %copy.65 = f32[64,512,256]{2,0,1:T(8,128)} copy(f32[64,512,256]{2,1,0:T(8,128)} %param.2) | data formatting | bytes 67108864 | tf_op jit(solution)/shard_map/optimization_barrier | solution.py:257
  434.5 2.5 dynamic-slice_bitcast_fusion.3
  437.0 11.1 %broadcast_in_dim.191 = f32[16,4,512,256]{3,2,1,0:T(8,128)} broadcast(f32[]{:T(128)} %constant.854.clone.1), dimensions={} | broadcast | bytes 33554436 | tf_op jit(solution)/shard_map/broadcast_in_dim | solution.py:308
  450.3 7.3 gram_x.4.before_ref
  459.4 2.8 collective-permute-start.19
  471.2 2.3 dynamic-slice_bitcast_fusion.16
  473.5 3.9 collective-permute-start.18
  477.4 2.3 dynamic-slice_bitcast_fusion.15
  479.7 13.8 %collective-permute-done.19 = f32[20,64,256]{2,1,0:T(8,128)S(1)} collective-permute-done((f32[20,64,256]{2,1,0:T(8,128)}, f32[20,64,256]{2,1,0:T(8,128)S(1)}, u32[]{:S(2)}, u32[]{:S(2)}) %collective-permute-start.19) | collective-permute-done | bytes 1310752 | tf_op jit(solution)/shard_map/ppermute | solution.py:270
  493.5 45.0 %collective-permute-start.20 = (f32[16,64,256]{2,0,1:T(8,128)}, f32[16,64,256]{2,0,1:T(8,128)}, u32[]{:S(2)}, u32[]{:S(2)}) collective-permute-start(f32[16,64,256]{2,0,1:T(8,128)} %dynamic-slice_bitcast_fusion.15), channel_id=1, source_target_pairs={{0,20},{4,16},{8,28},{12,24},{16,4},{20,0},{24,12},{28,8},{1,21},{... | collective-permute-start | bytes 3145736 | tf_op jit(solution)/shard_map/ppermute | solution.py:270
  539.2 3.9 copy-done
  549.2 7.2 gram_x.5.before_ref
  556.8 38.4 %collective-permute-done.14 = f32[16,64,256]{2,0,1:T(8,128)S(1)} collective-permute-done((f32[16,64,256]{2,0,1:T(8,128)S(1)}, f32[16,64,256]{2,0,1:T(8,128)S(1)}, u32[]{:S(2)}, u32[]{:S(2)}) %collective-permute-start.14) | collective-permute-done | bytes 1048608 | tf_op jit(solution)/shard_map/ppermute | solution.py:270
  602.0 6.3 collective-permute-start.24
  613.3 37.4 %collective-permute-done.20 = f32[16,64,256]{2,0,1:T(8,128)} collective-permute-done((f32[16,64,256]{2,0,1:T(8,128)}, f32[16,64,256]{2,0,1:T(8,128)}, u32[]{:S(2)}, u32[]{:S(2)}) %collective-permute-start.20) | collective-permute-done | bytes 1048608 | tf_op jit(solution)/shard_map/ppermute | solution.py:270
  657.1 15.9 %collective-permute-done.28 = f32[16,64,256]{2,0,1:T(8,128)S(1)} collective-permute-done((f32[16,64,256]{2,0,1:T(8,128)S(1)}, f32[16,64,256]{2,0,1:T(8,128)S(1)}, u32[]{:S(2)}, u32[]{:S(2)}) %collective-permute-start.28) | collective-permute-done | bytes 1048608 | tf_op jit(solution)/shard_map/ppermute | solution.py:270
  674.5 5.9 gram_x.6.before_ref
  681.5 2.5 collective-permute-start.25
  685.1 2.7 collective-permute-start.27
  690.7 28.1 %collective-permute-done.23 = f32[8,64,256]{2,0,1:T(8,128)S(1)} collective-permute-done((f32[8,64,256]{2,0,1:T(8,128)S(1)}, f32[8,64,256]{2,0,1:T(8,128)S(1)}, u32[]{:S(2)}, u32[]{:S(2)}) %collective-permute-start.23) | collective-permute-done | bytes 524320 | tf_op jit(solution)/shard_map/ppermute | solution.py:270
  721.2 22.0 %collective-permute-start.32 = (f32[8,64,256]{2,0,1:T(8,128)S(1)}, f32[8,64,256]{2,0,1:T(8,128)S(1)}, u32[]{:S(2)}, u32[]{:S(2)}) collective-permute-start(f32[8,64,256]{2,0,1:T(8,128)S(1)} %dynamic-slice_bitcast_fusion.21), channel_id=1, source_target_pairs={{0,8},{4,12},{8,16},{12,20},{16,24},{20,28},{24,0},{28,4},{1,9},{5... | collective-permute-start | bytes 1572872 | tf_op jit(solution)/shard_map/ppermute | solution.py:270
  744.3 9.3 collective-permute-done.29
  754.3 13.9 %collective-permute-done.33 = f32[8,64,256]{2,0,1:T(8,128)S(1)} collective-permute-done((f32[8,64,256]{2,0,1:T(8,128)S(1)}, f32[8,64,256]{2,0,1:T(8,128)S(1)}, u32[]{:S(2)}, u32[]{:S(2)}) %collective-permute-start.33) | collective-permute-done | bytes 524320 | tf_op jit(solution)/shard_map/ppermute | solution.py:270
  768.6 3.2 gram_x.7
  772.0 3.7 collective-permute-start.36
  777.3 3.6 bitcast_dynamic-update-slice_fusion.6
  781.6 2.6 collective-permute-done.35
  784.2 5.2 collective-permute-done.34
  794.8 2.9 collective-permute-done.42
  803.5 2.4 collective-permute-done.38
  806.6 2.9 collective-permute-start.45
  819.8 3.2 collective-permute-start.50
  826.8 3.6 bitcast_dynamic-update-slice_fusion.4
  831.9 53.0 %collective-permute-done.51.refs_1_ = f32[128,512]{1,0:T(8,128)S(1)} collective-permute-done((f32[128,512]{1,0:T(8,128)S(1)}, f32[128,512]{1,0:T(8,128)S(1)}, u32[]{:S(2)}, u32[]{:S(2)}) %collective-permute-start.51) | collective-permute-done | bytes 262176 | tf_op jit(solution)/shard_map/ppermute | solution.py:369
  885.5 2.4 collective-permute-done.52.refs_2_
  889.2 34.0 %subspace.1.basis_ref = f32[512,128]{1,0:T(8,128)} custom-call(s32[4]{0:T(128)S(1)} %pad_add_fusion.places_ref, f32[128,512]{1,0:T(8,128)S(1)} %bitcast.290, f32[128,512]{1,0:T(8,128)S(1)} %collective-permute-done.51.refs_1_, f32[128,512]{1,0:T(8,128)S(1)} %collective-permute-done.52.refs_2_, f32[128,512]{1,0:T(8,128)S(1)} %collective-permute-done.53.refs_3_, ...), custom_call_target="tpu_custom_call" | custom-call | tf_op jit(solution)/shard_map/subspace/pallas_call | solution.py:226
  932.3 16.4 %collective-permute-done.57 = f32[2,512,256]{2,1,0:T(8,128)S(1)} collective-permute-done((f32[2,512,256]{2,1,0:T(8,128)S(1)}, f32[2,512,256]{2,1,0:T(8,128)S(1)}, u32[]{:S(2)}, u32[]{:S(2)}) %collective-permute-start.57) | collective-permute-done | bytes 1048608 | tf_op jit(solution)/shard_map/ppermute | solution.py:270
  949.8 22.0 %collective-permute-done.58 = f32[2,512,256]{2,1,0:T(8,128)S(1)} collective-permute-done((f32[2,512,256]{2,1,0:T(8,128)S(1)}, f32[2,512,256]{2,1,0:T(8,128)S(1)}, u32[]{:S(2)}, u32[]{:S(2)}) %collective-permute-start.58) | collective-permute-done | bytes 1048608 | tf_op jit(solution)/shard_map/ppermute | solution.py:270
  974.0 21.9 %core_gram_y.1 = f32[1024,1024]{1,0:T(8,128)S(1)} custom-call(f32[16,4,512,256]{3,2,1,0:T(8,128)} %bitcast_dynamic-update-slice_fusion.28.field_ref, f32[512,128]{1,0:T(8,128)S(1)} %copy-done.4), custom_call_target="tpu_custom_call" | custom-call | flops 15032385536 | bytes 33554432 | tf_op jit(solution)/shard_map/core_gram_y/pallas_call | solution.py:115
  998.2 4.2 collective-permute-done.60
  1002.4 2.6 bitcast_add_fusion
  1006.5 24.0 %collective-permute-done.61 = f32[256,1024]{1,0:T(8,128)} collective-permute-done((f32[256,1024]{1,0:T(8,128)S(1)}, f32[256,1024]{1,0:T(8,128)}, u32[]{:S(2)}, u32[]{:S(2)}) %collective-permute-start.61) | collective-permute-done | bytes 1048608 | tf_op jit(solution)/shard_map/ppermute | solution.py:389
  1032.0 3.2 collective-permute-start.68
  1036.9 3.2 collective-permute-start.64
  1044.9 8.3 collective-permute-done.65
  1053.2 5.0 collective-permute-done.62
  (216 shorter events, 143.3 us)
Async XLA Ops:
  11.5 91.0 %collective-permute-start = (f32[20,64,256]{2,1,0:T(8,128)}, f32[20,64,256]{2,1,0:T(8,128)}, u32[]{:S(2)}, u32[]{:S(2)}) collective-permute-start(f32[20,64,256]{2,1,0:T(8,128)} %bitcast.262), channel_id=1, source_target_pairs={{0,16},{4,20},{8,24},{12,28},{16,0},{20,4},{24,8},{28,12},{1,17},{... | collective-permute-start | bytes 3932168 | tf_op jit(solution)/shard_map/ppermute | solution.py:270
  17.0 85.5 %collective-permute-start.1 = (f32[20,64,256]{2,1,0:T(8,128)}, f32[20,64,256]{2,1,0:T(8,128)}, u32[]{:S(2)}, u32[]{:S(2)}) collective-permute-start(f32[20,64,256]{2,1,0:T(8,128)} %bitcast.261), channel_id=1, source_target_pairs={{0,12},{4,8},{8,20},{12,16},{16,28},{20,24},{24,4},{28,0},{1,13},{... | collective-permute-start | bytes 3932168 | tf_op jit(solution)/shard_map/ppermute | solution.py:270
  21.0 120.6 %collective-permute-start.2 = (f32[20,64,256]{2,1,0:T(8,128)}, f32[20,64,256]{2,1,0:T(8,128)}, u32[]{:S(2)}, u32[]{:S(2)}) collective-permute-start(f32[20,64,256]{2,1,0:T(8,128)} %bitcast.260), channel_id=1, source_target_pairs={{0,24},{4,28},{8,0},{12,4},{16,8},{20,12},{24,16},{28,20},{1,25},{... | collective-permute-start | bytes 3932168 | tf_op jit(solution)/shard_map/ppermute | solution.py:270
  24.6 218.8 %collective-permute-start.3 = (f32[20,64,256]{2,1,0:T(8,128)}, f32[20,64,256]{2,1,0:T(8,128)}, u32[]{:S(2)}, u32[]{:S(2)}) collective-permute-start(f32[20,64,256]{2,1,0:T(8,128)} %bitcast.259), channel_id=1, source_target_pairs={{0,20},{4,16},{8,28},{12,24},{16,4},{20,0},{24,12},{28,8},{1,21},{... | collective-permute-start | bytes 3932168 | tf_op jit(solution)/shard_map/ppermute | solution.py:270
  26.2 250.5 %collective-permute-start.4 = (f32[20,64,256]{2,1,0:T(8,128)}, f32[20,64,256]{2,1,0:T(8,128)}, u32[]{:S(2)}, u32[]{:S(2)}) collective-permute-start(f32[20,64,256]{2,1,0:T(8,128)} %bitcast.258), channel_id=1, source_target_pairs={{0,4},{4,0},{8,12},{12,8},{16,20},{20,16},{24,28},{28,24},{1,5},{5... | collective-permute-start | bytes 3932168 | tf_op jit(solution)/shard_map/ppermute | solution.py:270
  102.5 254.9 %collective-permute-start.5 = (f32[20,64,256]{2,1,0:T(8,128)S(1)}, f32[20,64,256]{2,1,0:T(8,128)S(1)}, u32[]{:S(2)}, u32[]{:S(2)}) collective-permute-start(f32[20,64,256]{2,1,0:T(8,128)S(1)} %get-tuple-element.72), channel_id=1, source_target_pairs={{0,8},{4,12},{8,16},{12,20},{16,24},{20,28},{24,0},{28,4},{1,9},{5... | collective-permute-start | bytes 3932168 | tf_op jit(solution)/shard_map/ppermute | solution.py:270
  102.5 255.1 %collective-permute-start.6 = (f32[20,64,256]{2,1,0:T(8,128)S(1)}, f32[20,64,256]{2,1,0:T(8,128)S(1)}, u32[]{:S(2)}, u32[]{:S(2)}) collective-permute-start(f32[20,64,256]{2,1,0:T(8,128)S(1)} %get-tuple-element.73), channel_id=1, source_target_pairs={{0,28},{4,24},{8,4},{12,0},{16,12},{20,8},{24,20},{28,16},{1,29},{... | collective-permute-start | bytes 3932168 | tf_op jit(solution)/shard_map/ppermute | solution.py:270
  141.6 216.7 %collective-permute-start.7 = (f32[20,64,256]{2,1,0:T(8,128)S(1)}, f32[20,64,256]{2,1,0:T(8,128)S(1)}, u32[]{:S(2)}, u32[]{:S(2)}) collective-permute-start(f32[20,64,256]{2,1,0:T(8,128)S(1)} %dynamic-slice_bitcast_fusion.9), channel_id=1, source_target_pairs={{0,16},{4,20},{8,24},{12,28},{16,0},{20,4},{24,8},{28,12},{1,17},{... | collective-permute-start | bytes 3932168 | tf_op jit(solution)/shard_map/ppermute | solution.py:270
  243.4 114.8 %collective-permute-start.8 = (f32[20,64,256]{2,1,0:T(8,128)S(1)}, f32[20,64,256]{2,1,0:T(8,128)S(1)}, u32[]{:S(2)}, u32[]{:S(2)}) collective-permute-start(f32[20,64,256]{2,1,0:T(8,128)S(1)} %dynamic-slice_bitcast_fusion.8), channel_id=1, source_target_pairs={{0,12},{4,8},{8,20},{12,16},{16,28},{20,24},{24,4},{28,0},{1,13},{... | collective-permute-start | bytes 3932168 | tf_op jit(solution)/shard_map/ppermute | solution.py:270
  276.6 81.6 %collective-permute-start.9 = (f32[20,64,256]{2,1,0:T(8,128)S(1)}, f32[20,64,256]{2,1,0:T(8,128)S(1)}, u32[]{:S(2)}, u32[]{:S(2)}) collective-permute-start(f32[20,64,256]{2,1,0:T(8,128)S(1)} %dynamic-slice_bitcast_fusion.7), channel_id=1, source_target_pairs={{0,24},{4,28},{8,0},{12,4},{16,8},{20,12},{24,16},{28,20},{1,25},{... | collective-permute-start | bytes 3932168 | tf_op jit(solution)/shard_map/ppermute | solution.py:270
  358.3 99.2 %collective-permute-start.10 = (f32[20,64,256]{2,1,0:T(8,128)}, f32[20,64,256]{2,1,0:T(8,128)}, u32[]{:S(2)}, u32[]{:S(2)}) collective-permute-start(f32[20,64,256]{2,1,0:T(8,128)} %dynamic-slice_bitcast_fusion.6), channel_id=1, source_target_pairs={{0,20},{4,16},{8,28},{12,24},{16,4},{20,0},{24,12},{28,8},{1,21},{... | collective-permute-start | bytes 3932168 | tf_op jit(solution)/shard_map/ppermute | solution.py:270
  358.8 98.7 %collective-permute-start.11 = (f32[20,64,256]{2,1,0:T(8,128)}, f32[20,64,256]{2,1,0:T(8,128)}, u32[]{:S(2)}, u32[]{:S(2)}) collective-permute-start(f32[20,64,256]{2,1,0:T(8,128)} %dynamic-slice_bitcast_fusion.5), channel_id=1, source_target_pairs={{0,4},{4,0},{8,12},{12,8},{16,20},{20,16},{24,28},{28,24},{1,5},{5... | collective-permute-start | bytes 3932168 | tf_op jit(solution)/shard_map/ppermute | solution.py:270
  362.0 107.2 %collective-permute-start.13 = (f32[5,512,256]{2,1,0:T(8,128)}, f32[5,512,256]{2,1,0:T(8,128)S(1)}, u32[]{:S(2)}, u32[]{:S(2)}) collective-permute-start(f32[5,512,256]{2,1,0:T(8,128)} %constant_dynamic-slice_fusion.17), channel_id=1, source_target_pairs={{0,2},{1,3},{2,0},{3,1},{4,6},{5,7},{6,4},{7,5},{8,10},{9,11},{10,... | collective-permute-start | bytes 7864328 | tf_op jit(solution)/shard_map/ppermute | solution.py:270
  398.2 69.6 %collective-permute-start.15 = (f32[20,64,256]{2,1,0:T(8,128)}, f32[20,64,256]{2,1,0:T(8,128)}, u32[]{:S(2)}, u32[]{:S(2)}) collective-permute-start(f32[20,64,256]{2,1,0:T(8,128)} %dynamic-slice_bitcast_fusion.4), channel_id=1, source_target_pairs={{0,8},{4,12},{8,16},{12,20},{16,24},{20,28},{24,0},{28,4},{1,9},{5... | collective-permute-start | bytes 3932168 | tf_op jit(solution)/shard_map/ppermute | solution.py:270
  400.9 72.6 %collective-permute-start.17 = (f32[5,512,256]{2,1,0:T(8,128)}, f32[5,512,256]{2,1,0:T(8,128)S(1)}, u32[]{:S(2)}, u32[]{:S(2)}) collective-permute-start(f32[5,512,256]{2,1,0:T(8,128)} %constant_dynamic-slice_fusion.16), channel_id=1, source_target_pairs={{0,1},{1,2},{2,3},{3,0},{4,5},{5,6},{6,7},{7,4},{8,9},{9,10},{10,1... | collective-permute-start | bytes 7864328 | tf_op jit(solution)/shard_map/ppermute | solution.py:270
  457.5 140.5 %collective-permute-start.12 = (f32[5,512,256]{2,1,0:T(8,128)S(1)}, f32[5,512,256]{2,1,0:T(8,128)}, u32[]{:S(2)}, u32[]{:S(2)}) collective-permute-start(f32[5,512,256]{2,1,0:T(8,128)S(1)} %constant_dynamic-slice_fusion.18), channel_id=1, source_target_pairs={{0,3},{1,0},{2,1},{3,2},{4,7},{5,4},{6,5},{7,6},{8,11},{9,8},{10,9... | collective-permute-start | bytes 7864328 | tf_op jit(solution)/shard_map/ppermute | solution.py:270
  459.4 34.1 %collective-permute-start.19 = (f32[20,64,256]{2,1,0:T(8,128)}, f32[20,64,256]{2,1,0:T(8,128)S(1)}, u32[]{:S(2)}, u32[]{:S(2)}) collective-permute-start(f32[20,64,256]{2,1,0:T(8,128)} %dynamic-slice_bitcast_fusion.3), channel_id=1, source_target_pairs={{0,28},{4,24},{8,4},{12,0},{16,12},{20,8},{24,20},{28,16},{1,29},{... | collective-permute-start | bytes 3932168 | tf_op jit(solution)/shard_map/ppermute | solution.py:270
  469.2 126.0 %collective-permute-start.14 = (f32[16,64,256]{2,0,1:T(8,128)S(1)}, f32[16,64,256]{2,0,1:T(8,128)S(1)}, u32[]{:S(2)}, u32[]{:S(2)}) collective-permute-start(f32[16,64,256]{2,0,1:T(8,128)S(1)} %dynamic-slice_bitcast_fusion.18), channel_id=1, source_target_pairs={{0,16},{4,20},{8,24},{12,28},{16,0},{20,4},{24,8},{28,12},{1,17},{... | collective-permute-start | bytes 3145736 | tf_op jit(solution)/shard_map/ppermute | solution.py:270
  471.2 127.3 %collective-permute-start.16 = (f32[16,64,256]{2,0,1:T(8,128)S(1)}, f32[16,64,256]{2,0,1:T(8,128)}, u32[]{:S(2)}, u32[]{:S(2)}) collective-permute-start(f32[16,64,256]{2,0,1:T(8,128)S(1)} %dynamic-slice_bitcast_fusion.17), channel_id=1, source_target_pairs={{0,12},{4,8},{8,20},{12,16},{16,28},{20,24},{24,4},{28,0},{1,13},{... | collective-permute-start | bytes 3145736 | tf_op jit(solution)/shard_map/ppermute | solution.py:270
  473.5 136.5 %collective-permute-start.18 = (f32[16,64,256]{2,0,1:T(8,128)}, f32[16,64,256]{2,0,1:T(8,128)}, u32[]{:S(2)}, u32[]{:S(2)}) collective-permute-start(f32[16,64,256]{2,0,1:T(8,128)} %dynamic-slice_bitcast_fusion.16), channel_id=1, source_target_pairs={{0,24},{4,28},{8,0},{12,4},{16,8},{20,12},{24,16},{28,20},{1,25},{... | collective-permute-start | bytes 3145736 | tf_op jit(solution)/shard_map/ppermute | solution.py:270
  493.5 157.3 %collective-permute-start.20 = (f32[16,64,256]{2,0,1:T(8,128)}, f32[16,64,256]{2,0,1:T(8,128)}, u32[]{:S(2)}, u32[]{:S(2)}) collective-permute-start(f32[16,64,256]{2,0,1:T(8,128)} %dynamic-slice_bitcast_fusion.15), channel_id=1, source_target_pairs={{0,20},{4,16},{8,28},{12,24},{16,4},{20,0},{24,12},{28,8},{1,21},{... | collective-permute-start | bytes 3145736 | tf_op jit(solution)/shard_map/ppermute | solution.py:270
  598.0 76.3 %collective-permute-start.22 = (f32[5,512,256]{2,1,0:T(8,128)S(1)}, f32[5,512,256]{2,1,0:T(8,128)S(1)}, u32[]{:S(2)}, u32[]{:S(2)}) collective-permute-start(f32[5,512,256]{2,1,0:T(8,128)S(1)} %constant_dynamic-slice_fusion.15), channel_id=1, source_target_pairs={{0,2},{1,3},{2,0},{3,1},{4,6},{5,7},{6,4},{7,5},{8,10},{9,11},{10,... | collective-permute-start | bytes 7864328 | tf_op jit(solution)/shard_map/ppermute | solution.py:270
  600.5 53.9 %collective-permute-start.21 = (f32[16,64,256]{2,0,1:T(8,128)S(1)}, f32[16,64,256]{2,0,1:T(8,128)S(1)}, u32[]{:S(2)}, u32[]{:S(2)}) collective-permute-start(f32[16,64,256]{2,0,1:T(8,128)S(1)} %dynamic-slice_bitcast_fusion.14), channel_id=1, source_target_pairs={{0,4},{4,0},{8,12},{12,8},{16,20},{20,16},{24,28},{28,24},{1,5},{5... | collective-permute-start | bytes 3145736 | tf_op jit(solution)/shard_map/ppermute | solution.py:270
  602.0 54.4 %collective-permute-start.24 = (f32[16,64,256]{2,0,1:T(8,128)S(1)}, f32[16,64,256]{2,0,1:T(8,128)S(1)}, u32[]{:S(2)}, u32[]{:S(2)}) collective-permute-start(f32[16,64,256]{2,0,1:T(8,128)S(1)} %dynamic-slice_bitcast_fusion.13), channel_id=1, source_target_pairs={{0,8},{4,12},{8,16},{12,20},{16,24},{20,28},{24,0},{28,4},{1,9},{5... | collective-permute-start | bytes 3145736 | tf_op jit(solution)/shard_map/ppermute | solution.py:270
  610.0 75.1 %collective-permute-start.26 = (f32[5,512,256]{2,1,0:T(8,128)}, f32[5,512,256]{2,1,0:T(8,128)S(1)}, u32[]{:S(2)}, u32[]{:S(2)}) collective-permute-start(f32[5,512,256]{2,1,0:T(8,128)} %constant_dynamic-slice_fusion.14), channel_id=1, source_target_pairs={{0,1},{1,2},{2,3},{3,0},{4,5},{5,6},{6,7},{7,4},{8,9},{9,10},{10,1... | collective-permute-start | bytes 7864328 | tf_op jit(solution)/shard_map/ppermute | solution.py:270
  650.7 22.2 %collective-permute-start.28 = (f32[16,64,256]{2,0,1:T(8,128)S(1)}, f32[16,64,256]{2,0,1:T(8,128)S(1)}, u32[]{:S(2)}, u32[]{:S(2)}) collective-permute-start(f32[16,64,256]{2,0,1:T(8,128)S(1)} %dynamic-slice_bitcast_fusion.12), channel_id=1, source_target_pairs={{0,28},{4,24},{8,4},{12,0},{16,12},{20,8},{24,20},{28,16},{1,29},{... | collective-permute-start | bytes 3145736 | tf_op jit(solution)/shard_map/ppermute | solution.py:270
  654.4 65.4 %collective-permute-start.30 = (f32[5,512,256]{2,1,0:T(8,128)}, f32[5,512,256]{2,1,0:T(8,128)}, u32[]{:S(2)}, u32[]{:S(2)}) collective-permute-start(f32[5,512,256]{2,1,0:T(8,128)} %constant_dynamic-slice_fusion.13), channel_id=1, source_target_pairs={{0,3},{1,0},{2,1},{3,2},{4,7},{5,4},{6,5},{7,6},{8,11},{9,8},{10,9... | collective-permute-start | bytes 7864328 | tf_op jit(solution)/shard_map/ppermute | solution.py:270
  674.4 44.5 %collective-permute-start.23 = (f32[8,64,256]{2,0,1:T(8,128)S(1)}, f32[8,64,256]{2,0,1:T(8,128)S(1)}, u32[]{:S(2)}, u32[]{:S(2)}) collective-permute-start(f32[8,64,256]{2,0,1:T(8,128)S(1)} %dynamic-slice_bitcast_fusion.26), channel_id=1, source_target_pairs={{0,16},{4,20},{8,24},{12,28},{16,0},{20,4},{24,8},{28,12},{1,17},{... | collective-permute-start | bytes 1572872 | tf_op jit(solution)/shard_map/ppermute | solution.py:270
  681.5 38.1 %collective-permute-start.25 = (f32[8,64,256]{2,0,1:T(8,128)S(1)}, f32[8,64,256]{2,0,1:T(8,128)S(1)}, u32[]{:S(2)}, u32[]{:S(2)}) collective-permute-start(f32[8,64,256]{2,0,1:T(8,128)S(1)} %dynamic-slice_bitcast_fusion.25), channel_id=1, source_target_pairs={{0,12},{4,8},{8,20},{12,16},{16,28},{20,24},{24,4},{28,0},{1,13},{... | collective-permute-start | bytes 1572872 | tf_op jit(solution)/shard_map/ppermute | solution.py:270
  685.1 34.8 %collective-permute-start.27 = (f32[8,64,256]{2,0,1:T(8,128)S(1)}, f32[8,64,256]{2,0,1:T(8,128)S(1)}, u32[]{:S(2)}, u32[]{:S(2)}) collective-permute-start(f32[8,64,256]{2,0,1:T(8,128)S(1)} %dynamic-slice_bitcast_fusion.24), channel_id=1, source_target_pairs={{0,24},{4,28},{8,0},{12,4},{16,8},{20,12},{24,16},{28,20},{1,25},{... | collective-permute-start | bytes 1572872 | tf_op jit(solution)/shard_map/ppermute | solution.py:270
  688.8 64.7 %collective-permute-start.29 = (f32[8,64,256]{2,0,1:T(8,128)S(1)}, f32[8,64,256]{2,0,1:T(8,128)S(1)}, u32[]{:S(2)}, u32[]{:S(2)}) collective-permute-start(f32[8,64,256]{2,0,1:T(8,128)S(1)} %dynamic-slice_bitcast_fusion.23), channel_id=1, source_target_pairs={{0,20},{4,16},{8,28},{12,24},{16,4},{20,0},{24,12},{28,8},{1,21},{... | collective-permute-start | bytes 1572872 | tf_op jit(solution)/shard_map/ppermute | solution.py:270
  719.8 34.0 %collective-permute-start.31 = (f32[8,64,256]{2,0,1:T(8,128)S(1)}, f32[8,64,256]{2,0,1:T(8,128)S(1)}, u32[]{:S(2)}, u32[]{:S(2)}) collective-permute-start(f32[8,64,256]{2,0,1:T(8,128)S(1)} %dynamic-slice_bitcast_fusion.22), channel_id=1, source_target_pairs={{0,4},{4,0},{8,12},{12,8},{16,20},{20,16},{24,28},{28,24},{1,5},{5... | collective-permute-start | bytes 1572872 | tf_op jit(solution)/shard_map/ppermute | solution.py:270
  721.2 32.8 %collective-permute-start.32 = (f32[8,64,256]{2,0,1:T(8,128)S(1)}, f32[8,64,256]{2,0,1:T(8,128)S(1)}, u32[]{:S(2)}, u32[]{:S(2)}) collective-permute-start(f32[8,64,256]{2,0,1:T(8,128)S(1)} %dynamic-slice_bitcast_fusion.21), channel_id=1, source_target_pairs={{0,8},{4,12},{8,16},{12,20},{16,24},{20,28},{24,0},{28,4},{1,9},{5... | collective-permute-start | bytes 1572872 | tf_op jit(solution)/shard_map/ppermute | solution.py:270
  753.6 14.6 %collective-permute-start.33 = (f32[8,64,256]{2,0,1:T(8,128)S(1)}, f32[8,64,256]{2,0,1:T(8,128)S(1)}, u32[]{:S(2)}, u32[]{:S(2)}) collective-permute-start(f32[8,64,256]{2,0,1:T(8,128)S(1)} %dynamic-slice_bitcast_fusion.20), channel_id=1, source_target_pairs={{0,28},{4,24},{8,4},{12,0},{16,12},{20,8},{24,20},{28,16},{1,29},{... | collective-permute-start | bytes 1572872 | tf_op jit(solution)/shard_map/ppermute | solution.py:270
  772.0 9.7 collective-permute-start.36
  775.6 8.6 collective-permute-start.35
  775.6 13.8 %collective-permute-start.34 = (f32[128,512]{1,0:T(8,128)S(1)}, f32[128,512]{1,0:T(8,128)S(1)}, u32[]{:S(2)}, u32[]{:S(2)}) collective-permute-start(f32[128,512]{1,0:T(8,128)S(1)} %get-tuple-element.158), channel_id=1, source_target_pairs={{0,2},{1,3},{2,0},{3,1},{4,6},{5,7},{6,4},{7,5},{8,10},{9,11},{10,... | collective-permute-start | bytes 786440 | tf_op jit(solution)/shard_map/ppermute | solution.py:356
  781.0 142.2 %collective-permute-start.54 = (f32[4,512,256]{2,1,0:T(8,128)S(1)}, f32[4,512,256]{2,1,0:T(8,128)S(1)}, u32[]{:S(2)}, u32[]{:S(2)}) collective-permute-start(f32[4,512,256]{2,1,0:T(8,128)S(1)} %constant_dynamic-slice_fusion.12), channel_id=1, source_target_pairs={{0,2},{1,3},{2,0},{3,1},{4,6},{5,7},{6,4},{7,5},{8,10},{9,11},{10,... | collective-permute-start | bytes 6291464 | tf_op jit(solution)/shard_map/ppermute | solution.py:270
  791.8 5.9 collective-permute-start.42
  791.8 7.5 collective-permute-start.41
  794.0 7.3 collective-permute-start.40
  794.7 130.6 %collective-permute-start.55 = (f32[4,512,256]{2,1,0:T(8,128)S(1)}, f32[4,512,256]{2,1,0:T(8,128)S(1)}, u32[]{:S(2)}, u32[]{:S(2)}) collective-permute-start(f32[4,512,256]{2,1,0:T(8,128)S(1)} %constant_dynamic-slice_fusion.11), channel_id=1, source_target_pairs={{0,1},{1,2},{2,3},{3,0},{4,5},{5,6},{6,7},{7,4},{8,9},{9,10},{10,1... | collective-permute-start | bytes 6291464 | tf_op jit(solution)/shard_map/ppermute | solution.py:270
  797.7 5.8 collective-permute-start.39
  799.3 6.6 collective-permute-start.38
  806.3 5.5 collective-permute-start.44
  806.6 6.6 collective-permute-start.45
  811.9 117.8 %collective-permute-start.56 = (f32[4,512,256]{2,1,0:T(8,128)S(1)}, f32[4,512,256]{2,1,0:T(8,128)S(1)}, u32[]{:S(2)}, u32[]{:S(2)}) collective-permute-start(f32[4,512,256]{2,1,0:T(8,128)S(1)} %constant_dynamic-slice_fusion.10), channel_id=1, source_target_pairs={{0,3},{1,0},{2,1},{3,2},{4,7},{5,4},{6,5},{7,6},{8,11},{9,8},{10,9... | collective-permute-start | bytes 6291464 | tf_op jit(solution)/shard_map/ppermute | solution.py:270
  813.2 6.0 collective-permute-start.47
  814.1 5.6 collective-permute-start.48
  819.3 5.9 collective-permute-start.49
  819.8 5.5 collective-permute-start.50
  825.8 59.1 %collective-permute-start.51 = (f32[128,512]{1,0:T(8,128)S(1)}, f32[128,512]{1,0:T(8,128)S(1)}, u32[]{:S(2)}, u32[]{:S(2)}) collective-permute-start(f32[128,512]{1,0:T(8,128)S(1)} %bitcast.287), channel_id=1, source_target_pairs={{0,2},{1,3},{2,0},{3,1},{4,6},{5,7},{6,4},{7,5},{8,10},{9,11},{10,... | collective-permute-start | bytes 786440 | tf_op jit(solution)/shard_map/ppermute | solution.py:369
  831.9 56.0 %collective-permute-start.52 = (f32[128,512]{1,0:T(8,128)S(1)}, f32[128,512]{1,0:T(8,128)S(1)}, u32[]{:S(2)}, u32[]{:S(2)}) collective-permute-start(f32[128,512]{1,0:T(8,128)S(1)} %bitcast.288), channel_id=1, source_target_pairs={{0,1},{1,2},{2,3},{3,0},{4,5},{5,6},{6,7},{7,4},{8,9},{9,10},{10,1... | collective-permute-start | bytes 786440 | tf_op jit(solution)/shard_map/ppermute | solution.py:369
  923.2 25.5 %collective-permute-start.57 = (f32[2,512,256]{2,1,0:T(8,128)S(1)}, f32[2,512,256]{2,1,0:T(8,128)S(1)}, u32[]{:S(2)}, u32[]{:S(2)}) collective-permute-start(f32[2,512,256]{2,1,0:T(8,128)S(1)} %constant_dynamic-slice_fusion.9), channel_id=1, source_target_pairs={{0,2},{1,3},{2,0},{3,1},{4,6},{5,7},{6,4},{7,5},{8,10},{9,11},{10,... | collective-permute-start | bytes 3145736 | tf_op jit(solution)/shard_map/ppermute | solution.py:270
  924.5 47.2 %collective-permute-start.58 = (f32[2,512,256]{2,1,0:T(8,128)S(1)}, f32[2,512,256]{2,1,0:T(8,128)S(1)}, u32[]{:S(2)}, u32[]{:S(2)}) collective-permute-start(f32[2,512,256]{2,1,0:T(8,128)S(1)} %constant_dynamic-slice_fusion.8), channel_id=1, source_target_pairs={{0,1},{1,2},{2,3},{3,0},{4,5},{5,6},{6,7},{7,4},{8,9},{9,10},{10,1... | collective-permute-start | bytes 3145736 | tf_op jit(solution)/shard_map/ppermute | solution.py:270
  925.3 47.5 %collective-permute-start.59 = (f32[2,512,256]{2,1,0:T(8,128)S(1)}, f32[2,512,256]{2,1,0:T(8,128)S(1)}, u32[]{:S(2)}, u32[]{:S(2)}) collective-permute-start(f32[2,512,256]{2,1,0:T(8,128)S(1)} %constant_dynamic-slice_fusion.7), channel_id=1, source_target_pairs={{0,3},{1,0},{2,1},{3,2},{4,7},{5,4},{6,5},{7,6},{8,11},{9,8},{10,9... | collective-permute-start | bytes 3145736 | tf_op jit(solution)/shard_map/ppermute | solution.py:270
  1005.1 25.4 %collective-permute-start.61 = (f32[256,1024]{1,0:T(8,128)S(1)}, f32[256,1024]{1,0:T(8,128)}, u32[]{:S(2)}, u32[]{:S(2)}) collective-permute-start(f32[256,1024]{1,0:T(8,128)S(1)} %dynamic-slice_bitcast_fusion.10), channel_id=1, source_target_pairs={{0,2},{1,3},{2,0},{3,1},{4,6},{5,7},{6,4},{7,5},{8,10},{9,11},{10,... | collective-permute-start | bytes 3145736 | tf_op jit(solution)/shard_map/ppermute | solution.py:389
  1032.0 8.1 collective-permute-start.68
  1035.2 8.4 collective-permute-start.67
  1035.2 9.7 collective-permute-start.66
  1036.2 17.0 %collective-permute-start.65 = (f32[256,128]{1,0:T(8,128)S(1)}, f32[256,128]{1,0:T(8,128)S(1)}, u32[]{:S(2)}, u32[]{:S(2)}) collective-permute-start(f32[256,128]{1,0:T(8,128)S(1)} %get-tuple-element.155), channel_id=1, source_target_pairs={{0,20},{4,16},{8,28},{12,24},{16,4},{20,0},{24,12},{28,8},{1,21},{... | collective-permute-start | bytes 393224 | tf_op jit(solution)/shard_map/ppermute | solution.py:397
  1036.9 16.4 %collective-permute-start.64 = (f32[256,128]{1,0:T(8,128)S(1)}, f32[256,128]{1,0:T(8,128)S(1)}, u32[]{:S(2)}, u32[]{:S(2)}) collective-permute-start(f32[256,128]{1,0:T(8,128)S(1)} %get-tuple-element.156), channel_id=1, source_target_pairs={{0,24},{4,28},{8,0},{12,4},{16,8},{20,12},{24,16},{28,20},{1,25},{... | collective-permute-start | bytes 393224 | tf_op jit(solution)/shard_map/ppermute | solution.py:397
  1040.1 13.2 %collective-permute-start.63 = (f32[256,128]{1,0:T(8,128)S(1)}, f32[256,128]{1,0:T(8,128)S(1)}, u32[]{:S(2)}, u32[]{:S(2)}) collective-permute-start(f32[256,128]{1,0:T(8,128)S(1)} %get-tuple-element.157), channel_id=1, source_target_pairs={{0,12},{4,8},{8,20},{12,16},{16,28},{20,24},{24,4},{28,0},{1,13},{... | collective-permute-start | bytes 393224 | tf_op jit(solution)/shard_map/ppermute | solution.py:397
  1043.5 14.7 %collective-permute-start.62 = (f32[256,128]{1,0:T(8,128)S(1)}, f32[256,128]{1,0:T(8,128)S(1)}, u32[]{:S(2)}, u32[]{:S(2)}) collective-permute-start(f32[256,128]{1,0:T(8,128)S(1)} %get-tuple-element.151), channel_id=1, source_target_pairs={{0,16},{4,20},{8,24},{12,28},{16,0},{20,4},{24,8},{28,12},{1,17},{... | collective-permute-start | bytes 393224 | tf_op jit(solution)/shard_map/ppermute | solution.py:397
  (15 other events, 372.1 us)

commit v3 on v2

--- a/solution.py
+++ b/solution.py
@@ -1,4 +1,5 @@
 import functools
+import math
 
 import jax
 import jax.numpy as jnp
@@ -8,8 +9,8 @@
 from jax.sharding import PartitionSpec as P
 
 ITERS = 4
-CHUNKS = 4
 WINDOW = 5
+TALL = 8
 LINE = 4
 MIB = 1024 * 1024
 F32 = jnp.float32
@@ -231,6 +232,9 @@
         out_shape=jax.ShapeDtypeStruct((width_x, rank), F32),
         scratch_shapes=[pltpu.VMEM((width_x, width_x), F32)],
         compiler_params=pltpu.CompilerParams(vmem_limit_bytes=24 * MIB),
+        cost_estimate=pl.CostEstimate(
+            flops=4 * 10**10, bytes_accessed=8 * start.size, transcendentals=0
+        ),
         name="subspace",
     )(places, *pieces, start)
 
@@ -253,6 +257,30 @@
     )(places, *pieces)
 
 
+def pack_body(first_ref, field_ref, out_ref):
+    for z in range(field_ref.shape[1]):
+        out_ref[z] = field_ref[:, z, :]
+
+
+def pack(field, first, depth):
+    x_block, _, y_block = field.shape
+    return pl.pallas_call(
+        pack_body,
+        grid_spec=pltpu.PrefetchScalarGridSpec(
+            num_scalar_prefetch=1,
+            grid=(depth // TALL,),
+            in_specs=[pl.BlockSpec((x_block, TALL, y_block), lambda i, at: (0, at[0] + i, 0))],
+            out_specs=pl.BlockSpec((TALL, x_block, y_block), lambda i, at: (i, 0, 0)),
+        ),
+        out_shape=jax.ShapeDtypeStruct((depth, x_block, y_block), F32),
+        compiler_params=pltpu.CompilerParams(vmem_limit_bytes=8 * MIB),
+        cost_estimate=pl.CostEstimate(
+            flops=0, bytes_accessed=8 * depth * x_block * y_block, transcendentals=0
+        ),
+        name="pack_z",
+    )(first.astype(jnp.int32).reshape(1), field)
+
+
 def tie(value, others):
     return lax.optimization_barrier((value, *others))[0] if others else value
 
@@ -261,21 +289,22 @@
     def __init__(self):
         self.ends = []
 
-    def done(self, ahead):
-        last = len(self.ends) - WINDOW + 1 - ahead
-        return self.ends[max(0, last - WINDOW) : max(0, last)]
+    def done(self):
+        last = len(self.ends) - WINDOW + 1
+        return self.ends[max(0, last - 1) : max(0, last)]
 
     def send(self, cut, source, axis, perm):
-        value = cut(tie(source, self.done(2)))
-        got = lax.ppermute(tie(value, self.done(0)), axis, perm)
+        got = lax.ppermute(cut(tie(source, self.done())), axis, perm)
         self.ends.append(got)
         return got
 
 
-def chunk_depths(units):
-    last = max(1, units // 8)
-    others = min(CHUNKS - 1, units - last)
-    return [(units - last + k) // others for k in reversed(range(others))] + [last]
+def chunk_depths(groups):
+    if groups < 4:
+        return [groups]
+    third, last = max(1, groups // 4), max(1, groups // 8)
+    left = groups - third - last
+    return [left - left // 2, left // 2, third, last]
 
 
 def on_device(field, start):
@@ -308,26 +337,25 @@
     cells = jnp.zeros((slab // m, m, width_x, y_block), F32)
 
     def to_gx(first, zc, a, b, whole):
-        def cut(source):
-            place = moved(g, a, b) * slab + first
-            return jnp.swapaxes(lax.dynamic_slice_in_dim(source, place, zc, axis=1), 0, 1)
-
-        got = order.send(cut, field, "gx", gx_perm(a, b))
+        place = (moved(g, a, b) * slab + first) // TALL
+        got = order.send(lambda at: pack(field, at, zc), place, "gx", gx_perm(a, b))
         return lax.dynamic_update_slice_in_dim(whole, got[:, None], moved(g, a, b, -1), axis=1)
 
-    def to_yz(cells, first, d, whole):
+    def to_yz(cells, first, d, whole, after=()):
         zs = whole.shape[0] // m
 
         def cut(source):
             return lax.dynamic_slice_in_dim(source, (q + d) % m * zs, zs, axis=0)
 
-        got = order.send(cut, whole, "yz", yz_perm(d))
+        got = order.send(cut, tie(whole, after), "yz", yz_perm(d))
         return lax.dynamic_update_slice(cells, got[:, None], (first // m, (q - d) % m, 0, 0))
 
     gram = jnp.zeros((width_x, width_x), F32)
     before, start_z, first = None, 0, 0
-    for units in chunk_depths(slab // m):
-        zc = units * m
+    group = math.lcm(m, TALL)
+    for groups in chunk_depths(slab // group):
+        zc = groups * group
+        units = zc // m
         whole = jnp.zeros((zc, n, x_block, y_block), F32)
         waiting = list(turns) if before is not None else []
         for k, (a, b) in enumerate(shifts):
@@ -336,8 +364,8 @@
                 cells = to_yz(cells, start_z, waiting.pop(0), before)
         for d in waiting:
             cells = to_yz(cells, start_z, d, before)
-        own = lax.dynamic_slice_in_dim(field, g * slab + first, zc, axis=1)
-        own = jnp.swapaxes(own, 0, 1)[:, None]
+        across = order.ends[-len(shifts) - len(turns) :]
+        own = pack(field, (g * slab + first) // TALL, zc)[:, None]
         whole = lax.dynamic_update_slice_in_dim(whole, own, g, axis=1)
         before = whole.reshape(zc, width_x, y_block)
         gram = gram_of(before, gram)
@@ -346,7 +374,7 @@
         start_z, first = first, first + zc
 
     rows = width_x // m
-    slabs = gram.reshape(m, rows, width_x)
+    slabs = tie(gram, across).reshape(m, rows, width_x)
 
     def pick(array, index):
         return lax.dynamic_index_in_dim(array, index, axis=0, keepdims=False)
@@ -354,20 +382,18 @@
     summed = pick(slabs, q)
     for d in turns:
         summed = summed + lax.ppermute(pick(slabs, (q + d) % m), "yz", yz_perm(d))
-    before = tie(before, [summed])
-    cells = to_yz(cells, start_z, turns[0], before)
+    cells = to_yz(cells, start_z, turns[0], before, [summed])
     strips = summed.reshape(n, rows // n, width_x)
     summed = pick(strips, g)
     for a, b in shifts:
         summed = summed + lax.ppermute(pick(strips, moved(g, a, b)), "gx", gx_perm(a, b))
-    before = tie(before, [summed])
-    for d in turns[1:]:
-        cells = to_yz(cells, start_z, d, before)
     pieces = [summed] + [lax.ppermute(summed, "gx", gx_perm(a, b)) for a, b in shifts]
     places = jnp.stack([g] + [moved(g, a, b, -1) for a, b in shifts]).astype(jnp.int32)
     summed = stack(pieces, places).reshape(rows, width_x)
     pieces = [summed] + [lax.ppermute(summed, "yz", yz_perm(d)) for d in turns]
     places = jnp.stack([q] + [(q - d) % m for d in turns]).astype(jnp.int32)
+    for d in turns[1:]:
+        cells = to_yz(cells, start_z, d, before, pieces[1:])
     basis = iterate(pieces, places, start, float(width_y * depth))
 
     partial_y = core_gram(cells, basis, float(rank * depth))

time: 1070 us -> 1140 us (1.065)
  starting transfers between devices: 210 us -> 264 us
  local copies, waits for them, and re-layouts: 363 us -> 323 us
  waiting for transfers between devices: 399 us -> 434 us
  Pallas kernels: 80.2 us -> 105 us
    optimization_barrier x7 -> x0, local copies, waits for them, and re-layouts: 223 us -> none  [tie(): return lax.optimization_barrier((value, *others))[0] if others else value]
    unnamed x25 -> x76, local copies, waits for them, and re-layouts: 15.1 us -> 228 us
    ppermute x40, waiting for transfers between devices: 279 us -> 370 us  [send(): got = lax.ppermute(cut(tie(source, self.done())), axis, perm)]
    ppermute x3, waiting for transfers between devices: 56.7 us -> 5.96 us  [on_device(): pieces = [summed] + [lax.ppermute(summed, 'yz', yz_perm(d)) for d in turns]]
    ppermute x40, starting transfers between devices: 172 us -> 212 us  [send(): got = lax.ppermute(cut(tie(source, self.done())), axis, perm)]
    transpose x22 -> x0, local copies, waits for them, and re-layouts: 36.1 us -> none  [cut(): jnp.swapaxes(lax.dynamic_slice_in_dim(source, place, zc, axis=1), 0, 1)]
    pallas_call x0 -> x32, Pallas kernels: none -> 23.1 us  [pack(): pl.pallas_call(pack_body, grid_spec=pltpu.PrefetchScalarGridSpec(num_scal...]
    broadcast_in_dim x3 -> x0, local copies, waits for them, and re-layouts: 13.3 us -> none  [on_device(): own = jnp.swapaxes(own, 0, 1)[:, None]]
  transfers between devices with their start and end apart: 69 -> 69, of which waited for: 29 -> 28; matrix products, arithmetic and copies ran while one was open for 32% -> 8% of each run, Pallas kernels for 5% -> 7%
where the time goes in v3:
time: 1140 us; the launch traced here: 1130 us
  waiting for transfers between devices  434 us (38%)
  local copies, waits for them, and re-layouts  323 us (28%)
  starting transfers between devices  264 us (23%)
  Pallas kernels  105 us (9%)
    ppermute x40, waiting for transfers between devices, send(): got = lax.ppermute(cut(tie(source, self.done())), axis, perm)  370 us
    unnamed x76, local copies, waits for them, and re-layouts  228 us
    ppermute x40, starting transfers between devices, send(): got = lax.ppermute(cut(tie(source, self.done())), axis, perm)  212 us
    pallas_call x1, Pallas kernels, iterate(): pl.pallas_call(functools.partial(iterate_body, total), in_specs=[pl.Block...  34 us
    dynamic_update_slice x12, local copies, waits for them, and re-layouts, to_yz(): lax.dynamic_update_slice(cells, got[:, None], (first // m, (q - d) % m, 0...  28.6 us
    dynamic_update_slice x27, local copies, waits for them, and re-layouts, to_gx(): lax.dynamic_update_slice_in_dim(whole, got[:, None], moved(g, a, b, -1),...  26.9 us
    ppermute x1, waiting for transfers between devices, on_device(): lax.ppermute(pick(blocks_here, (chip + d) % chips), 'yz', perm)  24.8 us
    pallas_call x1, Pallas kernels, core_gram(): pl.pallas_call(functools.partial(core_body, steps, total), grid=(steps,),...  23.9 us
  transfers between devices with their start and end apart: 69, of which 28 were waited for; matrix products, arithmetic and copies ran while one was open for 8% of the time, Pallas kernels for 7%

profile of v3, /device:TPU:0, one launch (start us, length us, event | category | flops | bytes accessed | tf_op | source)
XLA Modules:
  0.0 1132.9 jit_solution(13103973402952828143)
XLA Ops:
  0.7 10.5 copy-done
  11.9 4.1 collective-permute-start.6
  16.0 10.5 copy-done.1
  29.9 10.5 copy-done.2
  44.7 10.5 copy-done.3
  57.3 10.5 copy-done.4
  70.4 49.3 %collective-permute-done.6 = f32[24,64,256]{2,1,0:T(8,128)} collective-permute-done((f32[24,64,256]{2,1,0:T(8,128)S(1)}, f32[24,64,256]{2,1,0:T(8,128)}, u32[]{:S(2)}, u32[]{:S(2)}) %collective-permute-start.6) | collective-permute-done | bytes 1572896 | tf_op jit(solution)/shard_map/ppermute | solution.py:297
  119.7 10.5 copy-done.5
  132.3 10.5 copy-done.6
  143.6 10.5 copy-done.7
  154.9 5.5 collective-permute-start.10
  160.8 59.3 %collective-permute-start.1 = (f32[16,64,256]{2,1,0:T(8,128)S(1)}, f32[16,64,256]{2,1,0:T(8,128)S(1)}, u32[]{:S(2)}, u32[]{:S(2)}) collective-permute-start(f32[16,64,256]{2,1,0:T(8,128)S(1)} %pack_z.33), channel_id=1, source_target_pairs={{0,16},{4,20},{8,24},{12,28},{16,0},{20,4},{24,8},{28,12},{1,17},{... | collective-permute-start | bytes 3145736 | tf_op jit(solution)/shard_map/ppermute | solution.py:297
  220.1 57.5 %collective-permute-done.2 = f32[24,64,256]{2,1,0:T(8,128)} collective-permute-done((f32[24,64,256]{2,1,0:T(8,128)}, f32[24,64,256]{2,1,0:T(8,128)}, u32[]{:S(2)}, u32[]{:S(2)}) %collective-permute-start.2) | collective-permute-done | bytes 1572896 | tf_op jit(solution)/shard_map/ppermute | solution.py:297
  279.3 3.4 collective-permute-start.5
  294.1 61.0 %collective-permute-done.1 = f32[16,64,256]{2,1,0:T(8,128)S(1)} collective-permute-done((f32[16,64,256]{2,1,0:T(8,128)S(1)}, f32[16,64,256]{2,1,0:T(8,128)S(1)}, u32[]{:S(2)}, u32[]{:S(2)}) %collective-permute-start.1) | collective-permute-done | bytes 1048608 | tf_op jit(solution)/shard_map/ppermute | solution.py:297
  358.9 10.5 copy-done.8
  371.5 10.5 copy-done.9
  382.6 5.6 collective-permute-start.12
  391.7 4.0 constant_dynamic-slice_fusion.16
  395.7 3.9 constant_dynamic-slice_fusion.14
  401.3 10.4 collective-permute-done.12
  411.7 10.5 copy-done.10
  423.5 26.0 %collective-permute-start.18 = (f32[16,64,256]{2,1,0:T(8,128)}, f32[16,64,256]{2,1,0:T(8,128)}, u32[]{:S(2)}, u32[]{:S(2)}) collective-permute-start(f32[16,64,256]{2,1,0:T(8,128)} %pack_z.50), channel_id=1, source_target_pairs={{0,12},{4,8},{8,20},{12,16},{16,28},{20,24},{24,4},{28,0},{1,13},{... | collective-permute-start | bytes 3145736 | tf_op jit(solution)/shard_map/ppermute | solution.py:297
  449.5 25.3 %collective-permute-done.8 = f32[16,64,256]{2,1,0:T(8,128)} collective-permute-done((f32[16,64,256]{2,1,0:T(8,128)S(1)}, f32[16,64,256]{2,1,0:T(8,128)}, u32[]{:S(2)}, u32[]{:S(2)}) %collective-permute-start.8) | collective-permute-done | bytes 1048608 | tf_op jit(solution)/shard_map/ppermute | solution.py:297
  476.1 10.5 copy-done.11
  487.2 10.5 copy-done.12
  498.0 10.5 copy-done.13
  513.3 3.3 copy-done.22
  516.6 10.5 copy-done.14
  527.6 3.2 collective-permute-start.19
  535.6 8.3 gram_x.4.before_ref
  544.0 11.1 broadcast_in_dim.191
  560.5 10.5 copy-done.15
  573.0 3.7 collective-permute-start.22
  579.4 55.2 %collective-permute-done.25 = f32[16,64,256]{2,1,0:T(8,128)} collective-permute-done((f32[16,64,256]{2,1,0:T(8,128)S(1)}, f32[16,64,256]{2,1,0:T(8,128)}, u32[]{:S(2)}, u32[]{:S(2)}) %collective-permute-start.25) | collective-permute-done | bytes 1048608 | tf_op jit(solution)/shard_map/ppermute | solution.py:297
  634.5 10.5 copy-done.16
  645.6 13.6 %collective-permute-start.26 = (f32[16,64,256]{2,1,0:T(8,128)S(1)}, f32[16,64,256]{2,1,0:T(8,128)}, u32[]{:S(2)}, u32[]{:S(2)}) collective-permute-start(f32[16,64,256]{2,1,0:T(8,128)S(1)} %pack_z.56), channel_id=1, source_target_pairs={{0,28},{4,24},{8,4},{12,0},{16,12},{20,8},{24,20},{28,16},{1,29},{... | collective-permute-start | bytes 3145736 | tf_op jit(solution)/shard_map/ppermute | solution.py:297
  659.4 40.4 %collective-permute-start.32 = (f32[8,64,256]{2,1,0:T(8,128)S(1)}, f32[8,64,256]{2,1,0:T(8,128)}, u32[]{:S(2)}, u32[]{:S(2)}) collective-permute-start(f32[8,64,256]{2,1,0:T(8,128)S(1)} %pack_z.60), channel_id=1, source_target_pairs={{0,8},{4,12},{8,16},{12,20},{16,24},{20,28},{24,0},{28,4},{1,9},{5... | collective-permute-start | bytes 1572872 | tf_op jit(solution)/shard_map/ppermute | solution.py:297
  707.2 17.1 %collective-permute-done.29 = f32[16,64,256]{2,1,0:T(8,128)S(1)} collective-permute-done((f32[16,64,256]{2,1,0:T(8,128)S(1)}, f32[16,64,256]{2,1,0:T(8,128)S(1)}, u32[]{:S(2)}, u32[]{:S(2)}) %collective-permute-start.29) | collective-permute-done | bytes 1048608 | tf_op jit(solution)/shard_map/ppermute | solution.py:297
  733.2 3.9 bitcast_dynamic-update-slice_fusion.1
  737.1 10.5 copy-done.17
  751.0 3.9 bitcast_dynamic-update-slice_fusion
  754.9 3.9 bitcast_dynamic-update-slice_fusion.2
  758.9 4.5 collective-permute-done.27
  764.2 10.5 copy-done.18
  774.9 15.3 %collective-permute-start.33 = (f32[8,64,256]{2,1,0:T(8,128)S(1)}, f32[8,64,256]{2,1,0:T(8,128)}, u32[]{:S(2)}, u32[]{:S(2)}) collective-permute-start(f32[8,64,256]{2,1,0:T(8,128)S(1)} %pack_z.61), channel_id=1, source_target_pairs={{0,28},{4,24},{8,4},{12,0},{16,12},{20,8},{24,20},{28,16},{1,29},{... | collective-permute-start | bytes 1572872 | tf_op jit(solution)/shard_map/ppermute | solution.py:297
  791.9 5.7 gram_x.5.before_ref
  797.6 5.8 gram_x.6.before_ref
  803.4 10.5 copy-done.19
  815.6 10.5 copy-done.20
  837.4 15.5 %collective-permute-done.24 = f32[8,64,256]{2,1,0:T(8,128)S(1)} collective-permute-done((f32[8,64,256]{2,1,0:T(8,128)S(1)}, f32[8,64,256]{2,1,0:T(8,128)S(1)}, u32[]{:S(2)}, u32[]{:S(2)}) %collective-permute-start.24) | collective-permute-done | bytes 524320 | tf_op jit(solution)/shard_map/ppermute | solution.py:297
  861.2 24.1 %collective-permute-done.34 = f32[4,512,256]{2,1,0:T(8,128)S(1)} collective-permute-done((f32[4,512,256]{2,1,0:T(8,128)S(1)}, f32[4,512,256]{2,1,0:T(8,128)S(1)}, u32[]{:S(2)}, u32[]{:S(2)}) %collective-permute-start.34) | collective-permute-done | bytes 2097184 | tf_op jit(solution)/shard_map/ppermute | solution.py:297
  885.3 43.1 %collective-permute-done.35 = f32[4,512,256]{2,1,0:T(8,128)S(1)} collective-permute-done((f32[4,512,256]{2,1,0:T(8,128)S(1)}, f32[4,512,256]{2,1,0:T(8,128)S(1)}, u32[]{:S(2)}, u32[]{:S(2)}) %collective-permute-start.35) | collective-permute-done | bytes 2097184 | tf_op jit(solution)/shard_map/ppermute | solution.py:297
  938.0 5.6 collective-permute-done.37
  943.8 14.0 %collective-permute-start.46 = (f32[16,512]{1,0:T(8,128)S(1)}, f32[16,512]{1,0:T(8,128)S(1)}, u32[]{:S(2)}, u32[]{:S(2)}) collective-permute-start(f32[16,512]{1,0:T(8,128)S(1)} %get-tuple-element.89), channel_id=1, source_target_pairs={{0,28},{4,24},{8,4},{12,0},{16,12},{20,8},{24,20},{28,16},{1,29},{... | collective-permute-start | bytes 98312 | tf_op jit(solution)/shard_map/ppermute | solution.py:389
  991.4 4.1 collective-permute-done.54.refs_1_
  997.4 3.6 collective-permute-start.58
  1001.5 34.0 %subspace.1.basis_ref = f32[512,128]{1,0:T(8,128)} custom-call(s32[4]{0:T(128)S(1)} %pad_add_fusion.places_ref, f32[128,512]{1,0:T(8,128)S(1)} %bitcast.305, f32[128,512]{1,0:T(8,128)S(1)} %collective-permute-done.54.refs_1_, f32[128,512]{1,0:T(8,128)S(1)} %collective-permute-done.55.refs_2_, f32[128,512]{1,0:T(8,128)S(1)} %collective-permute-done.56.refs_3_, ...), custom_call_target="tpu_custom_call" | custom-call | flops 40000000000 | bytes 524288 | tf_op jit(solution)/shard_map/subspace/pallas_call | solution.py:227
  1042.9 23.9 %core_gram_y.1 = f32[1024,1024]{1,0:T(8,128)} custom-call(f32[16,4,512,256]{3,2,1,0:T(8,128)} %bitcast_dynamic-update-slice_fusion.38.field_ref, f32[512,128]{1,0:T(8,128)S(1)} %copy-done.24), custom_call_target="tpu_custom_call" | custom-call | flops 15032385536 | bytes 33554432 | tf_op jit(solution)/shard_map/core_gram_y/pallas_call | solution.py:116
  1070.4 3.9 collective-permute-done.60
  1077.8 24.8 %collective-permute-done.61 = f32[256,1024]{1,0:T(8,128)} collective-permute-done((f32[256,1024]{1,0:T(8,128)S(1)}, f32[256,1024]{1,0:T(8,128)}, u32[]{:S(2)}, u32[]{:S(2)}) %collective-permute-start.61) | collective-permute-done | bytes 1048608 | tf_op jit(solution)/shard_map/ppermute | solution.py:415
  1104.1 4.3 collective-permute-start.68
  1118.1 8.7 collective-permute-done.65
  1126.8 4.9 collective-permute-done.62
  (268 shorter events, 180.3 us)
Async XLA Ops:
  11.9 107.8 %collective-permute-start.6 = (f32[24,64,256]{2,1,0:T(8,128)S(1)}, f32[24,64,256]{2,1,0:T(8,128)}, u32[]{:S(2)}, u32[]{:S(2)}) collective-permute-start(f32[24,64,256]{2,1,0:T(8,128)S(1)} %pack_z.38), channel_id=1, source_target_pairs={{0,16},{4,20},{8,24},{12,28},{16,0},{20,4},{24,8},{28,12},{1,17},{... | collective-permute-start | bytes 4718600 | tf_op jit(solution)/shard_map/ppermute | solution.py:297
  27.3 116.4 %collective-permute-start.9 = (f32[24,64,256]{2,1,0:T(8,128)S(1)}, f32[24,64,256]{2,1,0:T(8,128)}, u32[]{:S(2)}, u32[]{:S(2)}) collective-permute-start(f32[24,64,256]{2,1,0:T(8,128)S(1)} %pack_z.41), channel_id=1, source_target_pairs={{0,12},{4,8},{8,20},{12,16},{16,28},{20,24},{24,4},{28,0},{1,13},{... | collective-permute-start | bytes 4718600 | tf_op jit(solution)/shard_map/ppermute | solution.py:297
  42.5 117.8 %collective-permute-start = (f32[24,64,256]{2,1,0:T(8,128)}, f32[24,64,256]{2,1,0:T(8,128)}, u32[]{:S(2)}, u32[]{:S(2)}) collective-permute-start(f32[24,64,256]{2,1,0:T(8,128)} %pack_z.32), channel_id=1, source_target_pairs={{0,24},{4,28},{8,0},{12,4},{16,8},{20,12},{24,16},{28,20},{1,25},{... | collective-permute-start | bytes 4718600 | tf_op jit(solution)/shard_map/ppermute | solution.py:297
  57.3 220.2 %collective-permute-start.2 = (f32[24,64,256]{2,1,0:T(8,128)}, f32[24,64,256]{2,1,0:T(8,128)}, u32[]{:S(2)}, u32[]{:S(2)}) collective-permute-start(f32[24,64,256]{2,1,0:T(8,128)} %pack_z.34), channel_id=1, source_target_pairs={{0,20},{4,16},{8,28},{12,24},{16,4},{20,0},{24,12},{28,8},{1,21},{... | collective-permute-start | bytes 4718600 | tf_op jit(solution)/shard_map/ppermute | solution.py:297
  69.9 208.1 %collective-permute-start.4 = (f32[24,64,256]{2,1,0:T(8,128)}, f32[24,64,256]{2,1,0:T(8,128)}, u32[]{:S(2)}, u32[]{:S(2)}) collective-permute-start(f32[24,64,256]{2,1,0:T(8,128)} %pack_z.36), channel_id=1, source_target_pairs={{0,4},{4,0},{8,12},{12,8},{16,20},{20,16},{24,28},{28,24},{1,5},{5... | collective-permute-start | bytes 4718600 | tf_op jit(solution)/shard_map/ppermute | solution.py:297
  132.3 159.9 %collective-permute-start.7 = (f32[24,64,256]{2,1,0:T(8,128)}, f32[24,64,256]{2,1,0:T(8,128)}, u32[]{:S(2)}, u32[]{:S(2)}) collective-permute-start(f32[24,64,256]{2,1,0:T(8,128)} %pack_z.39), channel_id=1, source_target_pairs={{0,8},{4,12},{8,16},{12,20},{16,24},{20,28},{24,0},{28,4},{1,9},{5... | collective-permute-start | bytes 4718600 | tf_op jit(solution)/shard_map/ppermute | solution.py:297
  154.9 138.8 %collective-permute-start.10 = (f32[24,64,256]{2,1,0:T(8,128)S(1)}, f32[24,64,256]{2,1,0:T(8,128)S(1)}, u32[]{:S(2)}, u32[]{:S(2)}) collective-permute-start(f32[24,64,256]{2,1,0:T(8,128)S(1)} %pack_z.42), channel_id=1, source_target_pairs={{0,28},{4,24},{8,4},{12,0},{16,12},{20,8},{24,20},{28,16},{1,29},{... | collective-permute-start | bytes 4718600 | tf_op jit(solution)/shard_map/ppermute | solution.py:297
  160.8 194.3 %collective-permute-start.1 = (f32[16,64,256]{2,1,0:T(8,128)S(1)}, f32[16,64,256]{2,1,0:T(8,128)S(1)}, u32[]{:S(2)}, u32[]{:S(2)}) collective-permute-start(f32[16,64,256]{2,1,0:T(8,128)S(1)} %pack_z.33), channel_id=1, source_target_pairs={{0,16},{4,20},{8,24},{12,28},{16,0},{20,4},{24,8},{28,12},{1,17},{... | collective-permute-start | bytes 3145736 | tf_op jit(solution)/shard_map/ppermute | solution.py:297
  278.0 93.6 %collective-permute-start.3 = (f32[16,64,256]{2,1,0:T(8,128)S(1)}, f32[16,64,256]{2,1,0:T(8,128)}, u32[]{:S(2)}, u32[]{:S(2)}) collective-permute-start(f32[16,64,256]{2,1,0:T(8,128)S(1)} %pack_z.35), channel_id=1, source_target_pairs={{0,12},{4,8},{8,20},{12,16},{16,28},{20,24},{24,4},{28,0},{1,13},{... | collective-permute-start | bytes 3145736 | tf_op jit(solution)/shard_map/ppermute | solution.py:297
  279.3 108.8 %collective-permute-start.5 = (f32[16,64,256]{2,1,0:T(8,128)}, f32[16,64,256]{2,1,0:T(8,128)}, u32[]{:S(2)}, u32[]{:S(2)}) collective-permute-start(f32[16,64,256]{2,1,0:T(8,128)} %pack_z.37), channel_id=1, source_target_pairs={{0,24},{4,28},{8,0},{12,4},{16,8},{20,12},{24,16},{28,20},{1,25},{... | collective-permute-start | bytes 3145736 | tf_op jit(solution)/shard_map/ppermute | solution.py:297
  357.1 174.3 %collective-permute-start.14 = (f32[6,512,256]{2,1,0:T(8,128)}, f32[6,512,256]{2,1,0:T(8,128)}, u32[]{:S(2)}, u32[]{:S(2)}) collective-permute-start(f32[6,512,256]{2,1,0:T(8,128)} %constant_dynamic-slice_fusion.18), channel_id=1, source_target_pairs={{0,2},{1,3},{2,0},{3,1},{4,6},{5,7},{6,4},{7,5},{8,10},{9,11},{10,... | collective-permute-start | bytes 9437192 | tf_op jit(solution)/shard_map/ppermute | solution.py:297
  369.9 25.7 %collective-permute-start.11 = (f32[16,64,256]{2,1,0:T(8,128)S(1)}, f32[16,64,256]{2,1,0:T(8,128)}, u32[]{:S(2)}, u32[]{:S(2)}) collective-permute-start(f32[16,64,256]{2,1,0:T(8,128)S(1)} %pack_z.43), channel_id=1, source_target_pairs={{0,4},{4,0},{8,12},{12,8},{16,20},{20,16},{24,28},{28,24},{1,5},{5... | collective-permute-start | bytes 3145736 | tf_op jit(solution)/shard_map/ppermute | solution.py:297
  382.6 29.1 %collective-permute-start.12 = (f32[16,64,256]{2,1,0:T(8,128)S(1)}, f32[16,64,256]{2,1,0:T(8,128)}, u32[]{:S(2)}, u32[]{:S(2)}) collective-permute-start(f32[16,64,256]{2,1,0:T(8,128)S(1)} %pack_z.44), channel_id=1, source_target_pairs={{0,8},{4,12},{8,16},{12,20},{16,24},{20,28},{24,0},{28,4},{1,9},{5... | collective-permute-start | bytes 3145736 | tf_op jit(solution)/shard_map/ppermute | solution.py:297
  388.6 86.2 %collective-permute-start.8 = (f32[16,64,256]{2,1,0:T(8,128)S(1)}, f32[16,64,256]{2,1,0:T(8,128)}, u32[]{:S(2)}, u32[]{:S(2)}) collective-permute-start(f32[16,64,256]{2,1,0:T(8,128)S(1)} %pack_z.40), channel_id=1, source_target_pairs={{0,20},{4,16},{8,28},{12,24},{16,4},{20,0},{24,12},{28,8},{1,21},{... | collective-permute-start | bytes 3145736 | tf_op jit(solution)/shard_map/ppermute | solution.py:297
  395.6 176.1 %collective-permute-start.21 = (f32[6,512,256]{2,1,0:T(8,128)}, f32[6,512,256]{2,1,0:T(8,128)}, u32[]{:S(2)}, u32[]{:S(2)}) collective-permute-start(f32[6,512,256]{2,1,0:T(8,128)} %constant_dynamic-slice_fusion.16), channel_id=1, source_target_pairs={{0,1},{1,2},{2,3},{3,0},{4,5},{5,6},{6,7},{7,4},{8,9},{9,10},{10,1... | collective-permute-start | bytes 9437192 | tf_op jit(solution)/shard_map/ppermute | solution.py:297
  399.6 300.2 %collective-permute-start.28 = (f32[6,512,256]{2,1,0:T(8,128)}, f32[6,512,256]{2,1,0:T(8,128)}, u32[]{:S(2)}, u32[]{:S(2)}) collective-permute-start(f32[6,512,256]{2,1,0:T(8,128)} %constant_dynamic-slice_fusion.14), channel_id=1, source_target_pairs={{0,3},{1,0},{2,1},{3,2},{4,7},{5,4},{6,5},{7,6},{8,11},{9,8},{10,9... | collective-permute-start | bytes 9437192 | tf_op jit(solution)/shard_map/ppermute | solution.py:297
  423.5 89.8 %collective-permute-start.18 = (f32[16,64,256]{2,1,0:T(8,128)}, f32[16,64,256]{2,1,0:T(8,128)}, u32[]{:S(2)}, u32[]{:S(2)}) collective-permute-start(f32[16,64,256]{2,1,0:T(8,128)} %pack_z.50), channel_id=1, source_target_pairs={{0,12},{4,8},{8,20},{12,16},{16,28},{20,24},{24,4},{28,0},{1,13},{... | collective-permute-start | bytes 3145736 | tf_op jit(solution)/shard_map/ppermute | solution.py:297
  476.1 54.8 %collective-permute-start.13 = (f32[16,64,256]{2,1,0:T(8,128)}, f32[16,64,256]{2,1,0:T(8,128)}, u32[]{:S(2)}, u32[]{:S(2)}) collective-permute-start(f32[16,64,256]{2,1,0:T(8,128)} %pack_z.45), channel_id=1, source_target_pairs={{0,28},{4,24},{8,4},{12,0},{16,12},{20,8},{24,20},{28,16},{1,29},{... | collective-permute-start | bytes 3145736 | tf_op jit(solution)/shard_map/ppermute | solution.py:297
  527.6 31.9 %collective-permute-start.19 = (f32[16,64,256]{2,1,0:T(8,128)S(1)}, f32[16,64,256]{2,1,0:T(8,128)S(1)}, u32[]{:S(2)}, u32[]{:S(2)}) collective-permute-start(f32[16,64,256]{2,1,0:T(8,128)S(1)} %pack_z.51), channel_id=1, source_target_pairs={{0,8},{4,12},{8,16},{12,20},{16,24},{20,28},{24,0},{28,4},{1,9},{5... | collective-permute-start | bytes 3145736 | tf_op jit(solution)/shard_map/ppermute | solution.py:297
  531.3 103.2 %collective-permute-start.25 = (f32[16,64,256]{2,1,0:T(8,128)S(1)}, f32[16,64,256]{2,1,0:T(8,128)}, u32[]{:S(2)}, u32[]{:S(2)}) collective-permute-start(f32[16,64,256]{2,1,0:T(8,128)S(1)} %pack_z.55), channel_id=1, source_target_pairs={{0,20},{4,16},{8,28},{12,24},{16,4},{20,0},{24,12},{28,8},{1,21},{... | collective-permute-start | bytes 3145736 | tf_op jit(solution)/shard_map/ppermute | solution.py:297
  531.9 168.9 %collective-permute-start.15 = (f32[16,64,256]{2,1,0:T(8,128)S(1)}, f32[16,64,256]{2,1,0:T(8,128)}, u32[]{:S(2)}, u32[]{:S(2)}) collective-permute-start(f32[16,64,256]{2,1,0:T(8,128)S(1)} %pack_z.48), channel_id=1, source_target_pairs={{0,16},{4,20},{8,24},{12,28},{16,0},{20,4},{24,8},{28,12},{1,17},{... | collective-permute-start | bytes 3145736 | tf_op jit(solution)/shard_map/ppermute | solution.py:297
  571.3 87.9 %collective-permute-start.20 = (f32[8,64,256]{2,1,0:T(8,128)S(1)}, f32[8,64,256]{2,1,0:T(8,128)S(1)}, u32[]{:S(2)}, u32[]{:S(2)}) collective-permute-start(f32[8,64,256]{2,1,0:T(8,128)S(1)} %pack_z.52), channel_id=1, source_target_pairs={{0,12},{4,8},{8,20},{12,16},{16,28},{20,24},{24,4},{28,0},{1,13},{... | collective-permute-start | bytes 1572872 | tf_op jit(solution)/shard_map/ppermute | solution.py:297
  573.0 131.5 %collective-permute-start.22 = (f32[16,64,256]{2,1,0:T(8,128)}, f32[16,64,256]{2,1,0:T(8,128)}, u32[]{:S(2)}, u32[]{:S(2)}) collective-permute-start(f32[16,64,256]{2,1,0:T(8,128)} %pack_z.53), channel_id=1, source_target_pairs={{0,24},{4,28},{8,0},{12,4},{16,8},{20,12},{24,16},{28,20},{1,25},{... | collective-permute-start | bytes 3145736 | tf_op jit(solution)/shard_map/ppermute | solution.py:297
  645.6 79.0 %collective-permute-start.26 = (f32[16,64,256]{2,1,0:T(8,128)S(1)}, f32[16,64,256]{2,1,0:T(8,128)}, u32[]{:S(2)}, u32[]{:S(2)}) collective-permute-start(f32[16,64,256]{2,1,0:T(8,128)S(1)} %pack_z.56), channel_id=1, source_target_pairs={{0,28},{4,24},{8,4},{12,0},{16,12},{20,8},{24,20},{28,16},{1,29},{... | collective-permute-start | bytes 3145736 | tf_op jit(solution)/shard_map/ppermute | solution.py:297
  659.4 196.4 %collective-permute-start.32 = (f32[8,64,256]{2,1,0:T(8,128)S(1)}, f32[8,64,256]{2,1,0:T(8,128)}, u32[]{:S(2)}, u32[]{:S(2)}) collective-permute-start(f32[8,64,256]{2,1,0:T(8,128)S(1)} %pack_z.60), channel_id=1, source_target_pairs={{0,8},{4,12},{8,16},{12,20},{16,24},{20,28},{24,0},{28,4},{1,9},{5... | collective-permute-start | bytes 1572872 | tf_op jit(solution)/shard_map/ppermute | solution.py:297
  700.2 24.0 %collective-permute-start.29 = (f32[16,64,256]{2,1,0:T(8,128)S(1)}, f32[16,64,256]{2,1,0:T(8,128)S(1)}, u32[]{:S(2)}, u32[]{:S(2)}) collective-permute-start(f32[16,64,256]{2,1,0:T(8,128)S(1)} %pack_z.58), channel_id=1, source_target_pairs={{0,4},{4,0},{8,12},{12,8},{16,20},{20,16},{24,28},{28,24},{1,5},{5... | collective-permute-start | bytes 3145736 | tf_op jit(solution)/shard_map/ppermute | solution.py:297
  727.9 75.5 %collective-permute-start.16 = (f32[4,512,256]{2,1,0:T(8,128)}, f32[4,512,256]{2,1,0:T(8,128)}, u32[]{:S(2)}, u32[]{:S(2)}) collective-permute-start(f32[4,512,256]{2,1,0:T(8,128)} %constant_dynamic-slice_fusion.17), channel_id=1, source_target_pairs={{0,2},{1,3},{2,0},{3,1},{4,6},{5,7},{6,4},{7,5},{8,10},{9,11},{10,... | collective-permute-start | bytes 6291464 | tf_op jit(solution)/shard_map/ppermute | solution.py:297
  730.0 85.7 %collective-permute-start.23 = (f32[4,512,256]{2,1,0:T(8,128)}, f32[4,512,256]{2,1,0:T(8,128)}, u32[]{:S(2)}, u32[]{:S(2)}) collective-permute-start(f32[4,512,256]{2,1,0:T(8,128)} %constant_dynamic-slice_fusion.15), channel_id=1, source_target_pairs={{0,1},{1,2},{2,3},{3,0},{4,5},{5,6},{6,7},{7,4},{8,9},{9,10},{10,1... | collective-permute-start | bytes 6291464 | tf_op jit(solution)/shard_map/ppermute | solution.py:297
  731.4 95.2 %collective-permute-start.30 = (f32[4,512,256]{2,1,0:T(8,128)}, f32[4,512,256]{2,1,0:T(8,128)}, u32[]{:S(2)}, u32[]{:S(2)}) collective-permute-start(f32[4,512,256]{2,1,0:T(8,128)} %constant_dynamic-slice_fusion.13), channel_id=1, source_target_pairs={{0,3},{1,0},{2,1},{3,2},{4,7},{5,4},{6,5},{7,6},{8,11},{9,8},{10,9... | collective-permute-start | bytes 6291464 | tf_op jit(solution)/shard_map/ppermute | solution.py:297
  747.8 15.6 %collective-permute-start.27 = (f32[8,64,256]{2,1,0:T(8,128)S(1)}, f32[8,64,256]{2,1,0:T(8,128)S(1)}, u32[]{:S(2)}, u32[]{:S(2)}) collective-permute-start(f32[8,64,256]{2,1,0:T(8,128)S(1)} %pack_z.57), channel_id=1, source_target_pairs={{0,20},{4,16},{8,28},{12,24},{16,4},{20,0},{24,12},{28,8},{1,21},{... | collective-permute-start | bytes 1572872 | tf_op jit(solution)/shard_map/ppermute | solution.py:297
  774.9 82.0 %collective-permute-start.33 = (f32[8,64,256]{2,1,0:T(8,128)S(1)}, f32[8,64,256]{2,1,0:T(8,128)}, u32[]{:S(2)}, u32[]{:S(2)}) collective-permute-start(f32[8,64,256]{2,1,0:T(8,128)S(1)} %pack_z.61), channel_id=1, source_target_pairs={{0,28},{4,24},{8,4},{12,0},{16,12},{20,8},{24,20},{28,16},{1,29},{... | collective-permute-start | bytes 1572872 | tf_op jit(solution)/shard_map/ppermute | solution.py:297
  814.2 22.4 %collective-permute-start.17 = (f32[8,64,256]{2,1,0:T(8,128)S(1)}, f32[8,64,256]{2,1,0:T(8,128)S(1)}, u32[]{:S(2)}, u32[]{:S(2)}) collective-permute-start(f32[8,64,256]{2,1,0:T(8,128)S(1)} %pack_z.49), channel_id=1, source_target_pairs={{0,16},{4,20},{8,24},{12,28},{16,0},{20,4},{24,8},{28,12},{1,17},{... | collective-permute-start | bytes 1572872 | tf_op jit(solution)/shard_map/ppermute | solution.py:297
  826.4 26.5 %collective-permute-start.24 = (f32[8,64,256]{2,1,0:T(8,128)S(1)}, f32[8,64,256]{2,1,0:T(8,128)S(1)}, u32[]{:S(2)}, u32[]{:S(2)}) collective-permute-start(f32[8,64,256]{2,1,0:T(8,128)S(1)} %pack_z.54), channel_id=1, source_target_pairs={{0,24},{4,28},{8,0},{12,4},{16,8},{20,12},{24,16},{28,20},{1,25},{... | collective-permute-start | bytes 1572872 | tf_op jit(solution)/shard_map/ppermute | solution.py:297
  826.9 26.2 %collective-permute-start.31 = (f32[8,64,256]{2,1,0:T(8,128)S(1)}, f32[8,64,256]{2,1,0:T(8,128)S(1)}, u32[]{:S(2)}, u32[]{:S(2)}) collective-permute-start(f32[8,64,256]{2,1,0:T(8,128)S(1)} %pack_z.59), channel_id=1, source_target_pairs={{0,4},{4,0},{8,12},{12,8},{16,20},{20,16},{24,28},{28,24},{1,5},{5... | collective-permute-start | bytes 1572872 | tf_op jit(solution)/shard_map/ppermute | solution.py:297
  836.7 48.6 %collective-permute-start.34 = (f32[4,512,256]{2,1,0:T(8,128)S(1)}, f32[4,512,256]{2,1,0:T(8,128)S(1)}, u32[]{:S(2)}, u32[]{:S(2)}) collective-permute-start(f32[4,512,256]{2,1,0:T(8,128)S(1)} %constant_dynamic-slice_fusion.12), channel_id=1, source_target_pairs={{0,2},{1,3},{2,0},{3,1},{4,6},{5,7},{6,4},{7,5},{8,10},{9,11},{10,... | collective-permute-start | bytes 6291464 | tf_op jit(solution)/shard_map/ppermute | solution.py:297
  853.0 75.3 %collective-permute-start.35 = (f32[4,512,256]{2,1,0:T(8,128)S(1)}, f32[4,512,256]{2,1,0:T(8,128)S(1)}, u32[]{:S(2)}, u32[]{:S(2)}) collective-permute-start(f32[4,512,256]{2,1,0:T(8,128)S(1)} %constant_dynamic-slice_fusion.11), channel_id=1, source_target_pairs={{0,1},{1,2},{2,3},{3,0},{4,5},{5,6},{6,7},{7,4},{8,9},{9,10},{10,1... | collective-permute-start | bytes 6291464 | tf_op jit(solution)/shard_map/ppermute | solution.py:297
  853.2 75.1 %collective-permute-start.36 = (f32[4,512,256]{2,1,0:T(8,128)S(1)}, f32[4,512,256]{2,1,0:T(8,128)S(1)}, u32[]{:S(2)}, u32[]{:S(2)}) collective-permute-start(f32[4,512,256]{2,1,0:T(8,128)S(1)} %constant_dynamic-slice_fusion.10), channel_id=1, source_target_pairs={{0,3},{1,0},{2,1},{3,2},{4,7},{5,4},{6,5},{7,6},{8,11},{9,8},{10,9... | collective-permute-start | bytes 6291464 | tf_op jit(solution)/shard_map/ppermute | solution.py:297
  928.4 6.8 collective-permute-start.39
  929.4 8.6 collective-permute-start.38
  929.4 14.2 %collective-permute-start.37 = (f32[128,512]{1,0:T(8,128)S(1)}, f32[128,512]{1,0:T(8,128)S(1)}, u32[]{:S(2)}, u32[]{:S(2)}) collective-permute-start(f32[128,512]{1,0:T(8,128)S(1)} %get-tuple-element.85), channel_id=1, source_target_pairs={{0,2},{1,3},{2,0},{3,1},{4,6},{5,7},{6,4},{7,5},{8,10},{9,11},{10,... | collective-permute-start | bytes 786440 | tf_op jit(solution)/shard_map/ppermute | solution.py:384
  943.8 19.7 %collective-permute-start.46 = (f32[16,512]{1,0:T(8,128)S(1)}, f32[16,512]{1,0:T(8,128)S(1)}, u32[]{:S(2)}, u32[]{:S(2)}) collective-permute-start(f32[16,512]{1,0:T(8,128)S(1)} %get-tuple-element.89), channel_id=1, source_target_pairs={{0,28},{4,24},{8,4},{12,0},{16,12},{20,8},{24,20},{28,16},{1,29},{... | collective-permute-start | bytes 98312 | tf_op jit(solution)/shard_map/ppermute | solution.py:389
  957.8 7.2 collective-permute-start.45
  959.3 8.9 collective-permute-start.44
  959.7 8.5 collective-permute-start.43
  961.0 7.2 collective-permute-start.42
  970.2 9.1 collective-permute-start.47
  971.9 9.0 collective-permute-start.48
  975.2 9.2 collective-permute-start.49
  977.0 7.4 collective-permute-start.50
  977.6 6.8 collective-permute-start.51
  986.3 9.2 collective-permute-start.54
  986.5 9.0 collective-permute-start.55
  986.5 10.9 collective-permute-start.56
  989.4 46.1 %collective-permute-start.57 = (f32[2,512,256]{2,1,0:T(8,128)S(1)}, f32[2,512,256]{2,1,0:T(8,128)S(1)}, u32[]{:S(2)}, u32[]{:S(2)}) collective-permute-start(f32[2,512,256]{2,1,0:T(8,128)S(1)} %constant_dynamic-slice_fusion.9), channel_id=1, source_target_pairs={{0,2},{1,3},{2,0},{3,1},{4,6},{5,7},{6,4},{7,5},{8,10},{9,11},{10,... | collective-permute-start | bytes 3145736 | tf_op jit(solution)/shard_map/ppermute | solution.py:297
  997.4 42.2 %collective-permute-start.58 = (f32[2,512,256]{2,1,0:T(8,128)S(1)}, f32[2,512,256]{2,1,0:T(8,128)S(1)}, u32[]{:S(2)}, u32[]{:S(2)}) collective-permute-start(f32[2,512,256]{2,1,0:T(8,128)S(1)} %constant_dynamic-slice_fusion.8), channel_id=1, source_target_pairs={{0,1},{1,2},{2,3},{3,0},{4,5},{5,6},{6,7},{7,4},{8,9},{9,10},{10,1... | collective-permute-start | bytes 3145736 | tf_op jit(solution)/shard_map/ppermute | solution.py:297
  1001.1 39.8 %collective-permute-start.59 = (f32[2,512,256]{2,1,0:T(8,128)S(1)}, f32[2,512,256]{2,1,0:T(8,128)S(1)}, u32[]{:S(2)}, u32[]{:S(2)}) collective-permute-start(f32[2,512,256]{2,1,0:T(8,128)S(1)} %constant_dynamic-slice_fusion.7), channel_id=1, source_target_pairs={{0,3},{1,0},{2,1},{3,2},{4,7},{5,4},{6,5},{7,6},{8,11},{9,8},{10,9... | collective-permute-start | bytes 3145736 | tf_op jit(solution)/shard_map/ppermute | solution.py:297
  1077.0 25.6 %collective-permute-start.61 = (f32[256,1024]{1,0:T(8,128)S(1)}, f32[256,1024]{1,0:T(8,128)}, u32[]{:S(2)}, u32[]{:S(2)}) collective-permute-start(f32[256,1024]{1,0:T(8,128)S(1)} %dynamic-slice_bitcast_fusion.1), channel_id=1, source_target_pairs={{0,2},{1,3},{2,0},{3,1},{4,6},{5,7},{6,4},{7,5},{8,10},{9,11},{10,... | collective-permute-start | bytes 3145736 | tf_op jit(solution)/shard_map/ppermute | solution.py:415
  1104.1 9.3 collective-permute-start.68
  1108.4 8.3 collective-permute-start.67
  1108.4 9.7 collective-permute-start.66
  1109.6 17.2 %collective-permute-start.65 = (f32[256,128]{1,0:T(8,128)S(1)}, f32[256,128]{1,0:T(8,128)S(1)}, u32[]{:S(2)}, u32[]{:S(2)}) collective-permute-start(f32[256,128]{1,0:T(8,128)S(1)} %get-tuple-element.82), channel_id=1, source_target_pairs={{0,20},{4,16},{8,28},{12,24},{16,4},{20,0},{24,12},{28,8},{1,21},{... | collective-permute-start | bytes 393224 | tf_op jit(solution)/shard_map/ppermute | solution.py:423
  1110.2 16.6 %collective-permute-start.64 = (f32[256,128]{1,0:T(8,128)S(1)}, f32[256,128]{1,0:T(8,128)S(1)}, u32[]{:S(2)}, u32[]{:S(2)}) collective-permute-start(f32[256,128]{1,0:T(8,128)S(1)} %get-tuple-element.83), channel_id=1, source_target_pairs={{0,24},{4,28},{8,0},{12,4},{16,8},{20,12},{24,16},{28,20},{1,25},{... | collective-permute-start | bytes 393224 | tf_op jit(solution)/shard_map/ppermute | solution.py:423
  1113.4 13.4 %collective-permute-start.63 = (f32[256,128]{1,0:T(8,128)S(1)}, f32[256,128]{1,0:T(8,128)S(1)}, u32[]{:S(2)}, u32[]{:S(2)}) collective-permute-start(f32[256,128]{1,0:T(8,128)S(1)} %get-tuple-element.84), channel_id=1, source_target_pairs={{0,12},{4,8},{8,20},{12,16},{16,28},{20,24},{24,4},{28,0},{1,13},{... | collective-permute-start | bytes 393224 | tf_op jit(solution)/shard_map/ppermute | solution.py:423
  1116.7 15.0 %collective-permute-start.62 = (f32[256,128]{1,0:T(8,128)S(1)}, f32[256,128]{1,0:T(8,128)S(1)}, u32[]{:S(2)}, u32[]{:S(2)}) collective-permute-start(f32[256,128]{1,0:T(8,128)S(1)} %get-tuple-element.78), channel_id=1, source_target_pairs={{0,16},{4,20},{8,24},{12,28},{16,0},{20,4},{24,8},{28,12},{1,17},{... | collective-permute-start | bytes 393224 | tf_op jit(solution)/shard_map/ppermute | solution.py:423
  (43 other events, 445.6 us)

commit v4 on v3

--- a/solution.py
+++ b/solution.py
@@ -273,7 +273,7 @@
             out_specs=pl.BlockSpec((TALL, x_block, y_block), lambda i, at: (i, 0, 0)),
         ),
         out_shape=jax.ShapeDtypeStruct((depth, x_block, y_block), F32),
-        compiler_params=pltpu.CompilerParams(vmem_limit_bytes=8 * MIB),
+        compiler_params=pltpu.CompilerParams(vmem_limit_bytes=48 * MIB),
         cost_estimate=pl.CostEstimate(
             flops=0, bytes_accessed=8 * depth * x_block * y_block, transcendentals=0
         ),
@@ -302,9 +302,10 @@
 def chunk_depths(groups):
     if groups < 4:
         return [groups]
-    third, last = max(1, groups // 4), max(1, groups // 8)
-    left = groups - third - last
-    return [left - left // 2, left // 2, third, last]
+    last = max(1, groups // 8)
+    left = groups - 2 * last
+    first = [(left + k) // 3 for k in (2, 1, 0)]
+    return [depth for depth in first if depth] + [last, last]
 
 
 def on_device(field, start):

time: 1140 us -> 1090 us (0.956)
  local copies, waits for them, and re-layouts: 323 us -> 127 us
  waiting for transfers between devices: 434 us -> 564 us
  Pallas kernels: 105 us -> 142 us
  starting transfers between devices: 264 us -> 240 us
    unnamed x76 -> x44, local copies, waits for them, and re-layouts: 228 us -> 10.3 us
    ppermute x40 -> x50, waiting for transfers between devices: 370 us -> 496 us  [send(): got = lax.ppermute(cut(tie(source, self.done())), axis, perm)]
    pallas_call x32 -> x40, Pallas kernels: 23.1 us -> 59.9 us  [pack(): pl.pallas_call(pack_body, grid_spec=pltpu.PrefetchScalarGridSpec(num_scal...]
    ppermute x40 -> x50, starting transfers between devices: 212 us -> 198 us  [send(): got = lax.ppermute(cut(tie(source, self.done())), axis, perm)]
    ppermute x7, starting transfers between devices: 21.4 us -> 9.39 us  [on_device(): lax.ppermute(pick(strips, moved(g, a, b)), 'gx', gx_perm(a, b))]
    dynamic_update_slice x27 -> x34, local copies, waits for them, and re-layouts: 26.9 us -> 38.4 us  [to_gx(): lax.dynamic_update_slice_in_dim(whole, got[:, None], moved(g, a, b, -1),...]
    dynamic_update_slice x12 -> x15, local copies, waits for them, and re-layouts: 28.6 us -> 31.3 us  [to_yz(): lax.dynamic_update_slice(cells, got[:, None], (first // m, (q - d) % m, 0...]
    pallas_call x4 -> x5, Pallas kernels: 23 us -> 25.5 us  [gram_of(): pl.pallas_call(functools.partial(gram_body, steps), grid=(steps,), in_spe...]
  transfers between devices with their start and end apart: 69 -> 79, of which waited for: 28 -> 35; matrix products, arithmetic and copies ran while one was open for 8% -> 11% of each run, Pallas kernels for 7% -> 11%
where the time goes in v4:
time: 1090 us; the launch traced here: 1080 us
  waiting for transfers between devices  564 us (52%)
  starting transfers between devices  240 us (22%)
  Pallas kernels  142 us (13%)
  local copies, waits for them, and re-layouts  127 us (12%)
    ppermute x50, waiting for transfers between devices, send(): got = lax.ppermute(cut(tie(source, self.done())), axis, perm)  496 us
    ppermute x50, starting transfers between devices, send(): got = lax.ppermute(cut(tie(source, self.done())), axis, perm)  198 us
    pallas_call x40, Pallas kernels, pack(): pl.pallas_call(pack_body, grid_spec=pltpu.PrefetchScalarGridSpec(num_scal...  59.9 us
    dynamic_update_slice x34, local copies, waits for them, and re-layouts, to_gx(): lax.dynamic_update_slice_in_dim(whole, got[:, None], moved(g, a, b, -1),...  38.4 us
    pallas_call x1, Pallas kernels, iterate(): pl.pallas_call(functools.partial(iterate_body, total), in_specs=[pl.Block...  34 us
    dynamic_update_slice x15, local copies, waits for them, and re-layouts, to_yz(): lax.dynamic_update_slice(cells, got[:, None], (first // m, (q - d) % m, 0...  31.3 us
    pallas_call x5, Pallas kernels, gram_of(): pl.pallas_call(functools.partial(gram_body, steps), grid=(steps,), in_spe...  25.5 us
    ppermute x1, waiting for transfers between devices, on_device(): lax.ppermute(pick(blocks_here, (chip + d) % chips), 'yz', perm)  24.1 us
  transfers between devices with their start and end apart: 79, of which 35 were waited for; matrix products, arithmetic and copies ran while one was open for 11% of the time, Pallas kernels for 11%

profile of v4, /device:TPU:0, one launch (start us, length us, event | category | flops | bytes accessed | tf_op | source)
XLA Modules:
  0.0 1080.4 jit_solution(17745277624503512704)
XLA Ops:
  2.1 5.1 collective-permute-start.2
  21.3 9.6 collective-permute-done.2
  33.9 110.3 %collective-permute-done.3 = f32[16,64,256]{2,1,0:T(8,128)} collective-permute-done((f32[16,64,256]{2,1,0:T(8,128)S(1)}, f32[16,64,256]{2,1,0:T(8,128)}, u32[]{:S(2)}, u32[]{:S(2)}) %collective-permute-start.3) | collective-permute-done | bytes 1048608 | tf_op jit(solution)/shard_map/ppermute | solution.py:297
  147.0 3.8 collective-permute-start.13
  150.8 37.4 %collective-permute-done = f32[16,64,256]{2,1,0:T(8,128)} collective-permute-done((f32[16,64,256]{2,1,0:T(8,128)}, f32[16,64,256]{2,1,0:T(8,128)}, u32[]{:S(2)}, u32[]{:S(2)}) %collective-permute-start) | collective-permute-done | bytes 1048608 | tf_op jit(solution)/shard_map/ppermute | solution.py:297
  191.1 4.8 collective-permute-start.6
  203.6 14.1 %collective-permute-done.5 = f32[16,64,256]{2,1,0:T(8,128)} collective-permute-done((f32[16,64,256]{2,1,0:T(8,128)S(1)}, f32[16,64,256]{2,1,0:T(8,128)}, u32[]{:S(2)}, u32[]{:S(2)}) %collective-permute-start.5) | collective-permute-done | bytes 1048608 | tf_op jit(solution)/shard_map/ppermute | solution.py:297
  219.9 65.6 %collective-permute-start.16 = (f32[16,64,256]{2,1,0:T(8,128)}, f32[16,64,256]{2,1,0:T(8,128)}, u32[]{:S(2)}, u32[]{:S(2)}) collective-permute-start(f32[16,64,256]{2,1,0:T(8,128)} %pack_z.55), channel_id=1, source_target_pairs={{0,20},{4,16},{8,28},{12,24},{16,4},{20,0},{24,12},{28,8},{1,21},{... | collective-permute-start | bytes 3145736 | tf_op jit(solution)/shard_map/ppermute | solution.py:297
  292.8 3.3 copy-done
  299.1 3.4 constant_dynamic-slice_fusion.20
  308.5 44.7 %collective-permute-done.16 = f32[16,64,256]{2,1,0:T(8,128)} collective-permute-done((f32[16,64,256]{2,1,0:T(8,128)}, f32[16,64,256]{2,1,0:T(8,128)}, u32[]{:S(2)}, u32[]{:S(2)}) %collective-permute-start.16) | collective-permute-done | bytes 1048608 | tf_op jit(solution)/shard_map/ppermute | solution.py:297
  356.5 2.8 collective-permute-start.12
  361.3 4.3 broadcast.69.clone
  370.4 5.7 gram_x.5.before_ref
  378.7 24.9 %collective-permute-done.17 = f32[16,64,256]{2,1,0:T(8,128)} collective-permute-done((f32[16,64,256]{2,1,0:T(8,128)S(1)}, f32[16,64,256]{2,1,0:T(8,128)}, u32[]{:S(2)}, u32[]{:S(2)}) %collective-permute-start.17) | collective-permute-done | bytes 1048608 | tf_op jit(solution)/shard_map/ppermute | solution.py:297
  408.0 11.1 %broadcast_in_dim.227 = f32[16,4,512,256]{3,2,1,0:T(8,128)} broadcast(f32[]{:T(128)} %constant.1232.clone.1), dimensions={} | broadcast | bytes 33554436 | tf_op jit(solution)/shard_map/broadcast_in_dim | solution.py:338
  424.3 3.8 collective-permute-start.15
  434.9 78.5 %collective-permute-done.18 = f32[16,64,256]{2,1,0:T(8,128)} collective-permute-done((f32[16,64,256]{2,1,0:T(8,128)S(1)}, f32[16,64,256]{2,1,0:T(8,128)}, u32[]{:S(2)}, u32[]{:S(2)}) %collective-permute-start.18) | collective-permute-done | bytes 1048608 | tf_op jit(solution)/shard_map/ppermute | solution.py:297
  514.9 4.6 collective-permute-start.23
  520.7 39.0 %collective-permute-start.28 = (f32[8,64,256]{2,1,0:T(8,128)S(1)}, f32[8,64,256]{2,1,0:T(8,128)S(1)}, u32[]{:S(2)}, u32[]{:S(2)}) collective-permute-start(f32[8,64,256]{2,1,0:T(8,128)S(1)} %pack_z.66), channel_id=1, source_target_pairs={{0,12},{4,8},{8,20},{12,16},{16,28},{20,24},{24,4},{28,0},{1,13},{... | collective-permute-start | bytes 1572872 | tf_op jit(solution)/shard_map/ppermute | solution.py:297
  572.5 3.0 constant_dynamic-slice_fusion.18
  577.0 3.0 constant_dynamic-slice_fusion.16
  580.0 3.0 constant_dynamic-slice_fusion.14
  584.8 3.1 bitcast_dynamic-update-slice_fusion.5
  589.1 7.8 collective-permute-start.29
  598.1 3.1 bitcast_dynamic-update-slice_fusion.4
  601.2 3.1 bitcast_dynamic-update-slice_fusion.10
  604.4 4.9 collective-permute-done.29
  611.3 12.9 %collective-permute-start.30 = (f32[8,64,256]{2,1,0:T(8,128)S(1)}, f32[8,64,256]{2,1,0:T(8,128)S(1)}, u32[]{:S(2)}, u32[]{:S(2)}) collective-permute-start(f32[8,64,256]{2,1,0:T(8,128)S(1)} %pack_z.68), channel_id=1, source_target_pairs={{0,12},{4,8},{8,20},{12,16},{16,28},{20,24},{24,4},{28,0},{1,13},{... | collective-permute-start | bytes 1572872 | tf_op jit(solution)/shard_map/ppermute | solution.py:297
  624.2 14.9 %collective-permute-done.35 = f32[8,64,256]{2,1,0:T(8,128)S(1)} collective-permute-done((f32[8,64,256]{2,1,0:T(8,128)S(1)}, f32[8,64,256]{2,1,0:T(8,128)S(1)}, u32[]{:S(2)}, u32[]{:S(2)}) %collective-permute-start.35) | collective-permute-done | bytes 524320 | tf_op jit(solution)/shard_map/ppermute | solution.py:297
  640.7 7.7 gram_x.6.before_ref
  648.4 6.9 collective-permute-done.36
  657.6 3.1 bitcast_dynamic-update-slice_fusion.9
  660.6 5.7 gram_x.7.before_ref
  669.5 23.4 %collective-permute-done.37 = f32[8,64,256]{2,1,0:T(8,128)S(1)} collective-permute-done((f32[8,64,256]{2,1,0:T(8,128)S(1)}, f32[8,64,256]{2,1,0:T(8,128)S(1)}, u32[]{:S(2)}, u32[]{:S(2)}) %collective-permute-start.37) | collective-permute-done | bytes 524320 | tf_op jit(solution)/shard_map/ppermute | solution.py:297
  697.5 4.5 collective-permute-start.32
  704.7 3.1 bitcast_dynamic-update-slice_fusion.3
  707.7 3.1 bitcast_dynamic-update-slice_fusion.2
  710.8 3.1 bitcast_dynamic-update-slice_fusion.8
  715.4 13.6 %collective-permute-done.25 = f32[8,64,256]{2,1,0:T(8,128)S(1)} collective-permute-done((f32[8,64,256]{2,1,0:T(8,128)S(1)}, f32[8,64,256]{2,1,0:T(8,128)S(1)}, u32[]{:S(2)}, u32[]{:S(2)}) %collective-permute-start.25) | collective-permute-done | bytes 524320 | tf_op jit(solution)/shard_map/ppermute | solution.py:297
  739.3 3.2 gram_x.8.before_ref
  742.4 35.4 %collective-permute-done.26 = f32[4,512,256]{2,1,0:T(8,128)S(1)} collective-permute-done((f32[4,512,256]{2,1,0:T(8,128)S(1)}, f32[4,512,256]{2,1,0:T(8,128)S(1)}, u32[]{:S(2)}, u32[]{:S(2)}) %collective-permute-start.26) | collective-permute-done | bytes 2097184 | tf_op jit(solution)/shard_map/ppermute | solution.py:297
  780.4 38.1 %collective-permute-done.33 = f32[4,512,256]{2,1,0:T(8,128)} collective-permute-done((f32[4,512,256]{2,1,0:T(8,128)}, f32[4,512,256]{2,1,0:T(8,128)}, u32[]{:S(2)}, u32[]{:S(2)}) %collective-permute-start.33) | collective-permute-done | bytes 2097184 | tf_op jit(solution)/shard_map/ppermute | solution.py:297
  819.8 18.0 %collective-permute-start.34 = (f32[8,64,256]{2,1,0:T(8,128)S(1)}, f32[8,64,256]{2,1,0:T(8,128)}, u32[]{:S(2)}, u32[]{:S(2)}) collective-permute-start(f32[8,64,256]{2,1,0:T(8,128)S(1)} %pack_z.70), channel_id=1, source_target_pairs={{0,24},{4,28},{8,0},{12,4},{16,8},{20,12},{24,16},{28,20},{1,25},{... | collective-permute-start | bytes 1572872 | tf_op jit(solution)/shard_map/ppermute | solution.py:297
  841.4 3.2 bitcast_dynamic-update-slice_fusion
  848.4 3.5 collective-permute-done.41
  856.1 3.2 gram_x.9
  859.3 11.5 %collective-permute-done.44 = f32[2,512,256]{2,1,0:T(8,128)S(1)} collective-permute-done((f32[2,512,256]{2,1,0:T(8,128)S(1)}, f32[2,512,256]{2,1,0:T(8,128)S(1)}, u32[]{:S(2)}, u32[]{:S(2)}) %collective-permute-start.44) | collective-permute-done | bytes 1048608 | tf_op jit(solution)/shard_map/ppermute | solution.py:297
  870.8 17.5 %collective-permute-done.45 = f32[2,512,256]{2,1,0:T(8,128)S(1)} collective-permute-done((f32[2,512,256]{2,1,0:T(8,128)S(1)}, f32[2,512,256]{2,1,0:T(8,128)S(1)}, u32[]{:S(2)}, u32[]{:S(2)}) %collective-permute-start.45) | collective-permute-done | bytes 1048608 | tf_op jit(solution)/shard_map/ppermute | solution.py:297
  899.5 5.6 collective-permute-done.47
  909.9 3.1 collective-permute-start.52
  916.8 2.8 collective-permute-done.51
  928.3 3.6 collective-permute-start.63
  939.1 3.4 collective-permute-done.64.refs_1_
  944.4 3.7 collective-permute-done.66.refs_3_
  950.5 34.0 %subspace.1.basis_ref = f32[512,128]{1,0:T(8,128)} custom-call(s32[4]{0:T(128)S(1)} %pad_add_fusion.places_ref, f32[128,512]{1,0:T(8,128)S(1)} %bitcast.358, f32[128,512]{1,0:T(8,128)S(1)} %collective-permute-done.64.refs_1_, f32[128,512]{1,0:T(8,128)S(1)} %collective-permute-done.65.refs_2_, f32[128,512]{1,0:T(8,128)S(1)} %collective-permute-done.66.refs_3_, ...), custom_call_target="tpu_custom_call" | custom-call | flops 40000000000 | bytes 524288 | tf_op jit(solution)/shard_map/subspace/pallas_call | solution.py:227
  985.6 3.7 collective-permute-done.68
  992.5 21.9 %core_gram_y.1 = f32[1024,1024]{1,0:T(8,128)S(1)} custom-call(f32[16,4,512,256]{3,2,1,0:T(8,128)} %bitcast_dynamic-update-slice_fusion.40.field_ref, f32[512,128]{1,0:T(8,128)S(1)} %copy-done.3), custom_call_target="tpu_custom_call" | custom-call | flops 15032385536 | bytes 33554432 | tf_op jit(solution)/shard_map/core_gram_y/pallas_call | solution.py:116
  1017.1 3.9 collective-permute-done.70
  1025.3 24.1 %collective-permute-done.71 = f32[256,1024]{1,0:T(8,128)} collective-permute-done((f32[256,1024]{1,0:T(8,128)S(1)}, f32[256,1024]{1,0:T(8,128)}, u32[]{:S(2)}, u32[]{:S(2)}) %collective-permute-start.71) | collective-permute-done | bytes 1048608 | tf_op jit(solution)/shard_map/ppermute | solution.py:416
  1050.9 5.1 collective-permute-start.78
  1057.2 3.2 collective-permute-start.74
  1065.7 8.2 collective-permute-done.75
  1073.9 5.4 collective-permute-done.72
  (280 shorter events, 202.4 us)
Async XLA Ops:
  2.1 28.8 %collective-permute-start.2 = (f32[16,64,256]{2,1,0:T(8,128)S(1)}, f32[16,64,256]{2,1,0:T(8,128)}, u32[]{:S(2)}, u32[]{:S(2)}) collective-permute-start(f32[16,64,256]{2,1,0:T(8,128)S(1)} %pack_z.42), channel_id=1, source_target_pairs={{0,24},{4,28},{8,0},{12,4},{16,8},{20,12},{24,16},{28,20},{1,25},{... | collective-permute-start | bytes 3145736 | tf_op jit(solution)/shard_map/ppermute | solution.py:297
  8.7 135.5 %collective-permute-start.3 = (f32[16,64,256]{2,1,0:T(8,128)S(1)}, f32[16,64,256]{2,1,0:T(8,128)}, u32[]{:S(2)}, u32[]{:S(2)}) collective-permute-start(f32[16,64,256]{2,1,0:T(8,128)S(1)} %pack_z.43), channel_id=1, source_target_pairs={{0,20},{4,16},{8,28},{12,24},{16,4},{20,0},{24,12},{28,8},{1,21},{... | collective-permute-start | bytes 3145736 | tf_op jit(solution)/shard_map/ppermute | solution.py:297
  11.3 134.3 %collective-permute-start.4 = (f32[16,64,256]{2,1,0:T(8,128)}, f32[16,64,256]{2,1,0:T(8,128)}, u32[]{:S(2)}, u32[]{:S(2)}) collective-permute-start(f32[16,64,256]{2,1,0:T(8,128)} %pack_z.44), channel_id=1, source_target_pairs={{0,4},{4,0},{8,12},{12,8},{16,20},{20,16},{24,28},{28,24},{1,5},{5... | collective-permute-start | bytes 3145736 | tf_op jit(solution)/shard_map/ppermute | solution.py:297
  14.8 173.4 %collective-permute-start = (f32[16,64,256]{2,1,0:T(8,128)}, f32[16,64,256]{2,1,0:T(8,128)}, u32[]{:S(2)}, u32[]{:S(2)}) collective-permute-start(f32[16,64,256]{2,1,0:T(8,128)} %pack_z.40), channel_id=1, source_target_pairs={{0,16},{4,20},{8,24},{12,28},{16,0},{20,4},{24,8},{28,12},{1,17},{... | collective-permute-start | bytes 3145736 | tf_op jit(solution)/shard_map/ppermute | solution.py:297
  19.8 169.9 %collective-permute-start.1 = (f32[16,64,256]{2,1,0:T(8,128)}, f32[16,64,256]{2,1,0:T(8,128)}, u32[]{:S(2)}, u32[]{:S(2)}) collective-permute-start(f32[16,64,256]{2,1,0:T(8,128)} %pack_z.41), channel_id=1, source_target_pairs={{0,12},{4,8},{8,20},{12,16},{16,28},{20,24},{24,4},{28,0},{1,13},{... | collective-permute-start | bytes 3145736 | tf_op jit(solution)/shard_map/ppermute | solution.py:297
  32.3 260.5 %collective-permute-start.7 = (f32[16,64,256]{2,1,0:T(8,128)S(1)}, f32[16,64,256]{2,1,0:T(8,128)}, u32[]{:S(2)}, u32[]{:S(2)}) collective-permute-start(f32[16,64,256]{2,1,0:T(8,128)S(1)} %pack_z.48), channel_id=1, source_target_pairs={{0,16},{4,20},{8,24},{12,28},{16,0},{20,4},{24,8},{28,12},{1,17},{... | collective-permute-start | bytes 3145736 | tf_op jit(solution)/shard_map/ppermute | solution.py:297
  145.5 142.3 %collective-permute-start.10 = (f32[16,64,256]{2,1,0:T(8,128)S(1)}, f32[16,64,256]{2,1,0:T(8,128)}, u32[]{:S(2)}, u32[]{:S(2)}) collective-permute-start(f32[16,64,256]{2,1,0:T(8,128)S(1)} %pack_z.50), channel_id=1, source_target_pairs={{0,12},{4,8},{8,20},{12,16},{16,28},{20,24},{24,4},{28,0},{1,13},{... | collective-permute-start | bytes 3145736 | tf_op jit(solution)/shard_map/ppermute | solution.py:297
  147.0 152.0 %collective-permute-start.13 = (f32[16,64,256]{2,1,0:T(8,128)S(1)}, f32[16,64,256]{2,1,0:T(8,128)S(1)}, u32[]{:S(2)}, u32[]{:S(2)}) collective-permute-start(f32[16,64,256]{2,1,0:T(8,128)S(1)} %pack_z.53), channel_id=1, source_target_pairs={{0,24},{4,28},{8,0},{12,4},{16,8},{20,12},{24,16},{28,20},{1,25},{... | collective-permute-start | bytes 3145736 | tf_op jit(solution)/shard_map/ppermute | solution.py:297
  189.6 28.1 %collective-permute-start.5 = (f32[16,64,256]{2,1,0:T(8,128)S(1)}, f32[16,64,256]{2,1,0:T(8,128)}, u32[]{:S(2)}, u32[]{:S(2)}) collective-permute-start(f32[16,64,256]{2,1,0:T(8,128)S(1)} %pack_z.45), channel_id=1, source_target_pairs={{0,8},{4,12},{8,16},{12,20},{16,24},{20,28},{24,0},{28,4},{1,9},{5... | collective-permute-start | bytes 3145736 | tf_op jit(solution)/shard_map/ppermute | solution.py:297
  191.1 94.5 %collective-permute-start.6 = (f32[16,64,256]{2,1,0:T(8,128)S(1)}, f32[16,64,256]{2,1,0:T(8,128)}, u32[]{:S(2)}, u32[]{:S(2)}) collective-permute-start(f32[16,64,256]{2,1,0:T(8,128)S(1)} %pack_z.46), channel_id=1, source_target_pairs={{0,28},{4,24},{8,4},{12,0},{16,12},{20,8},{24,20},{28,16},{1,29},{... | collective-permute-start | bytes 3145736 | tf_op jit(solution)/shard_map/ppermute | solution.py:297
  219.9 133.3 %collective-permute-start.16 = (f32[16,64,256]{2,1,0:T(8,128)}, f32[16,64,256]{2,1,0:T(8,128)}, u32[]{:S(2)}, u32[]{:S(2)}) collective-permute-start(f32[16,64,256]{2,1,0:T(8,128)} %pack_z.55), channel_id=1, source_target_pairs={{0,20},{4,16},{8,28},{12,24},{16,4},{20,0},{24,12},{28,8},{1,21},{... | collective-permute-start | bytes 3145736 | tf_op jit(solution)/shard_map/ppermute | solution.py:297
  287.8 71.5 %collective-permute-start.19 = (f32[16,64,256]{2,1,0:T(8,128)}, f32[16,64,256]{2,1,0:T(8,128)}, u32[]{:S(2)}, u32[]{:S(2)}) collective-permute-start(f32[16,64,256]{2,1,0:T(8,128)} %pack_z.58), channel_id=1, source_target_pairs={{0,4},{4,0},{8,12},{12,8},{16,20},{20,16},{24,28},{28,24},{1,5},{5... | collective-permute-start | bytes 3145736 | tf_op jit(solution)/shard_map/ppermute | solution.py:297
  290.0 64.9 %collective-permute-start.11 = (f32[16,64,256]{2,1,0:T(8,128)}, f32[16,64,256]{2,1,0:T(8,128)}, u32[]{:S(2)}, u32[]{:S(2)}) collective-permute-start(f32[16,64,256]{2,1,0:T(8,128)} %pack_z.51), channel_id=1, source_target_pairs={{0,8},{4,12},{8,16},{12,20},{16,24},{20,28},{24,0},{28,4},{1,9},{5... | collective-permute-start | bytes 3145736 | tf_op jit(solution)/shard_map/ppermute | solution.py:297
  297.6 79.6 %collective-permute-start.8 = (f32[4,512,256]{2,1,0:T(8,128)}, f32[4,512,256]{2,1,0:T(8,128)}, u32[]{:S(2)}, u32[]{:S(2)}) collective-permute-start(f32[4,512,256]{2,1,0:T(8,128)} %constant_dynamic-slice_fusion.21), channel_id=1, source_target_pairs={{0,2},{1,3},{2,0},{3,1},{4,6},{5,7},{6,4},{7,5},{8,10},{9,11},{10,... | collective-permute-start | bytes 6291464 | tf_op jit(solution)/shard_map/ppermute | solution.py:297
  302.5 120.4 %collective-permute-start.14 = (f32[4,512,256]{2,1,0:T(8,128)}, f32[4,512,256]{2,1,0:T(8,128)}, u32[]{:S(2)}, u32[]{:S(2)}) collective-permute-start(f32[4,512,256]{2,1,0:T(8,128)} %constant_dynamic-slice_fusion.20), channel_id=1, source_target_pairs={{0,1},{1,2},{2,3},{3,0},{4,5},{5,6},{6,7},{7,4},{8,9},{9,10},{10,1... | collective-permute-start | bytes 6291464 | tf_op jit(solution)/shard_map/ppermute | solution.py:297
  354.8 48.7 %collective-permute-start.17 = (f32[16,64,256]{2,1,0:T(8,128)S(1)}, f32[16,64,256]{2,1,0:T(8,128)}, u32[]{:S(2)}, u32[]{:S(2)}) collective-permute-start(f32[16,64,256]{2,1,0:T(8,128)S(1)} %pack_z.56), channel_id=1, source_target_pairs={{0,28},{4,24},{8,4},{12,0},{16,12},{20,8},{24,20},{28,16},{1,29},{... | collective-permute-start | bytes 3145736 | tf_op jit(solution)/shard_map/ppermute | solution.py:297
  356.5 48.6 %collective-permute-start.12 = (f32[16,64,256]{2,1,0:T(8,128)S(1)}, f32[16,64,256]{2,1,0:T(8,128)}, u32[]{:S(2)}, u32[]{:S(2)}) collective-permute-start(f32[16,64,256]{2,1,0:T(8,128)S(1)} %pack_z.52), channel_id=1, source_target_pairs={{0,12},{4,8},{8,20},{12,16},{16,28},{20,24},{24,4},{28,0},{1,13},{... | collective-permute-start | bytes 3145736 | tf_op jit(solution)/shard_map/ppermute | solution.py:297
  360.8 71.9 %collective-permute-start.20 = (f32[4,512,256]{2,1,0:T(8,128)}, f32[4,512,256]{2,1,0:T(8,128)}, u32[]{:S(2)}, u32[]{:S(2)}) collective-permute-start(f32[4,512,256]{2,1,0:T(8,128)} %constant_dynamic-slice_fusion.19), channel_id=1, source_target_pairs={{0,3},{1,0},{2,1},{3,2},{4,7},{5,4},{6,5},{7,6},{8,11},{9,8},{10,9... | collective-permute-start | bytes 6291464 | tf_op jit(solution)/shard_map/ppermute | solution.py:297
  378.6 181.1 %collective-permute-start.9 = (f32[16,64,256]{2,1,0:T(8,128)S(1)}, f32[16,64,256]{2,1,0:T(8,128)}, u32[]{:S(2)}, u32[]{:S(2)}) collective-permute-start(f32[16,64,256]{2,1,0:T(8,128)S(1)} %pack_z.49), channel_id=1, source_target_pairs={{0,16},{4,20},{8,24},{12,28},{16,0},{20,4},{24,8},{28,12},{1,17},{... | collective-permute-start | bytes 3145736 | tf_op jit(solution)/shard_map/ppermute | solution.py:297
  405.0 108.5 %collective-permute-start.18 = (f32[16,64,256]{2,1,0:T(8,128)S(1)}, f32[16,64,256]{2,1,0:T(8,128)}, u32[]{:S(2)}, u32[]{:S(2)}) collective-permute-start(f32[16,64,256]{2,1,0:T(8,128)S(1)} %pack_z.57), channel_id=1, source_target_pairs={{0,20},{4,16},{8,28},{12,24},{16,4},{20,0},{24,12},{28,8},{1,21},{... | collective-permute-start | bytes 3145736 | tf_op jit(solution)/shard_map/ppermute | solution.py:297
  406.6 112.9 %collective-permute-start.22 = (f32[16,64,256]{2,1,0:T(8,128)S(1)}, f32[16,64,256]{2,1,0:T(8,128)}, u32[]{:S(2)}, u32[]{:S(2)}) collective-permute-start(f32[16,64,256]{2,1,0:T(8,128)S(1)} %pack_z.60), channel_id=1, source_target_pairs={{0,8},{4,12},{8,16},{12,20},{16,24},{20,28},{24,0},{28,4},{1,9},{5... | collective-permute-start | bytes 3145736 | tf_op jit(solution)/shard_map/ppermute | solution.py:297
  424.3 139.1 %collective-permute-start.15 = (f32[16,64,256]{2,1,0:T(8,128)S(1)}, f32[16,64,256]{2,1,0:T(8,128)}, u32[]{:S(2)}, u32[]{:S(2)}) collective-permute-start(f32[16,64,256]{2,1,0:T(8,128)S(1)} %pack_z.54), channel_id=1, source_target_pairs={{0,24},{4,28},{8,0},{12,4},{16,8},{20,12},{24,16},{28,20},{1,25},{... | collective-permute-start | bytes 3145736 | tf_op jit(solution)/shard_map/ppermute | solution.py:297
  434.9 131.1 %collective-permute-start.21 = (f32[16,64,256]{2,1,0:T(8,128)}, f32[16,64,256]{2,1,0:T(8,128)}, u32[]{:S(2)}, u32[]{:S(2)}) collective-permute-start(f32[16,64,256]{2,1,0:T(8,128)} %pack_z.59), channel_id=1, source_target_pairs={{0,4},{4,0},{8,12},{12,8},{16,20},{20,16},{24,28},{28,24},{1,5},{5... | collective-permute-start | bytes 3145736 | tf_op jit(solution)/shard_map/ppermute | solution.py:297
  514.9 53.8 %collective-permute-start.23 = (f32[16,64,256]{2,1,0:T(8,128)S(1)}, f32[16,64,256]{2,1,0:T(8,128)}, u32[]{:S(2)}, u32[]{:S(2)}) collective-permute-start(f32[16,64,256]{2,1,0:T(8,128)S(1)} %pack_z.61), channel_id=1, source_target_pairs={{0,28},{4,24},{8,4},{12,0},{16,12},{20,8},{24,20},{28,16},{1,29},{... | collective-permute-start | bytes 3145736 | tf_op jit(solution)/shard_map/ppermute | solution.py:297
  520.7 67.2 %collective-permute-start.28 = (f32[8,64,256]{2,1,0:T(8,128)S(1)}, f32[8,64,256]{2,1,0:T(8,128)S(1)}, u32[]{:S(2)}, u32[]{:S(2)}) collective-permute-start(f32[8,64,256]{2,1,0:T(8,128)S(1)} %pack_z.66), channel_id=1, source_target_pairs={{0,12},{4,8},{8,20},{12,16},{16,28},{20,24},{24,4},{28,0},{1,13},{... | collective-permute-start | bytes 1572872 | tf_op jit(solution)/shard_map/ppermute | solution.py:297
  575.5 119.5 %collective-permute-start.24 = (f32[4,512,256]{2,1,0:T(8,128)}, f32[4,512,256]{2,1,0:T(8,128)}, u32[]{:S(2)}, u32[]{:S(2)}) collective-permute-start(f32[4,512,256]{2,1,0:T(8,128)} %constant_dynamic-slice_fusion.18), channel_id=1, source_target_pairs={{0,2},{1,3},{2,0},{3,1},{4,6},{5,7},{6,4},{7,5},{8,10},{9,11},{10,... | collective-permute-start | bytes 6291464 | tf_op jit(solution)/shard_map/ppermute | solution.py:297
  580.0 116.3 %collective-permute-start.31 = (f32[4,512,256]{2,1,0:T(8,128)}, f32[4,512,256]{2,1,0:T(8,128)}, u32[]{:S(2)}, u32[]{:S(2)}) collective-permute-start(f32[4,512,256]{2,1,0:T(8,128)} %constant_dynamic-slice_fusion.16), channel_id=1, source_target_pairs={{0,1},{1,2},{2,3},{3,0},{4,5},{5,6},{6,7},{7,4},{8,9},{9,10},{10,1... | collective-permute-start | bytes 6291464 | tf_op jit(solution)/shard_map/ppermute | solution.py:297
  583.0 119.0 %collective-permute-start.38 = (f32[4,512,256]{2,1,0:T(8,128)}, f32[4,512,256]{2,1,0:T(8,128)}, u32[]{:S(2)}, u32[]{:S(2)}) collective-permute-start(f32[4,512,256]{2,1,0:T(8,128)} %constant_dynamic-slice_fusion.14), channel_id=1, source_target_pairs={{0,3},{1,0},{2,1},{3,2},{4,7},{5,4},{6,5},{7,6},{8,11},{9,8},{10,9... | collective-permute-start | bytes 6291464 | tf_op jit(solution)/shard_map/ppermute | solution.py:297
  589.1 20.1 %collective-permute-start.29 = (f32[8,64,256]{2,1,0:T(8,128)S(1)}, f32[8,64,256]{2,1,0:T(8,128)S(1)}, u32[]{:S(2)}, u32[]{:S(2)}) collective-permute-start(f32[8,64,256]{2,1,0:T(8,128)S(1)} %pack_z.67), channel_id=1, source_target_pairs={{0,8},{4,12},{8,16},{12,20},{16,24},{20,28},{24,0},{28,4},{1,9},{5... | collective-permute-start | bytes 1572872 | tf_op jit(solution)/shard_map/ppermute | solution.py:297
  598.0 41.0 %collective-permute-start.35 = (f32[8,64,256]{2,1,0:T(8,128)S(1)}, f32[8,64,256]{2,1,0:T(8,128)S(1)}, u32[]{:S(2)}, u32[]{:S(2)}) collective-permute-start(f32[8,64,256]{2,1,0:T(8,128)S(1)} %pack_z.71), channel_id=1, source_target_pairs={{0,20},{4,16},{8,28},{12,24},{16,4},{20,0},{24,12},{28,8},{1,21},{... | collective-permute-start | bytes 1572872 | tf_op jit(solution)/shard_map/ppermute | solution.py:297
  611.3 55.1 %collective-permute-start.30 = (f32[8,64,256]{2,1,0:T(8,128)S(1)}, f32[8,64,256]{2,1,0:T(8,128)S(1)}, u32[]{:S(2)}, u32[]{:S(2)}) collective-permute-start(f32[8,64,256]{2,1,0:T(8,128)S(1)} %pack_z.68), channel_id=1, source_target_pairs={{0,12},{4,8},{8,20},{12,16},{16,28},{20,24},{24,4},{28,0},{1,13},{... | collective-permute-start | bytes 1572872 | tf_op jit(solution)/shard_map/ppermute | solution.py:297
  640.5 14.8 %collective-permute-start.36 = (f32[8,64,256]{2,1,0:T(8,128)S(1)}, f32[8,64,256]{2,1,0:T(8,128)S(1)}, u32[]{:S(2)}, u32[]{:S(2)}) collective-permute-start(f32[8,64,256]{2,1,0:T(8,128)S(1)} %pack_z.72), channel_id=1, source_target_pairs={{0,28},{4,24},{8,4},{12,0},{16,12},{20,8},{24,20},{28,16},{1,29},{... | collective-permute-start | bytes 1572872 | tf_op jit(solution)/shard_map/ppermute | solution.py:297
  656.7 36.2 %collective-permute-start.37 = (f32[8,64,256]{2,1,0:T(8,128)S(1)}, f32[8,64,256]{2,1,0:T(8,128)S(1)}, u32[]{:S(2)}, u32[]{:S(2)}) collective-permute-start(f32[8,64,256]{2,1,0:T(8,128)S(1)} %pack_z.73), channel_id=1, source_target_pairs={{0,20},{4,16},{8,28},{12,24},{16,4},{20,0},{24,12},{28,8},{1,21},{... | collective-permute-start | bytes 1572872 | tf_op jit(solution)/shard_map/ppermute | solution.py:297
  667.6 186.3 %collective-permute-start.42 = (f32[8,64,256]{2,1,0:T(8,128)S(1)}, f32[8,64,256]{2,1,0:T(8,128)}, u32[]{:S(2)}, u32[]{:S(2)}) collective-permute-start(f32[8,64,256]{2,1,0:T(8,128)S(1)} %pack_z.76), channel_id=1, source_target_pairs={{0,8},{4,12},{8,16},{12,20},{16,24},{20,28},{24,0},{28,4},{1,9},{5... | collective-permute-start | bytes 1572872 | tf_op jit(solution)/shard_map/ppermute | solution.py:297
  694.9 160.0 %collective-permute-start.43 = (f32[8,64,256]{2,1,0:T(8,128)S(1)}, f32[8,64,256]{2,1,0:T(8,128)}, u32[]{:S(2)}, u32[]{:S(2)}) collective-permute-start(f32[8,64,256]{2,1,0:T(8,128)S(1)} %pack_z.77), channel_id=1, source_target_pairs={{0,28},{4,24},{8,4},{12,0},{16,12},{20,8},{24,20},{28,16},{1,29},{... | collective-permute-start | bytes 1572872 | tf_op jit(solution)/shard_map/ppermute | solution.py:297
  696.2 32.8 %collective-permute-start.25 = (f32[8,64,256]{2,1,0:T(8,128)S(1)}, f32[8,64,256]{2,1,0:T(8,128)S(1)}, u32[]{:S(2)}, u32[]{:S(2)}) collective-permute-start(f32[8,64,256]{2,1,0:T(8,128)S(1)} %pack_z.64), channel_id=1, source_target_pairs={{0,16},{4,20},{8,24},{12,28},{16,0},{20,4},{24,8},{28,12},{1,17},{... | collective-permute-start | bytes 1572872 | tf_op jit(solution)/shard_map/ppermute | solution.py:297
  697.5 33.9 %collective-permute-start.32 = (f32[8,64,256]{2,1,0:T(8,128)S(1)}, f32[8,64,256]{2,1,0:T(8,128)S(1)}, u32[]{:S(2)}, u32[]{:S(2)}) collective-permute-start(f32[8,64,256]{2,1,0:T(8,128)S(1)} %pack_z.69), channel_id=1, source_target_pairs={{0,24},{4,28},{8,0},{12,4},{16,8},{20,12},{24,16},{28,20},{1,25},{... | collective-permute-start | bytes 1572872 | tf_op jit(solution)/shard_map/ppermute | solution.py:297
  703.2 29.8 %collective-permute-start.39 = (f32[8,64,256]{2,1,0:T(8,128)S(1)}, f32[8,64,256]{2,1,0:T(8,128)S(1)}, u32[]{:S(2)}, u32[]{:S(2)}) collective-permute-start(f32[8,64,256]{2,1,0:T(8,128)S(1)} %pack_z.74), channel_id=1, source_target_pairs={{0,4},{4,0},{8,12},{12,8},{16,20},{20,16},{24,28},{28,24},{1,5},{5... | collective-permute-start | bytes 1572872 | tf_op jit(solution)/shard_map/ppermute | solution.py:297
  729.2 48.6 %collective-permute-start.26 = (f32[4,512,256]{2,1,0:T(8,128)S(1)}, f32[4,512,256]{2,1,0:T(8,128)S(1)}, u32[]{:S(2)}, u32[]{:S(2)}) collective-permute-start(f32[4,512,256]{2,1,0:T(8,128)S(1)} %constant_dynamic-slice_fusion.17), channel_id=1, source_target_pairs={{0,2},{1,3},{2,0},{3,1},{4,6},{5,7},{6,4},{7,5},{8,10},{9,11},{10,... | collective-permute-start | bytes 6291464 | tf_op jit(solution)/shard_map/ppermute | solution.py:297
  732.9 85.7 %collective-permute-start.33 = (f32[4,512,256]{2,1,0:T(8,128)}, f32[4,512,256]{2,1,0:T(8,128)}, u32[]{:S(2)}, u32[]{:S(2)}) collective-permute-start(f32[4,512,256]{2,1,0:T(8,128)} %constant_dynamic-slice_fusion.15), channel_id=1, source_target_pairs={{0,1},{1,2},{2,3},{3,0},{4,5},{5,6},{6,7},{7,4},{8,9},{9,10},{10,1... | collective-permute-start | bytes 6291464 | tf_op jit(solution)/shard_map/ppermute | solution.py:297
  734.5 103.2 %collective-permute-start.40 = (f32[4,512,256]{2,1,0:T(8,128)}, f32[4,512,256]{2,1,0:T(8,128)S(1)}, u32[]{:S(2)}, u32[]{:S(2)}) collective-permute-start(f32[4,512,256]{2,1,0:T(8,128)} %constant_dynamic-slice_fusion.13), channel_id=1, source_target_pairs={{0,3},{1,0},{2,1},{3,2},{4,7},{5,4},{6,5},{7,6},{8,11},{9,8},{10,9... | collective-permute-start | bytes 6291464 | tf_op jit(solution)/shard_map/ppermute | solution.py:297
  780.3 64.2 %collective-permute-start.27 = (f32[8,64,256]{2,1,0:T(8,128)S(1)}, f32[8,64,256]{2,1,0:T(8,128)S(1)}, u32[]{:S(2)}, u32[]{:S(2)}) collective-permute-start(f32[8,64,256]{2,1,0:T(8,128)S(1)} %pack_z.65), channel_id=1, source_target_pairs={{0,16},{4,20},{8,24},{12,28},{16,0},{20,4},{24,8},{28,12},{1,17},{... | collective-permute-start | bytes 1572872 | tf_op jit(solution)/shard_map/ppermute | solution.py:297
  819.8 28.5 %collective-permute-start.34 = (f32[8,64,256]{2,1,0:T(8,128)S(1)}, f32[8,64,256]{2,1,0:T(8,128)}, u32[]{:S(2)}, u32[]{:S(2)}) collective-permute-start(f32[8,64,256]{2,1,0:T(8,128)S(1)} %pack_z.70), channel_id=1, source_target_pairs={{0,24},{4,28},{8,0},{12,4},{16,8},{20,12},{24,16},{28,20},{1,25},{... | collective-permute-start | bytes 1572872 | tf_op jit(solution)/shard_map/ppermute | solution.py:297
  839.1 12.8 %collective-permute-start.41 = (f32[8,64,256]{2,1,0:T(8,128)S(1)}, f32[8,64,256]{2,1,0:T(8,128)S(1)}, u32[]{:S(2)}, u32[]{:S(2)}) collective-permute-start(f32[8,64,256]{2,1,0:T(8,128)S(1)} %pack_z.75), channel_id=1, source_target_pairs={{0,4},{4,0},{8,12},{12,8},{16,20},{20,16},{24,28},{28,24},{1,5},{5... | collective-permute-start | bytes 1572872 | tf_op jit(solution)/shard_map/ppermute | solution.py:297
  844.7 26.2 %collective-permute-start.44 = (f32[2,512,256]{2,1,0:T(8,128)S(1)}, f32[2,512,256]{2,1,0:T(8,128)S(1)}, u32[]{:S(2)}, u32[]{:S(2)}) collective-permute-start(f32[2,512,256]{2,1,0:T(8,128)S(1)} %constant_dynamic-slice_fusion.12), channel_id=1, source_target_pairs={{0,2},{1,3},{2,0},{3,1},{4,6},{5,7},{6,4},{7,5},{8,10},{9,11},{10,... | collective-permute-start | bytes 3145736 | tf_op jit(solution)/shard_map/ppermute | solution.py:297
  848.3 40.0 %collective-permute-start.45 = (f32[2,512,256]{2,1,0:T(8,128)S(1)}, f32[2,512,256]{2,1,0:T(8,128)S(1)}, u32[]{:S(2)}, u32[]{:S(2)}) collective-permute-start(f32[2,512,256]{2,1,0:T(8,128)S(1)} %constant_dynamic-slice_fusion.11), channel_id=1, source_target_pairs={{0,1},{1,2},{2,3},{3,0},{4,5},{5,6},{6,7},{7,4},{8,9},{9,10},{10,1... | collective-permute-start | bytes 3145736 | tf_op jit(solution)/shard_map/ppermute | solution.py:297
  852.0 36.9 %collective-permute-start.46 = (f32[2,512,256]{2,1,0:T(8,128)S(1)}, f32[2,512,256]{2,1,0:T(8,128)S(1)}, u32[]{:S(2)}, u32[]{:S(2)}) collective-permute-start(f32[2,512,256]{2,1,0:T(8,128)S(1)} %constant_dynamic-slice_fusion.10), channel_id=1, source_target_pairs={{0,3},{1,0},{2,1},{3,2},{4,7},{5,4},{6,5},{7,6},{8,11},{9,8},{10,9... | collective-permute-start | bytes 3145736 | tf_op jit(solution)/shard_map/ppermute | solution.py:297
  890.9 8.6 collective-permute-start.48
  890.9 14.2 %collective-permute-start.47 = (f32[128,512]{1,0:T(8,128)S(1)}, f32[128,512]{1,0:T(8,128)S(1)}, u32[]{:S(2)}, u32[]{:S(2)}) collective-permute-start(f32[128,512]{1,0:T(8,128)S(1)} %get-tuple-element.105), channel_id=1, source_target_pairs={{0,2},{1,3},{2,0},{3,1},{4,6},{5,7},{6,4},{7,5},{8,10},{9,11},{10,... | collective-permute-start | bytes 786440 | tf_op jit(solution)/shard_map/ppermute | solution.py:385
  924.3 8.7 collective-permute-start.59
  934.1 8.4 collective-permute-start.64
  935.8 8.6 collective-permute-start.65
  935.8 12.3 %collective-permute-start.66 = (f32[128,512]{1,0:T(8,128)S(1)}, f32[128,512]{1,0:T(8,128)S(1)}, u32[]{:S(2)}, u32[]{:S(2)}) collective-permute-start(f32[128,512]{1,0:T(8,128)S(1)} %bitcast.357), channel_id=1, source_target_pairs={{0,3},{1,0},{2,1},{3,2},{4,7},{5,4},{6,5},{7,6},{8,11},{9,8},{10,9... | collective-permute-start | bytes 786440 | tf_op jit(solution)/shard_map/ppermute | solution.py:394
  938.7 45.9 %collective-permute-start.67 = (f32[2,512,256]{2,1,0:T(8,128)S(1)}, f32[2,512,256]{2,1,0:T(8,128)S(1)}, u32[]{:S(2)}, u32[]{:S(2)}) collective-permute-start(f32[2,512,256]{2,1,0:T(8,128)S(1)} %constant_dynamic-slice_fusion.8), channel_id=1, source_target_pairs={{0,2},{1,3},{2,0},{3,1},{4,6},{5,7},{6,4},{7,5},{8,10},{9,11},{10,... | collective-permute-start | bytes 3145736 | tf_op jit(solution)/shard_map/ppermute | solution.py:297
  948.2 41.2 %collective-permute-start.68 = (f32[2,512,256]{2,1,0:T(8,128)S(1)}, f32[2,512,256]{2,1,0:T(8,128)S(1)}, u32[]{:S(2)}, u32[]{:S(2)}) collective-permute-start(f32[2,512,256]{2,1,0:T(8,128)S(1)} %constant_dynamic-slice_fusion.7), channel_id=1, source_target_pairs={{0,1},{1,2},{2,3},{3,0},{4,5},{5,6},{6,7},{7,4},{8,9},{9,10},{10,1... | collective-permute-start | bytes 3145736 | tf_op jit(solution)/shard_map/ppermute | solution.py:297
  948.3 42.1 %collective-permute-start.69 = (f32[2,512,256]{2,1,0:T(8,128)S(1)}, f32[2,512,256]{2,1,0:T(8,128)S(1)}, u32[]{:S(2)}, u32[]{:S(2)}) collective-permute-start(f32[2,512,256]{2,1,0:T(8,128)S(1)} %constant_dynamic-slice_fusion.6), channel_id=1, source_target_pairs={{0,3},{1,0},{2,1},{3,2},{4,7},{5,4},{6,5},{7,6},{8,11},{9,8},{10,9... | collective-permute-start | bytes 3145736 | tf_op jit(solution)/shard_map/ppermute | solution.py:297
  1023.7 25.6 %collective-permute-start.71 = (f32[256,1024]{1,0:T(8,128)S(1)}, f32[256,1024]{1,0:T(8,128)}, u32[]{:S(2)}, u32[]{:S(2)}) collective-permute-start(f32[256,1024]{1,0:T(8,128)S(1)} %dynamic-slice_bitcast_fusion.1), channel_id=1, source_target_pairs={{0,2},{1,3},{2,0},{3,1},{4,6},{5,7},{6,4},{7,5},{8,10},{9,11},{10,... | collective-permute-start | bytes 3145736 | tf_op jit(solution)/shard_map/ppermute | solution.py:416
  1050.9 9.6 collective-permute-start.78
  1055.9 8.3 collective-permute-start.77
  1055.9 9.7 collective-permute-start.76
  1056.6 17.2 %collective-permute-start.75 = (f32[256,128]{1,0:T(8,128)S(1)}, f32[256,128]{1,0:T(8,128)S(1)}, u32[]{:S(2)}, u32[]{:S(2)}) collective-permute-start(f32[256,128]{1,0:T(8,128)S(1)} %get-tuple-element.102), channel_id=1, source_target_pairs={{0,20},{4,16},{8,28},{12,24},{16,4},{20,0},{24,12},{28,8},{1,21},{... | collective-permute-start | bytes 393224 | tf_op jit(solution)/shard_map/ppermute | solution.py:424
  1057.2 16.6 %collective-permute-start.74 = (f32[256,128]{1,0:T(8,128)S(1)}, f32[256,128]{1,0:T(8,128)S(1)}, u32[]{:S(2)}, u32[]{:S(2)}) collective-permute-start(f32[256,128]{1,0:T(8,128)S(1)} %get-tuple-element.103), channel_id=1, source_target_pairs={{0,24},{4,28},{8,0},{12,4},{16,8},{20,12},{24,16},{28,20},{1,25},{... | collective-permute-start | bytes 393224 | tf_op jit(solution)/shard_map/ppermute | solution.py:424
  1060.4 13.4 %collective-permute-start.73 = (f32[256,128]{1,0:T(8,128)S(1)}, f32[256,128]{1,0:T(8,128)S(1)}, u32[]{:S(2)}, u32[]{:S(2)}) collective-permute-start(f32[256,128]{1,0:T(8,128)S(1)} %get-tuple-element.104), channel_id=1, source_target_pairs={{0,12},{4,8},{8,20},{12,16},{16,28},{20,24},{24,4},{28,0},{1,13},{... | collective-permute-start | bytes 393224 | tf_op jit(solution)/shard_map/ppermute | solution.py:424
  1064.3 15.0 %collective-permute-start.72 = (f32[256,128]{1,0:T(8,128)S(1)}, f32[256,128]{1,0:T(8,128)S(1)}, u32[]{:S(2)}, u32[]{:S(2)}) collective-permute-start(f32[256,128]{1,0:T(8,128)S(1)} %get-tuple-element.98), channel_id=1, source_target_pairs={{0,16},{4,20},{8,24},{12,28},{16,0},{20,4},{24,8},{28,12},{1,17},{... | collective-permute-start | bytes 393224 | tf_op jit(solution)/shard_map/ppermute | solution.py:424
  (37 other events, 224.1 us)

commit v5 on v4

--- a/solution.py
+++ b/solution.py
@@ -10,6 +10,7 @@
 
 ITERS = 4
 WINDOW = 5
+AHEAD = 2
 TALL = 8
 LINE = 4
 MIB = 1024 * 1024
@@ -289,12 +290,13 @@
     def __init__(self):
         self.ends = []
 
-    def done(self):
-        last = len(self.ends) - WINDOW + 1
+    def done(self, ahead):
+        last = len(self.ends) - WINDOW + 1 - ahead
         return self.ends[max(0, last - 1) : max(0, last)]
 
     def send(self, cut, source, axis, perm):
-        got = lax.ppermute(cut(tie(source, self.done())), axis, perm)
+        value = cut(tie(source, self.done(AHEAD)))
+        got = lax.ppermute(tie(value, self.done(0)), axis, perm)
         self.ends.append(got)
         return got
 

time: 1090 us -> 1000 us (0.917)
  waiting for transfers between devices: 564 us -> 383 us
  starting transfers between devices: 240 us -> 331 us
    ppermute x50, waiting for transfers between devices: 496 us -> 316 us  [send(): got = lax.ppermute(tie(value, self.done(0)), axis, perm)]
    ppermute x50, starting transfers between devices: 198 us -> 278 us  [send(): got = lax.ppermute(tie(value, self.done(0)), axis, perm)]
    ppermute x7, starting transfers between devices: 9.39 us -> 21.2 us  [on_device(): lax.ppermute(pick(strips, moved(g, a, b)), 'gx', gx_perm(a, b))]
    dynamic_update_slice x34 -> x35, local copies, waits for them, and re-layouts: 38.4 us -> 33.9 us  [to_gx(): lax.dynamic_update_slice_in_dim(whole, got[:, None], moved(g, a, b, -1),...]
  transfers between devices with their start and end apart: 79 -> 79, of which waited for: 35 -> 37; matrix products, arithmetic and copies ran while one was open for 11% -> 11% of each run, Pallas kernels for 11% -> 12%
where the time goes in v5:
time: 1000 us; the launch traced here: 992 us
  waiting for transfers between devices  383 us (38%)
  starting transfers between devices  331 us (33%)
  Pallas kernels  143 us (14%)
  local copies, waits for them, and re-layouts  127 us (13%)
    ppermute x50, waiting for transfers between devices, send(): got = lax.ppermute(tie(value, self.done(0)), axis, perm)  316 us
    ppermute x50, starting transfers between devices, send(): got = lax.ppermute(tie(value, self.done(0)), axis, perm)  278 us
    pallas_call x40, Pallas kernels, pack(): pl.pallas_call(pack_body, grid_spec=pltpu.PrefetchScalarGridSpec(num_scal...  60.9 us
    pallas_call x1, Pallas kernels, iterate(): pl.pallas_call(functools.partial(iterate_body, total), in_specs=[pl.Block...  34 us
    dynamic_update_slice x35, local copies, waits for them, and re-layouts, to_gx(): lax.dynamic_update_slice_in_dim(whole, got[:, None], moved(g, a, b, -1),...  33.9 us
    dynamic_update_slice x15, local copies, waits for them, and re-layouts, to_yz(): lax.dynamic_update_slice(cells, got[:, None], (first // m, (q - d) % m, 0...  31.3 us
    pallas_call x5, Pallas kernels, gram_of(): pl.pallas_call(functools.partial(gram_body, steps), grid=(steps,), in_spe...  26 us
    ppermute x1, waiting for transfers between devices, on_device(): lax.ppermute(pick(blocks_here, (chip + d) % chips), 'yz', perm)  24.2 us
  transfers between devices with their start and end apart: 79, of which 37 were waited for; matrix products, arithmetic and copies ran while one was open for 11% of the time, Pallas kernels for 12%

profile of v5, /device:TPU:0, one launch (start us, length us, event | category | flops | bytes accessed | tf_op | source)
XLA Modules:
  0.0 991.7 jit_solution(162817222582181305)
XLA Ops:
  2.9 4.0 collective-permute-start
  34.9 42.2 %collective-permute-done = f32[16,64,256]{2,1,0:T(8,128)} collective-permute-done((f32[16,64,256]{2,1,0:T(8,128)}, f32[16,64,256]{2,1,0:T(8,128)}, u32[]{:S(2)}, u32[]{:S(2)}) %collective-permute-start) | collective-permute-done | bytes 1048608 | tf_op jit(solution)/shard_map/ppermute | solution.py:299
  77.1 6.6 collective-permute-start.6
  85.1 43.0 %collective-permute-start.7 = (f32[16,64,256]{2,1,0:T(8,128)S(1)}, f32[16,64,256]{2,1,0:T(8,128)S(1)}, u32[]{:S(2)}, u32[]{:S(2)}) collective-permute-start(f32[16,64,256]{2,1,0:T(8,128)S(1)} %pack_z.48), channel_id=1, source_target_pairs={{0,24},{4,28},{8,0},{12,4},{16,8},{20,12},{24,16},{28,20},{1,25},{... | collective-permute-start | bytes 3145736 | tf_op jit(solution)/shard_map/ppermute | solution.py:299
  130.3 37.2 %collective-permute-done.3 = f32[16,64,256]{2,1,0:T(8,128)} collective-permute-done((f32[16,64,256]{2,1,0:T(8,128)}, f32[16,64,256]{2,1,0:T(8,128)}, u32[]{:S(2)}, u32[]{:S(2)}) %collective-permute-start.3) | collective-permute-done | bytes 1048608 | tf_op jit(solution)/shard_map/ppermute | solution.py:299
  167.5 22.1 %collective-permute-start.10 = (f32[16,64,256]{2,1,0:T(8,128)}, f32[16,64,256]{2,1,0:T(8,128)}, u32[]{:S(2)}, u32[]{:S(2)}) collective-permute-start(f32[16,64,256]{2,1,0:T(8,128)} %pack_z.53), channel_id=1, source_target_pairs={{0,12},{4,8},{8,20},{12,16},{16,28},{20,24},{24,4},{28,0},{1,13},{... | collective-permute-start | bytes 3145736 | tf_op jit(solution)/shard_map/ppermute | solution.py:299
  191.7 3.3 collective-permute-start.19
  210.8 5.9 collective-permute-done.10
  216.7 65.6 %collective-permute-start.11 = (f32[16,64,256]{2,1,0:T(8,128)S(1)}, f32[16,64,256]{2,1,0:T(8,128)}, u32[]{:S(2)}, u32[]{:S(2)}) collective-permute-start(f32[16,64,256]{2,1,0:T(8,128)S(1)} %pack_z.52), channel_id=1, source_target_pairs={{0,8},{4,12},{8,16},{12,20},{16,24},{20,28},{24,0},{28,4},{1,9},{5... | collective-permute-start | bytes 3145736 | tf_op jit(solution)/shard_map/ppermute | solution.py:299
  285.3 38.2 %collective-permute-done.19 = f32[16,64,256]{2,1,0:T(8,128)} collective-permute-done((f32[16,64,256]{2,1,0:T(8,128)}, f32[16,64,256]{2,1,0:T(8,128)}, u32[]{:S(2)}, u32[]{:S(2)}) %collective-permute-start.19) | collective-permute-done | bytes 1048608 | tf_op jit(solution)/shard_map/ppermute | solution.py:299
  326.8 4.4 broadcast.69.clone.2
  337.0 5.9 gram_x.5.before_ref
  346.1 6.0 collective-permute-start.15
  353.5 11.1 %broadcast_in_dim.227 = f32[16,4,512,256]{3,2,1,0:T(8,128)} broadcast(f32[]{:T(128)} %constant.1232.clone.1), dimensions={} | broadcast | bytes 33554436 | tf_op jit(solution)/shard_map/broadcast_in_dim | solution.py:340
  378.4 15.8 %collective-permute-done.15 = f32[16,64,256]{2,1,0:T(8,128)} collective-permute-done((f32[16,64,256]{2,1,0:T(8,128)S(1)}, f32[16,64,256]{2,1,0:T(8,128)}, u32[]{:S(2)}, u32[]{:S(2)}) %collective-permute-start.15) | collective-permute-done | bytes 1048608 | tf_op jit(solution)/shard_map/ppermute | solution.py:299
  394.3 3.6 collective-permute-start.16
  399.9 12.3 %collective-permute-done.22 = f32[4,512,256]{2,1,0:T(8,128)} collective-permute-done((f32[4,512,256]{2,1,0:T(8,128)}, f32[4,512,256]{2,1,0:T(8,128)}, u32[]{:S(2)}, u32[]{:S(2)}) %collective-permute-start.22) | collective-permute-done | bytes 2097184 | tf_op jit(solution)/shard_map/ppermute | solution.py:299
  415.9 3.1 bitcast_dynamic-update-slice_fusion.5
  426.3 7.7 gram_x.6.before_ref
  439.2 28.5 %collective-permute-done.16 = f32[16,64,256]{2,1,0:T(8,128)S(1)} collective-permute-done((f32[16,64,256]{2,1,0:T(8,128)S(1)}, f32[16,64,256]{2,1,0:T(8,128)S(1)}, u32[]{:S(2)}, u32[]{:S(2)}) %collective-permute-start.16) | collective-permute-done | bytes 1048608 | tf_op jit(solution)/shard_map/ppermute | solution.py:299
  467.8 25.3 %collective-permute-start.17 = (f32[16,64,256]{2,1,0:T(8,128)S(1)}, f32[16,64,256]{2,1,0:T(8,128)}, u32[]{:S(2)}, u32[]{:S(2)}) collective-permute-start(f32[16,64,256]{2,1,0:T(8,128)S(1)} %pack_z.55), channel_id=1, source_target_pairs={{0,28},{4,24},{8,4},{12,0},{16,12},{20,8},{24,20},{28,16},{1,29},{... | collective-permute-start | bytes 3145736 | tf_op jit(solution)/shard_map/ppermute | solution.py:299
  494.2 16.9 %collective-permute-done.21 = f32[16,64,256]{2,1,0:T(8,128)S(1)} collective-permute-done((f32[16,64,256]{2,1,0:T(8,128)S(1)}, f32[16,64,256]{2,1,0:T(8,128)S(1)}, u32[]{:S(2)}, u32[]{:S(2)}) %collective-permute-start.21) | collective-permute-done | bytes 1048608 | tf_op jit(solution)/shard_map/ppermute | solution.py:299
  511.2 3.4 constant_dynamic-slice_fusion.16
  526.8 6.7 collective-permute-done.17
  533.5 25.6 %collective-permute-start.18 = (f32[8,64,256]{2,1,0:T(8,128)S(1)}, f32[8,64,256]{2,1,0:T(8,128)S(1)}, u32[]{:S(2)}, u32[]{:S(2)}) collective-permute-start(f32[8,64,256]{2,1,0:T(8,128)S(1)} %pack_z.54), channel_id=1, source_target_pairs={{0,20},{4,16},{8,28},{12,24},{16,4},{20,0},{24,12},{28,8},{1,21},{... | collective-permute-start | bytes 1572872 | tf_op jit(solution)/shard_map/ppermute | solution.py:299
  563.3 5.9 gram_x.7.before_ref
  570.7 23.1 %collective-permute-done.18 = f32[8,64,256]{2,1,0:T(8,128)S(1)} collective-permute-done((f32[8,64,256]{2,1,0:T(8,128)S(1)}, f32[8,64,256]{2,1,0:T(8,128)S(1)}, u32[]{:S(2)}, u32[]{:S(2)}) %collective-permute-start.18) | collective-permute-done | bytes 524320 | tf_op jit(solution)/shard_map/ppermute | solution.py:299
  600.6 26.1 %collective-permute-start.35 = (f32[8,64,256]{2,1,0:T(8,128)S(1)}, f32[8,64,256]{2,1,0:T(8,128)S(1)}, u32[]{:S(2)}, u32[]{:S(2)}) collective-permute-start(f32[8,64,256]{2,1,0:T(8,128)S(1)} %pack_z.72), channel_id=1, source_target_pairs={{0,24},{4,28},{8,0},{12,4},{16,8},{20,12},{24,16},{28,20},{1,25},{... | collective-permute-start | bytes 1572872 | tf_op jit(solution)/shard_map/ppermute | solution.py:299
  631.0 3.2 bitcast_dynamic-update-slice_fusion.2
  636.5 4.5 collective-permute-done.35
  647.3 4.4 collective-permute-start.33
  660.8 6.5 collective-permute-done.33
  668.6 3.4 collective-permute-start.39
  675.6 3.2 gram_x.8.before_ref
  678.8 6.1 collective-permute-done.34
  686.1 20.3 %collective-permute-done.39 = f32[8,64,256]{2,1,0:T(8,128)S(1)} collective-permute-done((f32[8,64,256]{2,1,0:T(8,128)S(1)}, f32[8,64,256]{2,1,0:T(8,128)S(1)}, u32[]{:S(2)}, u32[]{:S(2)}) %collective-permute-start.39) | collective-permute-done | bytes 524320 | tf_op jit(solution)/shard_map/ppermute | solution.py:299
  707.8 14.5 %collective-permute-done.36 = f32[4,512,256]{2,1,0:T(8,128)} collective-permute-done((f32[4,512,256]{2,1,0:T(8,128)}, f32[4,512,256]{2,1,0:T(8,128)}, u32[]{:S(2)}, u32[]{:S(2)}) %collective-permute-start.36) | collective-permute-done | bytes 2097184 | tf_op jit(solution)/shard_map/ppermute | solution.py:299
  722.4 15.4 %collective-permute-start.37 = (f32[8,64,256]{2,1,0:T(8,128)S(1)}, f32[8,64,256]{2,1,0:T(8,128)S(1)}, u32[]{:S(2)}, u32[]{:S(2)}) collective-permute-start(f32[8,64,256]{2,1,0:T(8,128)S(1)} %pack_z.71), channel_id=1, source_target_pairs={{0,24},{4,28},{8,0},{12,4},{16,8},{20,12},{24,16},{28,20},{1,25},{... | collective-permute-start | bytes 1572872 | tf_op jit(solution)/shard_map/ppermute | solution.py:299
  737.8 3.1 bitcast_dynamic-update-slice_fusion.1
  742.1 3.1 bitcast_dynamic-update-slice_fusion
  746.6 4.0 collective-permute-done.37
  755.5 3.2 collective-permute-start.42
  758.8 8.2 collective-permute-done.41
  768.9 5.2 collective-permute-done.42
  775.3 3.2 gram_x.9
  778.6 8.6 collective-permute-done.45
  793.9 4.7 collective-permute-done.49
  800.5 3.4 collective-permute-done.47
  804.1 13.6 %collective-permute-start.56 = (f32[16,512]{1,0:T(8,128)S(1)}, f32[16,512]{1,0:T(8,128)S(1)}, u32[]{:S(2)}, u32[]{:S(2)}) collective-permute-start(f32[16,512]{1,0:T(8,128)S(1)} %get-tuple-element.195), channel_id=1, source_target_pairs={{0,28},{4,24},{8,4},{12,0},{16,12},{20,8},{24,20},{28,16},{1,29},{... | collective-permute-start | bytes 98312 | tf_op jit(solution)/shard_map/ppermute | solution.py:392
  821.1 3.2 collective-permute-start.52
  827.4 3.5 collective-permute-done.51
  831.3 3.2 collective-permute-start.58
  839.9 3.3 collective-permute-start.63
  850.4 3.5 collective-permute-done.64.refs_1_
  855.3 3.6 collective-permute-done.66.refs_3_
  861.4 34.0 %subspace.1.basis_ref = f32[512,128]{1,0:T(8,128)} custom-call(s32[4]{0:T(128)S(1)} %pad_add_fusion.places_ref, f32[128,512]{1,0:T(8,128)S(1)} %bitcast.356, f32[128,512]{1,0:T(8,128)S(1)} %collective-permute-done.64.refs_1_, f32[128,512]{1,0:T(8,128)S(1)} %collective-permute-done.65.refs_2_, f32[128,512]{1,0:T(8,128)S(1)} %collective-permute-done.66.refs_3_, ...), custom_call_target="tpu_custom_call" | custom-call | flops 40000000000 | bytes 524288 | tf_op jit(solution)/shard_map/subspace/pallas_call | solution.py:228
  896.5 3.8 collective-permute-done.68
  903.4 21.9 %core_gram_y.1 = f32[1024,1024]{1,0:T(8,128)S(1)} custom-call(f32[16,4,512,256]{3,2,1,0:T(8,128)} %bitcast_dynamic-update-slice_fusion.40.field_ref, f32[512,128]{1,0:T(8,128)S(1)} %copy-done.8), custom_call_target="tpu_custom_call" | custom-call | flops 15032385536 | bytes 33554432 | tf_op jit(solution)/shard_map/core_gram_y/pallas_call | solution.py:117
  928.4 3.9 collective-permute-done.70
  936.5 24.2 %collective-permute-done.71 = f32[256,1024]{1,0:T(8,128)} collective-permute-done((f32[256,1024]{1,0:T(8,128)S(1)}, f32[256,1024]{1,0:T(8,128)}, u32[]{:S(2)}, u32[]{:S(2)}) %collective-permute-start.71) | collective-permute-done | bytes 1048608 | tf_op jit(solution)/shard_map/ppermute | solution.py:418
  962.2 5.1 collective-permute-start.78
  968.3 3.2 collective-permute-start.74
  977.0 8.0 collective-permute-done.75
  984.9 5.6 collective-permute-done.72
  (300 shorter events, 217.4 us)
Async XLA Ops:
  2.9 74.1 %collective-permute-start = (f32[16,64,256]{2,1,0:T(8,128)}, f32[16,64,256]{2,1,0:T(8,128)}, u32[]{:S(2)}, u32[]{:S(2)}) collective-permute-start(f32[16,64,256]{2,1,0:T(8,128)} %pack_z.40), channel_id=1, source_target_pairs={{0,16},{4,20},{8,24},{12,28},{16,0},{20,4},{24,8},{28,12},{1,17},{... | collective-permute-start | bytes 3145736 | tf_op jit(solution)/shard_map/ppermute | solution.py:299
  9.1 67.9 %collective-permute-start.1 = (f32[16,64,256]{2,1,0:T(8,128)}, f32[16,64,256]{2,1,0:T(8,128)}, u32[]{:S(2)}, u32[]{:S(2)}) collective-permute-start(f32[16,64,256]{2,1,0:T(8,128)} %pack_z.41), channel_id=1, source_target_pairs={{0,12},{4,8},{8,20},{12,16},{16,28},{20,24},{24,4},{28,0},{1,13},{... | collective-permute-start | bytes 3145736 | tf_op jit(solution)/shard_map/ppermute | solution.py:299
  13.9 69.8 %collective-permute-start.2 = (f32[16,64,256]{2,1,0:T(8,128)}, f32[16,64,256]{2,1,0:T(8,128)}, u32[]{:S(2)}, u32[]{:S(2)}) collective-permute-start(f32[16,64,256]{2,1,0:T(8,128)} %pack_z.42), channel_id=1, source_target_pairs={{0,24},{4,28},{8,0},{12,4},{16,8},{20,12},{24,16},{28,20},{1,25},{... | collective-permute-start | bytes 3145736 | tf_op jit(solution)/shard_map/ppermute | solution.py:299
  18.4 66.7 %collective-permute-start.4 = (f32[16,64,256]{2,1,0:T(8,128)}, f32[16,64,256]{2,1,0:T(8,128)}, u32[]{:S(2)}, u32[]{:S(2)}) collective-permute-start(f32[16,64,256]{2,1,0:T(8,128)} %pack_z.44), channel_id=1, source_target_pairs={{0,4},{4,0},{8,12},{12,8},{16,20},{20,16},{24,28},{28,24},{1,5},{5... | collective-permute-start | bytes 3145736 | tf_op jit(solution)/shard_map/ppermute | solution.py:299
  21.1 146.4 %collective-permute-start.3 = (f32[16,64,256]{2,1,0:T(8,128)}, f32[16,64,256]{2,1,0:T(8,128)}, u32[]{:S(2)}, u32[]{:S(2)}) collective-permute-start(f32[16,64,256]{2,1,0:T(8,128)} %pack_z.43), channel_id=1, source_target_pairs={{0,20},{4,16},{8,28},{12,24},{16,4},{20,0},{24,12},{28,8},{1,21},{... | collective-permute-start | bytes 3145736 | tf_op jit(solution)/shard_map/ppermute | solution.py:299
  77.1 129.2 %collective-permute-start.5 = (f32[16,64,256]{2,1,0:T(8,128)}, f32[16,64,256]{2,1,0:T(8,128)S(1)}, u32[]{:S(2)}, u32[]{:S(2)}) collective-permute-start(f32[16,64,256]{2,1,0:T(8,128)} %copy-done.5), channel_id=1, source_target_pairs={{0,8},{4,12},{8,16},{12,20},{16,24},{20,28},{24,0},{28,4},{1,9},{5... | collective-permute-start | bytes 3145736 | tf_op jit(solution)/shard_map/ppermute | solution.py:299
  77.1 129.3 %collective-permute-start.6 = (f32[16,64,256]{2,1,0:T(8,128)}, f32[16,64,256]{2,1,0:T(8,128)}, u32[]{:S(2)}, u32[]{:S(2)}) collective-permute-start(f32[16,64,256]{2,1,0:T(8,128)} %copy-done.6), channel_id=1, source_target_pairs={{0,28},{4,24},{8,4},{12,0},{16,12},{20,8},{24,20},{28,16},{1,29},{... | collective-permute-start | bytes 3145736 | tf_op jit(solution)/shard_map/ppermute | solution.py:299
  85.1 122.7 %collective-permute-start.7 = (f32[16,64,256]{2,1,0:T(8,128)S(1)}, f32[16,64,256]{2,1,0:T(8,128)S(1)}, u32[]{:S(2)}, u32[]{:S(2)}) collective-permute-start(f32[16,64,256]{2,1,0:T(8,128)S(1)} %pack_z.48), channel_id=1, source_target_pairs={{0,24},{4,28},{8,0},{12,4},{16,8},{20,12},{24,16},{28,20},{1,25},{... | collective-permute-start | bytes 3145736 | tf_op jit(solution)/shard_map/ppermute | solution.py:299
  167.5 49.2 %collective-permute-start.10 = (f32[16,64,256]{2,1,0:T(8,128)}, f32[16,64,256]{2,1,0:T(8,128)}, u32[]{:S(2)}, u32[]{:S(2)}) collective-permute-start(f32[16,64,256]{2,1,0:T(8,128)} %pack_z.53), channel_id=1, source_target_pairs={{0,12},{4,8},{8,20},{12,16},{16,28},{20,24},{24,4},{28,0},{1,13},{... | collective-permute-start | bytes 3145736 | tf_op jit(solution)/shard_map/ppermute | solution.py:299
  191.7 131.7 %collective-permute-start.19 = (f32[16,64,256]{2,1,0:T(8,128)}, f32[16,64,256]{2,1,0:T(8,128)}, u32[]{:S(2)}, u32[]{:S(2)}) collective-permute-start(f32[16,64,256]{2,1,0:T(8,128)} %pack_z.61), channel_id=1, source_target_pairs={{0,16},{4,20},{8,24},{12,28},{16,0},{20,4},{24,8},{28,12},{1,17},{... | collective-permute-start | bytes 3145736 | tf_op jit(solution)/shard_map/ppermute | solution.py:299
  207.8 136.1 %collective-permute-start.8 = (f32[16,64,256]{2,1,0:T(8,128)}, f32[16,64,256]{2,1,0:T(8,128)}, u32[]{:S(2)}, u32[]{:S(2)}) collective-permute-start(f32[16,64,256]{2,1,0:T(8,128)} %pack_z.49), channel_id=1, source_target_pairs={{0,4},{4,0},{8,12},{12,8},{16,20},{20,16},{24,28},{28,24},{1,5},{5... | collective-permute-start | bytes 3145736 | tf_op jit(solution)/shard_map/ppermute | solution.py:299
  216.7 128.6 %collective-permute-start.11 = (f32[16,64,256]{2,1,0:T(8,128)S(1)}, f32[16,64,256]{2,1,0:T(8,128)}, u32[]{:S(2)}, u32[]{:S(2)}) collective-permute-start(f32[16,64,256]{2,1,0:T(8,128)S(1)} %pack_z.52), channel_id=1, source_target_pairs={{0,8},{4,12},{8,16},{12,20},{16,24},{20,28},{24,0},{28,4},{1,9},{5... | collective-permute-start | bytes 3145736 | tf_op jit(solution)/shard_map/ppermute | solution.py:299
  283.7 62.4 %collective-permute-start.14 = (f32[16,64,256]{2,1,0:T(8,128)S(1)}, f32[16,64,256]{2,1,0:T(8,128)}, u32[]{:S(2)}, u32[]{:S(2)}) collective-permute-start(f32[16,64,256]{2,1,0:T(8,128)S(1)} %pack_z.58), channel_id=1, source_target_pairs={{0,20},{4,16},{8,28},{12,24},{16,4},{20,0},{24,12},{28,8},{1,21},{... | collective-permute-start | bytes 3145736 | tf_op jit(solution)/shard_map/ppermute | solution.py:299
  323.5 74.4 %collective-permute-start.20 = (f32[4,512,256]{2,1,0:T(8,128)}, f32[4,512,256]{2,1,0:T(8,128)}, u32[]{:S(2)}, u32[]{:S(2)}) collective-permute-start(f32[4,512,256]{2,1,0:T(8,128)} %constant_dynamic-slice_fusion.20), channel_id=1, source_target_pairs={{0,2},{1,3},{2,0},{3,1},{4,6},{5,7},{6,4},{7,5},{8,10},{9,11},{10,... | collective-permute-start | bytes 6291464 | tf_op jit(solution)/shard_map/ppermute | solution.py:299
  326.8 85.3 %collective-permute-start.22 = (f32[4,512,256]{2,1,0:T(8,128)}, f32[4,512,256]{2,1,0:T(8,128)}, u32[]{:S(2)}, u32[]{:S(2)}) collective-permute-start(f32[4,512,256]{2,1,0:T(8,128)} %constant_dynamic-slice_fusion.19), channel_id=1, source_target_pairs={{0,1},{1,2},{2,3},{3,0},{4,5},{5,6},{6,7},{7,4},{8,9},{9,10},{10,1... | collective-permute-start | bytes 6291464 | tf_op jit(solution)/shard_map/ppermute | solution.py:299
  345.3 30.7 %collective-permute-start.12 = (f32[16,64,256]{2,1,0:T(8,128)S(1)}, f32[16,64,256]{2,1,0:T(8,128)S(1)}, u32[]{:S(2)}, u32[]{:S(2)}) collective-permute-start(f32[16,64,256]{2,1,0:T(8,128)S(1)} %pack_z.51), channel_id=1, source_target_pairs={{0,12},{4,8},{8,20},{12,16},{16,28},{20,24},{24,4},{28,0},{1,13},{... | collective-permute-start | bytes 3145736 | tf_op jit(solution)/shard_map/ppermute | solution.py:299
  346.1 48.2 %collective-permute-start.15 = (f32[16,64,256]{2,1,0:T(8,128)S(1)}, f32[16,64,256]{2,1,0:T(8,128)}, u32[]{:S(2)}, u32[]{:S(2)}) collective-permute-start(f32[16,64,256]{2,1,0:T(8,128)S(1)} %pack_z.57), channel_id=1, source_target_pairs={{0,28},{4,24},{8,4},{12,0},{16,12},{20,8},{24,20},{28,16},{1,29},{... | collective-permute-start | bytes 3145736 | tf_op jit(solution)/shard_map/ppermute | solution.py:299
  366.1 68.9 %collective-permute-start.9 = (f32[4,512,256]{2,1,0:T(8,128)}, f32[4,512,256]{2,1,0:T(8,128)S(1)}, u32[]{:S(2)}, u32[]{:S(2)}) collective-permute-start(f32[4,512,256]{2,1,0:T(8,128)} %constant_dynamic-slice_fusion.21), channel_id=1, source_target_pairs={{0,3},{1,0},{2,1},{3,2},{4,7},{5,4},{6,5},{7,6},{8,11},{9,8},{10,9... | collective-permute-start | bytes 6291464 | tf_op jit(solution)/shard_map/ppermute | solution.py:299
  394.3 73.5 %collective-permute-start.16 = (f32[16,64,256]{2,1,0:T(8,128)S(1)}, f32[16,64,256]{2,1,0:T(8,128)S(1)}, u32[]{:S(2)}, u32[]{:S(2)}) collective-permute-start(f32[16,64,256]{2,1,0:T(8,128)S(1)} %pack_z.56), channel_id=1, source_target_pairs={{0,20},{4,16},{8,28},{12,24},{16,4},{20,0},{24,12},{28,8},{1,21},{... | collective-permute-start | bytes 3145736 | tf_op jit(solution)/shard_map/ppermute | solution.py:299
  397.8 113.4 %collective-permute-start.21 = (f32[16,64,256]{2,1,0:T(8,128)S(1)}, f32[16,64,256]{2,1,0:T(8,128)S(1)}, u32[]{:S(2)}, u32[]{:S(2)}) collective-permute-start(f32[16,64,256]{2,1,0:T(8,128)S(1)} %pack_z.60), channel_id=1, source_target_pairs={{0,16},{4,20},{8,24},{12,28},{16,0},{20,4},{24,8},{28,12},{1,17},{... | collective-permute-start | bytes 3145736 | tf_op jit(solution)/shard_map/ppermute | solution.py:299
  412.1 102.5 %collective-permute-start.23 = (f32[16,64,256]{2,1,0:T(8,128)S(1)}, f32[16,64,256]{2,1,0:T(8,128)S(1)}, u32[]{:S(2)}, u32[]{:S(2)}) collective-permute-start(f32[16,64,256]{2,1,0:T(8,128)S(1)} %pack_z.62), channel_id=1, source_target_pairs={{0,24},{4,28},{8,0},{12,4},{16,8},{20,12},{24,16},{28,20},{1,25},{... | collective-permute-start | bytes 3145736 | tf_op jit(solution)/shard_map/ppermute | solution.py:299
  437.1 88.5 %collective-permute-start.13 = (f32[16,64,256]{2,1,0:T(8,128)S(1)}, f32[16,64,256]{2,1,0:T(8,128)S(1)}, u32[]{:S(2)}, u32[]{:S(2)}) collective-permute-start(f32[16,64,256]{2,1,0:T(8,128)S(1)} %pack_z.50), channel_id=1, source_target_pairs={{0,8},{4,12},{8,16},{12,20},{16,24},{20,28},{24,0},{28,4},{1,9},{5... | collective-permute-start | bytes 3145736 | tf_op jit(solution)/shard_map/ppermute | solution.py:299
  467.8 65.7 %collective-permute-start.17 = (f32[16,64,256]{2,1,0:T(8,128)S(1)}, f32[16,64,256]{2,1,0:T(8,128)}, u32[]{:S(2)}, u32[]{:S(2)}) collective-permute-start(f32[16,64,256]{2,1,0:T(8,128)S(1)} %pack_z.55), channel_id=1, source_target_pairs={{0,28},{4,24},{8,4},{12,0},{16,12},{20,8},{24,20},{28,16},{1,29},{... | collective-permute-start | bytes 3145736 | tf_op jit(solution)/shard_map/ppermute | solution.py:299
  493.0 66.1 %collective-permute-start.24 = (f32[16,64,256]{2,1,0:T(8,128)S(1)}, f32[16,64,256]{2,1,0:T(8,128)}, u32[]{:S(2)}, u32[]{:S(2)}) collective-permute-start(f32[16,64,256]{2,1,0:T(8,128)S(1)} %pack_z.63), channel_id=1, source_target_pairs={{0,4},{4,0},{8,12},{12,8},{16,20},{20,16},{24,28},{28,24},{1,5},{5... | collective-permute-start | bytes 3145736 | tf_op jit(solution)/shard_map/ppermute | solution.py:299
  511.2 85.5 %collective-permute-start.25 = (f32[4,512,256]{2,1,0:T(8,128)}, f32[4,512,256]{2,1,0:T(8,128)}, u32[]{:S(2)}, u32[]{:S(2)}) collective-permute-start(f32[4,512,256]{2,1,0:T(8,128)} %constant_dynamic-slice_fusion.17), channel_id=1, source_target_pairs={{0,2},{1,3},{2,0},{3,1},{4,6},{5,7},{6,4},{7,5},{8,10},{9,11},{10,... | collective-permute-start | bytes 6291464 | tf_op jit(solution)/shard_map/ppermute | solution.py:299
  514.7 85.9 %collective-permute-start.29 = (f32[4,512,256]{2,1,0:T(8,128)}, f32[4,512,256]{2,1,0:T(8,128)}, u32[]{:S(2)}, u32[]{:S(2)}) collective-permute-start(f32[4,512,256]{2,1,0:T(8,128)} %constant_dynamic-slice_fusion.16), channel_id=1, source_target_pairs={{0,1},{1,2},{2,3},{3,0},{4,5},{5,6},{6,7},{7,4},{8,9},{9,10},{10,1... | collective-permute-start | bytes 6291464 | tf_op jit(solution)/shard_map/ppermute | solution.py:299
  533.5 60.3 %collective-permute-start.18 = (f32[8,64,256]{2,1,0:T(8,128)S(1)}, f32[8,64,256]{2,1,0:T(8,128)S(1)}, u32[]{:S(2)}, u32[]{:S(2)}) collective-permute-start(f32[8,64,256]{2,1,0:T(8,128)S(1)} %pack_z.54), channel_id=1, source_target_pairs={{0,20},{4,16},{8,28},{12,24},{16,4},{20,0},{24,12},{28,8},{1,21},{... | collective-permute-start | bytes 1572872 | tf_op jit(solution)/shard_map/ppermute | solution.py:299
  559.1 85.6 %collective-permute-start.30 = (f32[4,512,256]{2,1,0:T(8,128)}, f32[4,512,256]{2,1,0:T(8,128)}, u32[]{:S(2)}, u32[]{:S(2)}) collective-permute-start(f32[4,512,256]{2,1,0:T(8,128)} %constant_dynamic-slice_fusion.15), channel_id=1, source_target_pairs={{0,3},{1,0},{2,1},{3,2},{4,7},{5,4},{6,5},{7,6},{8,11},{9,8},{10,9... | collective-permute-start | bytes 6291464 | tf_op jit(solution)/shard_map/ppermute | solution.py:299
  560.3 34.9 %collective-permute-start.32 = (f32[8,64,256]{2,1,0:T(8,128)S(1)}, f32[8,64,256]{2,1,0:T(8,128)S(1)}, u32[]{:S(2)}, u32[]{:S(2)}) collective-permute-start(f32[8,64,256]{2,1,0:T(8,128)S(1)} %pack_z.70), channel_id=1, source_target_pairs={{0,12},{4,8},{8,20},{12,16},{16,28},{20,24},{24,4},{28,0},{1,13},{... | collective-permute-start | bytes 1572872 | tf_op jit(solution)/shard_map/ppermute | solution.py:299
  596.6 71.9 %collective-permute-start.38 = (f32[8,64,256]{2,1,0:T(8,128)S(1)}, f32[8,64,256]{2,1,0:T(8,128)S(1)}, u32[]{:S(2)}, u32[]{:S(2)}) collective-permute-start(f32[8,64,256]{2,1,0:T(8,128)S(1)} %pack_z.74), channel_id=1, source_target_pairs={{0,28},{4,24},{8,4},{12,0},{16,12},{20,8},{24,20},{28,16},{1,29},{... | collective-permute-start | bytes 1572872 | tf_op jit(solution)/shard_map/ppermute | solution.py:299
  596.7 37.5 %collective-permute-start.26 = (f32[8,64,256]{2,1,0:T(8,128)S(1)}, f32[8,64,256]{2,1,0:T(8,128)S(1)}, u32[]{:S(2)}, u32[]{:S(2)}) collective-permute-start(f32[8,64,256]{2,1,0:T(8,128)S(1)} %pack_z.65), channel_id=1, source_target_pairs={{0,16},{4,20},{8,24},{12,28},{16,0},{20,4},{24,8},{28,12},{1,17},{... | collective-permute-start | bytes 1572872 | tf_op jit(solution)/shard_map/ppermute | solution.py:299
  600.6 40.4 %collective-permute-start.35 = (f32[8,64,256]{2,1,0:T(8,128)S(1)}, f32[8,64,256]{2,1,0:T(8,128)S(1)}, u32[]{:S(2)}, u32[]{:S(2)}) collective-permute-start(f32[8,64,256]{2,1,0:T(8,128)S(1)} %pack_z.72), channel_id=1, source_target_pairs={{0,24},{4,28},{8,0},{12,4},{16,8},{20,12},{24,16},{28,20},{1,25},{... | collective-permute-start | bytes 1572872 | tf_op jit(solution)/shard_map/ppermute | solution.py:299
  634.3 72.2 %collective-permute-start.27 = (f32[4,512,256]{2,1,0:T(8,128)}, f32[4,512,256]{2,1,0:T(8,128)}, u32[]{:S(2)}, u32[]{:S(2)}) collective-permute-start(f32[4,512,256]{2,1,0:T(8,128)} %constant_dynamic-slice_fusion.18), channel_id=1, source_target_pairs={{0,2},{1,3},{2,0},{3,1},{4,6},{5,7},{6,4},{7,5},{8,10},{9,11},{10,... | collective-permute-start | bytes 6291464 | tf_op jit(solution)/shard_map/ppermute | solution.py:299
  641.8 80.6 %collective-permute-start.36 = (f32[4,512,256]{2,1,0:T(8,128)}, f32[4,512,256]{2,1,0:T(8,128)}, u32[]{:S(2)}, u32[]{:S(2)}) collective-permute-start(f32[4,512,256]{2,1,0:T(8,128)} %constant_dynamic-slice_fusion.14), channel_id=1, source_target_pairs={{0,1},{1,2},{2,3},{3,0},{4,5},{5,6},{6,7},{7,4},{8,9},{9,10},{10,1... | collective-permute-start | bytes 6291464 | tf_op jit(solution)/shard_map/ppermute | solution.py:299
  644.7 14.8 %collective-permute-start.31 = (f32[8,64,256]{2,1,0:T(8,128)S(1)}, f32[8,64,256]{2,1,0:T(8,128)}, u32[]{:S(2)}, u32[]{:S(2)}) collective-permute-start(f32[8,64,256]{2,1,0:T(8,128)S(1)} %pack_z.67), channel_id=1, source_target_pairs={{0,4},{4,0},{8,12},{12,8},{16,20},{20,16},{24,28},{28,24},{1,5},{5... | collective-permute-start | bytes 1572872 | tf_op jit(solution)/shard_map/ppermute | solution.py:299
  647.3 20.1 %collective-permute-start.33 = (f32[8,64,256]{2,1,0:T(8,128)S(1)}, f32[8,64,256]{2,1,0:T(8,128)}, u32[]{:S(2)}, u32[]{:S(2)}) collective-permute-start(f32[8,64,256]{2,1,0:T(8,128)S(1)} %pack_z.69), channel_id=1, source_target_pairs={{0,8},{4,12},{8,16},{12,20},{16,24},{20,28},{24,0},{28,4},{1,9},{5... | collective-permute-start | bytes 1572872 | tf_op jit(solution)/shard_map/ppermute | solution.py:299
  667.3 17.6 %collective-permute-start.34 = (f32[8,64,256]{2,1,0:T(8,128)S(1)}, f32[8,64,256]{2,1,0:T(8,128)S(1)}, u32[]{:S(2)}, u32[]{:S(2)}) collective-permute-start(f32[8,64,256]{2,1,0:T(8,128)S(1)} %pack_z.68), channel_id=1, source_target_pairs={{0,12},{4,8},{8,20},{12,16},{16,28},{20,24},{24,4},{28,0},{1,13},{... | collective-permute-start | bytes 1572872 | tf_op jit(solution)/shard_map/ppermute | solution.py:299
  668.6 37.8 %collective-permute-start.39 = (f32[8,64,256]{2,1,0:T(8,128)S(1)}, f32[8,64,256]{2,1,0:T(8,128)S(1)}, u32[]{:S(2)}, u32[]{:S(2)}) collective-permute-start(f32[8,64,256]{2,1,0:T(8,128)S(1)} %pack_z.73), channel_id=1, source_target_pairs={{0,20},{4,16},{8,28},{12,24},{16,4},{20,0},{24,12},{28,8},{1,21},{... | collective-permute-start | bytes 1572872 | tf_op jit(solution)/shard_map/ppermute | solution.py:299
  672.0 80.2 %collective-permute-start.40 = (f32[4,512,256]{2,1,0:T(8,128)}, f32[4,512,256]{2,1,0:T(8,128)S(1)}, u32[]{:S(2)}, u32[]{:S(2)}) collective-permute-start(f32[4,512,256]{2,1,0:T(8,128)} %constant_dynamic-slice_fusion.13), channel_id=1, source_target_pairs={{0,3},{1,0},{2,1},{3,2},{4,7},{5,4},{6,5},{7,6},{8,11},{9,8},{10,9... | collective-permute-start | bytes 6291464 | tf_op jit(solution)/shard_map/ppermute | solution.py:299
  706.4 67.7 %collective-permute-start.43 = (f32[8,64,256]{2,1,0:T(8,128)S(1)}, f32[8,64,256]{2,1,0:T(8,128)}, u32[]{:S(2)}, u32[]{:S(2)}) collective-permute-start(f32[8,64,256]{2,1,0:T(8,128)S(1)} %pack_z.77), channel_id=1, source_target_pairs={{0,28},{4,24},{8,4},{12,0},{16,12},{20,8},{24,20},{28,16},{1,29},{... | collective-permute-start | bytes 1572872 | tf_op jit(solution)/shard_map/ppermute | solution.py:299
  706.4 38.8 %collective-permute-start.28 = (f32[8,64,256]{2,1,0:T(8,128)S(1)}, f32[8,64,256]{2,1,0:T(8,128)S(1)}, u32[]{:S(2)}, u32[]{:S(2)}) collective-permute-start(f32[8,64,256]{2,1,0:T(8,128)S(1)} %pack_z.59), channel_id=1, source_target_pairs={{0,16},{4,20},{8,24},{12,28},{16,0},{20,4},{24,8},{28,12},{1,17},{... | collective-permute-start | bytes 1572872 | tf_op jit(solution)/shard_map/ppermute | solution.py:299
  722.4 28.2 %collective-permute-start.37 = (f32[8,64,256]{2,1,0:T(8,128)S(1)}, f32[8,64,256]{2,1,0:T(8,128)S(1)}, u32[]{:S(2)}, u32[]{:S(2)}) collective-permute-start(f32[8,64,256]{2,1,0:T(8,128)S(1)} %pack_z.71), channel_id=1, source_target_pairs={{0,24},{4,28},{8,0},{12,4},{16,8},{20,12},{24,16},{28,20},{1,25},{... | collective-permute-start | bytes 1572872 | tf_op jit(solution)/shard_map/ppermute | solution.py:299
  745.2 33.3 %collective-permute-start.44 = (f32[2,512,256]{2,1,0:T(8,128)}, f32[2,512,256]{2,1,0:T(8,128)S(1)}, u32[]{:S(2)}, u32[]{:S(2)}) collective-permute-start(f32[2,512,256]{2,1,0:T(8,128)} %constant_dynamic-slice_fusion.12), channel_id=1, source_target_pairs={{0,2},{1,3},{2,0},{3,1},{4,6},{5,7},{6,4},{7,5},{8,10},{9,11},{10,... | collective-permute-start | bytes 3145736 | tf_op jit(solution)/shard_map/ppermute | solution.py:299
  750.6 36.7 %collective-permute-start.45 = (f32[2,512,256]{2,1,0:T(8,128)}, f32[2,512,256]{2,1,0:T(8,128)S(1)}, u32[]{:S(2)}, u32[]{:S(2)}) collective-permute-start(f32[2,512,256]{2,1,0:T(8,128)} %constant_dynamic-slice_fusion.11), channel_id=1, source_target_pairs={{0,1},{1,2},{2,3},{3,0},{4,5},{5,6},{6,7},{7,4},{8,9},{9,10},{10,1... | collective-permute-start | bytes 3145736 | tf_op jit(solution)/shard_map/ppermute | solution.py:299
  752.2 14.8 %collective-permute-start.41 = (f32[8,64,256]{2,1,0:T(8,128)S(1)}, f32[8,64,256]{2,1,0:T(8,128)}, u32[]{:S(2)}, u32[]{:S(2)}) collective-permute-start(f32[8,64,256]{2,1,0:T(8,128)S(1)} %pack_z.75), channel_id=1, source_target_pairs={{0,4},{4,0},{8,12},{12,8},{16,20},{20,16},{24,28},{28,24},{1,5},{5... | collective-permute-start | bytes 1572872 | tf_op jit(solution)/shard_map/ppermute | solution.py:299
  755.5 18.6 %collective-permute-start.42 = (f32[8,64,256]{2,1,0:T(8,128)S(1)}, f32[8,64,256]{2,1,0:T(8,128)S(1)}, u32[]{:S(2)}, u32[]{:S(2)}) collective-permute-start(f32[8,64,256]{2,1,0:T(8,128)S(1)} %pack_z.76), channel_id=1, source_target_pairs={{0,8},{4,12},{8,16},{12,20},{16,24},{20,28},{24,0},{28,4},{1,9},{5... | collective-permute-start | bytes 1572872 | tf_op jit(solution)/shard_map/ppermute | solution.py:299
  767.0 22.8 %collective-permute-start.46 = (f32[2,512,256]{2,1,0:T(8,128)S(1)}, f32[2,512,256]{2,1,0:T(8,128)S(1)}, u32[]{:S(2)}, u32[]{:S(2)}) collective-permute-start(f32[2,512,256]{2,1,0:T(8,128)S(1)} %constant_dynamic-slice_fusion.10), channel_id=1, source_target_pairs={{0,3},{1,0},{2,1},{3,2},{4,7},{5,4},{6,5},{7,6},{8,11},{9,8},{10,9... | collective-permute-start | bytes 3145736 | tf_op jit(solution)/shard_map/ppermute | solution.py:299
  789.9 8.7 collective-permute-start.49
  791.9 8.6 collective-permute-start.48
  791.9 12.0 %collective-permute-start.47 = (f32[128,512]{1,0:T(8,128)S(1)}, f32[128,512]{1,0:T(8,128)S(1)}, u32[]{:S(2)}, u32[]{:S(2)}) collective-permute-start(f32[128,512]{1,0:T(8,128)S(1)} %get-tuple-element.191), channel_id=1, source_target_pairs={{0,2},{1,3},{2,0},{3,1},{4,6},{5,7},{6,4},{7,5},{8,10},{9,11},{10,... | collective-permute-start | bytes 786440 | tf_op jit(solution)/shard_map/ppermute | solution.py:387
  804.1 20.2 %collective-permute-start.56 = (f32[16,512]{1,0:T(8,128)S(1)}, f32[16,512]{1,0:T(8,128)S(1)}, u32[]{:S(2)}, u32[]{:S(2)}) collective-permute-start(f32[16,512]{1,0:T(8,128)S(1)} %get-tuple-element.195), channel_id=1, source_target_pairs={{0,28},{4,24},{8,4},{12,0},{16,12},{20,8},{24,20},{28,16},{1,29},{... | collective-permute-start | bytes 98312 | tf_op jit(solution)/shard_map/ppermute | solution.py:392
  818.7 8.7 collective-permute-start.54
  835.5 8.7 collective-permute-start.59
  846.8 12.2 %collective-permute-start.66 = (f32[128,512]{1,0:T(8,128)S(1)}, f32[128,512]{1,0:T(8,128)S(1)}, u32[]{:S(2)}, u32[]{:S(2)}) collective-permute-start(f32[128,512]{1,0:T(8,128)S(1)} %bitcast.355), channel_id=1, source_target_pairs={{0,3},{1,0},{2,1},{3,2},{4,7},{5,4},{6,5},{7,6},{8,11},{9,8},{10,9... | collective-permute-start | bytes 786440 | tf_op jit(solution)/shard_map/ppermute | solution.py:396
  849.7 45.8 %collective-permute-start.67 = (f32[2,512,256]{2,1,0:T(8,128)S(1)}, f32[2,512,256]{2,1,0:T(8,128)S(1)}, u32[]{:S(2)}, u32[]{:S(2)}) collective-permute-start(f32[2,512,256]{2,1,0:T(8,128)S(1)} %constant_dynamic-slice_fusion.8), channel_id=1, source_target_pairs={{0,2},{1,3},{2,0},{3,1},{4,6},{5,7},{6,4},{7,5},{8,10},{9,11},{10,... | collective-permute-start | bytes 3145736 | tf_op jit(solution)/shard_map/ppermute | solution.py:299
  859.0 41.2 %collective-permute-start.68 = (f32[2,512,256]{2,1,0:T(8,128)S(1)}, f32[2,512,256]{2,1,0:T(8,128)S(1)}, u32[]{:S(2)}, u32[]{:S(2)}) collective-permute-start(f32[2,512,256]{2,1,0:T(8,128)S(1)} %constant_dynamic-slice_fusion.7), channel_id=1, source_target_pairs={{0,1},{1,2},{2,3},{3,0},{4,5},{5,6},{6,7},{7,4},{8,9},{9,10},{10,1... | collective-permute-start | bytes 3145736 | tf_op jit(solution)/shard_map/ppermute | solution.py:299
  859.5 41.9 %collective-permute-start.69 = (f32[2,512,256]{2,1,0:T(8,128)S(1)}, f32[2,512,256]{2,1,0:T(8,128)S(1)}, u32[]{:S(2)}, u32[]{:S(2)}) collective-permute-start(f32[2,512,256]{2,1,0:T(8,128)S(1)} %constant_dynamic-slice_fusion.6), channel_id=1, source_target_pairs={{0,3},{1,0},{2,1},{3,2},{4,7},{5,4},{6,5},{7,6},{8,11},{9,8},{10,9... | collective-permute-start | bytes 3145736 | tf_op jit(solution)/shard_map/ppermute | solution.py:299
  935.0 25.6 %collective-permute-start.71 = (f32[256,1024]{1,0:T(8,128)S(1)}, f32[256,1024]{1,0:T(8,128)}, u32[]{:S(2)}, u32[]{:S(2)}) collective-permute-start(f32[256,1024]{1,0:T(8,128)S(1)} %dynamic-slice_bitcast_fusion.1), channel_id=1, source_target_pairs={{0,2},{1,3},{2,0},{3,1},{4,6},{5,7},{6,4},{7,5},{8,10},{9,11},{10,... | collective-permute-start | bytes 3145736 | tf_op jit(solution)/shard_map/ppermute | solution.py:418
  962.2 9.4 collective-permute-start.78
  967.2 9.7 collective-permute-start.76
  967.7 17.2 %collective-permute-start.75 = (f32[256,128]{1,0:T(8,128)S(1)}, f32[256,128]{1,0:T(8,128)S(1)}, u32[]{:S(2)}, u32[]{:S(2)}) collective-permute-start(f32[256,128]{1,0:T(8,128)S(1)} %get-tuple-element.188), channel_id=1, source_target_pairs={{0,20},{4,16},{8,28},{12,24},{16,4},{20,0},{24,12},{28,8},{1,21},{... | collective-permute-start | bytes 393224 | tf_op jit(solution)/shard_map/ppermute | solution.py:426
  968.3 16.6 %collective-permute-start.74 = (f32[256,128]{1,0:T(8,128)S(1)}, f32[256,128]{1,0:T(8,128)S(1)}, u32[]{:S(2)}, u32[]{:S(2)}) collective-permute-start(f32[256,128]{1,0:T(8,128)S(1)} %get-tuple-element.189), channel_id=1, source_target_pairs={{0,24},{4,28},{8,0},{12,4},{16,8},{20,12},{24,16},{28,20},{1,25},{... | collective-permute-start | bytes 393224 | tf_op jit(solution)/shard_map/ppermute | solution.py:426
  971.5 13.4 %collective-permute-start.73 = (f32[256,128]{1,0:T(8,128)S(1)}, f32[256,128]{1,0:T(8,128)S(1)}, u32[]{:S(2)}, u32[]{:S(2)}) collective-permute-start(f32[256,128]{1,0:T(8,128)S(1)} %get-tuple-element.190), channel_id=1, source_target_pairs={{0,12},{4,8},{8,20},{12,16},{16,28},{20,24},{24,4},{28,0},{1,13},{... | collective-permute-start | bytes 393224 | tf_op jit(solution)/shard_map/ppermute | solution.py:426
  975.6 15.0 %collective-permute-start.72 = (f32[256,128]{1,0:T(8,128)S(1)}, f32[256,128]{1,0:T(8,128)S(1)}, u32[]{:S(2)}, u32[]{:S(2)}) collective-permute-start(f32[256,128]{1,0:T(8,128)S(1)} %get-tuple-element.184), channel_id=1, source_target_pairs={{0,16},{4,20},{8,24},{12,28},{16,0},{20,4},{24,8},{28,12},{1,17},{... | collective-permute-start | bytes 393224 | tf_op jit(solution)/shard_map/ppermute | solution.py:426
  (47 other events, 293.6 us)

commit v6 on v5

--- a/solution.py
+++ b/solution.py
@@ -9,8 +9,10 @@
 from jax.sharding import PartitionSpec as P
 
 ITERS = 4
-WINDOW = 5
+WINDOW = 14
 AHEAD = 2
+CORE = -2
+CHIP = -5
 TALL = 8
 LINE = 4
 MIB = 1024 * 1024
@@ -152,21 +154,21 @@
 
 def inverse_factor(cross):
     size = cross.shape[0]
-    tall = 8
     wide = 4
-    groups = size // tall
-    shape = (tall, size)
+    groups = size // TALL
+    shape = (TALL, size)
     sublane = lax.broadcasted_iota(jnp.int32, shape, 0)
     lane = lax.broadcasted_iota(jnp.int32, shape, 1)
-    left = [cross[t * tall : (t + 1) * tall] for t in range(groups)]
-    right = [(lane == sublane + t * tall).astype(F32) for t in range(groups)]
+    left = [cross[t * TALL : (t + 1) * TALL] for t in range(groups)]
+    right = [(lane == sublane + t * TALL).astype(F32) for t in range(groups)]
     pivots = [jnp.ones(shape, F32) for _ in range(groups)]
+    ratios = [jnp.zeros(shape, F32) for _ in range(groups)]
 
     def row(value, s):
         return jnp.broadcast_to(value[s : s + 1, :], shape)
 
     for first in range(0, size, wide):
-        top, s0 = first // tall, first % tall
+        top, s0 = first // TALL, first % TALL
         below = range(top, groups)
         columns = [
             {t: jnp.broadcast_to(left[t][:, first + k : first + k + 1], shape) for t in below}
@@ -174,35 +176,48 @@
         ]
         rows = [row(left[top], s0 + k) for k in range(wide)]
         eyes = [row(right[top], s0 + k) for k in range(wide)]
-        scaled = []
-        for i in range(wide):
-            pivot = row(columns[i][top], s0 + i)
-            inverse = 1.0 / pivot
-            scaled.append((rows[i] * inverse, eyes[i] * inverse))
-            for k in range(i + 1, wide):
-                ratio = row(columns[i][top], s0 + k) * inverse
+        for i in range(0, wide, 2):
+            a = row(columns[i][top], s0 + i)
+            b = row(columns[i][top], s0 + i + 1)
+            c = row(columns[i + 1][top], s0 + i + 1)
+            inverse = 1.0 / (a * c - b * b)
+            solved = (
+                (rows[i] * c - rows[i + 1] * b) * inverse,
+                (rows[i + 1] * a - rows[i] * b) * inverse,
+                (eyes[i] * c - eyes[i + 1] * b) * inverse,
+                (eyes[i + 1] * a - eyes[i] * b) * inverse,
+            )
+            ratio = b / a
+            pivots[top] = jnp.where(sublane == s0 + i, a, pivots[top])
+            pivots[top] = jnp.where(sublane == s0 + i + 1, c - b * ratio, pivots[top])
+            ratios[top] = jnp.where(sublane == s0 + i + 1, ratio, ratios[top])
+            for k in range(i + 2, wide):
+                one, two = (row(columns[j][top], s0 + k) for j in (i, i + 1))
+                first_part = (one * c - two * b) * inverse
+                second_part = (two * a - one * b) * inverse
                 for t in below:
-                    columns[k][t] = columns[k][t] - ratio * columns[i][t]
-                rows[k] = rows[k] - ratio * rows[i]
-                eyes[k] = eyes[k] - ratio * eyes[i]
-            here = sublane == s0 + i
-            pivots[top] = jnp.where(here, pivot, pivots[top])
-        rest = sublane >= s0 + wide
-        for t in below:
-            new_left, new_right = left[t], right[t]
-            for i in range(wide):
-                new_left = new_left - columns[i][t] * scaled[i][0]
-                new_right = new_right - columns[i][t] * scaled[i][1]
-            if t == top:
-                new_left = jnp.where(rest, new_left, left[t])
-                new_right = jnp.where(rest, new_right, right[t])
-                for i in range(wide):
-                    new_right = jnp.where(sublane == s0 + i, eyes[i], new_right)
-            left[t], right[t] = new_left, new_right
+                    columns[k][t] = columns[k][t] - (
+                        first_part * columns[i][t] + second_part * columns[i + 1][t]
+                    )
+                rows[k] = rows[k] - (first_part * rows[i] + second_part * rows[i + 1])
+                eyes[k] = eyes[k] - (first_part * eyes[i] + second_part * eyes[i + 1])
+            rest = sublane >= s0 + wide
+            for t in below:
+                one, two = columns[i][t], columns[i + 1][t]
+                new_left = left[t] - (one * solved[0] + two * solved[1])
+                new_right = right[t] - (one * solved[2] + two * solved[3])
+                if t == top:
+                    new_left = jnp.where(rest, new_left, left[t])
+                    new_right = jnp.where(rest, new_right, right[t])
+                    for j in (i, i + 1):
+                        new_right = jnp.where(sublane == s0 + j, eyes[j], new_right)
+                left[t], right[t] = new_left, new_right
     for t in range(groups):
+        above = jnp.concatenate([right[t][:1], right[t][:-1]], axis=0)
+        value = right[t] - ratios[t] * above
         root = lax.rsqrt(pivots[t])
         root = root * (1.5 - 0.5 * pivots[t] * root * root)
-        right[t] = right[t] * root
+        right[t] = value * root
     return jnp.concatenate(right, axis=0)
 
 
@@ -216,6 +231,7 @@
 
     def step(_, carry):
         product = full_dot(gram[...], out_ref[...], (1, 0))
+        product = product * lax.rsqrt(jnp.sum(product * product, axis=0, keepdims=True))
         inverse = inverse_factor(full_dot(product, product, (0, 0)))
         out_ref[...] = full_dot(product, inverse, (1, 1))
         return carry
@@ -276,7 +292,7 @@
         out_shape=jax.ShapeDtypeStruct((depth, x_block, y_block), F32),
         compiler_params=pltpu.CompilerParams(vmem_limit_bytes=48 * MIB),
         cost_estimate=pl.CostEstimate(
-            flops=0, bytes_accessed=8 * depth * x_block * y_block, transcendentals=0
+            flops=0, bytes_accessed=1, transcendentals=0
         ),
         name="pack_z",
     )(first.astype(jnp.int32).reshape(1), field)
@@ -294,9 +310,9 @@
         last = len(self.ends) - WINDOW + 1 - ahead
         return self.ends[max(0, last - 1) : max(0, last)]
 
-    def send(self, cut, source, axis, perm):
-        value = cut(tie(source, self.done(AHEAD)))
-        got = lax.ppermute(tie(value, self.done(0)), axis, perm)
+    def send(self, cut, index, axis, perm, after=()):
+        value = cut(tie(index, self.done(AHEAD)))
+        got = lax.ppermute(tie(value, self.done(0) + list(after)), axis, perm)
         self.ends.append(got)
         return got
 
@@ -339,45 +355,73 @@
 
     cells = jnp.zeros((slab // m, m, width_x, y_block), F32)
 
-    def to_gx(first, zc, a, b, whole):
+    def to_gx(first, zc, a, b, whole, after):
         place = (moved(g, a, b) * slab + first) // TALL
-        got = order.send(lambda at: pack(field, at, zc), place, "gx", gx_perm(a, b))
+        got = order.send(lambda at: pack(field, at, zc), place, "gx", gx_perm(a, b), after)
         return lax.dynamic_update_slice_in_dim(whole, got[:, None], moved(g, a, b, -1), axis=1)
 
-    def to_yz(cells, first, d, whole, after=()):
-        zs = whole.shape[0] // m
-
-        def cut(source):
-            return lax.dynamic_slice_in_dim(source, (q + d) % m * zs, zs, axis=0)
-
-        got = order.send(cut, tie(whole, after), "yz", yz_perm(d))
-        return lax.dynamic_update_slice(cells, got[:, None], (first // m, (q - d) % m, 0, 0))
+    cores = 2 if m % 2 == 0 else 1
+    chips = m // cores
+    core, chip = q % cores, q // cores
+
+    def core_perm(d):
+        return [(i, i // cores * cores + (i + d) % cores) for i in range(m)]
+
+    def chip_perm(d):
+        return [(i, (i + d * cores) % m) for i in range(m)]
+
+    def part(array, index, count):
+        depth = array.shape[0] // count
+        return lax.dynamic_slice_in_dim(array, index * depth, depth, axis=0)
+
+    def to_core(whole):
+        both = jnp.zeros((whole.shape[0] // cores, cores, width_x, y_block), F32)
+        own = part(whole, core, cores)[:, None]
+        both = lax.dynamic_update_slice_in_dim(both, own, core, axis=1)
+        for d in range(1, cores):
+            cut = part(whole, (core + d) % cores, cores)
+            got = lax.ppermute(cut, "yz", core_perm(d))
+            both = lax.dynamic_update_slice_in_dim(both, got[:, None], (core - d) % cores, axis=1)
+        return both
+
+    def to_chip(cells, first, both, after=()):
+        def put(cells, value, source):
+            return lax.dynamic_update_slice(cells, value, (first // m, source * cores, 0, 0))
+
+        cells, ends = put(cells, part(both, chip, chips), chip), []
+        for d in range(1, chips):
+            cut = part(tie(both, after), (chip + d) % chips, chips)
+            got = lax.ppermute(cut, "yz", chip_perm(d))
+            ends.append(got)
+            cells = put(cells, got, (chip - d) % chips)
+        return cells, ends
 
     gram = jnp.zeros((width_x, width_x), F32)
-    before, start_z, first = None, 0, 0
+    before, start_z, first, across = None, 0, 0, []
     group = math.lcm(m, TALL)
     for groups in chunk_depths(slab // group):
         zc = groups * group
-        units = zc // m
         whole = jnp.zeros((zc, n, x_block, y_block), F32)
-        waiting = list(turns) if before is not None else []
+        if before is not None:
+            both = to_core(before)
+            cells, ends = to_chip(cells, start_z, both)
+            across.append(ends)
         for k, (a, b) in enumerate(shifts):
-            whole = to_gx(first, zc, a, b, whole)
-            if k >= WINDOW - 1 and waiting:
-                cells = to_yz(cells, start_z, waiting.pop(0), before)
-        for d in waiting:
-            cells = to_yz(cells, start_z, d, before)
-        across = order.ends[-len(shifts) - len(turns) :]
+            after = []
+            if k == len(shifts) + CORE and before is not None:
+                after = [both]
+            if k == len(shifts) + CHIP and len(across) > 1:
+                after = across[-2]
+            whole = to_gx(first, zc, a, b, whole, after)
         own = pack(field, (g * slab + first) // TALL, zc)[:, None]
         whole = lax.dynamic_update_slice_in_dim(whole, own, g, axis=1)
         before = whole.reshape(zc, width_x, y_block)
         gram = gram_of(before, gram)
-        own = lax.dynamic_slice_in_dim(before, q * units, units, axis=0)
-        cells = lax.dynamic_update_slice(cells, own[:, None], (first // m, q, 0, 0))
         start_z, first = first, first + zc
 
     rows = width_x // m
-    slabs = tie(gram, across).reshape(m, rows, width_x)
+    both = to_core(before)
+    slabs = tie(gram, across[-1] if across else []).reshape(m, rows, width_x)
 
     def pick(array, index):
         return lax.dynamic_index_in_dim(array, index, axis=0, keepdims=False)
@@ -385,7 +429,7 @@
     summed = pick(slabs, q)
     for d in turns:
         summed = summed + lax.ppermute(pick(slabs, (q + d) % m), "yz", yz_perm(d))
-    cells = to_yz(cells, start_z, turns[0], before, [summed])
+    cells, _ = to_chip(cells, start_z, both, [summed])
     strips = summed.reshape(n, rows // n, width_x)
     summed = pick(strips, g)
     for a, b in shifts:
@@ -395,14 +439,9 @@
     summed = stack(pieces, places).reshape(rows, width_x)
     pieces = [summed] + [lax.ppermute(summed, "yz", yz_perm(d)) for d in turns]
     places = jnp.stack([q] + [(q - d) % m for d in turns]).astype(jnp.int32)
-    for d in turns[1:]:
-        cells = to_yz(cells, start_z, d, before, pieces[1:])
     basis = iterate(pieces, places, start, float(width_y * depth))
 
     partial_y = core_gram(cells, basis, float(rank * depth))
-    cores = 2 if m % 2 == 0 else 1
-    chips = m // cores
-    core, chip = q % cores, q // cores
     blocks = partial_y.reshape(chips, cores, y_block, width_y)
 
     def of_core(index):
@@ -410,12 +449,14 @@
 
     blocks_here = of_core(core)
     for d in range(1, cores):
-        perm = [(i, i // cores * cores + (i + d) % cores) for i in range(m)]
-        blocks_here = blocks_here + lax.ppermute(of_core((core + d) % cores), "yz", perm)
+        blocks_here = blocks_here + lax.ppermute(
+            of_core((core + d) % cores), "yz", core_perm(d)
+        )
     rows_y = pick(blocks_here, chip)
     for d in range(1, chips):
-        perm = [(i, (i + d * cores) % m) for i in range(m)]
-        rows_y = rows_y + lax.ppermute(pick(blocks_here, (chip + d) % chips), "yz", perm)
+        rows_y = rows_y + lax.ppermute(
+            pick(blocks_here, (chip + d) % chips), "yz", chip_perm(d)
+        )
     width = width_y // n
 
     def block(index):

time: 1000 us -> 1070 us (1.070)
  waiting for transfers between devices: 383 us -> 598 us
  starting transfers between devices: 331 us -> 171 us
  local copies, waits for them, and re-layouts: 127 us -> 139 us
    ppermute x52 -> x47, waiting for transfers between devices: 345 us -> 560 us  [the longest x35 410 us: send(): got = lax.ppermute(tie(value, self.done(0) + list(after)), axis, perm)]
    ppermute x52 -> x47, starting transfers between devices: 280 us -> 134 us  [the longest x35 128 us: send(): got = lax.ppermute(tie(value, self.done(0) + list(after)), axis, perm)]
    dynamic_update_slice x20, local copies, waits for them, and re-layouts: 39.5 us -> 61.2 us  [the longest x10 42.3 us: put(): lax.dynamic_update_slice(cells, value, (first // m, source * cores, 0, 0))]
    dynamic_update_slice x35, local copies, waits for them, and re-layouts: 33.9 us -> 18.9 us  [to_gx(): lax.dynamic_update_slice_in_dim(whole, got[:, None], moved(g, a, b, -1),...]
    unnamed x64, local copies, waits for them, and re-layouts: 12.1 us -> 25.4 us
    ppermute x7, starting transfers between devices: 21.2 us -> 9.1 us  [on_device(): lax.ppermute(pick(strips, moved(g, a, b)), 'gx', gx_perm(a, b))]
  transfers between devices with their start and end apart: 79 -> 74, of which waited for: 37 -> 28; matrix products, arithmetic and copies ran while one was open for 11% -> 10% of each run, Pallas kernels for 12% -> 11%
where the time goes in v6:
time: 1070 us; the launch traced here: 1060 us
  waiting for transfers between devices  598 us (56%)
  starting transfers between devices  171 us (16%)
  Pallas kernels  139 us (13%)
  local copies, waits for them, and re-layouts  139 us (13%)
    ppermute x35, waiting for transfers between devices, send(): got = lax.ppermute(tie(value, self.done(0) + list(after)), axis, perm)  410 us
    ppermute x35, starting transfers between devices, send(): got = lax.ppermute(tie(value, self.done(0) + list(after)), axis, perm)  128 us
    ppermute x5, waiting for transfers between devices, to_chip(): got = lax.ppermute(cut, 'yz', chip_perm(d))  121 us
    pallas_call x40, Pallas kernels, pack(): pl.pallas_call(pack_body, grid_spec=pltpu.PrefetchScalarGridSpec(num_scal...  59.5 us
    dynamic_update_slice x10, local copies, waits for them, and re-layouts, put(): lax.dynamic_update_slice(cells, value, (first // m, source * cores, 0, 0))  42.3 us
    pallas_call x1, Pallas kernels, iterate(): pl.pallas_call(functools.partial(iterate_body, total), in_specs=[pl.Block...  33.2 us
    unnamed x64, local copies, waits for them, and re-layouts  25.4 us
    ppermute x1, waiting for transfers between devices, on_device(): lax.ppermute(pick(blocks_here, (chip + d) % chips), 'yz', chip_perm(d))  24.8 us
  transfers between devices with their start and end apart: 74, of which 28 were waited for; matrix products, arithmetic and copies ran while one was open for 10% of the time, Pallas kernels for 11%

profile of v6, /device:TPU:0, one launch (start us, length us, event | category | flops | bytes accessed | tf_op | source)
XLA Modules:
  0.0 1056.0 jit_solution(7627207400875137305)
XLA Ops:
  2.1 4.1 collective-permute-start
  7.7 2.6 collective-permute-start.1
  25.8 50.3 %collective-permute-done = f32[16,64,256]{2,1,0:T(8,128)} collective-permute-done((f32[16,64,256]{2,1,0:T(8,128)S(1)}, f32[16,64,256]{2,1,0:T(8,128)}, u32[]{:S(2)}, u32[]{:S(2)}) %collective-permute-start) | collective-permute-done | bytes 1048608 | tf_op jit(solution)/shard_map/ppermute | solution.py:315
  78.5 5.5 collective-permute-start.6
  86.7 79.9 %collective-permute-done.3 = f32[16,64,256]{2,1,0:T(8,128)} collective-permute-done((f32[16,64,256]{2,1,0:T(8,128)}, f32[16,64,256]{2,1,0:T(8,128)}, u32[]{:S(2)}, u32[]{:S(2)}) %collective-permute-start.3) | collective-permute-done | bytes 1048608 | tf_op jit(solution)/shard_map/ppermute | solution.py:315
  169.6 3.3 copy-done
  172.9 2.5 constant_dynamic-slice_fusion.16
  176.8 20.2 %collective-permute-start.18 = (f32[16,64,256]{2,1,0:T(8,128)S(1)}, f32[16,64,256]{2,1,0:T(8,128)}, u32[]{:S(2)}, u32[]{:S(2)}) collective-permute-start(f32[16,64,256]{2,1,0:T(8,128)S(1)} %pack_z.59), channel_id=1, source_target_pairs={{0,16},{4,20},{8,24},{12,28},{16,0},{20,4},{24,8},{28,12},{1,17},{... | collective-permute-start | bytes 3145736 | tf_op jit(solution)/shard_map/ppermute | solution.py:315
  200.6 4.8 collective-permute-start.11
  216.4 49.7 %collective-permute-done.18 = f32[16,64,256]{2,1,0:T(8,128)} collective-permute-done((f32[16,64,256]{2,1,0:T(8,128)S(1)}, f32[16,64,256]{2,1,0:T(8,128)}, u32[]{:S(2)}, u32[]{:S(2)}) %collective-permute-start.18) | collective-permute-done | bytes 1048608 | tf_op jit(solution)/shard_map/ppermute | solution.py:315
  273.1 2.8 bitcast_dynamic-update-slice_fusion.4
  275.9 62.7 %collective-permute-start.8 = (f32[16,64,256]{2,1,0:T(8,128)S(1)}, f32[16,64,256]{2,1,0:T(8,128)S(1)}, u32[]{:S(2)}, u32[]{:S(2)}) collective-permute-start(f32[16,64,256]{2,1,0:T(8,128)S(1)} %copy-done.9), channel_id=1, source_target_pairs={{0,8},{4,12},{8,16},{12,20},{16,24},{20,28},{24,0},{28,4},{1,9},{5... | collective-permute-start | bytes 3145736 | tf_op jit(solution)/shard_map/ppermute | solution.py:315
  340.0 39.2 %collective-permute-done.21 = f32[16,64,256]{2,1,0:T(8,128)S(1)} collective-permute-done((f32[16,64,256]{2,1,0:T(8,128)}, f32[16,64,256]{2,1,0:T(8,128)S(1)}, u32[]{:S(2)}, u32[]{:S(2)}) %collective-permute-start.21) | collective-permute-done | bytes 1048608 | tf_op jit(solution)/shard_map/ppermute | solution.py:315
  379.4 11.1 %broadcast_in_dim.205 = f32[16,4,512,256]{3,2,1,0:T(8,128)} broadcast(f32[]{:T(128)} %constant.1220.clone.1), dimensions={} | broadcast | bytes 33554436 | tf_op jit(solution)/shard_map/broadcast_in_dim | solution.py:356
  390.5 7.4 dynamic-slice_dynamic-update-slice_fusion.2
  401.0 3.3 copy-done.2
  404.3 2.4 constant_dynamic-slice_fusion.13
  416.3 2.8 collective-permute-start.16
  424.2 56.1 %collective-permute-done.9 = f32[16,64,256]{2,1,0:T(8,128)} collective-permute-done((f32[16,64,256]{2,1,0:T(8,128)S(1)}, f32[16,64,256]{2,1,0:T(8,128)}, u32[]{:S(2)}, u32[]{:S(2)}) %collective-permute-start.9) | collective-permute-done | bytes 1048608 | tf_op jit(solution)/shard_map/ppermute | solution.py:315
  484.4 6.2 collective-permute-done.14
  494.5 4.4 constant_dynamic-update-slice_fusion.4
  498.9 2.8 bitcast_dynamic-update-slice_fusion.2
  502.7 67.4 %collective-permute-done.15 = f32[16,64,256]{2,1,0:T(8,128)S(1)} collective-permute-done((f32[16,64,256]{2,1,0:T(8,128)S(1)}, f32[16,64,256]{2,1,0:T(8,128)S(1)}, u32[]{:S(2)}, u32[]{:S(2)}) %collective-permute-start.15) | collective-permute-done | bytes 1048608 | tf_op jit(solution)/shard_map/ppermute | solution.py:315
  571.6 7.7 dynamic-slice_dynamic-update-slice_fusion.1
  580.2 3.3 copy-done.3
  583.5 2.3 constant_dynamic-slice_fusion.12
  593.5 3.0 collective-permute-start.35
  600.5 4.1 broadcast.77
  606.9 65.3 %collective-permute-done.33 = f32[4,2,512,256]{3,2,1,0:T(8,128)} collective-permute-done((f32[4,2,512,256]{3,2,1,0:T(8,128)}, f32[4,2,512,256]{3,2,1,0:T(8,128)}, u32[]{:S(2)}, u32[]{:S(2)}) %collective-permute-start.33) | collective-permute-done | bytes 4194336 | tf_op jit(solution)/shard_map/ppermute | solution.py:394
  673.7 4.5 constant_dynamic-update-slice_fusion.3
  678.2 4.4 bitcast_dynamic-update-slice_fusion
  682.6 7.5 dynamic-slice_dynamic-update-slice_fusion
  693.7 22.5 %collective-permute-done.37 = f32[8,64,256]{2,1,0:T(8,128)S(1)} collective-permute-done((f32[8,64,256]{2,1,0:T(8,128)S(1)}, f32[8,64,256]{2,1,0:T(8,128)S(1)}, u32[]{:S(2)}, u32[]{:S(2)}) %collective-permute-start.37) | collective-permute-done | bytes 524320 | tf_op jit(solution)/shard_map/ppermute | solution.py:315
  723.1 3.4 copy-done.1
  726.5 5.7 gram_x.5.before_ref
  743.3 5.7 gram_x.6.before_ref
  749.0 21.4 %collective-permute-done.10 = f32[8,64,256]{2,1,0:T(8,128)S(1)} collective-permute-done((f32[8,64,256]{2,1,0:T(8,128)S(1)}, f32[8,64,256]{2,1,0:T(8,128)S(1)}, u32[]{:S(2)}, u32[]{:S(2)}) %collective-permute-start.10) | collective-permute-done | bytes 524320 | tf_op jit(solution)/shard_map/ppermute | solution.py:315
  774.5 7.3 collective-permute-done.27
  785.9 4.4 constant_dynamic-update-slice_fusion.2
  792.2 23.2 %collective-permute-done.28 = f32[8,64,256]{2,1,0:T(8,128)S(1)} collective-permute-done((f32[8,64,256]{2,1,0:T(8,128)S(1)}, f32[8,64,256]{2,1,0:T(8,128)S(1)}, u32[]{:S(2)}, u32[]{:S(2)}) %collective-permute-start.28) | collective-permute-done | bytes 524320 | tf_op jit(solution)/shard_map/ppermute | solution.py:315
  820.0 5.8 gram_x.7.before_ref
  825.7 3.2 gram_x.8.before_ref
  828.9 3.2 gram_x.9
  832.1 30.9 %collective-permute-done.42 = f32[2,2,512,256]{3,2,1,0:T(8,128)S(1)} collective-permute-done((f32[2,2,512,256]{3,2,1,0:T(8,128)S(1)}, f32[2,2,512,256]{3,2,1,0:T(8,128)S(1)}, u32[]{:S(2)}, u32[]{:S(2)}) %collective-permute-start.42) | collective-permute-done | bytes 2097184 | tf_op jit(solution)/shard_map/ppermute | solution.py:394
  865.8 4.7 collective-permute-done.45
  870.5 2.5 collective-permute-done.44
  873.0 5.1 collective-permute-done.43
  879.4 3.0 collective-permute-start.51
  884.2 2.6 collective-permute-start.48
  888.9 4.5 collective-permute-done.47
  893.6 3.4 collective-permute-start.54
  903.1 3.8 collective-permute-start.59
  918.3 2.9 collective-permute-done.62.refs_3_
  921.3 33.2 %subspace.1.basis_ref = f32[512,128]{1,0:T(8,128)} custom-call(s32[4]{0:T(128)S(1)} %pad_add_fusion.places_ref, f32[128,512]{1,0:T(8,128)S(1)} %bitcast.321, f32[128,512]{1,0:T(8,128)S(1)} %collective-permute-done.60.refs_1_, f32[128,512]{1,0:T(8,128)S(1)} %collective-permute-done.61.refs_2_, f32[128,512]{1,0:T(8,128)S(1)} %collective-permute-done.62.refs_3_, ...), custom_call_target="tpu_custom_call" | custom-call | flops 40000000000 | bytes 524288 | tf_op jit(solution)/shard_map/subspace/pallas_call | solution.py:244
  954.5 11.6 %collective-permute-done.64 = f32[2,2,512,256]{3,2,1,0:T(8,128)S(1)} collective-permute-done((f32[2,2,512,256]{3,2,1,0:T(8,128)S(1)}, f32[2,2,512,256]{3,2,1,0:T(8,128)S(1)}, u32[]{:S(2)}, u32[]{:S(2)}) %collective-permute-start.64) | collective-permute-done | bytes 2097184 | tf_op jit(solution)/shard_map/ppermute | solution.py:394
  968.6 21.9 %core_gram_y.1 = f32[1024,1024]{1,0:T(8,128)S(1)} custom-call(f32[16,4,512,256]{3,2,1,0:T(8,128)} %constant_dynamic-update-slice_fusion.field_ref, f32[512,128]{1,0:T(8,128)S(1)} %copy-done.19), custom_call_target="tpu_custom_call" | custom-call | flops 15032385536 | bytes 33554432 | tf_op jit(solution)/shard_map/core_gram_y/pallas_call | solution.py:119
  992.8 4.3 collective-permute-done.65
  997.0 2.6 bitcast_add_fusion
  1000.4 24.8 %collective-permute-done.66 = f32[256,1024]{1,0:T(8,128)} collective-permute-done((f32[256,1024]{1,0:T(8,128)S(1)}, f32[256,1024]{1,0:T(8,128)}, u32[]{:S(2)}, u32[]{:S(2)}) %collective-permute-start.66) | collective-permute-done | bytes 1048608 | tf_op jit(solution)/shard_map/ppermute | solution.py:457
  1026.7 5.1 collective-permute-start.73
  1032.9 3.2 collective-permute-start.69
  1037.6 2.5 collective-permute-done.72
  1041.4 7.8 collective-permute-done.70
  1049.3 5.5 collective-permute-done.67
  (291 shorter events, 167.6 us)
Async XLA Ops:
  2.1 74.0 %collective-permute-start = (f32[16,64,256]{2,1,0:T(8,128)S(1)}, f32[16,64,256]{2,1,0:T(8,128)}, u32[]{:S(2)}, u32[]{:S(2)}) collective-permute-start(f32[16,64,256]{2,1,0:T(8,128)S(1)} %pack_z.41), channel_id=1, source_target_pairs={{0,16},{4,20},{8,24},{12,28},{16,0},{20,4},{24,8},{28,12},{1,17},{... | collective-permute-start | bytes 3145736 | tf_op jit(solution)/shard_map/ppermute | solution.py:315
  7.7 70.9 %collective-permute-start.1 = (f32[16,64,256]{2,1,0:T(8,128)S(1)}, f32[16,64,256]{2,1,0:T(8,128)}, u32[]{:S(2)}, u32[]{:S(2)}) collective-permute-start(f32[16,64,256]{2,1,0:T(8,128)S(1)} %pack_z.42), channel_id=1, source_target_pairs={{0,12},{4,8},{8,20},{12,16},{16,28},{20,24},{24,4},{28,0},{1,13},{... | collective-permute-start | bytes 3145736 | tf_op jit(solution)/shard_map/ppermute | solution.py:315
  12.4 72.9 %collective-permute-start.2 = (f32[16,64,256]{2,1,0:T(8,128)}, f32[16,64,256]{2,1,0:T(8,128)}, u32[]{:S(2)}, u32[]{:S(2)}) collective-permute-start(f32[16,64,256]{2,1,0:T(8,128)} %pack_z.43), channel_id=1, source_target_pairs={{0,24},{4,28},{8,0},{12,4},{16,8},{20,12},{24,16},{28,20},{1,25},{... | collective-permute-start | bytes 3145736 | tf_op jit(solution)/shard_map/ppermute | solution.py:315
  16.9 149.7 %collective-permute-start.3 = (f32[16,64,256]{2,1,0:T(8,128)}, f32[16,64,256]{2,1,0:T(8,128)}, u32[]{:S(2)}, u32[]{:S(2)}) collective-permute-start(f32[16,64,256]{2,1,0:T(8,128)} %pack_z.44), channel_id=1, source_target_pairs={{0,20},{4,16},{8,28},{12,24},{16,4},{20,0},{24,12},{28,8},{1,21},{... | collective-permute-start | bytes 3145736 | tf_op jit(solution)/shard_map/ppermute | solution.py:315
  19.1 148.8 %collective-permute-start.4 = (f32[16,64,256]{2,1,0:T(8,128)}, f32[16,64,256]{2,1,0:T(8,128)}, u32[]{:S(2)}, u32[]{:S(2)}) collective-permute-start(f32[16,64,256]{2,1,0:T(8,128)} %pack_z.45), channel_id=1, source_target_pairs={{0,4},{4,0},{8,12},{12,8},{16,20},{20,16},{24,28},{28,24},{1,5},{5... | collective-permute-start | bytes 3145736 | tf_op jit(solution)/shard_map/ppermute | solution.py:315
  76.1 93.1 %collective-permute-start.5 = (f32[16,64,256]{2,1,0:T(8,128)}, f32[16,64,256]{2,1,0:T(8,128)S(1)}, u32[]{:S(2)}, u32[]{:S(2)}) collective-permute-start(f32[16,64,256]{2,1,0:T(8,128)} %copy-done.10), channel_id=1, source_target_pairs={{0,8},{4,12},{8,16},{12,20},{16,24},{20,28},{24,0},{28,4},{1,9},{5... | collective-permute-start | bytes 3145736 | tf_op jit(solution)/shard_map/ppermute | solution.py:315
  78.5 90.8 %collective-permute-start.6 = (f32[16,64,256]{2,1,0:T(8,128)S(1)}, f32[16,64,256]{2,1,0:T(8,128)S(1)}, u32[]{:S(2)}, u32[]{:S(2)}) collective-permute-start(f32[16,64,256]{2,1,0:T(8,128)S(1)} %copy-done.13), channel_id=1, source_target_pairs={{0,28},{4,24},{8,4},{12,0},{16,12},{20,8},{24,20},{28,16},{1,29},{... | collective-permute-start | bytes 3145736 | tf_op jit(solution)/shard_map/ppermute | solution.py:315
  175.4 97.7 %collective-permute-start.7 = (f32[8,512,256]{2,1,0:T(8,128)}, f32[8,512,256]{2,1,0:T(8,128)}, u32[]{:S(2)}, u32[]{:S(2)}) collective-permute-start(f32[8,512,256]{2,1,0:T(8,128)} %constant_dynamic-slice_fusion.16), channel_id=1, source_target_pairs={{0,1},{1,0},{2,3},{3,2},{4,5},{5,4},{6,7},{7,6},{8,9},{9,8},{10,11... | collective-permute-start | bytes 12582920 | tf_op jit(solution)/shard_map/ppermute | solution.py:383
  176.8 89.3 %collective-permute-start.18 = (f32[16,64,256]{2,1,0:T(8,128)S(1)}, f32[16,64,256]{2,1,0:T(8,128)}, u32[]{:S(2)}, u32[]{:S(2)}) collective-permute-start(f32[16,64,256]{2,1,0:T(8,128)S(1)} %pack_z.59), channel_id=1, source_target_pairs={{0,16},{4,20},{8,24},{12,28},{16,0},{20,4},{24,8},{28,12},{1,17},{... | collective-permute-start | bytes 3145736 | tf_op jit(solution)/shard_map/ppermute | solution.py:315
  199.2 69.9 %collective-permute-start.19 = (f32[16,64,256]{2,1,0:T(8,128)}, f32[16,64,256]{2,1,0:T(8,128)}, u32[]{:S(2)}, u32[]{:S(2)}) collective-permute-start(f32[16,64,256]{2,1,0:T(8,128)} %pack_z.60), channel_id=1, source_target_pairs={{0,12},{4,8},{8,20},{12,16},{16,28},{20,24},{24,4},{28,0},{1,13},{... | collective-permute-start | bytes 3145736 | tf_op jit(solution)/shard_map/ppermute | solution.py:315
  200.6 198.9 %collective-permute-start.11 = (f32[16,64,256]{2,1,0:T(8,128)S(1)}, f32[16,64,256]{2,1,0:T(8,128)}, u32[]{:S(2)}, u32[]{:S(2)}) collective-permute-start(f32[16,64,256]{2,1,0:T(8,128)S(1)} %pack_z.51), channel_id=1, source_target_pairs={{0,28},{4,24},{8,4},{12,0},{16,12},{20,8},{24,20},{28,16},{1,29},{... | collective-permute-start | bytes 3145736 | tf_op jit(solution)/shard_map/ppermute | solution.py:315
  207.6 131.0 %collective-permute-start.20 = (f32[16,64,256]{2,1,0:T(8,128)}, f32[16,64,256]{2,1,0:T(8,128)}, u32[]{:S(2)}, u32[]{:S(2)}) collective-permute-start(f32[16,64,256]{2,1,0:T(8,128)} %pack_z.61), channel_id=1, source_target_pairs={{0,24},{4,28},{8,0},{12,4},{16,8},{20,12},{24,16},{28,20},{1,25},{... | collective-permute-start | bytes 3145736 | tf_op jit(solution)/shard_map/ppermute | solution.py:315
  266.1 113.0 %collective-permute-start.21 = (f32[16,64,256]{2,1,0:T(8,128)}, f32[16,64,256]{2,1,0:T(8,128)S(1)}, u32[]{:S(2)}, u32[]{:S(2)}) collective-permute-start(f32[16,64,256]{2,1,0:T(8,128)} %copy-done.11), channel_id=1, source_target_pairs={{0,20},{4,16},{8,28},{12,24},{16,4},{20,0},{24,12},{28,8},{1,21},{... | collective-permute-start | bytes 3145736 | tf_op jit(solution)/shard_map/ppermute | solution.py:315
  269.1 110.1 %collective-permute-start.22 = (f32[16,64,256]{2,1,0:T(8,128)S(1)}, f32[16,64,256]{2,1,0:T(8,128)S(1)}, u32[]{:S(2)}, u32[]{:S(2)}) collective-permute-start(f32[16,64,256]{2,1,0:T(8,128)S(1)} %copy-done.15), channel_id=1, source_target_pairs={{0,4},{4,0},{8,12},{12,8},{16,20},{20,16},{24,28},{28,24},{1,5},{5... | collective-permute-start | bytes 3145736 | tf_op jit(solution)/shard_map/ppermute | solution.py:315
  275.9 123.5 %collective-permute-start.8 = (f32[16,64,256]{2,1,0:T(8,128)S(1)}, f32[16,64,256]{2,1,0:T(8,128)S(1)}, u32[]{:S(2)}, u32[]{:S(2)}) collective-permute-start(f32[16,64,256]{2,1,0:T(8,128)S(1)} %copy-done.9), channel_id=1, source_target_pairs={{0,8},{4,12},{8,16},{12,20},{16,24},{20,28},{24,0},{28,4},{1,9},{5... | collective-permute-start | bytes 3145736 | tf_op jit(solution)/shard_map/ppermute | solution.py:315
  397.9 92.7 %collective-permute-start.14 = (f32[4,2,512,256]{3,2,1,0:T(8,128)}, f32[4,2,512,256]{3,2,1,0:T(8,128)}, u32[]{:S(2)}, u32[]{:S(2)}) collective-permute-start(f32[4,2,512,256]{3,2,1,0:T(8,128)} %get-tuple-element.93), channel_id=1, source_target_pairs={{0,2},{1,3},{2,0},{3,1},{4,6},{5,7},{6,4},{7,5},{8,10},{9,11},{10,... | collective-permute-start | bytes 12582920 | tf_op jit(solution)/shard_map/ppermute | solution.py:394
  406.6 92.3 %collective-permute-start.23 = (f32[8,512,256]{2,1,0:T(8,128)}, f32[8,512,256]{2,1,0:T(8,128)}, u32[]{:S(2)}, u32[]{:S(2)}) collective-permute-start(f32[8,512,256]{2,1,0:T(8,128)} %constant_dynamic-slice_fusion.13), channel_id=1, source_target_pairs={{0,1},{1,0},{2,3},{3,2},{4,5},{5,4},{6,7},{7,6},{8,9},{9,8},{10,11... | collective-permute-start | bytes 12582920 | tf_op jit(solution)/shard_map/ppermute | solution.py:383
  408.0 72.3 %collective-permute-start.9 = (f32[16,64,256]{2,1,0:T(8,128)S(1)}, f32[16,64,256]{2,1,0:T(8,128)}, u32[]{:S(2)}, u32[]{:S(2)}) collective-permute-start(f32[16,64,256]{2,1,0:T(8,128)S(1)} %pack_z.50), channel_id=1, source_target_pairs={{0,16},{4,20},{8,24},{12,28},{16,0},{20,4},{24,8},{28,12},{1,17},{... | collective-permute-start | bytes 3145736 | tf_op jit(solution)/shard_map/ppermute | solution.py:315
  409.6 81.1 %collective-permute-start.12 = (f32[16,64,256]{2,1,0:T(8,128)S(1)}, f32[16,64,256]{2,1,0:T(8,128)}, u32[]{:S(2)}, u32[]{:S(2)}) collective-permute-start(f32[16,64,256]{2,1,0:T(8,128)S(1)} %pack_z.53), channel_id=1, source_target_pairs={{0,12},{4,8},{8,20},{12,16},{16,28},{20,24},{24,4},{28,0},{1,13},{... | collective-permute-start | bytes 3145736 | tf_op jit(solution)/shard_map/ppermute | solution.py:315
  416.3 153.9 %collective-permute-start.16 = (f32[16,64,256]{2,1,0:T(8,128)}, f32[16,64,256]{2,1,0:T(8,128)}, u32[]{:S(2)}, u32[]{:S(2)}) collective-permute-start(f32[16,64,256]{2,1,0:T(8,128)} %pack_z.56), channel_id=1, source_target_pairs={{0,20},{4,16},{8,28},{12,24},{16,4},{20,0},{24,12},{28,8},{1,21},{... | collective-permute-start | bytes 3145736 | tf_op jit(solution)/shard_map/ppermute | solution.py:315
  480.3 91.2 %collective-permute-start.17 = (f32[16,64,256]{2,1,0:T(8,128)}, f32[16,64,256]{2,1,0:T(8,128)S(1)}, u32[]{:S(2)}, u32[]{:S(2)}) collective-permute-start(f32[16,64,256]{2,1,0:T(8,128)} %pack_z.57), channel_id=1, source_target_pairs={{0,4},{4,0},{8,12},{12,8},{16,20},{20,16},{24,28},{28,24},{1,5},{5... | collective-permute-start | bytes 3145736 | tf_op jit(solution)/shard_map/ppermute | solution.py:315
  490.6 89.3 %collective-permute-start.25 = (f32[16,64,256]{2,1,0:T(8,128)S(1)}, f32[16,64,256]{2,1,0:T(8,128)S(1)}, u32[]{:S(2)}, u32[]{:S(2)}) collective-permute-start(f32[16,64,256]{2,1,0:T(8,128)S(1)} %pack_z.65), channel_id=1, source_target_pairs={{0,28},{4,24},{8,4},{12,0},{16,12},{20,8},{24,20},{28,16},{1,29},{... | collective-permute-start | bytes 3145736 | tf_op jit(solution)/shard_map/ppermute | solution.py:315
  490.6 79.5 %collective-permute-start.15 = (f32[16,64,256]{2,1,0:T(8,128)S(1)}, f32[16,64,256]{2,1,0:T(8,128)S(1)}, u32[]{:S(2)}, u32[]{:S(2)}) collective-permute-start(f32[16,64,256]{2,1,0:T(8,128)S(1)} %copy-done.17), channel_id=1, source_target_pairs={{0,24},{4,28},{8,0},{12,4},{16,8},{20,12},{24,16},{28,20},{1,25},{... | collective-permute-start | bytes 3145736 | tf_op jit(solution)/shard_map/ppermute | solution.py:315
  501.7 78.1 %collective-permute-start.24 = (f32[16,64,256]{2,1,0:T(8,128)S(1)}, f32[16,64,256]{2,1,0:T(8,128)S(1)}, u32[]{:S(2)}, u32[]{:S(2)}) collective-permute-start(f32[16,64,256]{2,1,0:T(8,128)S(1)} %pack_z.58), channel_id=1, source_target_pairs={{0,8},{4,12},{8,16},{12,20},{16,24},{20,28},{24,0},{28,4},{1,9},{5... | collective-permute-start | bytes 3145736 | tf_op jit(solution)/shard_map/ppermute | solution.py:315
  579.3 92.8 %collective-permute-start.33 = (f32[4,2,512,256]{3,2,1,0:T(8,128)}, f32[4,2,512,256]{3,2,1,0:T(8,128)}, u32[]{:S(2)}, u32[]{:S(2)}) collective-permute-start(f32[4,2,512,256]{3,2,1,0:T(8,128)} %get-tuple-element.91), channel_id=1, source_target_pairs={{0,2},{1,3},{2,0},{3,1},{4,6},{5,7},{6,4},{7,5},{8,10},{9,11},{10,... | collective-permute-start | bytes 12582920 | tf_op jit(solution)/shard_map/ppermute | solution.py:394
  585.8 92.4 %collective-permute-start.26 = (f32[8,512,256]{2,1,0:T(8,128)}, f32[8,512,256]{2,1,0:T(8,128)}, u32[]{:S(2)}, u32[]{:S(2)}) collective-permute-start(f32[8,512,256]{2,1,0:T(8,128)} %constant_dynamic-slice_fusion.12), channel_id=1, source_target_pairs={{0,1},{1,0},{2,3},{3,2},{4,5},{5,4},{6,7},{7,6},{8,9},{9,8},{10,11... | collective-permute-start | bytes 12582920 | tf_op jit(solution)/shard_map/ppermute | solution.py:383
  588.3 101.8 %collective-permute-start.31 = (f32[8,64,256]{2,1,0:T(8,128)S(1)}, f32[8,64,256]{2,1,0:T(8,128)S(1)}, u32[]{:S(2)}, u32[]{:S(2)}) collective-permute-start(f32[8,64,256]{2,1,0:T(8,128)S(1)} %pack_z.70), channel_id=1, source_target_pairs={{0,16},{4,20},{8,24},{12,28},{16,0},{20,4},{24,8},{28,12},{1,17},{... | collective-permute-start | bytes 1572872 | tf_op jit(solution)/shard_map/ppermute | solution.py:315
  589.6 101.6 %collective-permute-start.32 = (f32[8,64,256]{2,1,0:T(8,128)S(1)}, f32[8,64,256]{2,1,0:T(8,128)S(1)}, u32[]{:S(2)}, u32[]{:S(2)}) collective-permute-start(f32[8,64,256]{2,1,0:T(8,128)S(1)} %pack_z.71), channel_id=1, source_target_pairs={{0,12},{4,8},{8,20},{12,16},{16,28},{20,24},{24,4},{28,0},{1,13},{... | collective-permute-start | bytes 1572872 | tf_op jit(solution)/shard_map/ppermute | solution.py:315
  593.5 100.1 %collective-permute-start.35 = (f32[8,64,256]{2,1,0:T(8,128)S(1)}, f32[8,64,256]{2,1,0:T(8,128)S(1)}, u32[]{:S(2)}, u32[]{:S(2)}) collective-permute-start(f32[8,64,256]{2,1,0:T(8,128)S(1)} %pack_z.73), channel_id=1, source_target_pairs={{0,20},{4,16},{8,28},{12,24},{16,4},{20,0},{24,12},{28,8},{1,21},{... | collective-permute-start | bytes 1572872 | tf_op jit(solution)/shard_map/ppermute | solution.py:315
  672.1 21.5 %collective-permute-start.36 = (f32[8,64,256]{2,1,0:T(8,128)S(1)}, f32[8,64,256]{2,1,0:T(8,128)S(1)}, u32[]{:S(2)}, u32[]{:S(2)}) collective-permute-start(f32[8,64,256]{2,1,0:T(8,128)S(1)} %pack_z.74), channel_id=1, source_target_pairs={{0,4},{4,0},{8,12},{12,8},{16,20},{20,16},{24,28},{28,24},{1,5},{5... | collective-permute-start | bytes 1572872 | tf_op jit(solution)/shard_map/ppermute | solution.py:315
  678.1 14.2 %collective-permute-start.34 = (f32[8,64,256]{2,1,0:T(8,128)S(1)}, f32[8,64,256]{2,1,0:T(8,128)S(1)}, u32[]{:S(2)}, u32[]{:S(2)}) collective-permute-start(f32[8,64,256]{2,1,0:T(8,128)S(1)} %pack_z.72), channel_id=1, source_target_pairs={{0,24},{4,28},{8,0},{12,4},{16,8},{20,12},{24,16},{28,20},{1,25},{... | collective-permute-start | bytes 1572872 | tf_op jit(solution)/shard_map/ppermute | solution.py:315
  690.1 91.7 %collective-permute-start.27 = (f32[4,2,512,256]{3,2,1,0:T(8,128)}, f32[4,2,512,256]{3,2,1,0:T(8,128)}, u32[]{:S(2)}, u32[]{:S(2)}) collective-permute-start(f32[4,2,512,256]{3,2,1,0:T(8,128)} %get-tuple-element.89), channel_id=1, source_target_pairs={{0,2},{1,3},{2,0},{3,1},{4,6},{5,7},{6,4},{7,5},{8,10},{9,11},{10,... | collective-permute-start | bytes 12582920 | tf_op jit(solution)/shard_map/ppermute | solution.py:394
  691.1 25.2 %collective-permute-start.38 = (f32[8,64,256]{2,1,0:T(8,128)S(1)}, f32[8,64,256]{2,1,0:T(8,128)S(1)}, u32[]{:S(2)}, u32[]{:S(2)}) collective-permute-start(f32[8,64,256]{2,1,0:T(8,128)S(1)} %pack_z.76), channel_id=1, source_target_pairs={{0,28},{4,24},{8,4},{12,0},{16,12},{20,8},{24,20},{28,16},{1,29},{... | collective-permute-start | bytes 1572872 | tf_op jit(solution)/shard_map/ppermute | solution.py:315
  692.4 23.9 %collective-permute-start.37 = (f32[8,64,256]{2,1,0:T(8,128)S(1)}, f32[8,64,256]{2,1,0:T(8,128)S(1)}, u32[]{:S(2)}, u32[]{:S(2)}) collective-permute-start(f32[8,64,256]{2,1,0:T(8,128)S(1)} %pack_z.75), channel_id=1, source_target_pairs={{0,8},{4,12},{8,16},{12,20},{16,24},{20,28},{24,0},{28,4},{1,9},{5... | collective-permute-start | bytes 1572872 | tf_op jit(solution)/shard_map/ppermute | solution.py:315
  719.9 62.8 %collective-permute-start.39 = (f32[4,512,256]{2,1,0:T(8,128)}, f32[4,512,256]{2,1,0:T(8,128)}, u32[]{:S(2)}, u32[]{:S(2)}) collective-permute-start(f32[4,512,256]{2,1,0:T(8,128)} %constant_dynamic-slice_fusion.9), channel_id=1, source_target_pairs={{0,1},{1,0},{2,3},{3,2},{4,5},{5,4},{6,7},{7,6},{8,9},{9,8},{10,11... | collective-permute-start | bytes 6291464 | tf_op jit(solution)/shard_map/ppermute | solution.py:383
  722.4 48.0 %collective-permute-start.10 = (f32[8,64,256]{2,1,0:T(8,128)S(1)}, f32[8,64,256]{2,1,0:T(8,128)S(1)}, u32[]{:S(2)}, u32[]{:S(2)}) collective-permute-start(f32[8,64,256]{2,1,0:T(8,128)S(1)} %pack_z.49), channel_id=1, source_target_pairs={{0,16},{4,20},{8,24},{12,28},{16,0},{20,4},{24,8},{28,12},{1,17},{... | collective-permute-start | bytes 1572872 | tf_op jit(solution)/shard_map/ppermute | solution.py:315
  733.5 37.5 %collective-permute-start.13 = (f32[8,64,256]{2,1,0:T(8,128)S(1)}, f32[8,64,256]{2,1,0:T(8,128)S(1)}, u32[]{:S(2)}, u32[]{:S(2)}) collective-permute-start(f32[8,64,256]{2,1,0:T(8,128)S(1)} %pack_z.52), channel_id=1, source_target_pairs={{0,12},{4,8},{8,20},{12,16},{16,28},{20,24},{24,4},{28,0},{1,13},{... | collective-permute-start | bytes 1572872 | tf_op jit(solution)/shard_map/ppermute | solution.py:315
  738.2 78.7 %collective-permute-start.29 = (f32[8,64,256]{2,1,0:T(8,128)S(1)}, f32[8,64,256]{2,1,0:T(8,128)}, u32[]{:S(2)}, u32[]{:S(2)}) collective-permute-start(f32[8,64,256]{2,1,0:T(8,128)S(1)} %pack_z.67), channel_id=1, source_target_pairs={{0,20},{4,16},{8,28},{12,24},{16,4},{20,0},{24,12},{28,8},{1,21},{... | collective-permute-start | bytes 1572872 | tf_op jit(solution)/shard_map/ppermute | solution.py:315
  770.4 47.8 %collective-permute-start.41 = (f32[8,64,256]{2,1,0:T(8,128)S(1)}, f32[8,64,256]{2,1,0:T(8,128)S(1)}, u32[]{:S(2)}, u32[]{:S(2)}) collective-permute-start(f32[8,64,256]{2,1,0:T(8,128)S(1)} %pack_z.78), channel_id=1, source_target_pairs={{0,28},{4,24},{8,4},{12,0},{16,12},{20,8},{24,20},{28,16},{1,29},{... | collective-permute-start | bytes 1572872 | tf_op jit(solution)/shard_map/ppermute | solution.py:315
  772.4 45.7 %collective-permute-start.30 = (f32[8,64,256]{2,1,0:T(8,128)S(1)}, f32[8,64,256]{2,1,0:T(8,128)S(1)}, u32[]{:S(2)}, u32[]{:S(2)}) collective-permute-start(f32[8,64,256]{2,1,0:T(8,128)S(1)} %pack_z.68), channel_id=1, source_target_pairs={{0,4},{4,0},{8,12},{12,8},{16,20},{20,16},{24,28},{28,24},{1,5},{5... | collective-permute-start | bytes 1572872 | tf_op jit(solution)/shard_map/ppermute | solution.py:315
  781.8 33.6 %collective-permute-start.28 = (f32[8,64,256]{2,1,0:T(8,128)S(1)}, f32[8,64,256]{2,1,0:T(8,128)S(1)}, u32[]{:S(2)}, u32[]{:S(2)}) collective-permute-start(f32[8,64,256]{2,1,0:T(8,128)S(1)} %pack_z.54), channel_id=1, source_target_pairs={{0,24},{4,28},{8,0},{12,4},{16,8},{20,12},{24,16},{28,20},{1,25},{... | collective-permute-start | bytes 1572872 | tf_op jit(solution)/shard_map/ppermute | solution.py:315
  784.5 33.7 %collective-permute-start.40 = (f32[8,64,256]{2,1,0:T(8,128)S(1)}, f32[8,64,256]{2,1,0:T(8,128)S(1)}, u32[]{:S(2)}, u32[]{:S(2)}) collective-permute-start(f32[8,64,256]{2,1,0:T(8,128)S(1)} %pack_z.69), channel_id=1, source_target_pairs={{0,8},{4,12},{8,16},{12,20},{16,24},{20,28},{24,0},{28,4},{1,9},{5... | collective-permute-start | bytes 1572872 | tf_op jit(solution)/shard_map/ppermute | solution.py:315
  815.4 47.6 %collective-permute-start.42 = (f32[2,2,512,256]{3,2,1,0:T(8,128)S(1)}, f32[2,2,512,256]{3,2,1,0:T(8,128)S(1)}, u32[]{:S(2)}, u32[]{:S(2)}) collective-permute-start(f32[2,2,512,256]{3,2,1,0:T(8,128)S(1)} %get-tuple-element.95), channel_id=1, source_target_pairs={{0,2},{1,3},{2,0},{3,1},{4,6},{5,7},{6,4},{7,5},{8,10},{9,11},{10,... | collective-permute-start | bytes 6291464 | tf_op jit(solution)/shard_map/ppermute | solution.py:394
  820.0 91.8 %collective-permute-start.63 = (f32[4,512,256]{2,1,0:T(8,128)}, f32[4,512,256]{2,1,0:T(8,128)}, u32[]{:S(2)}, u32[]{:S(2)}) collective-permute-start(f32[4,512,256]{2,1,0:T(8,128)} %constant_dynamic-slice_fusion.6), channel_id=1, source_target_pairs={{0,1},{1,0},{2,3},{3,2},{4,5},{5,4},{6,7},{7,6},{8,9},{9,8},{10,11... | collective-permute-start | bytes 6291464 | tf_op jit(solution)/shard_map/ppermute | solution.py:383
  863.8 6.7 collective-permute-start.45
  864.0 8.9 collective-permute-start.44
  864.3 13.8 %collective-permute-start.43 = (f32[128,512]{1,0:T(8,128)S(1)}, f32[128,512]{1,0:T(8,128)}, u32[]{:S(2)}, u32[]{:S(2)}) collective-permute-start(f32[128,512]{1,0:T(8,128)S(1)} %get-tuple-element.103), channel_id=1, source_target_pairs={{0,2},{1,3},{2,0},{3,1},{4,6},{5,7},{6,4},{7,5},{8,10},{9,11},{10,... | collective-permute-start | bytes 786440 | tf_op jit(solution)/shard_map/ppermute | solution.py:431
  879.4 7.4 collective-permute-start.51
  893.5 8.1 collective-permute-start.53
  893.6 8.6 collective-permute-start.54
  900.5 7.8 collective-permute-start.56
  901.6 6.7 collective-permute-start.57
  909.1 9.2 collective-permute-start.60
  909.7 8.6 collective-permute-start.61
  909.7 11.5 %collective-permute-start.62 = (f32[128,512]{1,0:T(8,128)S(1)}, f32[128,512]{1,0:T(8,128)S(1)}, u32[]{:S(2)}, u32[]{:S(2)}) collective-permute-start(f32[128,512]{1,0:T(8,128)S(1)} %bitcast.320), channel_id=1, source_target_pairs={{0,3},{1,0},{2,1},{3,2},{4,7},{5,4},{6,5},{7,6},{8,11},{9,8},{10,9... | collective-permute-start | bytes 786440 | tf_op jit(solution)/shard_map/ppermute | solution.py:440
  913.6 52.4 %collective-permute-start.64 = (f32[2,2,512,256]{3,2,1,0:T(8,128)S(1)}, f32[2,2,512,256]{3,2,1,0:T(8,128)S(1)}, u32[]{:S(2)}, u32[]{:S(2)}) collective-permute-start(f32[2,2,512,256]{3,2,1,0:T(8,128)S(1)} %constant_dynamic-slice_fusion.4), channel_id=1, source_target_pairs={{0,2},{1,3},{2,0},{3,1},{4,6},{5,7},{6,4},{7,5},{8,10},{9,11},{10,... | collective-permute-start | bytes 6291464 | tf_op jit(solution)/shard_map/ppermute | solution.py:394
  999.8 25.4 %collective-permute-start.66 = (f32[256,1024]{1,0:T(8,128)S(1)}, f32[256,1024]{1,0:T(8,128)}, u32[]{:S(2)}, u32[]{:S(2)}) collective-permute-start(f32[256,1024]{1,0:T(8,128)S(1)} %dynamic-slice_bitcast_fusion.1), channel_id=1, source_target_pairs={{0,2},{1,3},{2,0},{3,1},{4,6},{5,7},{6,4},{7,5},{8,10},{9,11},{10,... | collective-permute-start | bytes 3145736 | tf_op jit(solution)/shard_map/ppermute | solution.py:457
  1026.7 9.5 collective-permute-start.73
  1031.7 8.4 collective-permute-start.72
  1031.7 9.7 collective-permute-start.71
  1032.3 17.0 %collective-permute-start.70 = (f32[256,128]{1,0:T(8,128)S(1)}, f32[256,128]{1,0:T(8,128)S(1)}, u32[]{:S(2)}, u32[]{:S(2)}) collective-permute-start(f32[256,128]{1,0:T(8,128)S(1)} %get-tuple-element.100), channel_id=1, source_target_pairs={{0,20},{4,16},{8,28},{12,24},{16,4},{20,0},{24,12},{28,8},{1,21},{... | collective-permute-start | bytes 393224 | tf_op jit(solution)/shard_map/ppermute | solution.py:467
  1032.9 16.4 %collective-permute-start.69 = (f32[256,128]{1,0:T(8,128)S(1)}, f32[256,128]{1,0:T(8,128)S(1)}, u32[]{:S(2)}, u32[]{:S(2)}) collective-permute-start(f32[256,128]{1,0:T(8,128)S(1)} %get-tuple-element.101), channel_id=1, source_target_pairs={{0,24},{4,28},{8,0},{12,4},{16,8},{20,12},{24,16},{28,20},{1,25},{... | collective-permute-start | bytes 393224 | tf_op jit(solution)/shard_map/ppermute | solution.py:467
  1036.1 13.2 %collective-permute-start.68 = (f32[256,128]{1,0:T(8,128)S(1)}, f32[256,128]{1,0:T(8,128)S(1)}, u32[]{:S(2)}, u32[]{:S(2)}) collective-permute-start(f32[256,128]{1,0:T(8,128)S(1)} %get-tuple-element.102), channel_id=1, source_target_pairs={{0,12},{4,8},{8,20},{12,16},{16,28},{20,24},{24,4},{28,0},{1,13},{... | collective-permute-start | bytes 393224 | tf_op jit(solution)/shard_map/ppermute | solution.py:467
  1040.1 14.7 %collective-permute-start.67 = (f32[256,128]{1,0:T(8,128)S(1)}, f32[256,128]{1,0:T(8,128)S(1)}, u32[]{:S(2)}, u32[]{:S(2)}) collective-permute-start(f32[256,128]{1,0:T(8,128)S(1)} %get-tuple-element.96), channel_id=1, source_target_pairs={{0,16},{4,20},{8,24},{12,28},{16,0},{20,4},{24,8},{28,12},{1,17},{... | collective-permute-start | bytes 393224 | tf_op jit(solution)/shard_map/ppermute | solution.py:467
  (42 other events, 537.5 us)

commit v7 on v6

--- a/solution.py
+++ b/solution.py
@@ -9,10 +9,9 @@
 from jax.sharding import PartitionSpec as P
 
 ITERS = 4
-WINDOW = 14
-AHEAD = 2
-CORE = -2
-CHIP = -5
+WINDOW = 8
+AHEAD = 0
+LATE = 1
 TALL = 8
 LINE = 4
 MIB = 1024 * 1024
@@ -89,11 +88,11 @@
         stacked_ref[:rank] = basis_high
         stacked_ref[rank:] = basis_low
 
-    depth, blocks, _, width = field_ref.shape
+    blocks, depth, _, width = field_ref.shape
     stacked = stacked_ref[...]
     for z in range(depth):
         for b in range(blocks):
-            high, low = halves(field_ref[z, b])
+            high, low = halves(field_ref[b, z])
             both = jnp.dot(stacked, high, preferred_element_type=F32)
             core = both[:rank] + both[rank:]
             core += jnp.dot(stacked[:rank], low, preferred_element_type=F32)
@@ -111,7 +110,7 @@
 
 
 def core_gram(cells, basis, total):
-    depth, blocks, width_x, width = cells.shape
+    blocks, depth, width_x, width = cells.shape
     rank = basis.shape[1]
     width_y = blocks * width
     block = 2 if depth % 2 == 0 else 1
@@ -120,7 +119,7 @@
         functools.partial(core_body, steps, total),
         grid=(steps,),
         in_specs=[
-            pl.BlockSpec((block, blocks, width_x, width), lambda i: (i, 0, 0, 0)),
+            pl.BlockSpec((blocks, block, width_x, width), lambda i: (0, i, 0, 0)),
             pl.BlockSpec((width_x, rank), lambda i: (0, 0)),
         ],
         out_specs=pl.BlockSpec((width_y, width_y), lambda i: (0, 0)),
@@ -353,7 +352,7 @@
     shifts[4:4] = [(0, b) for b in range(1, rest)]
     turns = sorted(range(1, m), key=lambda d: abs(2 * d - m))
 
-    cells = jnp.zeros((slab // m, m, width_x, y_block), F32)
+    cells = jnp.zeros((m, slab // m, width_x, y_block), F32)
 
     def to_gx(first, zc, a, b, whole, after):
         place = (moved(g, a, b) * slab + first) // TALL
@@ -375,44 +374,46 @@
         return lax.dynamic_slice_in_dim(array, index * depth, depth, axis=0)
 
     def to_core(whole):
-        both = jnp.zeros((whole.shape[0] // cores, cores, width_x, y_block), F32)
-        own = part(whole, core, cores)[:, None]
-        both = lax.dynamic_update_slice_in_dim(both, own, core, axis=1)
+        both = jnp.zeros((cores, whole.shape[0] // cores, width_x, y_block), F32)
+        own = part(whole, core, cores)[None]
+        both = lax.dynamic_update_slice_in_dim(both, own, core, axis=0)
         for d in range(1, cores):
             cut = part(whole, (core + d) % cores, cores)
             got = lax.ppermute(cut, "yz", core_perm(d))
-            both = lax.dynamic_update_slice_in_dim(both, got[:, None], (core - d) % cores, axis=1)
+            both = lax.dynamic_update_slice_in_dim(both, got[None], (core - d) % cores, axis=0)
         return both
 
-    def to_chip(cells, first, both, after=()):
+    def to_chip(cells, first, both, after):
+        zs = both.shape[1] // chips
+
         def put(cells, value, source):
-            return lax.dynamic_update_slice(cells, value, (first // m, source * cores, 0, 0))
-
-        cells, ends = put(cells, part(both, chip, chips), chip), []
+            return lax.dynamic_update_slice(cells, value, (source * cores, first // m, 0, 0))
+
+        def cut(array, index):
+            return lax.dynamic_slice_in_dim(array, index * zs, zs, axis=1)
+
+        cells = put(cells, cut(both, chip), chip)
         for d in range(1, chips):
-            cut = part(tie(both, after), (chip + d) % chips, chips)
-            got = lax.ppermute(cut, "yz", chip_perm(d))
-            ends.append(got)
+            got = lax.ppermute(cut(tie(both, after), (chip + d) % chips), "yz", chip_perm(d))
             cells = put(cells, got, (chip - d) % chips)
-        return cells, ends
+        return cells
+
+    def to_yz(cells, first, whole):
+        parts = whole.reshape(m, whole.shape[0] // m, width_x, y_block)
+        got = lax.all_to_all(parts, "yz", split_axis=0, concat_axis=0)
+        return lax.dynamic_update_slice_in_dim(cells, got, first // m, axis=1), got
 
     gram = jnp.zeros((width_x, width_x), F32)
-    before, start_z, first, across = None, 0, 0, []
+    before, start_z, first, across = None, 0, 0, None
     group = math.lcm(m, TALL)
     for groups in chunk_depths(slab // group):
         zc = groups * group
         whole = jnp.zeros((zc, n, x_block, y_block), F32)
-        if before is not None:
-            both = to_core(before)
-            cells, ends = to_chip(cells, start_z, both)
-            across.append(ends)
         for k, (a, b) in enumerate(shifts):
-            after = []
-            if k == len(shifts) + CORE and before is not None:
-                after = [both]
-            if k == len(shifts) + CHIP and len(across) > 1:
-                after = across[-2]
+            after = [across] if before is not None and k == len(shifts) - 1 else []
             whole = to_gx(first, zc, a, b, whole, after)
+            if before is not None and k == LATE:
+                cells, across = to_yz(cells, start_z, tie(before, [order.ends[-1]]))
         own = pack(field, (g * slab + first) // TALL, zc)[:, None]
         whole = lax.dynamic_update_slice_in_dim(whole, own, g, axis=1)
         before = whole.reshape(zc, width_x, y_block)
@@ -421,7 +422,7 @@
 
     rows = width_x // m
     both = to_core(before)
-    slabs = tie(gram, across[-1] if across else []).reshape(m, rows, width_x)
+    slabs = gram.reshape(m, rows, width_x)
 
     def pick(array, index):
         return lax.dynamic_index_in_dim(array, index, axis=0, keepdims=False)
@@ -429,7 +430,7 @@
     summed = pick(slabs, q)
     for d in turns:
         summed = summed + lax.ppermute(pick(slabs, (q + d) % m), "yz", yz_perm(d))
-    cells, _ = to_chip(cells, start_z, both, [summed])
+    cells = to_chip(cells, start_z, both, [summed])
     strips = summed.reshape(n, rows // n, width_x)
     summed = pick(strips, g)
     for a, b in shifts:

time: 1070 us -> 1050 us (0.981)
  waiting for transfers between devices: 598 us -> 430 us
  starting transfers between devices: 171 us -> 316 us
    ppermute x35, starting transfers between devices: 128 us -> 250 us  [send(): got = lax.ppermute(tie(value, self.done(0) + list(after)), axis, perm)]
    ppermute x5 -> x1, waiting for transfers between devices: 121 us -> 8.33 us  [to_chip(): lax.ppermute(cut(tie(both, after), (chip + d) % chips), 'yz', chip_perm(d))]
    ppermute x35, waiting for transfers between devices: 410 us -> 336 us  [send(): got = lax.ppermute(tie(value, self.done(0) + list(after)), axis, perm)]
    dynamic_update_slice x35, local copies, waits for them, and re-layouts: 18.9 us -> 56.4 us  [to_gx(): lax.dynamic_update_slice_in_dim(whole, got[:, None], moved(g, a, b, -1),...]
    all_to_all x0 -> x4, waiting for transfers between devices: none -> 33.4 us  [to_yz(): got = lax.all_to_all(parts, 'yz', split_axis=0, concat_axis=0)]
    all_to_all x0 -> x4, starting transfers between devices: none -> 21.7 us  [to_yz(): got = lax.all_to_all(parts, 'yz', split_axis=0, concat_axis=0)]
    dynamic_update_slice x20 -> x8, local copies, waits for them, and re-layouts: 61.2 us -> 39.7 us  [the longest x4 33.1 us: to_yz(): lax.dynamic_update_slice_in_dim(cells, got, first // m, axis=1)]
    unnamed x64 -> x26, local copies, waits for them, and re-layouts: 25.4 us -> 13.1 us
  transfers between devices with their start and end apart: 74 -> 70, of which waited for: 28 -> 23; matrix products, arithmetic and copies ran while one was open for 10% -> 11% of each run, Pallas kernels for 11% -> 12%
where the time goes in v7:
time: 1050 us; the launch traced here: 1030 us
  waiting for transfers between devices  430 us (41%)
  starting transfers between devices  316 us (30%)
  Pallas kernels  148 us (14%)
  local copies, waits for them, and re-layouts  132 us (13%)
    ppermute x35, waiting for transfers between devices, send(): got = lax.ppermute(tie(value, self.done(0) + list(after)), axis, perm)  336 us
    ppermute x35, starting transfers between devices, send(): got = lax.ppermute(tie(value, self.done(0) + list(after)), axis, perm)  250 us
    pallas_call x40, Pallas kernels, pack(): pl.pallas_call(pack_body, grid_spec=pltpu.PrefetchScalarGridSpec(num_scal...  62 us
    dynamic_update_slice x35, local copies, waits for them, and re-layouts, to_gx(): lax.dynamic_update_slice_in_dim(whole, got[:, None], moved(g, a, b, -1),...  56.4 us
    all_to_all x4, waiting for transfers between devices, to_yz(): got = lax.all_to_all(parts, 'yz', split_axis=0, concat_axis=0)  33.4 us
    pallas_call x1, Pallas kernels, iterate(): pl.pallas_call(functools.partial(iterate_body, total), in_specs=[pl.Block...  33.2 us
    dynamic_update_slice x4, local copies, waits for them, and re-layouts, to_yz(): lax.dynamic_update_slice_in_dim(cells, got, first // m, axis=1)  33.1 us
    pallas_call x5, Pallas kernels, gram_of(): pl.pallas_call(functools.partial(gram_body, steps), grid=(steps,), in_spe...  30.6 us
  transfers between devices with their start and end apart: 70, of which 23 were waited for; matrix products, arithmetic and copies ran while one was open for 11% of the time, Pallas kernels for 12%

profile of v7, /device:TPU:0, one launch (start us, length us, event | category | flops | bytes accessed | tf_op | source)
XLA Modules:
  0.0 1033.7 jit_solution(7361362729657763671)
XLA Ops:
  2.1 4.1 collective-permute-start.3
  7.7 2.6 collective-permute-start.5
  25.9 50.3 %collective-permute-done.3 = f32[16,64,256]{2,1,0:T(8,128)} collective-permute-done((f32[16,64,256]{2,1,0:T(8,128)S(1)}, f32[16,64,256]{2,1,0:T(8,128)}, u32[]{:S(2)}, u32[]{:S(2)}) %collective-permute-start.3) | collective-permute-done | bytes 1048608 | tf_op jit(solution)/shard_map/ppermute | solution.py:314
  80.0 5.5 collective-permute-start.12
  86.8 57.8 %collective-permute-start.4 = (f32[16,64,256]{2,1,0:T(8,128)S(1)}, f32[16,64,256]{2,1,0:T(8,128)S(1)}, u32[]{:S(2)}, u32[]{:S(2)}) collective-permute-start(f32[16,64,256]{2,1,0:T(8,128)S(1)} %pack_z.45), channel_id=1, source_target_pairs={{0,12},{4,8},{8,20},{12,16},{16,28},{20,24},{24,4},{28,0},{1,13},{... | collective-permute-start | bytes 3145736 | tf_op jit(solution)/shard_map/ppermute | solution.py:314
  145.9 43.1 %collective-permute-done.9 = f32[16,64,256]{2,1,0:T(8,128)} collective-permute-done((f32[16,64,256]{2,1,0:T(8,128)}, f32[16,64,256]{2,1,0:T(8,128)}, u32[]{:S(2)}, u32[]{:S(2)}) %collective-permute-start.9) | collective-permute-done | bytes 1048608 | tf_op jit(solution)/shard_map/ppermute | solution.py:314
  193.1 2.6 copy-done
  195.8 5.6 all-to-all-start
  202.8 18.1 %collective-permute-start.2 = (f32[16,64,256]{2,1,0:T(8,128)S(1)}, f32[16,64,256]{2,1,0:T(8,128)}, u32[]{:S(2)}, u32[]{:S(2)}) collective-permute-start(f32[16,64,256]{2,1,0:T(8,128)S(1)} %pack_z.43), channel_id=1, source_target_pairs={{0,16},{4,20},{8,24},{12,28},{16,0},{20,4},{24,8},{28,12},{1,17},{... | collective-permute-start | bytes 3145736 | tf_op jit(solution)/shard_map/ppermute | solution.py:314
  222.4 3.3 collective-permute-start.6
  238.3 29.2 %collective-permute-done.2 = f32[16,64,256]{2,1,0:T(8,128)} collective-permute-done((f32[16,64,256]{2,1,0:T(8,128)S(1)}, f32[16,64,256]{2,1,0:T(8,128)}, u32[]{:S(2)}, u32[]{:S(2)}) %collective-permute-start.2) | collective-permute-done | bytes 1048608 | tf_op jit(solution)/shard_map/ppermute | solution.py:314
  269.0 45.3 %collective-permute-start.14 = (f32[16,64,256]{2,1,0:T(8,128)S(1)}, f32[16,64,256]{2,1,0:T(8,128)}, u32[]{:S(2)}, u32[]{:S(2)}) collective-permute-start(f32[16,64,256]{2,1,0:T(8,128)S(1)} %pack_z.57), channel_id=1, source_target_pairs={{0,12},{4,8},{8,20},{12,16},{16,28},{20,24},{24,4},{28,0},{1,13},{... | collective-permute-start | bytes 3145736 | tf_op jit(solution)/shard_map/ppermute | solution.py:314
  314.3 4.4 broadcast.73.clone
  322.1 2.9 collective-permute-start.13
  327.3 52.6 %collective-permute-done.8 = f32[16,64,256]{2,1,0:T(8,128)} collective-permute-done((f32[16,64,256]{2,1,0:T(8,128)}, f32[16,64,256]{2,1,0:T(8,128)}, u32[]{:S(2)}, u32[]{:S(2)}) %collective-permute-start.8) | collective-permute-done | bytes 1048608 | tf_op jit(solution)/shard_map/ppermute | solution.py:314
  386.7 15.2 %collective-permute-done.13 = f32[16,64,256]{2,1,0:T(8,128)S(1)} collective-permute-done((f32[16,64,256]{2,1,0:T(8,128)}, f32[16,64,256]{2,1,0:T(8,128)S(1)}, u32[]{:S(2)}, u32[]{:S(2)}) %collective-permute-start.13) | collective-permute-done | bytes 1048608 | tf_op jit(solution)/shard_map/ppermute | solution.py:314
  404.1 5.6 all-to-all-start.1
  422.6 38.2 %collective-permute-done.19 = f32[16,64,256]{2,1,0:T(8,128)} collective-permute-done((f32[16,64,256]{2,1,0:T(8,128)S(1)}, f32[16,64,256]{2,1,0:T(8,128)}, u32[]{:S(2)}, u32[]{:S(2)}) %collective-permute-start.19) | collective-permute-done | bytes 1048608 | tf_op jit(solution)/shard_map/ppermute | solution.py:314
  462.8 43.0 %collective-permute-start.20 = (f32[8,64,256]{2,1,0:T(8,128)}, f32[8,64,256]{2,1,0:T(8,128)}, u32[]{:S(2)}, u32[]{:S(2)}) collective-permute-start(f32[8,64,256]{2,1,0:T(8,128)} %pack_z.62), channel_id=1, source_target_pairs={{0,12},{4,8},{8,20},{12,16},{16,28},{20,24},{24,4},{28,0},{1,13},{... | collective-permute-start | bytes 1572872 | tf_op jit(solution)/shard_map/ppermute | solution.py:314
  510.8 4.4 broadcast.73.clone.2
  515.2 2.3 bitcast_dynamic-update-slice_fusion.9
  519.8 5.0 collective-permute-start.15
  527.0 35.5 %collective-permute-done.27 = f32[16,64,256]{2,1,0:T(8,128)} collective-permute-done((f32[16,64,256]{2,1,0:T(8,128)}, f32[16,64,256]{2,1,0:T(8,128)}, u32[]{:S(2)}, u32[]{:S(2)}) %collective-permute-start.27) | collective-permute-done | bytes 1048608 | tf_op jit(solution)/shard_map/ppermute | solution.py:314
  569.5 15.2 %collective-permute-done.15 = f32[16,64,256]{2,1,0:T(8,128)S(1)} collective-permute-done((f32[16,64,256]{2,1,0:T(8,128)S(1)}, f32[16,64,256]{2,1,0:T(8,128)S(1)}, u32[]{:S(2)}, u32[]{:S(2)}) %collective-permute-start.15) | collective-permute-done | bytes 1048608 | tf_op jit(solution)/shard_map/ppermute | solution.py:314
  586.9 5.6 all-to-all-start.2
  595.9 4.1 collective-permute-start.22
  610.6 10.2 collective-permute-done.17
  622.0 22.0 %collective-permute-start.18 = (f32[8,64,256]{2,1,0:T(8,128)S(1)}, f32[8,64,256]{2,1,0:T(8,128)}, u32[]{:S(2)}, u32[]{:S(2)}) collective-permute-start(f32[8,64,256]{2,1,0:T(8,128)S(1)} %pack_z.60), channel_id=1, source_target_pairs={{0,12},{4,8},{8,20},{12,16},{16,28},{20,24},{24,4},{28,0},{1,13},{... | collective-permute-start | bytes 1572872 | tf_op jit(solution)/shard_map/ppermute | solution.py:314
  644.0 2.6 broadcast.72.clone.1
  652.3 33.4 %all-to-all-done.2 = f32[4,4,512,256]{3,2,1,0:T(8,128)} async-done(((f32[4,4,512,256]{3,2,1,0:T(8,128)}), f32[4,4,512,256]{3,2,1,0:T(8,128)}, u32[]{:S(2)}, u32[]{:S(2)}) %all-to-all-start.2) | async-done | bytes 8388640 | tf_op jit(solution)/shard_map/all_to_all | solution.py:403
  685.6 5.0 collective-permute-start.33
  696.2 5.4 collective-permute-done.33
  703.3 4.9 all-to-all-start.3
  709.8 3.4 copy-done.1
  713.2 5.7 gram_x.5.before_ref
  720.2 5.2 collective-permute-start.21
  733.7 2.4 collective-permute-start.16
  736.1 7.7 gram_x.6.before_ref
  743.8 7.7 gram_x.7.before_ref
  751.5 38.6 %collective-permute-done.16 = f32[8,64,256]{2,1,0:T(8,128)S(1)} collective-permute-done((f32[8,64,256]{2,1,0:T(8,128)S(1)}, f32[8,64,256]{2,1,0:T(8,128)S(1)}, u32[]{:S(2)}, u32[]{:S(2)}) %collective-permute-start.16) | collective-permute-done | bytes 524320 | tf_op jit(solution)/shard_map/ppermute | solution.py:314
  790.1 2.5 broadcast.72.clone
  797.0 7.6 collective-permute-start.34
  808.3 4.7 gram_x.8.before_ref
  813.0 2.9 collective-permute-done.34
  817.7 3.1 constant_dynamic-slice_fusion.8
  820.7 4.7 gram_x.9
  828.0 13.8 %dynamic_update_slice.184 = f32[4,16,512,256]{3,2,1,0:T(8,128)} pad(f32[4,4,512,256]{3,2,1,0:T(8,128)} %all-to-all-done, f32[]{:T(128)} %constant.1187.clone.1), padding=0_0x0_12x0_0x0_0 | pad | bytes 41943044 | tf_op jit(solution)/shard_map/dynamic_update_slice | solution.py:404
  841.9 5.2 collective-permute-start.44
  848.6 7.5 constant_dynamic-update-slice_fusion.3
  856.7 3.2 collective-permute-start.40
  862.0 7.4 constant_dynamic-update-slice_fusion.2
  869.5 2.4 collective-permute-start.45
  875.7 4.4 constant_dynamic-update-slice_fusion.1
  899.2 3.7 collective-permute-done.54.refs_3_
  902.9 33.2 %subspace.1.basis_ref = f32[512,128]{1,0:T(8,128)} custom-call(s32[4]{0:T(128)S(1)} %pad_add_fusion.places_ref, f32[128,512]{1,0:T(8,128)S(1)} %bitcast.286, f32[128,512]{1,0:T(8,128)S(1)} %collective-permute-done.52.refs_1_, f32[128,512]{1,0:T(8,128)S(1)} %collective-permute-done.53.refs_2_, f32[128,512]{1,0:T(8,128)S(1)} %collective-permute-done.54.refs_3_, ...), custom_call_target="tpu_custom_call" | custom-call | flops 40000000000 | bytes 524288 | tf_op jit(solution)/shard_map/subspace/pallas_call | solution.py:243
  937.6 8.3 collective-permute-done.56
  947.5 22.0 %core_gram_y.1 = f32[1024,1024]{1,0:T(8,128)S(1)} custom-call(f32[4,16,512,256]{3,2,1,0:T(8,128)} %constant_dynamic-update-slice_fusion.field_ref, f32[512,128]{1,0:T(8,128)S(1)} %copy-done.10), custom_call_target="tpu_custom_call" | custom-call | flops 15032385536 | bytes 33554432 | tf_op jit(solution)/shard_map/core_gram_y/pallas_call | solution.py:118
  971.8 4.3 collective-permute-done.57
  976.0 2.6 bitcast_add_fusion
  980.2 23.9 %collective-permute-done.58 = f32[256,1024]{1,0:T(8,128)} collective-permute-done((f32[256,1024]{1,0:T(8,128)S(1)}, f32[256,1024]{1,0:T(8,128)}, u32[]{:S(2)}, u32[]{:S(2)}) %collective-permute-start.58) | collective-permute-done | bytes 1048608 | tf_op jit(solution)/shard_map/ppermute | solution.py:458
  1005.6 3.8 collective-permute-start.65
  1011.5 3.2 collective-permute-start.61
  1019.1 8.7 collective-permute-done.62
  1027.9 4.6 collective-permute-done.59
  (219 shorter events, 187.7 us)
Async XLA Ops:
  2.1 74.0 %collective-permute-start.3 = (f32[16,64,256]{2,1,0:T(8,128)S(1)}, f32[16,64,256]{2,1,0:T(8,128)}, u32[]{:S(2)}, u32[]{:S(2)}) collective-permute-start(f32[16,64,256]{2,1,0:T(8,128)S(1)} %pack_z.44), channel_id=1, source_target_pairs={{0,16},{4,20},{8,24},{12,28},{16,0},{20,4},{24,8},{28,12},{1,17},{... | collective-permute-start | bytes 3145736 | tf_op jit(solution)/shard_map/ppermute | solution.py:314
  7.7 72.3 %collective-permute-start.5 = (f32[16,64,256]{2,1,0:T(8,128)S(1)}, f32[16,64,256]{2,1,0:T(8,128)}, u32[]{:S(2)}, u32[]{:S(2)}) collective-permute-start(f32[16,64,256]{2,1,0:T(8,128)S(1)} %pack_z.46), channel_id=1, source_target_pairs={{0,12},{4,8},{8,20},{12,16},{16,28},{20,24},{24,4},{28,0},{1,13},{... | collective-permute-start | bytes 3145736 | tf_op jit(solution)/shard_map/ppermute | solution.py:314
  12.4 74.3 %collective-permute-start.7 = (f32[16,64,256]{2,1,0:T(8,128)}, f32[16,64,256]{2,1,0:T(8,128)}, u32[]{:S(2)}, u32[]{:S(2)}) collective-permute-start(f32[16,64,256]{2,1,0:T(8,128)} %pack_z.48), channel_id=1, source_target_pairs={{0,24},{4,28},{8,0},{12,4},{16,8},{20,12},{24,16},{28,20},{1,25},{... | collective-permute-start | bytes 3145736 | tf_op jit(solution)/shard_map/ppermute | solution.py:314
  16.9 172.1 %collective-permute-start.9 = (f32[16,64,256]{2,1,0:T(8,128)}, f32[16,64,256]{2,1,0:T(8,128)}, u32[]{:S(2)}, u32[]{:S(2)}) collective-permute-start(f32[16,64,256]{2,1,0:T(8,128)} %pack_z.50), channel_id=1, source_target_pairs={{0,20},{4,16},{8,28},{12,24},{16,4},{20,0},{24,12},{28,8},{1,21},{... | collective-permute-start | bytes 3145736 | tf_op jit(solution)/shard_map/ppermute | solution.py:314
  19.1 171.3 %collective-permute-start = (f32[16,64,256]{2,1,0:T(8,128)}, f32[16,64,256]{2,1,0:T(8,128)}, u32[]{:S(2)}, u32[]{:S(2)}) collective-permute-start(f32[16,64,256]{2,1,0:T(8,128)} %pack_z.40), channel_id=1, source_target_pairs={{0,4},{4,0},{8,12},{12,8},{16,20},{20,16},{24,28},{28,24},{1,5},{5... | collective-permute-start | bytes 3145736 | tf_op jit(solution)/shard_map/ppermute | solution.py:314
  76.1 115.6 %collective-permute-start.11 = (f32[16,64,256]{2,1,0:T(8,128)}, f32[16,64,256]{2,1,0:T(8,128)S(1)}, u32[]{:S(2)}, u32[]{:S(2)}) collective-permute-start(f32[16,64,256]{2,1,0:T(8,128)} %copy-done.3), channel_id=1, source_target_pairs={{0,8},{4,12},{8,16},{12,20},{16,24},{20,28},{24,0},{28,4},{1,9},{5... | collective-permute-start | bytes 3145736 | tf_op jit(solution)/shard_map/ppermute | solution.py:314
  80.0 111.9 %collective-permute-start.12 = (f32[16,64,256]{2,1,0:T(8,128)S(1)}, f32[16,64,256]{2,1,0:T(8,128)S(1)}, u32[]{:S(2)}, u32[]{:S(2)}) collective-permute-start(f32[16,64,256]{2,1,0:T(8,128)S(1)} %copy-done.5), channel_id=1, source_target_pairs={{0,28},{4,24},{8,4},{12,0},{16,12},{20,8},{24,20},{28,16},{1,29},{... | collective-permute-start | bytes 3145736 | tf_op jit(solution)/shard_map/ppermute | solution.py:314
  86.8 105.3 %collective-permute-start.4 = (f32[16,64,256]{2,1,0:T(8,128)S(1)}, f32[16,64,256]{2,1,0:T(8,128)S(1)}, u32[]{:S(2)}, u32[]{:S(2)}) collective-permute-start(f32[16,64,256]{2,1,0:T(8,128)S(1)} %pack_z.45), channel_id=1, source_target_pairs={{0,12},{4,8},{8,20},{12,16},{16,28},{20,24},{24,4},{28,0},{1,13},{... | collective-permute-start | bytes 3145736 | tf_op jit(solution)/shard_map/ppermute | solution.py:314
  195.8 126.3 %all-to-all-start = ((f32[4,4,512,256]{3,2,1,0:T(8,128)}), f32[4,4,512,256]{3,2,1,0:T(8,128)}, u32[]{:S(2)}, u32[]{:S(2)}) async-start(f32[4,4,512,256]{3,2,1,0:T(8,128)} %bitcast.277), calls=%async_computation | async-start | bytes 16777216 | tf_op jit(solution)/shard_map/all_to_all | solution.py:403
  202.8 64.7 %collective-permute-start.2 = (f32[16,64,256]{2,1,0:T(8,128)S(1)}, f32[16,64,256]{2,1,0:T(8,128)}, u32[]{:S(2)}, u32[]{:S(2)}) collective-permute-start(f32[16,64,256]{2,1,0:T(8,128)S(1)} %pack_z.43), channel_id=1, source_target_pairs={{0,16},{4,20},{8,24},{12,28},{16,0},{20,4},{24,8},{28,12},{1,17},{... | collective-permute-start | bytes 3145736 | tf_op jit(solution)/shard_map/ppermute | solution.py:314
  222.4 99.7 %collective-permute-start.6 = (f32[16,64,256]{2,1,0:T(8,128)S(1)}, f32[16,64,256]{2,1,0:T(8,128)}, u32[]{:S(2)}, u32[]{:S(2)}) collective-permute-start(f32[16,64,256]{2,1,0:T(8,128)S(1)} %pack_z.47), channel_id=1, source_target_pairs={{0,24},{4,28},{8,0},{12,4},{16,8},{20,12},{24,16},{28,20},{1,25},{... | collective-permute-start | bytes 3145736 | tf_op jit(solution)/shard_map/ppermute | solution.py:314
  227.9 152.0 %collective-permute-start.8 = (f32[16,64,256]{2,1,0:T(8,128)}, f32[16,64,256]{2,1,0:T(8,128)}, u32[]{:S(2)}, u32[]{:S(2)}) collective-permute-start(f32[16,64,256]{2,1,0:T(8,128)} %pack_z.49), channel_id=1, source_target_pairs={{0,20},{4,16},{8,28},{12,24},{16,4},{20,0},{24,12},{28,8},{1,21},{... | collective-permute-start | bytes 3145736 | tf_op jit(solution)/shard_map/ppermute | solution.py:314
  231.6 152.9 %collective-permute-start.1 = (f32[16,64,256]{2,1,0:T(8,128)}, f32[16,64,256]{2,1,0:T(8,128)}, u32[]{:S(2)}, u32[]{:S(2)}) collective-permute-start(f32[16,64,256]{2,1,0:T(8,128)} %pack_z.41), channel_id=1, source_target_pairs={{0,8},{4,12},{8,16},{12,20},{16,24},{20,28},{24,0},{28,4},{1,9},{5... | collective-permute-start | bytes 3145736 | tf_op jit(solution)/shard_map/ppermute | solution.py:314
  234.3 147.9 %collective-permute-start.10 = (f32[16,64,256]{2,1,0:T(8,128)}, f32[16,64,256]{2,1,0:T(8,128)}, u32[]{:S(2)}, u32[]{:S(2)}) collective-permute-start(f32[16,64,256]{2,1,0:T(8,128)} %pack_z.51), channel_id=1, source_target_pairs={{0,4},{4,0},{8,12},{12,8},{16,20},{20,16},{24,28},{28,24},{1,5},{5... | collective-permute-start | bytes 3145736 | tf_op jit(solution)/shard_map/ppermute | solution.py:314
  269.0 135.2 %collective-permute-start.14 = (f32[16,64,256]{2,1,0:T(8,128)S(1)}, f32[16,64,256]{2,1,0:T(8,128)}, u32[]{:S(2)}, u32[]{:S(2)}) collective-permute-start(f32[16,64,256]{2,1,0:T(8,128)S(1)} %pack_z.57), channel_id=1, source_target_pairs={{0,12},{4,8},{8,20},{12,16},{16,28},{20,24},{24,4},{28,0},{1,13},{... | collective-permute-start | bytes 3145736 | tf_op jit(solution)/shard_map/ppermute | solution.py:314
  322.1 79.9 %collective-permute-start.13 = (f32[16,64,256]{2,1,0:T(8,128)}, f32[16,64,256]{2,1,0:T(8,128)S(1)}, u32[]{:S(2)}, u32[]{:S(2)}) collective-permute-start(f32[16,64,256]{2,1,0:T(8,128)} %copy-done.8), channel_id=1, source_target_pairs={{0,28},{4,24},{8,4},{12,0},{16,12},{20,8},{24,20},{28,16},{1,29},{... | collective-permute-start | bytes 3145736 | tf_op jit(solution)/shard_map/ppermute | solution.py:314
  404.1 115.6 %all-to-all-start.1 = ((f32[4,4,512,256]{3,2,1,0:T(8,128)}), f32[4,4,512,256]{3,2,1,0:T(8,128)}, u32[]{:S(2)}, u32[]{:S(2)}) async-start(f32[4,4,512,256]{3,2,1,0:T(8,128)} %bitcast.65), calls=%async_computation.1 | async-start | bytes 16777216 | tf_op jit(solution)/shard_map/all_to_all | solution.py:403
  411.2 49.6 %collective-permute-start.19 = (f32[16,64,256]{2,1,0:T(8,128)S(1)}, f32[16,64,256]{2,1,0:T(8,128)}, u32[]{:S(2)}, u32[]{:S(2)}) collective-permute-start(f32[16,64,256]{2,1,0:T(8,128)S(1)} %pack_z.61), channel_id=1, source_target_pairs={{0,16},{4,20},{8,24},{12,28},{16,0},{20,4},{24,8},{28,12},{1,17},{... | collective-permute-start | bytes 3145736 | tf_op jit(solution)/shard_map/ppermute | solution.py:314
  413.8 106.0 %collective-permute-start.24 = (f32[16,64,256]{2,1,0:T(8,128)S(1)}, f32[16,64,256]{2,1,0:T(8,128)}, u32[]{:S(2)}, u32[]{:S(2)}) collective-permute-start(f32[16,64,256]{2,1,0:T(8,128)S(1)} %pack_z.66), channel_id=1, source_target_pairs={{0,24},{4,28},{8,0},{12,4},{16,8},{20,12},{24,16},{28,20},{1,25},{... | collective-permute-start | bytes 3145736 | tf_op jit(solution)/shard_map/ppermute | solution.py:314
  417.9 144.7 %collective-permute-start.27 = (f32[16,64,256]{2,1,0:T(8,128)}, f32[16,64,256]{2,1,0:T(8,128)}, u32[]{:S(2)}, u32[]{:S(2)}) collective-permute-start(f32[16,64,256]{2,1,0:T(8,128)} %pack_z.69), channel_id=1, source_target_pairs={{0,20},{4,16},{8,28},{12,24},{16,4},{20,0},{24,12},{28,8},{1,21},{... | collective-permute-start | bytes 3145736 | tf_op jit(solution)/shard_map/ppermute | solution.py:314
  462.8 124.0 %collective-permute-start.20 = (f32[8,64,256]{2,1,0:T(8,128)}, f32[8,64,256]{2,1,0:T(8,128)}, u32[]{:S(2)}, u32[]{:S(2)}) collective-permute-start(f32[8,64,256]{2,1,0:T(8,128)} %pack_z.62), channel_id=1, source_target_pairs={{0,12},{4,8},{8,20},{12,16},{16,28},{20,24},{24,4},{28,0},{1,13},{... | collective-permute-start | bytes 1572872 | tf_op jit(solution)/shard_map/ppermute | solution.py:314
  508.0 56.9 %collective-permute-start.30 = (f32[16,64,256]{2,1,0:T(8,128)}, f32[16,64,256]{2,1,0:T(8,128)}, u32[]{:S(2)}, u32[]{:S(2)}) collective-permute-start(f32[16,64,256]{2,1,0:T(8,128)} %pack_z.72), channel_id=1, source_target_pairs={{0,4},{4,0},{8,12},{12,8},{16,20},{20,16},{24,28},{28,24},{1,5},{5... | collective-permute-start | bytes 3145736 | tf_op jit(solution)/shard_map/ppermute | solution.py:314
  510.7 56.5 %collective-permute-start.32 = (f32[16,64,256]{2,1,0:T(8,128)}, f32[16,64,256]{2,1,0:T(8,128)}, u32[]{:S(2)}, u32[]{:S(2)}) collective-permute-start(f32[16,64,256]{2,1,0:T(8,128)} %pack_z.75), channel_id=1, source_target_pairs={{0,8},{4,12},{8,16},{12,20},{16,24},{20,28},{24,0},{28,4},{1,9},{5... | collective-permute-start | bytes 3145736 | tf_op jit(solution)/shard_map/ppermute | solution.py:314
  519.8 64.9 %collective-permute-start.15 = (f32[16,64,256]{2,1,0:T(8,128)S(1)}, f32[16,64,256]{2,1,0:T(8,128)S(1)}, u32[]{:S(2)}, u32[]{:S(2)}) collective-permute-start(f32[16,64,256]{2,1,0:T(8,128)S(1)} %copy-done.7), channel_id=1, source_target_pairs={{0,28},{4,24},{8,4},{12,0},{16,12},{20,8},{24,20},{28,16},{1,29},{... | collective-permute-start | bytes 3145736 | tf_op jit(solution)/shard_map/ppermute | solution.py:314
  586.9 98.8 %all-to-all-start.2 = ((f32[4,4,512,256]{3,2,1,0:T(8,128)}), f32[4,4,512,256]{3,2,1,0:T(8,128)}, u32[]{:S(2)}, u32[]{:S(2)}) async-start(f32[4,4,512,256]{3,2,1,0:T(8,128)} %bitcast.127), calls=%async_computation.2 | async-start | bytes 16777216 | tf_op jit(solution)/shard_map/all_to_all | solution.py:403
  593.7 27.1 %collective-permute-start.17 = (f32[8,64,256]{2,1,0:T(8,128)S(1)}, f32[8,64,256]{2,1,0:T(8,128)}, u32[]{:S(2)}, u32[]{:S(2)}) collective-permute-start(f32[8,64,256]{2,1,0:T(8,128)S(1)} %pack_z.59), channel_id=1, source_target_pairs={{0,16},{4,20},{8,24},{12,28},{16,0},{20,4},{24,8},{28,12},{1,17},{... | collective-permute-start | bytes 1572872 | tf_op jit(solution)/shard_map/ppermute | solution.py:314
  595.9 54.5 %collective-permute-start.22 = (f32[8,64,256]{2,1,0:T(8,128)S(1)}, f32[8,64,256]{2,1,0:T(8,128)}, u32[]{:S(2)}, u32[]{:S(2)}) collective-permute-start(f32[8,64,256]{2,1,0:T(8,128)S(1)} %pack_z.64), channel_id=1, source_target_pairs={{0,24},{4,28},{8,0},{12,4},{16,8},{20,12},{24,16},{28,20},{1,25},{... | collective-permute-start | bytes 1572872 | tf_op jit(solution)/shard_map/ppermute | solution.py:314
  603.4 87.3 %collective-permute-start.25 = (f32[8,64,256]{2,1,0:T(8,128)}, f32[8,64,256]{2,1,0:T(8,128)}, u32[]{:S(2)}, u32[]{:S(2)}) collective-permute-start(f32[8,64,256]{2,1,0:T(8,128)} %pack_z.67), channel_id=1, source_target_pairs={{0,20},{4,16},{8,28},{12,24},{16,4},{20,0},{24,12},{28,8},{1,21},{... | collective-permute-start | bytes 1572872 | tf_op jit(solution)/shard_map/ppermute | solution.py:314
  606.5 86.0 %collective-permute-start.28 = (f32[8,64,256]{2,1,0:T(8,128)S(1)}, f32[8,64,256]{2,1,0:T(8,128)}, u32[]{:S(2)}, u32[]{:S(2)}) collective-permute-start(f32[8,64,256]{2,1,0:T(8,128)S(1)} %pack_z.70), channel_id=1, source_target_pairs={{0,4},{4,0},{8,12},{12,8},{16,20},{20,16},{24,28},{28,24},{1,5},{5... | collective-permute-start | bytes 1572872 | tf_op jit(solution)/shard_map/ppermute | solution.py:314
  609.3 85.1 %collective-permute-start.31 = (f32[8,64,256]{2,1,0:T(8,128)S(1)}, f32[8,64,256]{2,1,0:T(8,128)}, u32[]{:S(2)}, u32[]{:S(2)}) collective-permute-start(f32[8,64,256]{2,1,0:T(8,128)S(1)} %pack_z.73), channel_id=1, source_target_pairs={{0,8},{4,12},{8,16},{12,20},{16,24},{20,28},{24,0},{28,4},{1,9},{5... | collective-permute-start | bytes 1572872 | tf_op jit(solution)/shard_map/ppermute | solution.py:314
  622.0 81.3 %collective-permute-start.18 = (f32[8,64,256]{2,1,0:T(8,128)S(1)}, f32[8,64,256]{2,1,0:T(8,128)}, u32[]{:S(2)}, u32[]{:S(2)}) collective-permute-start(f32[8,64,256]{2,1,0:T(8,128)S(1)} %pack_z.60), channel_id=1, source_target_pairs={{0,12},{4,8},{8,20},{12,16},{16,28},{20,24},{24,4},{28,0},{1,13},{... | collective-permute-start | bytes 1572872 | tf_op jit(solution)/shard_map/ppermute | solution.py:314
  685.6 15.9 %collective-permute-start.33 = (f32[8,64,256]{2,1,0:T(8,128)S(1)}, f32[8,64,256]{2,1,0:T(8,128)S(1)}, u32[]{:S(2)}, u32[]{:S(2)}) collective-permute-start(f32[8,64,256]{2,1,0:T(8,128)S(1)} %pack_z.76), channel_id=1, source_target_pairs={{0,28},{4,24},{8,4},{12,0},{16,12},{20,8},{24,20},{28,16},{1,29},{... | collective-permute-start | bytes 1572872 | tf_op jit(solution)/shard_map/ppermute | solution.py:314
  703.3 93.7 %all-to-all-start.3 = ((f32[4,2,512,256]{3,2,1,0:T(8,128)}), f32[4,2,512,256]{3,2,1,0:T(8,128)}, u32[]{:S(2)}, u32[]{:S(2)}) async-start(f32[4,2,512,256]{3,2,1,0:T(8,128)} %bitcast.134), calls=%async_computation.3 | async-start | bytes 8388608 | tf_op jit(solution)/shard_map/all_to_all | solution.py:403
  720.2 75.1 %collective-permute-start.21 = (f32[8,64,256]{2,1,0:T(8,128)S(1)}, f32[8,64,256]{2,1,0:T(8,128)S(1)}, u32[]{:S(2)}, u32[]{:S(2)}) collective-permute-start(f32[8,64,256]{2,1,0:T(8,128)S(1)} %pack_z.63), channel_id=1, source_target_pairs={{0,24},{4,28},{8,0},{12,4},{16,8},{20,12},{24,16},{28,20},{1,25},{... | collective-permute-start | bytes 1572872 | tf_op jit(solution)/shard_map/ppermute | solution.py:314
  726.6 69.6 %collective-permute-start.23 = (f32[8,64,256]{2,1,0:T(8,128)S(1)}, f32[8,64,256]{2,1,0:T(8,128)S(1)}, u32[]{:S(2)}, u32[]{:S(2)}) collective-permute-start(f32[8,64,256]{2,1,0:T(8,128)S(1)} %pack_z.65), channel_id=1, source_target_pairs={{0,20},{4,16},{8,28},{12,24},{16,4},{20,0},{24,12},{28,8},{1,21},{... | collective-permute-start | bytes 1572872 | tf_op jit(solution)/shard_map/ppermute | solution.py:314
  727.9 76.7 %collective-permute-start.26 = (f32[8,64,256]{2,1,0:T(8,128)S(1)}, f32[8,64,256]{2,1,0:T(8,128)}, u32[]{:S(2)}, u32[]{:S(2)}) collective-permute-start(f32[8,64,256]{2,1,0:T(8,128)S(1)} %pack_z.68), channel_id=1, source_target_pairs={{0,4},{4,0},{8,12},{12,8},{16,20},{20,16},{24,28},{28,24},{1,5},{5... | collective-permute-start | bytes 1572872 | tf_op jit(solution)/shard_map/ppermute | solution.py:314
  729.7 76.7 %collective-permute-start.29 = (f32[8,64,256]{2,1,0:T(8,128)S(1)}, f32[8,64,256]{2,1,0:T(8,128)}, u32[]{:S(2)}, u32[]{:S(2)}) collective-permute-start(f32[8,64,256]{2,1,0:T(8,128)S(1)} %pack_z.71), channel_id=1, source_target_pairs={{0,8},{4,12},{8,16},{12,20},{16,24},{20,28},{24,0},{28,4},{1,9},{5... | collective-permute-start | bytes 1572872 | tf_op jit(solution)/shard_map/ppermute | solution.py:314
  733.7 56.5 %collective-permute-start.16 = (f32[8,64,256]{2,1,0:T(8,128)S(1)}, f32[8,64,256]{2,1,0:T(8,128)S(1)}, u32[]{:S(2)}, u32[]{:S(2)}) collective-permute-start(f32[8,64,256]{2,1,0:T(8,128)S(1)} %pack_z.58), channel_id=1, source_target_pairs={{0,16},{4,20},{8,24},{12,28},{16,0},{20,4},{24,8},{28,12},{1,17},{... | collective-permute-start | bytes 1572872 | tf_op jit(solution)/shard_map/ppermute | solution.py:314
  797.0 19.0 %collective-permute-start.34 = (f32[8,64,256]{2,1,0:T(8,128)S(1)}, f32[8,64,256]{2,1,0:T(8,128)S(1)}, u32[]{:S(2)}, u32[]{:S(2)}) collective-permute-start(f32[8,64,256]{2,1,0:T(8,128)S(1)} %pack_z.74), channel_id=1, source_target_pairs={{0,28},{4,24},{8,4},{12,0},{16,12},{20,8},{24,20},{28,16},{1,29},{... | collective-permute-start | bytes 1572872 | tf_op jit(solution)/shard_map/ppermute | solution.py:314
  820.7 71.9 %collective-permute-start.55 = (f32[4,512,256]{2,1,0:T(8,128)}, f32[4,512,256]{2,1,0:T(8,128)}, u32[]{:S(2)}, u32[]{:S(2)}) collective-permute-start(f32[4,512,256]{2,1,0:T(8,128)} %constant_dynamic-slice_fusion.8), channel_id=1, source_target_pairs={{0,1},{1,0},{2,3},{3,2},{4,5},{5,4},{6,7},{7,6},{8,9},{9,8},{10,11... | collective-permute-start | bytes 6291464 | tf_op jit(solution)/shard_map/ppermute | solution.py:382
  825.5 16.2 %collective-permute-start.37 = (f32[128,512]{1,0:T(8,128)S(1)}, f32[128,512]{1,0:T(8,128)S(1)}, u32[]{:S(2)}, u32[]{:S(2)}) collective-permute-start(f32[128,512]{1,0:T(8,128)S(1)} %get-tuple-element.128), channel_id=1, source_target_pairs={{0,3},{1,0},{2,1},{3,2},{4,7},{5,4},{6,5},{7,6},{8,11},{9,8},{10,9... | collective-permute-start | bytes 786440 | tf_op jit(solution)/shard_map/ppermute | solution.py:432
  827.4 14.4 %collective-permute-start.36 = (f32[128,512]{1,0:T(8,128)S(1)}, f32[128,512]{1,0:T(8,128)S(1)}, u32[]{:S(2)}, u32[]{:S(2)}) collective-permute-start(f32[128,512]{1,0:T(8,128)S(1)} %get-tuple-element.129), channel_id=1, source_target_pairs={{0,1},{1,2},{2,3},{3,0},{4,5},{5,6},{6,7},{7,4},{8,9},{9,10},{10,1... | collective-permute-start | bytes 786440 | tf_op jit(solution)/shard_map/ppermute | solution.py:432
  827.4 14.4 %collective-permute-start.35 = (f32[128,512]{1,0:T(8,128)S(1)}, f32[128,512]{1,0:T(8,128)S(1)}, u32[]{:S(2)}, u32[]{:S(2)}) collective-permute-start(f32[128,512]{1,0:T(8,128)S(1)} %get-tuple-element.127), channel_id=1, source_target_pairs={{0,2},{1,3},{2,0},{3,1},{4,6},{5,7},{6,4},{7,5},{8,10},{9,11},{10,... | collective-permute-start | bytes 786440 | tf_op jit(solution)/shard_map/ppermute | solution.py:432
  841.9 14.8 %collective-permute-start.44 = (f32[16,512]{1,0:T(8,128)S(1)}, f32[16,512]{1,0:T(8,128)S(1)}, u32[]{:S(2)}, u32[]{:S(2)}) collective-permute-start(f32[16,512]{1,0:T(8,128)S(1)} %get-tuple-element.131), channel_id=1, source_target_pairs={{0,28},{4,24},{8,4},{12,0},{16,12},{20,8},{24,20},{28,16},{1,29},{... | collective-permute-start | bytes 98312 | tf_op jit(solution)/shard_map/ppermute | solution.py:437
  847.1 12.8 %collective-permute-start.43 = (f32[16,512]{1,0:T(8,128)S(1)}, f32[16,512]{1,0:T(8,128)S(1)}, u32[]{:S(2)}, u32[]{:S(2)}) collective-permute-start(f32[16,512]{1,0:T(8,128)S(1)} %get-tuple-element.132), channel_id=1, source_target_pairs={{0,8},{4,12},{8,16},{12,20},{16,24},{20,28},{24,0},{28,4},{1,9},{5... | collective-permute-start | bytes 98312 | tf_op jit(solution)/shard_map/ppermute | solution.py:437
  847.1 14.3 %collective-permute-start.42 = (f32[16,512]{1,0:T(8,128)S(1)}, f32[16,512]{1,0:T(8,128)S(1)}, u32[]{:S(2)}, u32[]{:S(2)}) collective-permute-start(f32[16,512]{1,0:T(8,128)S(1)} %get-tuple-element.133), channel_id=1, source_target_pairs={{0,4},{4,0},{8,12},{12,8},{16,20},{20,16},{24,28},{28,24},{1,5},{5... | collective-permute-start | bytes 98312 | tf_op jit(solution)/shard_map/ppermute | solution.py:437
  856.1 13.3 %collective-permute-start.41 = (f32[16,512]{1,0:T(8,128)S(1)}, f32[16,512]{1,0:T(8,128)S(1)}, u32[]{:S(2)}, u32[]{:S(2)}) collective-permute-start(f32[16,512]{1,0:T(8,128)S(1)} %get-tuple-element.134), channel_id=1, source_target_pairs={{0,20},{4,16},{8,28},{12,24},{16,4},{20,0},{24,12},{28,8},{1,21},{... | collective-permute-start | bytes 98312 | tf_op jit(solution)/shard_map/ppermute | solution.py:437
  856.7 12.7 %collective-permute-start.40 = (f32[16,512]{1,0:T(8,128)S(1)}, f32[16,512]{1,0:T(8,128)S(1)}, u32[]{:S(2)}, u32[]{:S(2)}) collective-permute-start(f32[16,512]{1,0:T(8,128)S(1)} %get-tuple-element.135), channel_id=1, source_target_pairs={{0,24},{4,28},{8,0},{12,4},{16,8},{20,12},{24,16},{28,20},{1,25},{... | collective-permute-start | bytes 98312 | tf_op jit(solution)/shard_map/ppermute | solution.py:437
  859.9 9.5 collective-permute-start.39
  869.5 10.7 %collective-permute-start.45 = (f32[16,512]{1,0:T(8,128)S(1)}, f32[16,512]{1,0:T(8,128)S(1)}, u32[]{:S(2)}, u32[]{:S(2)}) collective-permute-start(f32[16,512]{1,0:T(8,128)S(1)} %fusion.7.refs_0_), channel_id=1, source_target_pairs={{0,16},{4,20},{8,24},{12,28},{16,0},{20,4},{24,8},{28,12},{1,17},{... | collective-permute-start | bytes 98312 | tf_op jit(solution)/shard_map/ppermute | solution.py:438
  871.9 9.8 collective-permute-start.46
  873.8 9.7 collective-permute-start.47
  889.0 8.4 collective-permute-start.52
  890.6 8.6 collective-permute-start.53
  890.6 12.3 %collective-permute-start.54 = (f32[128,512]{1,0:T(8,128)S(1)}, f32[128,512]{1,0:T(8,128)S(1)}, u32[]{:S(2)}, u32[]{:S(2)}) collective-permute-start(f32[128,512]{1,0:T(8,128)S(1)} %bitcast.285), channel_id=1, source_target_pairs={{0,3},{1,0},{2,1},{3,2},{4,7},{5,4},{6,5},{7,6},{8,11},{9,8},{10,9... | collective-permute-start | bytes 786440 | tf_op jit(solution)/shard_map/ppermute | solution.py:441
  894.6 51.4 %collective-permute-start.56 = (f32[2,2,512,256]{3,2,1,0:T(8,128)S(1)}, f32[2,2,512,256]{3,2,1,0:T(8,128)S(1)}, u32[]{:S(2)}, u32[]{:S(2)}) collective-permute-start(f32[2,2,512,256]{3,2,1,0:T(8,128)S(1)} %constant_dynamic-slice_fusion.7), channel_id=1, source_target_pairs={{0,2},{1,3},{2,0},{3,1},{4,6},{5,7},{6,4},{7,5},{8,10},{9,11},{10,... | collective-permute-start | bytes 6291464 | tf_op jit(solution)/shard_map/ppermute | solution.py:397
  978.8 25.4 %collective-permute-start.58 = (f32[256,1024]{1,0:T(8,128)S(1)}, f32[256,1024]{1,0:T(8,128)}, u32[]{:S(2)}, u32[]{:S(2)}) collective-permute-start(f32[256,1024]{1,0:T(8,128)S(1)} %dynamic-slice_bitcast_fusion.1), channel_id=1, source_target_pairs={{0,2},{1,3},{2,0},{3,1},{4,6},{5,7},{6,4},{7,5},{8,10},{9,11},{10,... | collective-permute-start | bytes 3145736 | tf_op jit(solution)/shard_map/ppermute | solution.py:458
  1005.6 9.1 collective-permute-start.65
  1009.4 8.4 collective-permute-start.64
  1009.4 9.7 collective-permute-start.63
  1010.9 17.0 %collective-permute-start.62 = (f32[256,128]{1,0:T(8,128)S(1)}, f32[256,128]{1,0:T(8,128)S(1)}, u32[]{:S(2)}, u32[]{:S(2)}) collective-permute-start(f32[256,128]{1,0:T(8,128)S(1)} %get-tuple-element.124), channel_id=1, source_target_pairs={{0,20},{4,16},{8,28},{12,24},{16,4},{20,0},{24,12},{28,8},{1,21},{... | collective-permute-start | bytes 393224 | tf_op jit(solution)/shard_map/ppermute | solution.py:468
  1011.5 16.4 %collective-permute-start.61 = (f32[256,128]{1,0:T(8,128)S(1)}, f32[256,128]{1,0:T(8,128)S(1)}, u32[]{:S(2)}, u32[]{:S(2)}) collective-permute-start(f32[256,128]{1,0:T(8,128)S(1)} %get-tuple-element.125), channel_id=1, source_target_pairs={{0,24},{4,28},{8,0},{12,4},{16,8},{20,12},{24,16},{28,20},{1,25},{... | collective-permute-start | bytes 393224 | tf_op jit(solution)/shard_map/ppermute | solution.py:468
  1014.7 13.2 %collective-permute-start.60 = (f32[256,128]{1,0:T(8,128)S(1)}, f32[256,128]{1,0:T(8,128)S(1)}, u32[]{:S(2)}, u32[]{:S(2)}) collective-permute-start(f32[256,128]{1,0:T(8,128)S(1)} %get-tuple-element.126), channel_id=1, source_target_pairs={{0,12},{4,8},{8,20},{12,16},{16,28},{20,24},{24,4},{28,0},{1,13},{... | collective-permute-start | bytes 393224 | tf_op jit(solution)/shard_map/ppermute | solution.py:468
  1017.8 14.7 %collective-permute-start.59 = (f32[256,128]{1,0:T(8,128)S(1)}, f32[256,128]{1,0:T(8,128)S(1)}, u32[]{:S(2)}, u32[]{:S(2)}) collective-permute-start(f32[256,128]{1,0:T(8,128)S(1)} %get-tuple-element.120), channel_id=1, source_target_pairs={{0,16},{4,20},{8,24},{12,28},{16,0},{20,4},{24,8},{28,12},{1,17},{... | collective-permute-start | bytes 393224 | tf_op jit(solution)/shard_map/ppermute | solution.py:468
  (19 other events, 150.1 us)

commit v8 on v5

--- a/solution.py
+++ b/solution.py
@@ -354,30 +354,28 @@
         return lax.dynamic_update_slice(cells, got[:, None], (first // m, (q - d) % m, 0, 0))
 
     gram = jnp.zeros((width_x, width_x), F32)
-    before, start_z, first = None, 0, 0
+    first, waiting = 0, []
     group = math.lcm(m, TALL)
     for groups in chunk_depths(slab // group):
         zc = groups * group
         units = zc // m
         whole = jnp.zeros((zc, n, x_block, y_block), F32)
-        waiting = list(turns) if before is not None else []
         for k, (a, b) in enumerate(shifts):
             whole = to_gx(first, zc, a, b, whole)
-            if k >= WINDOW - 1 and waiting:
-                cells = to_yz(cells, start_z, waiting.pop(0), before)
-        for d in waiting:
-            cells = to_yz(cells, start_z, d, before)
-        across = order.ends[-len(shifts) - len(turns) :]
+            if k % 3 == 1 or k == len(shifts) - 1:
+                if waiting and (k >= WINDOW - 1 or len(waiting) > len(turns)):
+                    cells = to_yz(cells, *waiting.pop(0))
         own = pack(field, (g * slab + first) // TALL, zc)[:, None]
         whole = lax.dynamic_update_slice_in_dim(whole, own, g, axis=1)
         before = whole.reshape(zc, width_x, y_block)
         gram = gram_of(before, gram)
         own = lax.dynamic_slice_in_dim(before, q * units, units, axis=0)
         cells = lax.dynamic_update_slice(cells, own[:, None], (first // m, q, 0, 0))
-        start_z, first = first, first + zc
+        waiting += [(first, d, before) for d in turns]
+        first += zc
 
     rows = width_x // m
-    slabs = tie(gram, across).reshape(m, rows, width_x)
+    slabs = gram.reshape(m, rows, width_x)
 
     def pick(array, index):
         return lax.dynamic_index_in_dim(array, index, axis=0, keepdims=False)
@@ -385,7 +383,8 @@
     summed = pick(slabs, q)
     for d in turns:
         summed = summed + lax.ppermute(pick(slabs, (q + d) % m), "yz", yz_perm(d))
-    cells = to_yz(cells, start_z, turns[0], before, [summed])
+    while len(waiting) >= len(turns):
+        cells = to_yz(cells, *waiting.pop(0), [summed])
     strips = summed.reshape(n, rows // n, width_x)
     summed = pick(strips, g)
     for a, b in shifts:
@@ -395,8 +394,8 @@
     summed = stack(pieces, places).reshape(rows, width_x)
     pieces = [summed] + [lax.ppermute(summed, "yz", yz_perm(d)) for d in turns]
     places = jnp.stack([q] + [(q - d) % m for d in turns]).astype(jnp.int32)
-    for d in turns[1:]:
-        cells = to_yz(cells, start_z, d, before, pieces[1:])
+    for entry in waiting:
+        cells = to_yz(cells, *entry, pieces[1:])
     basis = iterate(pieces, places, start, float(width_y * depth))
 
     partial_y = core_gram(cells, basis, float(rank * depth))

time: 1000 us -> 999 us (level)
  starting transfers between devices: 331 us -> 275 us
  waiting for transfers between devices: 383 us -> 430 us
    ppermute x50, starting transfers between devices: 278 us -> 238 us  [send(): got = lax.ppermute(tie(value, self.done(0)), axis, perm)]
    ppermute x50, waiting for transfers between devices: 316 us -> 346 us  [send(): got = lax.ppermute(tie(value, self.done(0)), axis, perm)]
    ppermute x3, waiting for transfers between devices: 8.54 us -> 27 us  [on_device(): pieces = [summed] + [lax.ppermute(summed, 'yz', yz_perm(d)) for d in turns]]
    ppermute x7, starting transfers between devices: 21.2 us -> 9.39 us  [on_device(): lax.ppermute(pick(strips, moved(g, a, b)), 'gx', gx_perm(a, b))]
    dynamic_slice x15 -> x14, local copies, waits for them, and re-layouts: 20.7 us -> 17.2 us  [cut(): return lax.dynamic_slice_in_dim(source, (q + d) % m * zs, zs, axis=0)]
  transfers between devices with their start and end apart: 79 -> 79, of which waited for: 37 -> 31; matrix products, arithmetic and copies ran while one was open for 11% -> 12% of each run, Pallas kernels for 12% -> 12%
where the time goes in v8:
time: 999 us; the launch traced here: 988 us
  waiting for transfers between devices  430 us (43%)
  starting transfers between devices  275 us (28%)
  Pallas kernels  145 us (15%)
  local copies, waits for them, and re-layouts  130 us (13%)
    ppermute x50, waiting for transfers between devices, send(): got = lax.ppermute(tie(value, self.done(0)), axis, perm)  346 us
    ppermute x50, starting transfers between devices, send(): got = lax.ppermute(tie(value, self.done(0)), axis, perm)  238 us
    pallas_call x40, Pallas kernels, pack(): pl.pallas_call(pack_body, grid_spec=pltpu.PrefetchScalarGridSpec(num_scal...  62.8 us
    dynamic_update_slice x35, local copies, waits for them, and re-layouts, to_gx(): lax.dynamic_update_slice_in_dim(whole, got[:, None], moved(g, a, b, -1),...  42.1 us
    pallas_call x1, Pallas kernels, iterate(): pl.pallas_call(functools.partial(iterate_body, total), in_specs=[pl.Block...  34 us
    dynamic_update_slice x15, local copies, waits for them, and re-layouts, to_yz(): lax.dynamic_update_slice(cells, got[:, None], (first // m, (q - d) % m, 0...  31.2 us
    ppermute x3, waiting for transfers between devices, on_device(): pieces = [summed] + [lax.ppermute(summed, 'yz', yz_perm(d)) for d in turns]  27 us
    pallas_call x5, Pallas kernels, gram_of(): pl.pallas_call(functools.partial(gram_body, steps), grid=(steps,), in_spe...  26 us
  transfers between devices with their start and end apart: 79, of which 31 were waited for; matrix products, arithmetic and copies ran while one was open for 12% of the time, Pallas kernels for 12%

profile of v8, /device:TPU:0, one launch (start us, length us, event | category | flops | bytes accessed | tf_op | source)
XLA Modules:
  0.0 988.2 jit_solution(1024148244422136422)
XLA Ops:
  2.9 4.0 collective-permute-start
  34.3 20.3 %collective-permute-done = f32[16,64,256]{2,1,0:T(8,128)} collective-permute-done((f32[16,64,256]{2,1,0:T(8,128)}, f32[16,64,256]{2,1,0:T(8,128)}, u32[]{:S(2)}, u32[]{:S(2)}) %collective-permute-start) | collective-permute-done | bytes 1048608 | tf_op jit(solution)/shard_map/ppermute | solution.py:299
  56.8 21.0 %collective-permute-done.1 = f32[16,64,256]{2,1,0:T(8,128)} collective-permute-done((f32[16,64,256]{2,1,0:T(8,128)}, f32[16,64,256]{2,1,0:T(8,128)}, u32[]{:S(2)}, u32[]{:S(2)}) %collective-permute-start.1) | collective-permute-done | bytes 1048608 | tf_op jit(solution)/shard_map/ppermute | solution.py:299
  77.9 42.9 %collective-permute-start.2 = (f32[16,64,256]{2,1,0:T(8,128)}, f32[16,64,256]{2,1,0:T(8,128)}, u32[]{:S(2)}, u32[]{:S(2)}) collective-permute-start(f32[16,64,256]{2,1,0:T(8,128)} %pack_z.41), channel_id=1, source_target_pairs={{0,16},{4,20},{8,24},{12,28},{16,0},{20,4},{24,8},{28,12},{1,17},{... | collective-permute-start | bytes 3145736 | tf_op jit(solution)/shard_map/ppermute | solution.py:299
  122.9 44.5 %collective-permute-done.4 = f32[16,64,256]{2,1,0:T(8,128)} collective-permute-done((f32[16,64,256]{2,1,0:T(8,128)}, f32[16,64,256]{2,1,0:T(8,128)}, u32[]{:S(2)}, u32[]{:S(2)}) %collective-permute-start.4) | collective-permute-done | bytes 1048608 | tf_op jit(solution)/shard_map/ppermute | solution.py:299
  169.7 3.4 collective-permute-start.7
  176.2 5.1 collective-permute-start.10
  188.9 51.3 %collective-permute-done.8 = f32[16,64,256]{2,1,0:T(8,128)} collective-permute-done((f32[16,64,256]{2,1,0:T(8,128)S(1)}, f32[16,64,256]{2,1,0:T(8,128)}, u32[]{:S(2)}, u32[]{:S(2)}) %collective-permute-start.8) | collective-permute-done | bytes 1048608 | tf_op jit(solution)/shard_map/ppermute | solution.py:299
  240.3 41.0 %collective-permute-start.9 = (f32[16,64,256]{2,1,0:T(8,128)S(1)}, f32[16,64,256]{2,1,0:T(8,128)}, u32[]{:S(2)}, u32[]{:S(2)}) collective-permute-start(f32[16,64,256]{2,1,0:T(8,128)S(1)} %pack_z.48), channel_id=1, source_target_pairs={{0,20},{4,16},{8,28},{12,24},{16,4},{20,0},{24,12},{28,8},{1,21},{... | collective-permute-start | bytes 3145736 | tf_op jit(solution)/shard_map/ppermute | solution.py:299
  288.1 2.9 collective-permute-start.13
  296.7 5.9 gram_x.5.before_ref
  307.9 11.6 %broadcast_in_dim.227 = f32[16,4,512,256]{3,2,1,0:T(8,128)} broadcast(f32[]{:T(128)} %constant.1232.clone.1), dimensions={} | broadcast | bytes 33554436 | tf_op jit(solution)/shard_map/broadcast_in_dim | solution.py:340
  326.3 24.3 %collective-permute-done.9 = f32[16,64,256]{2,1,0:T(8,128)} collective-permute-done((f32[16,64,256]{2,1,0:T(8,128)S(1)}, f32[16,64,256]{2,1,0:T(8,128)}, u32[]{:S(2)}, u32[]{:S(2)}) %collective-permute-start.9) | collective-permute-done | bytes 1048608 | tf_op jit(solution)/shard_map/ppermute | solution.py:299
  356.3 2.4 bitcast_dynamic-update-slice_fusion.35
  366.0 58.2 %collective-permute-start.16 = (f32[16,64,256]{2,1,0:T(8,128)S(1)}, f32[16,64,256]{2,1,0:T(8,128)}, u32[]{:S(2)}, u32[]{:S(2)}) collective-permute-start(f32[16,64,256]{2,1,0:T(8,128)S(1)} %pack_z.56), channel_id=1, source_target_pairs={{0,12},{4,8},{8,20},{12,16},{16,28},{20,24},{24,4},{28,0},{1,13},{... | collective-permute-start | bytes 3145736 | tf_op jit(solution)/shard_map/ppermute | solution.py:299
  425.7 13.6 %collective-permute-done.21 = f32[16,64,256]{2,1,0:T(8,128)} collective-permute-done((f32[16,64,256]{2,1,0:T(8,128)}, f32[16,64,256]{2,1,0:T(8,128)}, u32[]{:S(2)}, u32[]{:S(2)}) %collective-permute-start.21) | collective-permute-done | bytes 1048608 | tf_op jit(solution)/shard_map/ppermute | solution.py:299
  440.8 5.9 gram_x.6.before_ref
  449.1 4.3 broadcast.69.clone.2
  455.8 3.1 bitcast_dynamic-update-slice_fusion.5
  463.2 4.9 collective-permute-done.18
  468.1 5.3 collective-permute-start.19
  474.8 19.3 %collective-permute-start.27 = (f32[16,64,256]{2,1,0:T(8,128)S(1)}, f32[16,64,256]{2,1,0:T(8,128)}, u32[]{:S(2)}, u32[]{:S(2)}) collective-permute-start(f32[16,64,256]{2,1,0:T(8,128)S(1)} %pack_z.65), channel_id=1, source_target_pairs={{0,8},{4,12},{8,16},{12,20},{16,24},{20,28},{24,0},{28,4},{1,9},{5... | collective-permute-start | bytes 3145736 | tf_op jit(solution)/shard_map/ppermute | solution.py:299
  494.1 2.9 collective-permute-start.28
  501.6 3.1 bitcast_dynamic-update-slice_fusion.4
  507.8 3.1 bitcast_dynamic-update-slice_fusion.9
  510.9 44.1 %collective-permute-done.23 = f32[8,64,256]{2,1,0:T(8,128)S(1)} collective-permute-done((f32[8,64,256]{2,1,0:T(8,128)S(1)}, f32[8,64,256]{2,1,0:T(8,128)S(1)}, u32[]{:S(2)}, u32[]{:S(2)}) %collective-permute-start.23) | collective-permute-done | bytes 524320 | tf_op jit(solution)/shard_map/ppermute | solution.py:299
  558.5 18.3 %collective-permute-done.28 = f32[16,64,256]{2,1,0:T(8,128)} collective-permute-done((f32[16,64,256]{2,1,0:T(8,128)S(1)}, f32[16,64,256]{2,1,0:T(8,128)}, u32[]{:S(2)}, u32[]{:S(2)}) %collective-permute-start.28) | collective-permute-done | bytes 1048608 | tf_op jit(solution)/shard_map/ppermute | solution.py:299
  591.4 11.6 %collective-permute-start.20 = (f32[8,64,256]{2,1,0:T(8,128)S(1)}, f32[8,64,256]{2,1,0:T(8,128)S(1)}, u32[]{:S(2)}, u32[]{:S(2)}) collective-permute-start(f32[8,64,256]{2,1,0:T(8,128)S(1)} %pack_z.57), channel_id=1, source_target_pairs={{0,24},{4,28},{8,0},{12,4},{16,8},{20,12},{24,16},{28,20},{1,25},{... | collective-permute-start | bytes 1572872 | tf_op jit(solution)/shard_map/ppermute | solution.py:299
  603.0 7.7 gram_x.7.before_ref
  611.9 3.2 constant_dynamic-slice_fusion.13
  615.1 3.1 bitcast_dynamic-update-slice_fusion.3
  621.0 6.9 collective-permute-done.31
  629.1 4.6 collective-permute-start.34
  633.9 3.0 constant_dynamic-slice_fusion.16
  638.2 3.7 collective-permute-start.37
  642.0 3.1 bitcast_dynamic-update-slice_fusion.2
  645.1 3.0 constant_dynamic-slice_fusion.14
  648.1 3.1 bitcast_dynamic-update-slice_fusion.8
  651.2 43.3 %collective-permute-done.30 = f32[8,64,256]{2,1,0:T(8,128)S(1)} collective-permute-done((f32[8,64,256]{2,1,0:T(8,128)S(1)}, f32[8,64,256]{2,1,0:T(8,128)S(1)}, u32[]{:S(2)}, u32[]{:S(2)}) %collective-permute-start.30) | collective-permute-done | bytes 524320 | tf_op jit(solution)/shard_map/ppermute | solution.py:299
  705.8 4.7 collective-permute-start.35
  710.5 3.2 gram_x.8.before_ref
  713.7 3.1 bitcast_dynamic-update-slice_fusion.1
  716.8 24.8 %collective-permute-done.38 = f32[4,512,256]{2,1,0:T(8,128)} collective-permute-done((f32[4,512,256]{2,1,0:T(8,128)}, f32[4,512,256]{2,1,0:T(8,128)}, u32[]{:S(2)}, u32[]{:S(2)}) %collective-permute-start.38) | collective-permute-done | bytes 2097184 | tf_op jit(solution)/shard_map/ppermute | solution.py:299
  743.8 3.9 collective-permute-start.43
  750.5 19.1 %collective-permute-done.39 = f32[8,64,256]{2,1,0:T(8,128)} collective-permute-done((f32[8,64,256]{2,1,0:T(8,128)S(1)}, f32[8,64,256]{2,1,0:T(8,128)}, u32[]{:S(2)}, u32[]{:S(2)}) %collective-permute-start.39) | collective-permute-done | bytes 524320 | tf_op jit(solution)/shard_map/ppermute | solution.py:299
  772.9 4.0 collective-permute-done.43
  777.0 3.3 gram_x.9
  783.5 3.1 bitcast_dynamic-update-slice_fusion
  786.5 2.7 collective-permute-done.46
  791.2 3.5 collective-permute-done.44
  806.9 2.9 collective-permute-done.48
  810.6 2.8 collective-permute-start.55
  818.2 3.7 collective-permute-start.60
  828.9 4.4 collective-permute-done.61.refs_1_
  833.3 22.6 %collective-permute-done.62.refs_2_ = f32[128,512]{1,0:T(8,128)S(1)} collective-permute-done((f32[128,512]{1,0:T(8,128)S(1)}, f32[128,512]{1,0:T(8,128)S(1)}, u32[]{:S(2)}, u32[]{:S(2)}) %collective-permute-start.62) | collective-permute-done | bytes 262176 | tf_op jit(solution)/shard_map/ppermute | solution.py:395
  858.2 34.0 %subspace.1.basis_ref = f32[512,128]{1,0:T(8,128)} custom-call(s32[4]{0:T(128)S(1)} %pad_add_fusion.places_ref, f32[128,512]{1,0:T(8,128)S(1)} %bitcast.358, f32[128,512]{1,0:T(8,128)S(1)} %collective-permute-done.61.refs_1_, f32[128,512]{1,0:T(8,128)S(1)} %collective-permute-done.62.refs_2_, f32[128,512]{1,0:T(8,128)S(1)} %collective-permute-done.63.refs_3_, ...), custom_call_target="tpu_custom_call" | custom-call | flops 40000000000 | bytes 524288 | tf_op jit(solution)/shard_map/subspace/pallas_call | solution.py:228
  896.5 4.3 collective-permute-done.68
  903.6 21.9 %core_gram_y.1 = f32[1024,1024]{1,0:T(8,128)S(1)} custom-call(f32[16,4,512,256]{3,2,1,0:T(8,128)} %bitcast_dynamic-update-slice_fusion.40.field_ref, f32[512,128]{1,0:T(8,128)S(1)} %copy-done.11), custom_call_target="tpu_custom_call" | custom-call | flops 15032385536 | bytes 33554432 | tf_op jit(solution)/shard_map/core_gram_y/pallas_call | solution.py:117
  928.7 3.9 collective-permute-done.70
  932.6 2.6 bitcast_add_fusion
  936.8 24.1 %collective-permute-done.71 = f32[256,1024]{1,0:T(8,128)} collective-permute-done((f32[256,1024]{1,0:T(8,128)S(1)}, f32[256,1024]{1,0:T(8,128)}, u32[]{:S(2)}, u32[]{:S(2)}) %collective-permute-start.71) | collective-permute-done | bytes 1048608 | tf_op jit(solution)/shard_map/ppermute | solution.py:417
  966.5 2.6 collective-permute-start.74
  972.6 10.0 %collective-permute-done.75 = f32[256,128]{1,0:T(8,128)S(1)} collective-permute-done((f32[256,128]{1,0:T(8,128)S(1)}, f32[256,128]{1,0:T(8,128)S(1)}, u32[]{:S(2)}, u32[]{:S(2)}) %collective-permute-start.75) | collective-permute-done | bytes 131104 | tf_op jit(solution)/shard_map/ppermute | solution.py:425
  982.6 4.5 collective-permute-done.72
  (284 shorter events, 202.6 us)
Async XLA Ops:
  2.9 51.7 %collective-permute-start = (f32[16,64,256]{2,1,0:T(8,128)}, f32[16,64,256]{2,1,0:T(8,128)}, u32[]{:S(2)}, u32[]{:S(2)}) collective-permute-start(f32[16,64,256]{2,1,0:T(8,128)} %pack_z.40), channel_id=1, source_target_pairs={{0,16},{4,20},{8,24},{12,28},{16,0},{20,4},{24,8},{28,12},{1,17},{... | collective-permute-start | bytes 3145736 | tf_op jit(solution)/shard_map/ppermute | solution.py:299
  9.1 68.7 %collective-permute-start.1 = (f32[16,64,256]{2,1,0:T(8,128)}, f32[16,64,256]{2,1,0:T(8,128)}, u32[]{:S(2)}, u32[]{:S(2)}) collective-permute-start(f32[16,64,256]{2,1,0:T(8,128)} %pack_z.42), channel_id=1, source_target_pairs={{0,24},{4,28},{8,0},{12,4},{16,8},{20,12},{24,16},{28,20},{1,25},{... | collective-permute-start | bytes 3145736 | tf_op jit(solution)/shard_map/ppermute | solution.py:299
  12.7 108.0 %collective-permute-start.3 = (f32[16,64,256]{2,1,0:T(8,128)}, f32[16,64,256]{2,1,0:T(8,128)}, u32[]{:S(2)}, u32[]{:S(2)}) collective-permute-start(f32[16,64,256]{2,1,0:T(8,128)} %pack_z.43), channel_id=1, source_target_pairs={{0,12},{4,8},{8,20},{12,16},{16,28},{20,24},{24,4},{28,0},{1,13},{... | collective-permute-start | bytes 3145736 | tf_op jit(solution)/shard_map/ppermute | solution.py:299
  16.6 150.8 %collective-permute-start.4 = (f32[16,64,256]{2,1,0:T(8,128)}, f32[16,64,256]{2,1,0:T(8,128)}, u32[]{:S(2)}, u32[]{:S(2)}) collective-permute-start(f32[16,64,256]{2,1,0:T(8,128)} %pack_z.45), channel_id=1, source_target_pairs={{0,20},{4,16},{8,28},{12,24},{16,4},{20,0},{24,12},{28,8},{1,21},{... | collective-permute-start | bytes 3145736 | tf_op jit(solution)/shard_map/ppermute | solution.py:299
  19.8 149.9 %collective-permute-start.6 = (f32[16,64,256]{2,1,0:T(8,128)}, f32[16,64,256]{2,1,0:T(8,128)}, u32[]{:S(2)}, u32[]{:S(2)}) collective-permute-start(f32[16,64,256]{2,1,0:T(8,128)} %pack_z.47), channel_id=1, source_target_pairs={{0,4},{4,0},{8,12},{12,8},{16,20},{20,16},{24,28},{28,24},{1,5},{5... | collective-permute-start | bytes 3145736 | tf_op jit(solution)/shard_map/ppermute | solution.py:299
  77.9 208.0 %collective-permute-start.2 = (f32[16,64,256]{2,1,0:T(8,128)}, f32[16,64,256]{2,1,0:T(8,128)}, u32[]{:S(2)}, u32[]{:S(2)}) collective-permute-start(f32[16,64,256]{2,1,0:T(8,128)} %pack_z.41), channel_id=1, source_target_pairs={{0,16},{4,20},{8,24},{12,28},{16,0},{20,4},{24,8},{28,12},{1,17},{... | collective-permute-start | bytes 3145736 | tf_op jit(solution)/shard_map/ppermute | solution.py:299
  167.4 117.0 %collective-permute-start.5 = (f32[16,64,256]{2,1,0:T(8,128)}, f32[16,64,256]{2,1,0:T(8,128)}, u32[]{:S(2)}, u32[]{:S(2)}) collective-permute-start(f32[16,64,256]{2,1,0:T(8,128)} %pack_z.44), channel_id=1, source_target_pairs={{0,12},{4,8},{8,20},{12,16},{16,28},{20,24},{24,4},{28,0},{1,13},{... | collective-permute-start | bytes 3145736 | tf_op jit(solution)/shard_map/ppermute | solution.py:299
  169.7 118.4 %collective-permute-start.7 = (f32[16,64,256]{2,1,0:T(8,128)}, f32[16,64,256]{2,1,0:T(8,128)}, u32[]{:S(2)}, u32[]{:S(2)}) collective-permute-start(f32[16,64,256]{2,1,0:T(8,128)} %pack_z.46), channel_id=1, source_target_pairs={{0,24},{4,28},{8,0},{12,4},{16,8},{20,12},{24,16},{28,20},{1,25},{... | collective-permute-start | bytes 3145736 | tf_op jit(solution)/shard_map/ppermute | solution.py:299
  174.6 65.6 %collective-permute-start.8 = (f32[16,64,256]{2,1,0:T(8,128)S(1)}, f32[16,64,256]{2,1,0:T(8,128)}, u32[]{:S(2)}, u32[]{:S(2)}) collective-permute-start(f32[16,64,256]{2,1,0:T(8,128)S(1)} %copy-done.7), channel_id=1, source_target_pairs={{0,8},{4,12},{8,16},{12,20},{16,24},{20,28},{24,0},{28,4},{1,9},{5... | collective-permute-start | bytes 3145736 | tf_op jit(solution)/shard_map/ppermute | solution.py:299
  176.2 105.1 %collective-permute-start.10 = (f32[16,64,256]{2,1,0:T(8,128)S(1)}, f32[16,64,256]{2,1,0:T(8,128)S(1)}, u32[]{:S(2)}, u32[]{:S(2)}) collective-permute-start(f32[16,64,256]{2,1,0:T(8,128)S(1)} %copy-done.9), channel_id=1, source_target_pairs={{0,28},{4,24},{8,4},{12,0},{16,12},{20,8},{24,20},{28,16},{1,29},{... | collective-permute-start | bytes 3145736 | tf_op jit(solution)/shard_map/ppermute | solution.py:299
  240.3 110.4 %collective-permute-start.9 = (f32[16,64,256]{2,1,0:T(8,128)S(1)}, f32[16,64,256]{2,1,0:T(8,128)}, u32[]{:S(2)}, u32[]{:S(2)}) collective-permute-start(f32[16,64,256]{2,1,0:T(8,128)S(1)} %pack_z.48), channel_id=1, source_target_pairs={{0,20},{4,16},{8,28},{12,24},{16,4},{20,0},{24,12},{28,8},{1,21},{... | collective-permute-start | bytes 3145736 | tf_op jit(solution)/shard_map/ppermute | solution.py:299
  281.3 69.3 %collective-permute-start.11 = (f32[16,64,256]{2,1,0:T(8,128)S(1)}, f32[16,64,256]{2,1,0:T(8,128)}, u32[]{:S(2)}, u32[]{:S(2)}) collective-permute-start(f32[16,64,256]{2,1,0:T(8,128)S(1)} %pack_z.50), channel_id=1, source_target_pairs={{0,4},{4,0},{8,12},{12,8},{16,20},{20,16},{24,28},{28,24},{1,5},{5... | collective-permute-start | bytes 3145736 | tf_op jit(solution)/shard_map/ppermute | solution.py:299
  284.5 67.7 %collective-permute-start.12 = (f32[16,64,256]{2,1,0:T(8,128)}, f32[16,64,256]{2,1,0:T(8,128)S(1)}, u32[]{:S(2)}, u32[]{:S(2)}) collective-permute-start(f32[16,64,256]{2,1,0:T(8,128)} %pack_z.52), channel_id=1, source_target_pairs={{0,8},{4,12},{8,16},{12,20},{16,24},{20,28},{24,0},{28,4},{1,9},{5... | collective-permute-start | bytes 3145736 | tf_op jit(solution)/shard_map/ppermute | solution.py:299
  288.1 72.0 %collective-permute-start.13 = (f32[16,64,256]{2,1,0:T(8,128)}, f32[16,64,256]{2,1,0:T(8,128)}, u32[]{:S(2)}, u32[]{:S(2)}) collective-permute-start(f32[16,64,256]{2,1,0:T(8,128)} %pack_z.53), channel_id=1, source_target_pairs={{0,28},{4,24},{8,4},{12,0},{16,12},{20,8},{24,20},{28,16},{1,29},{... | collective-permute-start | bytes 3145736 | tf_op jit(solution)/shard_map/ppermute | solution.py:299
  295.1 70.8 %collective-permute-start.15 = (f32[4,512,256]{2,1,0:T(8,128)}, f32[4,512,256]{2,1,0:T(8,128)}, u32[]{:S(2)}, u32[]{:S(2)}) collective-permute-start(f32[4,512,256]{2,1,0:T(8,128)} %constant_dynamic-slice_fusion.19), channel_id=1, source_target_pairs={{0,2},{1,3},{2,0},{3,1},{4,6},{5,7},{6,4},{7,5},{8,10},{9,11},{10,... | collective-permute-start | bytes 6291464 | tf_op jit(solution)/shard_map/ppermute | solution.py:299
  350.6 108.3 %collective-permute-start.14 = (f32[4,512,256]{2,1,0:T(8,128)}, f32[4,512,256]{2,1,0:T(8,128)}, u32[]{:S(2)}, u32[]{:S(2)}) collective-permute-start(f32[4,512,256]{2,1,0:T(8,128)} %constant_dynamic-slice_fusion.21), channel_id=1, source_target_pairs={{0,1},{1,2},{2,3},{3,0},{4,5},{5,6},{6,7},{7,4},{8,9},{9,10},{10,1... | collective-permute-start | bytes 6291464 | tf_op jit(solution)/shard_map/ppermute | solution.py:299
  350.6 88.7 %collective-permute-start.21 = (f32[16,64,256]{2,1,0:T(8,128)}, f32[16,64,256]{2,1,0:T(8,128)}, u32[]{:S(2)}, u32[]{:S(2)}) collective-permute-start(f32[16,64,256]{2,1,0:T(8,128)} %pack_z.64), channel_id=1, source_target_pairs={{0,16},{4,20},{8,24},{12,28},{16,0},{20,4},{24,8},{28,12},{1,17},{... | collective-permute-start | bytes 3145736 | tf_op jit(solution)/shard_map/ppermute | solution.py:299
  352.1 122.6 %collective-permute-start.26 = (f32[4,512,256]{2,1,0:T(8,128)}, f32[4,512,256]{2,1,0:T(8,128)}, u32[]{:S(2)}, u32[]{:S(2)}) collective-permute-start(f32[4,512,256]{2,1,0:T(8,128)} %constant_dynamic-slice_fusion.18), channel_id=1, source_target_pairs={{0,3},{1,0},{2,1},{3,2},{4,7},{5,4},{6,5},{7,6},{8,11},{9,8},{10,9... | collective-permute-start | bytes 6291464 | tf_op jit(solution)/shard_map/ppermute | solution.py:299
  366.0 94.4 %collective-permute-start.16 = (f32[16,64,256]{2,1,0:T(8,128)S(1)}, f32[16,64,256]{2,1,0:T(8,128)}, u32[]{:S(2)}, u32[]{:S(2)}) collective-permute-start(f32[16,64,256]{2,1,0:T(8,128)S(1)} %pack_z.56), channel_id=1, source_target_pairs={{0,12},{4,8},{8,20},{12,16},{16,28},{20,24},{24,4},{28,0},{1,13},{... | collective-permute-start | bytes 3145736 | tf_op jit(solution)/shard_map/ppermute | solution.py:299
  425.7 42.5 %collective-permute-start.18 = (f32[16,64,256]{2,1,0:T(8,128)S(1)}, f32[16,64,256]{2,1,0:T(8,128)}, u32[]{:S(2)}, u32[]{:S(2)}) collective-permute-start(f32[16,64,256]{2,1,0:T(8,128)S(1)} %pack_z.59), channel_id=1, source_target_pairs={{0,24},{4,28},{8,0},{12,4},{16,8},{20,12},{24,16},{28,20},{1,25},{... | collective-permute-start | bytes 3145736 | tf_op jit(solution)/shard_map/ppermute | solution.py:299
  439.3 35.4 %collective-permute-start.22 = (f32[16,64,256]{2,1,0:T(8,128)S(1)}, f32[16,64,256]{2,1,0:T(8,128)}, u32[]{:S(2)}, u32[]{:S(2)}) collective-permute-start(f32[16,64,256]{2,1,0:T(8,128)S(1)} %pack_z.63), channel_id=1, source_target_pairs={{0,4},{4,0},{8,12},{12,8},{16,20},{20,16},{24,28},{28,24},{1,5},{5... | collective-permute-start | bytes 3145736 | tf_op jit(solution)/shard_map/ppermute | solution.py:299
  460.3 129.7 %collective-permute-start.17 = (f32[4,512,256]{2,1,0:T(8,128)}, f32[4,512,256]{2,1,0:T(8,128)}, u32[]{:S(2)}, u32[]{:S(2)}) collective-permute-start(f32[4,512,256]{2,1,0:T(8,128)} %constant_dynamic-slice_fusion.20), channel_id=1, source_target_pairs={{0,2},{1,3},{2,0},{3,1},{4,6},{5,7},{6,4},{7,5},{8,10},{9,11},{10,... | collective-permute-start | bytes 6291464 | tf_op jit(solution)/shard_map/ppermute | solution.py:299
  468.1 88.6 %collective-permute-start.19 = (f32[16,64,256]{2,1,0:T(8,128)S(1)}, f32[16,64,256]{2,1,0:T(8,128)}, u32[]{:S(2)}, u32[]{:S(2)}) collective-permute-start(f32[16,64,256]{2,1,0:T(8,128)S(1)} %pack_z.58), channel_id=1, source_target_pairs={{0,28},{4,24},{8,4},{12,0},{16,12},{20,8},{24,20},{28,16},{1,29},{... | collective-permute-start | bytes 3145736 | tf_op jit(solution)/shard_map/ppermute | solution.py:299
  474.7 80.3 %collective-permute-start.23 = (f32[8,64,256]{2,1,0:T(8,128)S(1)}, f32[8,64,256]{2,1,0:T(8,128)S(1)}, u32[]{:S(2)}, u32[]{:S(2)}) collective-permute-start(f32[8,64,256]{2,1,0:T(8,128)S(1)} %pack_z.62), channel_id=1, source_target_pairs={{0,16},{4,20},{8,24},{12,28},{16,0},{20,4},{24,8},{28,12},{1,17},{... | collective-permute-start | bytes 1572872 | tf_op jit(solution)/shard_map/ppermute | solution.py:299
  474.8 102.0 %collective-permute-start.27 = (f32[16,64,256]{2,1,0:T(8,128)S(1)}, f32[16,64,256]{2,1,0:T(8,128)}, u32[]{:S(2)}, u32[]{:S(2)}) collective-permute-start(f32[16,64,256]{2,1,0:T(8,128)S(1)} %pack_z.65), channel_id=1, source_target_pairs={{0,8},{4,12},{8,16},{12,20},{16,24},{20,28},{24,0},{28,4},{1,9},{5... | collective-permute-start | bytes 3145736 | tf_op jit(solution)/shard_map/ppermute | solution.py:299
  494.1 82.7 %collective-permute-start.28 = (f32[16,64,256]{2,1,0:T(8,128)S(1)}, f32[16,64,256]{2,1,0:T(8,128)}, u32[]{:S(2)}, u32[]{:S(2)}) collective-permute-start(f32[16,64,256]{2,1,0:T(8,128)S(1)} %pack_z.67), channel_id=1, source_target_pairs={{0,20},{4,16},{8,28},{12,24},{16,4},{20,0},{24,12},{28,8},{1,21},{... | collective-permute-start | bytes 3145736 | tf_op jit(solution)/shard_map/ppermute | solution.py:299
  557.9 54.0 %collective-permute-start.24 = (f32[8,64,256]{2,1,0:T(8,128)S(1)}, f32[8,64,256]{2,1,0:T(8,128)S(1)}, u32[]{:S(2)}, u32[]{:S(2)}) collective-permute-start(f32[8,64,256]{2,1,0:T(8,128)S(1)} %pack_z.61), channel_id=1, source_target_pairs={{0,4},{4,0},{8,12},{12,8},{16,20},{20,16},{24,28},{28,24},{1,5},{5... | collective-permute-start | bytes 1572872 | tf_op jit(solution)/shard_map/ppermute | solution.py:299
  576.8 57.0 %collective-permute-start.29 = (f32[4,512,256]{2,1,0:T(8,128)}, f32[4,512,256]{2,1,0:T(8,128)}, u32[]{:S(2)}, u32[]{:S(2)}) collective-permute-start(f32[4,512,256]{2,1,0:T(8,128)} %constant_dynamic-slice_fusion.17), channel_id=1, source_target_pairs={{0,1},{1,2},{2,3},{3,0},{4,5},{5,6},{6,7},{7,4},{8,9},{9,10},{10,1... | collective-permute-start | bytes 6291464 | tf_op jit(solution)/shard_map/ppermute | solution.py:299
  576.8 61.4 %collective-permute-start.36 = (f32[4,512,256]{2,1,0:T(8,128)S(1)}, f32[4,512,256]{2,1,0:T(8,128)S(1)}, u32[]{:S(2)}, u32[]{:S(2)}) collective-permute-start(f32[4,512,256]{2,1,0:T(8,128)S(1)} %constant_dynamic-slice_fusion.15), channel_id=1, source_target_pairs={{0,3},{1,0},{2,1},{3,2},{4,7},{5,4},{6,5},{7,6},{8,11},{9,8},{10,9... | collective-permute-start | bytes 6291464 | tf_op jit(solution)/shard_map/ppermute | solution.py:299
  591.4 26.8 %collective-permute-start.20 = (f32[8,64,256]{2,1,0:T(8,128)S(1)}, f32[8,64,256]{2,1,0:T(8,128)S(1)}, u32[]{:S(2)}, u32[]{:S(2)}) collective-permute-start(f32[8,64,256]{2,1,0:T(8,128)S(1)} %pack_z.57), channel_id=1, source_target_pairs={{0,24},{4,28},{8,0},{12,4},{16,8},{20,12},{24,16},{28,20},{1,25},{... | collective-permute-start | bytes 1572872 | tf_op jit(solution)/shard_map/ppermute | solution.py:299
  603.0 25.0 %collective-permute-start.31 = (f32[8,64,256]{2,1,0:T(8,128)S(1)}, f32[8,64,256]{2,1,0:T(8,128)S(1)}, u32[]{:S(2)}, u32[]{:S(2)}) collective-permute-start(f32[8,64,256]{2,1,0:T(8,128)S(1)} %pack_z.70), channel_id=1, source_target_pairs={{0,12},{4,8},{8,20},{12,16},{16,28},{20,24},{24,4},{28,0},{1,13},{... | collective-permute-start | bytes 1572872 | tf_op jit(solution)/shard_map/ppermute | solution.py:299
  619.4 79.8 %collective-permute-start.25 = (f32[8,64,256]{2,1,0:T(8,128)S(1)}, f32[8,64,256]{2,1,0:T(8,128)S(1)}, u32[]{:S(2)}, u32[]{:S(2)}) collective-permute-start(f32[8,64,256]{2,1,0:T(8,128)S(1)} %pack_z.60), channel_id=1, source_target_pairs={{0,16},{4,20},{8,24},{12,28},{16,0},{20,4},{24,8},{28,12},{1,17},{... | collective-permute-start | bytes 1572872 | tf_op jit(solution)/shard_map/ppermute | solution.py:299
  629.1 68.9 %collective-permute-start.34 = (f32[8,64,256]{2,1,0:T(8,128)S(1)}, f32[8,64,256]{2,1,0:T(8,128)S(1)}, u32[]{:S(2)}, u32[]{:S(2)}) collective-permute-start(f32[8,64,256]{2,1,0:T(8,128)S(1)} %pack_z.72), channel_id=1, source_target_pairs={{0,28},{4,24},{8,4},{12,0},{16,12},{20,8},{24,20},{28,16},{1,29},{... | collective-permute-start | bytes 1572872 | tf_op jit(solution)/shard_map/ppermute | solution.py:299
  633.8 60.6 %collective-permute-start.30 = (f32[8,64,256]{2,1,0:T(8,128)S(1)}, f32[8,64,256]{2,1,0:T(8,128)S(1)}, u32[]{:S(2)}, u32[]{:S(2)}) collective-permute-start(f32[8,64,256]{2,1,0:T(8,128)S(1)} %pack_z.66), channel_id=1, source_target_pairs={{0,20},{4,16},{8,28},{12,24},{16,4},{20,0},{24,12},{28,8},{1,21},{... | collective-permute-start | bytes 1572872 | tf_op jit(solution)/shard_map/ppermute | solution.py:299
  636.9 67.6 %collective-permute-start.32 = (f32[4,512,256]{2,1,0:T(8,128)}, f32[4,512,256]{2,1,0:T(8,128)}, u32[]{:S(2)}, u32[]{:S(2)}) collective-permute-start(f32[4,512,256]{2,1,0:T(8,128)} %constant_dynamic-slice_fusion.16), channel_id=1, source_target_pairs={{0,2},{1,3},{2,0},{3,1},{4,6},{5,7},{6,4},{7,5},{8,10},{9,11},{10,... | collective-permute-start | bytes 6291464 | tf_op jit(solution)/shard_map/ppermute | solution.py:299
  638.2 56.3 %collective-permute-start.37 = (f32[8,64,256]{2,1,0:T(8,128)S(1)}, f32[8,64,256]{2,1,0:T(8,128)S(1)}, u32[]{:S(2)}, u32[]{:S(2)}) collective-permute-start(f32[8,64,256]{2,1,0:T(8,128)S(1)} %pack_z.73), channel_id=1, source_target_pairs={{0,8},{4,12},{8,16},{12,20},{16,24},{20,28},{24,0},{28,4},{1,9},{5... | collective-permute-start | bytes 1572872 | tf_op jit(solution)/shard_map/ppermute | solution.py:299
  694.5 47.2 %collective-permute-start.38 = (f32[4,512,256]{2,1,0:T(8,128)}, f32[4,512,256]{2,1,0:T(8,128)}, u32[]{:S(2)}, u32[]{:S(2)}) collective-permute-start(f32[4,512,256]{2,1,0:T(8,128)} %constant_dynamic-slice_fusion.14), channel_id=1, source_target_pairs={{0,1},{1,2},{2,3},{3,0},{4,5},{5,6},{6,7},{7,4},{8,9},{9,10},{10,1... | collective-permute-start | bytes 6291464 | tf_op jit(solution)/shard_map/ppermute | solution.py:299
  694.5 47.2 %collective-permute-start.41 = (f32[4,512,256]{2,1,0:T(8,128)}, f32[4,512,256]{2,1,0:T(8,128)S(1)}, u32[]{:S(2)}, u32[]{:S(2)}) collective-permute-start(f32[4,512,256]{2,1,0:T(8,128)} %constant_dynamic-slice_fusion.13), channel_id=1, source_target_pairs={{0,3},{1,0},{2,1},{3,2},{4,7},{5,4},{6,5},{7,6},{8,11},{9,8},{10,9... | collective-permute-start | bytes 6291464 | tf_op jit(solution)/shard_map/ppermute | solution.py:299
  699.2 71.5 %collective-permute-start.40 = (f32[8,64,256]{2,1,0:T(8,128)S(1)}, f32[8,64,256]{2,1,0:T(8,128)}, u32[]{:S(2)}, u32[]{:S(2)}) collective-permute-start(f32[8,64,256]{2,1,0:T(8,128)S(1)} %pack_z.75), channel_id=1, source_target_pairs={{0,4},{4,0},{8,12},{12,8},{16,20},{20,16},{24,28},{28,24},{1,5},{5... | collective-permute-start | bytes 1572872 | tf_op jit(solution)/shard_map/ppermute | solution.py:299
  704.5 37.2 %collective-permute-start.33 = (f32[8,64,256]{2,1,0:T(8,128)S(1)}, f32[8,64,256]{2,1,0:T(8,128)S(1)}, u32[]{:S(2)}, u32[]{:S(2)}) collective-permute-start(f32[8,64,256]{2,1,0:T(8,128)S(1)} %pack_z.68), channel_id=1, source_target_pairs={{0,12},{4,8},{8,20},{12,16},{16,28},{20,24},{24,4},{28,0},{1,13},{... | collective-permute-start | bytes 1572872 | tf_op jit(solution)/shard_map/ppermute | solution.py:299
  705.8 38.0 %collective-permute-start.35 = (f32[8,64,256]{2,1,0:T(8,128)S(1)}, f32[8,64,256]{2,1,0:T(8,128)}, u32[]{:S(2)}, u32[]{:S(2)}) collective-permute-start(f32[8,64,256]{2,1,0:T(8,128)S(1)} %pack_z.71), channel_id=1, source_target_pairs={{0,24},{4,28},{8,0},{12,4},{16,8},{20,12},{24,16},{28,20},{1,25},{... | collective-permute-start | bytes 1572872 | tf_op jit(solution)/shard_map/ppermute | solution.py:299
  741.7 28.0 %collective-permute-start.39 = (f32[8,64,256]{2,1,0:T(8,128)S(1)}, f32[8,64,256]{2,1,0:T(8,128)}, u32[]{:S(2)}, u32[]{:S(2)}) collective-permute-start(f32[8,64,256]{2,1,0:T(8,128)S(1)} %pack_z.74), channel_id=1, source_target_pairs={{0,20},{4,16},{8,28},{12,24},{16,4},{20,0},{24,12},{28,8},{1,21},{... | collective-permute-start | bytes 1572872 | tf_op jit(solution)/shard_map/ppermute | solution.py:299
  741.7 30.1 %collective-permute-start.42 = (f32[8,64,256]{2,1,0:T(8,128)S(1)}, f32[8,64,256]{2,1,0:T(8,128)}, u32[]{:S(2)}, u32[]{:S(2)}) collective-permute-start(f32[8,64,256]{2,1,0:T(8,128)S(1)} %pack_z.76), channel_id=1, source_target_pairs={{0,8},{4,12},{8,16},{12,20},{16,24},{20,28},{24,0},{28,4},{1,9},{5... | collective-permute-start | bytes 1572872 | tf_op jit(solution)/shard_map/ppermute | solution.py:299
  743.8 33.2 %collective-permute-start.43 = (f32[8,64,256]{2,1,0:T(8,128)S(1)}, f32[8,64,256]{2,1,0:T(8,128)S(1)}, u32[]{:S(2)}, u32[]{:S(2)}) collective-permute-start(f32[8,64,256]{2,1,0:T(8,128)S(1)} %pack_z.77), channel_id=1, source_target_pairs={{0,28},{4,24},{8,4},{12,0},{16,12},{20,8},{24,20},{28,16},{1,29},{... | collective-permute-start | bytes 1572872 | tf_op jit(solution)/shard_map/ppermute | solution.py:299
  747.7 79.9 %collective-permute-start.64 = (f32[2,512,256]{2,1,0:T(8,128)S(1)}, f32[2,512,256]{2,1,0:T(8,128)S(1)}, u32[]{:S(2)}, u32[]{:S(2)}) collective-permute-start(f32[2,512,256]{2,1,0:T(8,128)S(1)} %constant_dynamic-slice_fusion.11), channel_id=1, source_target_pairs={{0,2},{1,3},{2,0},{3,1},{4,6},{5,7},{6,4},{7,5},{8,10},{9,11},{10,... | collective-permute-start | bytes 3145736 | tf_op jit(solution)/shard_map/ppermute | solution.py:299
  780.4 8.9 collective-permute-start.46
  782.6 8.6 collective-permute-start.45
  782.6 12.1 %collective-permute-start.44 = (f32[128,512]{1,0:T(8,128)S(1)}, f32[128,512]{1,0:T(8,128)S(1)}, u32[]{:S(2)}, u32[]{:S(2)}) collective-permute-start(f32[128,512]{1,0:T(8,128)S(1)} %get-tuple-element.191), channel_id=1, source_target_pairs={{0,2},{1,3},{2,0},{3,1},{4,6},{5,7},{6,4},{7,5},{8,10},{9,11},{10,... | collective-permute-start | bytes 786440 | tf_op jit(solution)/shard_map/ppermute | solution.py:385
  797.0 8.0 collective-permute-start.51
  821.9 70.4 %collective-permute-start.65 = (f32[2,512,256]{2,1,0:T(8,128)S(1)}, f32[2,512,256]{2,1,0:T(8,128)S(1)}, u32[]{:S(2)}, u32[]{:S(2)}) collective-permute-start(f32[2,512,256]{2,1,0:T(8,128)S(1)} %constant_dynamic-slice_fusion.10), channel_id=1, source_target_pairs={{0,1},{1,2},{2,3},{3,0},{4,5},{5,6},{6,7},{7,4},{8,9},{9,10},{10,1... | collective-permute-start | bytes 3145736 | tf_op jit(solution)/shard_map/ppermute | solution.py:299
  824.0 9.3 collective-permute-start.61
  825.9 30.0 %collective-permute-start.62 = (f32[128,512]{1,0:T(8,128)S(1)}, f32[128,512]{1,0:T(8,128)S(1)}, u32[]{:S(2)}, u32[]{:S(2)}) collective-permute-start(f32[128,512]{1,0:T(8,128)S(1)} %bitcast.356), channel_id=1, source_target_pairs={{0,1},{1,2},{2,3},{3,0},{4,5},{5,6},{6,7},{7,4},{8,9},{9,10},{10,1... | collective-permute-start | bytes 786440 | tf_op jit(solution)/shard_map/ppermute | solution.py:395
  825.9 30.0 %collective-permute-start.63 = (f32[128,512]{1,0:T(8,128)S(1)}, f32[128,512]{1,0:T(8,128)S(1)}, u32[]{:S(2)}, u32[]{:S(2)}) collective-permute-start(f32[128,512]{1,0:T(8,128)S(1)} %bitcast.357), channel_id=1, source_target_pairs={{0,3},{1,0},{2,1},{3,2},{4,7},{5,4},{6,5},{7,6},{8,11},{9,8},{10,9... | collective-permute-start | bytes 786440 | tf_op jit(solution)/shard_map/ppermute | solution.py:395
  827.6 67.8 %collective-permute-start.67 = (f32[2,512,256]{2,1,0:T(8,128)S(1)}, f32[2,512,256]{2,1,0:T(8,128)S(1)}, u32[]{:S(2)}, u32[]{:S(2)}) collective-permute-start(f32[2,512,256]{2,1,0:T(8,128)S(1)} %constant_dynamic-slice_fusion.8), channel_id=1, source_target_pairs={{0,2},{1,3},{2,0},{3,1},{4,6},{5,7},{6,4},{7,5},{8,10},{9,11},{10,... | collective-permute-start | bytes 3145736 | tf_op jit(solution)/shard_map/ppermute | solution.py:299
  856.1 38.3 %collective-permute-start.66 = (f32[2,512,256]{2,1,0:T(8,128)S(1)}, f32[2,512,256]{2,1,0:T(8,128)S(1)}, u32[]{:S(2)}, u32[]{:S(2)}) collective-permute-start(f32[2,512,256]{2,1,0:T(8,128)S(1)} %get-tuple-element.175), channel_id=1, source_target_pairs={{0,3},{1,0},{2,1},{3,2},{4,7},{5,4},{6,5},{7,6},{8,11},{9,8},{10,9... | collective-permute-start | bytes 3145736 | tf_op jit(solution)/shard_map/ppermute | solution.py:299
  856.2 44.6 %collective-permute-start.68 = (f32[2,512,256]{2,1,0:T(8,128)S(1)}, f32[2,512,256]{2,1,0:T(8,128)S(1)}, u32[]{:S(2)}, u32[]{:S(2)}) collective-permute-start(f32[2,512,256]{2,1,0:T(8,128)S(1)} %constant_dynamic-slice_fusion.7), channel_id=1, source_target_pairs={{0,1},{1,2},{2,3},{3,0},{4,5},{5,6},{6,7},{7,4},{8,9},{9,10},{10,1... | collective-permute-start | bytes 3145736 | tf_op jit(solution)/shard_map/ppermute | solution.py:299
  856.7 45.8 %collective-permute-start.69 = (f32[2,512,256]{2,1,0:T(8,128)S(1)}, f32[2,512,256]{2,1,0:T(8,128)S(1)}, u32[]{:S(2)}, u32[]{:S(2)}) collective-permute-start(f32[2,512,256]{2,1,0:T(8,128)S(1)} %get-tuple-element.183), channel_id=1, source_target_pairs={{0,3},{1,0},{2,1},{3,2},{4,7},{5,4},{6,5},{7,6},{8,11},{9,8},{10,9... | collective-permute-start | bytes 3145736 | tf_op jit(solution)/shard_map/ppermute | solution.py:299
  935.3 25.6 %collective-permute-start.71 = (f32[256,1024]{1,0:T(8,128)S(1)}, f32[256,1024]{1,0:T(8,128)}, u32[]{:S(2)}, u32[]{:S(2)}) collective-permute-start(f32[256,1024]{1,0:T(8,128)S(1)} %dynamic-slice_bitcast_fusion.1), channel_id=1, source_target_pairs={{0,2},{1,3},{2,0},{3,1},{4,6},{5,7},{6,4},{7,5},{8,10},{9,11},{10,... | collective-permute-start | bytes 3145736 | tf_op jit(solution)/shard_map/ppermute | solution.py:417
  962.4 8.3 collective-permute-start.78
  963.0 8.2 collective-permute-start.77
  966.0 16.6 %collective-permute-start.75 = (f32[256,128]{1,0:T(8,128)S(1)}, f32[256,128]{1,0:T(8,128)S(1)}, u32[]{:S(2)}, u32[]{:S(2)}) collective-permute-start(f32[256,128]{1,0:T(8,128)S(1)} %get-tuple-element.188), channel_id=1, source_target_pairs={{0,20},{4,16},{8,28},{12,24},{16,4},{20,0},{24,12},{28,8},{1,21},{... | collective-permute-start | bytes 393224 | tf_op jit(solution)/shard_map/ppermute | solution.py:425
  966.5 16.2 %collective-permute-start.74 = (f32[256,128]{1,0:T(8,128)S(1)}, f32[256,128]{1,0:T(8,128)S(1)}, u32[]{:S(2)}, u32[]{:S(2)}) collective-permute-start(f32[256,128]{1,0:T(8,128)S(1)} %get-tuple-element.189), channel_id=1, source_target_pairs={{0,24},{4,28},{8,0},{12,4},{16,8},{20,12},{24,16},{28,20},{1,25},{... | collective-permute-start | bytes 393224 | tf_op jit(solution)/shard_map/ppermute | solution.py:425
  970.7 11.9 %collective-permute-start.73 = (f32[256,128]{1,0:T(8,128)S(1)}, f32[256,128]{1,0:T(8,128)S(1)}, u32[]{:S(2)}, u32[]{:S(2)}) collective-permute-start(f32[256,128]{1,0:T(8,128)S(1)} %get-tuple-element.190), channel_id=1, source_target_pairs={{0,12},{4,8},{8,20},{12,16},{16,28},{20,24},{24,4},{28,0},{1,13},{... | collective-permute-start | bytes 393224 | tf_op jit(solution)/shard_map/ppermute | solution.py:425
  971.2 15.9 %collective-permute-start.72 = (f32[256,128]{1,0:T(8,128)S(1)}, f32[256,128]{1,0:T(8,128)S(1)}, u32[]{:S(2)}, u32[]{:S(2)}) collective-permute-start(f32[256,128]{1,0:T(8,128)S(1)} %get-tuple-element.184), channel_id=1, source_target_pairs={{0,16},{4,20},{8,24},{12,28},{16,0},{20,4},{24,8},{28,12},{1,17},{... | collective-permute-start | bytes 393224 | tf_op jit(solution)/shard_map/ppermute | solution.py:425
  (39 other events, 270.8 us)

commit v9 on v8

--- a/solution.py
+++ b/solution.py
@@ -75,14 +75,18 @@
     )(slab, before)
 
 
-def core_body(steps, total, field_ref, basis_ref, out_ref, stacked_ref, high_ref, low_ref, main, cross):
+def core_body(steps, total, carried, field_ref, basis_ref, *refs):
+    before, refs = refs[: 2 * carried], refs[2 * carried :]
+    out_ref = refs[0] if total else None
+    stacked_ref, high_ref, low_ref = refs[1:4] if total else refs[2:5]
+    main, cross = refs[4:6] if total else refs[:2]
     step = pl.program_id(0)
     rank = basis_ref.shape[1]
 
     @pl.when(step == 0)
     def _():
-        main[...] = jnp.zeros_like(main)
-        cross[...] = jnp.zeros_like(cross)
+        main[...] = before[0][...] if carried else jnp.zeros_like(main)
+        cross[...] = before[1][...] if carried else jnp.zeros_like(cross)
         basis_high, basis_low = halves(basis_ref[...].T)
         stacked_ref[:rank] = basis_high
         stacked_ref[rank:] = basis_low
@@ -102,42 +106,47 @@
     main[...] += dot_tn(high, high)
     cross[...] += dot_tn(high, low_ref[...])
 
-    @pl.when(step == steps - 1)
-    def _():
-        mixed = cross[...]
-        out_ref[...] = (main[...] + mixed + mixed.T) / total
-
-
-def core_gram(cells, basis, total):
+    if total:
+
+        @pl.when(step == steps - 1)
+        def _():
+            mixed = cross[...]
+            out_ref[...] = (main[...] + mixed + mixed.T) / total
+
+
+def core_gram(cells, basis, before=(), total=None):
     depth, blocks, width_x, width = cells.shape
     rank = basis.shape[1]
     width_y = blocks * width
     block = 2 if depth % 2 == 0 else 1
     steps = depth // block
+    square = pl.BlockSpec((width_y, width_y), lambda i: (0, 0))
+    shape = jax.ShapeDtypeStruct((width_y, width_y), F32)
+    sums = [pltpu.VMEM((width_y, width_y), F32)] * 2
     return pl.pallas_call(
-        functools.partial(core_body, steps, total),
+        functools.partial(core_body, steps, total, bool(before)),
         grid=(steps,),
         in_specs=[
             pl.BlockSpec((block, blocks, width_x, width), lambda i: (i, 0, 0, 0)),
             pl.BlockSpec((width_x, rank), lambda i: (0, 0)),
-        ],
-        out_specs=pl.BlockSpec((width_y, width_y), lambda i: (0, 0)),
-        out_shape=jax.ShapeDtypeStruct((width_y, width_y), F32),
+        ]
+        + [square] * len(before),
+        out_specs=square if total else [square] * 2,
+        out_shape=shape if total else [shape] * 2,
         scratch_shapes=[
             pltpu.VMEM((2 * rank, width_x), BF16),
             pltpu.VMEM((block * rank, width_y), BF16),
             pltpu.VMEM((block * rank, width_y), BF16),
-            pltpu.VMEM((width_y, width_y), F32),
-            pltpu.VMEM((width_y, width_y), F32),
-        ],
-        compiler_params=pltpu.CompilerParams(vmem_limit_bytes=48 * MIB),
+        ]
+        + (sums if total else []),
+        compiler_params=pltpu.CompilerParams(vmem_limit_bytes=52 * MIB),
         cost_estimate=pl.CostEstimate(
             flops=6 * rank * cells.size + 4 * rank * depth * width_y * width_y,
             bytes_accessed=cells.size * 4,
             transcendentals=0,
         ),
         name="core_gram_y",
-    )(cells, basis)
+    )(cells, basis, *before)
 
 
 def full_dot(left, right, contract):
@@ -337,7 +346,6 @@
     shifts[4:4] = [(0, b) for b in range(1, rest)]
     turns = sorted(range(1, m), key=lambda d: abs(2 * d - m))
 
-    cells = jnp.zeros((slab // m, m, width_x, y_block), F32)
 
     def to_gx(first, zc, a, b, whole):
         place = (moved(g, a, b) * slab + first) // TALL
@@ -353,12 +361,19 @@
         got = order.send(cut, tie(whole, after), "yz", yz_perm(d))
         return lax.dynamic_update_slice(cells, got[:, None], (first // m, (q - d) % m, 0, 0))
 
+    def put_own(cells, first, whole):
+        zs = whole.shape[0] // m
+        own = lax.dynamic_slice_in_dim(whole, q * zs, zs, axis=0)
+        return lax.dynamic_update_slice(cells, own[:, None], (first // m, q, 0, 0))
+
     gram = jnp.zeros((width_x, width_x), F32)
     first, waiting = 0, []
     group = math.lcm(m, TALL)
-    for groups in chunk_depths(slab // group):
+    depths = chunk_depths(slab // group)
+    start_last = (sum(depths) - depths[-1]) * group
+    cells = jnp.zeros((start_last // m, m, width_x, y_block), F32)
+    for groups in depths:
         zc = groups * group
-        units = zc // m
         whole = jnp.zeros((zc, n, x_block, y_block), F32)
         for k, (a, b) in enumerate(shifts):
             whole = to_gx(first, zc, a, b, whole)
@@ -369,10 +384,10 @@
         whole = lax.dynamic_update_slice_in_dim(whole, own, g, axis=1)
         before = whole.reshape(zc, width_x, y_block)
         gram = gram_of(before, gram)
-        own = lax.dynamic_slice_in_dim(before, q * units, units, axis=0)
-        cells = lax.dynamic_update_slice(cells, own[:, None], (first // m, q, 0, 0))
-        waiting += [(first, d, before) for d in turns]
-        first += zc
+        if first < start_last:
+            cells = put_own(cells, first, before)
+            waiting += [(first, d, before) for d in turns]
+            first += zc
 
     rows = width_x // m
     slabs = gram.reshape(m, rows, width_x)
@@ -383,8 +398,8 @@
     summed = pick(slabs, q)
     for d in turns:
         summed = summed + lax.ppermute(pick(slabs, (q + d) % m), "yz", yz_perm(d))
-    while len(waiting) >= len(turns):
-        cells = to_yz(cells, *waiting.pop(0), [summed])
+    for entry in waiting:
+        cells = to_yz(cells, *entry)
     strips = summed.reshape(n, rows // n, width_x)
     summed = pick(strips, g)
     for a, b in shifts:
@@ -394,11 +409,15 @@
     summed = stack(pieces, places).reshape(rows, width_x)
     pieces = [summed] + [lax.ppermute(summed, "yz", yz_perm(d)) for d in turns]
     places = jnp.stack([q] + [(q - d) % m for d in turns]).astype(jnp.int32)
-    for entry in waiting:
-        cells = to_yz(cells, *entry, pieces[1:])
+    ready = pieces[1:]
     basis = iterate(pieces, places, start, float(width_y * depth))
 
-    partial_y = core_gram(cells, basis, float(rank * depth))
+    sums = core_gram(cells, basis) if start_last else ()
+    cells = jnp.zeros((before.shape[0] // m, m, width_x, y_block), F32)
+    cells = put_own(cells, 0, before)
+    for d in turns:
+        cells = to_yz(cells, 0, d, before, ready)
+    partial_y = core_gram(cells, basis, sums, float(rank * depth))
     cores = 2 if m % 2 == 0 else 1
     chips = m // cores
     core, chip = q % cores, q // cores

time: 999 us -> 1010 us (1.011)
  starting transfers between devices: 275 us -> 233 us
  waiting for transfers between devices: 430 us -> 459 us
  local copies, waits for them, and re-layouts: 130 us -> 144 us
    ppermute x50, starting transfers between devices: 238 us -> 184 us  [send(): got = lax.ppermute(tie(value, self.done(0)), axis, perm)]
    ppermute x50, waiting for transfers between devices: 346 us -> 380 us  [send(): got = lax.ppermute(tie(value, self.done(0)), axis, perm)]
    pallas_call x1 -> x2, Pallas kernels: 21.9 us -> 31 us  [core_gram(): pl.pallas_call(functools.partial(core_body, steps, total, bool(before)),...]
    dynamic_slice x14 -> x15, local copies, waits for them, and re-layouts: 17.2 us -> 23.7 us  [cut(): return lax.dynamic_slice_in_dim(source, (q + d) % m * zs, zs, axis=0)]
  transfers between devices with their start and end apart: 79 -> 79, of which waited for: 31 -> 31; matrix products, arithmetic and copies ran while one was open for 12% -> 13% of each run, Pallas kernels for 12% -> 14%
where the time goes in v9:
time: 1010 us; the launch traced here: 997 us
  waiting for transfers between devices  459 us (45%)
  starting transfers between devices  233 us (23%)
  Pallas kernels  153 us (15%)
  local copies, waits for them, and re-layouts  144 us (14%)
    ppermute x50, waiting for transfers between devices, send(): got = lax.ppermute(tie(value, self.done(0)), axis, perm)  380 us
    ppermute x50, starting transfers between devices, send(): got = lax.ppermute(tie(value, self.done(0)), axis, perm)  184 us
    pallas_call x40, Pallas kernels, pack(): pl.pallas_call(pack_body, grid_spec=pltpu.PrefetchScalarGridSpec(num_scal...  62.2 us
    dynamic_update_slice x35, local copies, waits for them, and re-layouts, to_gx(): lax.dynamic_update_slice_in_dim(whole, got[:, None], moved(g, a, b, -1),...  41.4 us
    pallas_call x1, Pallas kernels, iterate(): pl.pallas_call(functools.partial(iterate_body, total), in_specs=[pl.Block...  34 us
    dynamic_update_slice x15, local copies, waits for them, and re-layouts, to_yz(): lax.dynamic_update_slice(cells, got[:, None], (first // m, (q - d) % m, 0...  33.6 us
    pallas_call x2, Pallas kernels, core_gram(): pl.pallas_call(functools.partial(core_body, steps, total, bool(before)),...  31 us
    ppermute x3, waiting for transfers between devices, on_device(): pieces = [summed] + [lax.ppermute(summed, 'yz', yz_perm(d)) for d in turns]  28.8 us
  transfers between devices with their start and end apart: 79, of which 31 were waited for; matrix products, arithmetic and copies ran while one was open for 13% of the time, Pallas kernels for 14%

profile of v9, /device:TPU:0, one launch (start us, length us, event | category | flops | bytes accessed | tf_op | source)
XLA Modules:
  0.0 996.7 jit_solution(12116922519879039735)
XLA Ops:
  2.9 4.0 collective-permute-start
  9.2 2.5 collective-permute-start.3
  35.0 42.1 %collective-permute-done = f32[16,64,256]{2,1,0:T(8,128)} collective-permute-done((f32[16,64,256]{2,1,0:T(8,128)}, f32[16,64,256]{2,1,0:T(8,128)}, u32[]{:S(2)}, u32[]{:S(2)}) %collective-permute-start) | collective-permute-done | bytes 1048608 | tf_op jit(solution)/shard_map/ppermute | solution.py:308
  77.1 6.6 collective-permute-start.10
  85.1 82.4 %collective-permute-done.4 = f32[16,64,256]{2,1,0:T(8,128)} collective-permute-done((f32[16,64,256]{2,1,0:T(8,128)}, f32[16,64,256]{2,1,0:T(8,128)}, u32[]{:S(2)}, u32[]{:S(2)}) %collective-permute-start.4) | collective-permute-done | bytes 1048608 | tf_op jit(solution)/shard_map/ppermute | solution.py:308
  168.9 3.0 collective-permute-start.2
  188.8 7.7 collective-permute-done.5
  196.5 62.3 %collective-permute-start.9 = (f32[16,64,256]{2,1,0:T(8,128)}, f32[16,64,256]{2,1,0:T(8,128)}, u32[]{:S(2)}, u32[]{:S(2)}) collective-permute-start(f32[16,64,256]{2,1,0:T(8,128)} %pack_z.48), channel_id=1, source_target_pairs={{0,20},{4,16},{8,28},{12,24},{16,4},{20,0},{24,12},{28,8},{1,21},{... | collective-permute-start | bytes 3145736 | tf_op jit(solution)/shard_map/ppermute | solution.py:308
  265.4 42.6 %collective-permute-start.13 = (f32[16,64,256]{2,1,0:T(8,128)S(1)}, f32[16,64,256]{2,1,0:T(8,128)}, u32[]{:S(2)}, u32[]{:S(2)}) collective-permute-start(f32[16,64,256]{2,1,0:T(8,128)S(1)} %pack_z.53), channel_id=1, source_target_pairs={{0,28},{4,24},{8,4},{12,0},{16,12},{20,8},{24,20},{28,16},{1,29},{... | collective-permute-start | bytes 3145736 | tf_op jit(solution)/shard_map/ppermute | solution.py:308
  308.7 5.7 gram_x.5.before_ref
  315.5 4.4 broadcast.69.clone
  325.9 13.3 %broadcast_in_dim.235 = f32[14,4,512,256]{3,2,1,0:T(8,128)} broadcast(f32[]{:T(128)} %constant.1232.clone.1), dimensions={} | broadcast | bytes 29360132 | tf_op jit(solution)/shard_map/broadcast_in_dim | solution.py:374
  339.2 3.1 bitcast_dynamic-update-slice_fusion.11
  347.7 29.9 %collective-permute-done.11 = f32[16,64,256]{2,1,0:T(8,128)} collective-permute-done((f32[16,64,256]{2,1,0:T(8,128)}, f32[16,64,256]{2,1,0:T(8,128)}, u32[]{:S(2)}, u32[]{:S(2)}) %collective-permute-start.11) | collective-permute-done | bytes 1048608 | tf_op jit(solution)/shard_map/ppermute | solution.py:308
  377.7 3.0 constant_dynamic-slice_fusion.18
  397.0 43.3 %collective-permute-done.21 = f32[16,64,256]{2,1,0:T(8,128)S(1)} collective-permute-done((f32[16,64,256]{2,1,0:T(8,128)S(1)}, f32[16,64,256]{2,1,0:T(8,128)S(1)}, u32[]{:S(2)}, u32[]{:S(2)}) %collective-permute-start.21) | collective-permute-done | bytes 1048608 | tf_op jit(solution)/shard_map/ppermute | solution.py:308
  442.5 7.7 gram_x.6.before_ref
  454.0 3.1 bitcast_dynamic-update-slice_fusion.5
  457.5 3.0 constant_dynamic-slice_fusion.20
  462.0 6.7 collective-permute-done.18
  472.2 2.7 collective-permute-start.19
  478.3 3.1 bitcast_dynamic-update-slice_fusion.4
  481.3 3.0 constant_dynamic-slice_fusion.17
  484.3 3.0 constant_dynamic-slice_fusion.15
  487.4 3.0 bitcast_dynamic-update-slice_fusion.10
  490.4 3.1 bitcast_dynamic-update-slice_fusion.9
  493.6 62.4 %collective-permute-done.23 = f32[8,64,256]{2,1,0:T(8,128)S(1)} collective-permute-done((f32[8,64,256]{2,1,0:T(8,128)S(1)}, f32[8,64,256]{2,1,0:T(8,128)S(1)}, u32[]{:S(2)}, u32[]{:S(2)}) %collective-permute-start.23) | collective-permute-done | bytes 524320 | tf_op jit(solution)/shard_map/ppermute | solution.py:308
  571.4 29.2 %collective-permute-start.31 = (f32[8,64,256]{2,1,0:T(8,128)S(1)}, f32[8,64,256]{2,1,0:T(8,128)}, u32[]{:S(2)}, u32[]{:S(2)}) collective-permute-start(f32[8,64,256]{2,1,0:T(8,128)S(1)} %pack_z.70), channel_id=1, source_target_pairs={{0,12},{4,8},{8,20},{12,16},{16,28},{20,24},{24,4},{28,0},{1,13},{... | collective-permute-start | bytes 1572872 | tf_op jit(solution)/shard_map/ppermute | solution.py:308
  603.1 5.7 gram_x.7.before_ref
  611.5 3.1 bitcast_dynamic-update-slice_fusion.3
  615.8 7.9 collective-permute-done.20
  623.7 4.4 collective-permute-start.34
  631.6 3.8 collective-permute-start.30
  638.4 3.0 bitcast_dynamic-update-slice_fusion.2
  644.3 45.1 %collective-permute-done.30 = f32[8,64,256]{2,1,0:T(8,128)S(1)} collective-permute-done((f32[8,64,256]{2,1,0:T(8,128)S(1)}, f32[8,64,256]{2,1,0:T(8,128)S(1)}, u32[]{:S(2)}, u32[]{:S(2)}) %collective-permute-start.30) | collective-permute-done | bytes 524320 | tf_op jit(solution)/shard_map/ppermute | solution.py:308
  689.4 3.3 bitcast_dynamic-update-slice_fusion.7
  703.7 2.9 collective-permute-start.33
  706.5 3.2 gram_x.8.before_ref
  710.9 3.1 bitcast_dynamic-update-slice_fusion.1
  714.0 15.8 %collective-permute-done.38 = f32[4,512,256]{2,1,0:T(8,128)} collective-permute-done((f32[4,512,256]{2,1,0:T(8,128)}, f32[4,512,256]{2,1,0:T(8,128)}, u32[]{:S(2)}, u32[]{:S(2)}) %collective-permute-start.38) | collective-permute-done | bytes 2097184 | tf_op jit(solution)/shard_map/ppermute | solution.py:308
  734.7 6.1 collective-permute-done.41
  741.1 12.5 %collective-permute-done.39 = f32[8,64,256]{2,1,0:T(8,128)} collective-permute-done((f32[8,64,256]{2,1,0:T(8,128)S(1)}, f32[8,64,256]{2,1,0:T(8,128)}, u32[]{:S(2)}, u32[]{:S(2)}) %collective-permute-start.39) | collective-permute-done | bytes 524320 | tf_op jit(solution)/shard_map/ppermute | solution.py:308
  754.7 12.3 %collective-permute-done.42 = f32[8,64,256]{2,1,0:T(8,128)S(1)} collective-permute-done((f32[8,64,256]{2,1,0:T(8,128)S(1)}, f32[8,64,256]{2,1,0:T(8,128)S(1)}, u32[]{:S(2)}, u32[]{:S(2)}) %collective-permute-start.42) | collective-permute-done | bytes 524320 | tf_op jit(solution)/shard_map/ppermute | solution.py:308
  767.1 3.2 collective-permute-done.43
  770.3 3.1 gram_x.9
  776.3 3.1 bitcast_dynamic-update-slice_fusion
  784.2 7.6 collective-permute-start.47
  793.9 4.4 collective-permute-start.49
  802.0 3.3 collective-permute-start.53
  806.9 2.4 collective-permute-start.54
  809.3 3.2 collective-permute-start.55
  816.5 3.3 collective-permute-start.60
  827.2 22.2 %collective-permute-done.61.refs_1_ = f32[128,512]{1,0:T(8,128)S(1)} collective-permute-done((f32[128,512]{1,0:T(8,128)S(1)}, f32[128,512]{1,0:T(8,128)S(1)}, u32[]{:S(2)}, u32[]{:S(2)}) %collective-permute-start.61) | collective-permute-done | bytes 262176 | tf_op jit(solution)/shard_map/ppermute | solution.py:410
  849.5 6.6 collective-permute-done.62.refs_2_
  861.3 34.0 %subspace.1.basis_ref = f32[512,128]{1,0:T(8,128)} custom-call(s32[4]{0:T(128)S(1)} %pad_add_fusion.places_ref, f32[128,512]{1,0:T(8,128)S(1)} %bitcast.354, f32[128,512]{1,0:T(8,128)S(1)} %collective-permute-done.61.refs_1_, f32[128,512]{1,0:T(8,128)S(1)} %collective-permute-done.62.refs_2_, f32[128,512]{1,0:T(8,128)S(1)} %collective-permute-done.63.refs_3_, ...), custom_call_target="tpu_custom_call" | custom-call | flops 40000000000 | bytes 524288 | tf_op jit(solution)/shard_map/subspace/pallas_call | solution.py:237
  898.4 21.1 %core_gram_y.2 = (f32[1024,1024]{1,0:T(8,128)}, f32[1024,1024]{1,0:T(8,128)}) custom-call(f32[14,4,512,256]{3,2,1,0:T(8,128)} %bitcast_dynamic-update-slice_fusion.40.field_ref, f32[512,128]{1,0:T(8,128)S(1)} %copy-done.7), custom_call_target="tpu_custom_call" | custom-call | flops 13153337344 | bytes 29360128 | tf_op jit(solution)/shard_map/core_gram_y/pallas_call | solution.py:126
  924.3 9.9 core_gram_y.3
  937.1 3.9 collective-permute-done.70
  941.0 2.6 bitcast_add_fusion
  944.3 25.0 %collective-permute-done.71 = f32[256,1024]{1,0:T(8,128)} collective-permute-done((f32[256,1024]{1,0:T(8,128)S(1)}, f32[256,1024]{1,0:T(8,128)}, u32[]{:S(2)}, u32[]{:S(2)}) %collective-permute-start.71) | collective-permute-done | bytes 1048608 | tf_op jit(solution)/shard_map/ppermute | solution.py:436
  978.1 4.7 collective-permute-done.72
  982.8 4.5 collective-permute-start.78
  987.3 5.8 collective-permute-done.75
  993.1 2.7 collective-permute-done.78
  (278 shorter events, 199.2 us)
Async XLA Ops:
  2.9 74.1 %collective-permute-start = (f32[16,64,256]{2,1,0:T(8,128)}, f32[16,64,256]{2,1,0:T(8,128)}, u32[]{:S(2)}, u32[]{:S(2)}) collective-permute-start(f32[16,64,256]{2,1,0:T(8,128)} %pack_z.40), channel_id=1, source_target_pairs={{0,16},{4,20},{8,24},{12,28},{16,0},{20,4},{24,8},{28,12},{1,17},{... | collective-permute-start | bytes 3145736 | tf_op jit(solution)/shard_map/ppermute | solution.py:308
  9.2 67.9 %collective-permute-start.3 = (f32[16,64,256]{2,1,0:T(8,128)}, f32[16,64,256]{2,1,0:T(8,128)}, u32[]{:S(2)}, u32[]{:S(2)}) collective-permute-start(f32[16,64,256]{2,1,0:T(8,128)} %pack_z.43), channel_id=1, source_target_pairs={{0,12},{4,8},{8,20},{12,16},{16,28},{20,24},{24,4},{28,0},{1,13},{... | collective-permute-start | bytes 3145736 | tf_op jit(solution)/shard_map/ppermute | solution.py:308
  13.9 155.1 %collective-permute-start.1 = (f32[16,64,256]{2,1,0:T(8,128)}, f32[16,64,256]{2,1,0:T(8,128)}, u32[]{:S(2)}, u32[]{:S(2)}) collective-permute-start(f32[16,64,256]{2,1,0:T(8,128)} %pack_z.42), channel_id=1, source_target_pairs={{0,24},{4,28},{8,0},{12,4},{16,8},{20,12},{24,16},{28,20},{1,25},{... | collective-permute-start | bytes 3145736 | tf_op jit(solution)/shard_map/ppermute | solution.py:308
  18.3 149.2 %collective-permute-start.4 = (f32[16,64,256]{2,1,0:T(8,128)}, f32[16,64,256]{2,1,0:T(8,128)}, u32[]{:S(2)}, u32[]{:S(2)}) collective-permute-start(f32[16,64,256]{2,1,0:T(8,128)} %pack_z.45), channel_id=1, source_target_pairs={{0,20},{4,16},{8,28},{12,24},{16,4},{20,0},{24,12},{28,8},{1,21},{... | collective-permute-start | bytes 3145736 | tf_op jit(solution)/shard_map/ppermute | solution.py:308
  20.6 152.7 %collective-permute-start.6 = (f32[16,64,256]{2,1,0:T(8,128)}, f32[16,64,256]{2,1,0:T(8,128)}, u32[]{:S(2)}, u32[]{:S(2)}) collective-permute-start(f32[16,64,256]{2,1,0:T(8,128)} %pack_z.47), channel_id=1, source_target_pairs={{0,4},{4,0},{8,12},{12,8},{16,20},{20,16},{24,28},{28,24},{1,5},{5... | collective-permute-start | bytes 3145736 | tf_op jit(solution)/shard_map/ppermute | solution.py:308
  77.1 108.9 %collective-permute-start.8 = (f32[16,64,256]{2,1,0:T(8,128)}, f32[16,64,256]{2,1,0:T(8,128)}, u32[]{:S(2)}, u32[]{:S(2)}) collective-permute-start(f32[16,64,256]{2,1,0:T(8,128)} %copy-done.5), channel_id=1, source_target_pairs={{0,8},{4,12},{8,16},{12,20},{16,24},{20,28},{24,0},{28,4},{1,9},{5... | collective-permute-start | bytes 3145736 | tf_op jit(solution)/shard_map/ppermute | solution.py:308
  77.1 110.3 %collective-permute-start.10 = (f32[16,64,256]{2,1,0:T(8,128)}, f32[16,64,256]{2,1,0:T(8,128)}, u32[]{:S(2)}, u32[]{:S(2)}) collective-permute-start(f32[16,64,256]{2,1,0:T(8,128)} %copy-done.6), channel_id=1, source_target_pairs={{0,28},{4,24},{8,4},{12,0},{16,12},{20,8},{24,20},{28,16},{1,29},{... | collective-permute-start | bytes 3145736 | tf_op jit(solution)/shard_map/ppermute | solution.py:308
  167.5 29.0 %collective-permute-start.5 = (f32[16,64,256]{2,1,0:T(8,128)S(1)}, f32[16,64,256]{2,1,0:T(8,128)}, u32[]{:S(2)}, u32[]{:S(2)}) collective-permute-start(f32[16,64,256]{2,1,0:T(8,128)S(1)} %pack_z.44), channel_id=1, source_target_pairs={{0,12},{4,8},{8,20},{12,16},{16,28},{20,24},{24,4},{28,0},{1,13},{... | collective-permute-start | bytes 3145736 | tf_op jit(solution)/shard_map/ppermute | solution.py:308
  168.9 93.6 %collective-permute-start.2 = (f32[16,64,256]{2,1,0:T(8,128)S(1)}, f32[16,64,256]{2,1,0:T(8,128)}, u32[]{:S(2)}, u32[]{:S(2)}) collective-permute-start(f32[16,64,256]{2,1,0:T(8,128)S(1)} %pack_z.41), channel_id=1, source_target_pairs={{0,16},{4,20},{8,24},{12,28},{16,0},{20,4},{24,8},{28,12},{1,17},{... | collective-permute-start | bytes 3145736 | tf_op jit(solution)/shard_map/ppermute | solution.py:308
  173.3 92.1 %collective-permute-start.7 = (f32[16,64,256]{2,1,0:T(8,128)S(1)}, f32[16,64,256]{2,1,0:T(8,128)}, u32[]{:S(2)}, u32[]{:S(2)}) collective-permute-start(f32[16,64,256]{2,1,0:T(8,128)S(1)} %pack_z.46), channel_id=1, source_target_pairs={{0,24},{4,28},{8,0},{12,4},{16,8},{20,12},{24,16},{28,20},{1,25},{... | collective-permute-start | bytes 3145736 | tf_op jit(solution)/shard_map/ppermute | solution.py:308
  196.5 151.2 %collective-permute-start.9 = (f32[16,64,256]{2,1,0:T(8,128)}, f32[16,64,256]{2,1,0:T(8,128)}, u32[]{:S(2)}, u32[]{:S(2)}) collective-permute-start(f32[16,64,256]{2,1,0:T(8,128)} %pack_z.48), channel_id=1, source_target_pairs={{0,20},{4,16},{8,28},{12,24},{16,4},{20,0},{24,12},{28,8},{1,21},{... | collective-permute-start | bytes 3145736 | tf_op jit(solution)/shard_map/ppermute | solution.py:308
  261.0 119.7 %collective-permute-start.12 = (f32[16,64,256]{2,1,0:T(8,128)}, f32[16,64,256]{2,1,0:T(8,128)}, u32[]{:S(2)}, u32[]{:S(2)}) collective-permute-start(f32[16,64,256]{2,1,0:T(8,128)} %pack_z.52), channel_id=1, source_target_pairs={{0,8},{4,12},{8,16},{12,20},{16,24},{20,28},{24,0},{28,4},{1,9},{5... | collective-permute-start | bytes 3145736 | tf_op jit(solution)/shard_map/ppermute | solution.py:308
  262.5 134.5 %collective-permute-start.15 = (f32[4,512,256]{2,1,0:T(8,128)}, f32[4,512,256]{2,1,0:T(8,128)}, u32[]{:S(2)}, u32[]{:S(2)}) collective-permute-start(f32[4,512,256]{2,1,0:T(8,128)} %constant_dynamic-slice_fusion.19), channel_id=1, source_target_pairs={{0,2},{1,3},{2,0},{3,1},{4,6},{5,7},{6,4},{7,5},{8,10},{9,11},{10,... | collective-permute-start | bytes 6291464 | tf_op jit(solution)/shard_map/ppermute | solution.py:308
  265.4 124.4 %collective-permute-start.13 = (f32[16,64,256]{2,1,0:T(8,128)S(1)}, f32[16,64,256]{2,1,0:T(8,128)}, u32[]{:S(2)}, u32[]{:S(2)}) collective-permute-start(f32[16,64,256]{2,1,0:T(8,128)S(1)} %pack_z.53), channel_id=1, source_target_pairs={{0,28},{4,24},{8,4},{12,0},{16,12},{20,8},{24,20},{28,16},{1,29},{... | collective-permute-start | bytes 3145736 | tf_op jit(solution)/shard_map/ppermute | solution.py:308
  308.0 69.7 %collective-permute-start.11 = (f32[16,64,256]{2,1,0:T(8,128)}, f32[16,64,256]{2,1,0:T(8,128)}, u32[]{:S(2)}, u32[]{:S(2)}) collective-permute-start(f32[16,64,256]{2,1,0:T(8,128)} %pack_z.50), channel_id=1, source_target_pairs={{0,4},{4,0},{8,12},{12,8},{16,20},{20,16},{24,28},{28,24},{1,5},{5... | collective-permute-start | bytes 3145736 | tf_op jit(solution)/shard_map/ppermute | solution.py:308
  347.7 109.3 %collective-permute-start.14 = (f32[4,512,256]{2,1,0:T(8,128)}, f32[4,512,256]{2,1,0:T(8,128)}, u32[]{:S(2)}, u32[]{:S(2)}) collective-permute-start(f32[4,512,256]{2,1,0:T(8,128)} %constant_dynamic-slice_fusion.21), channel_id=1, source_target_pairs={{0,1},{1,2},{2,3},{3,0},{4,5},{5,6},{6,7},{7,4},{8,9},{9,10},{10,1... | collective-permute-start | bytes 6291464 | tf_op jit(solution)/shard_map/ppermute | solution.py:308
  377.7 62.7 %collective-permute-start.21 = (f32[16,64,256]{2,1,0:T(8,128)S(1)}, f32[16,64,256]{2,1,0:T(8,128)S(1)}, u32[]{:S(2)}, u32[]{:S(2)}) collective-permute-start(f32[16,64,256]{2,1,0:T(8,128)S(1)} %pack_z.64), channel_id=1, source_target_pairs={{0,16},{4,20},{8,24},{12,28},{16,0},{20,4},{24,8},{28,12},{1,17},{... | collective-permute-start | bytes 3145736 | tf_op jit(solution)/shard_map/ppermute | solution.py:308
  380.7 94.2 %collective-permute-start.26 = (f32[4,512,256]{2,1,0:T(8,128)}, f32[4,512,256]{2,1,0:T(8,128)}, u32[]{:S(2)}, u32[]{:S(2)}) collective-permute-start(f32[4,512,256]{2,1,0:T(8,128)} %constant_dynamic-slice_fusion.18), channel_id=1, source_target_pairs={{0,3},{1,0},{2,1},{3,2},{4,7},{5,4},{6,5},{7,6},{8,11},{9,8},{10,9... | collective-permute-start | bytes 6291464 | tf_op jit(solution)/shard_map/ppermute | solution.py:308
  397.0 63.5 %collective-permute-start.16 = (f32[16,64,256]{2,1,0:T(8,128)}, f32[16,64,256]{2,1,0:T(8,128)}, u32[]{:S(2)}, u32[]{:S(2)}) collective-permute-start(f32[16,64,256]{2,1,0:T(8,128)} %pack_z.56), channel_id=1, source_target_pairs={{0,12},{4,8},{8,20},{12,16},{16,28},{20,24},{24,4},{28,0},{1,13},{... | collective-permute-start | bytes 3145736 | tf_op jit(solution)/shard_map/ppermute | solution.py:308
  440.3 29.6 %collective-permute-start.22 = (f32[16,64,256]{2,1,0:T(8,128)S(1)}, f32[16,64,256]{2,1,0:T(8,128)}, u32[]{:S(2)}, u32[]{:S(2)}) collective-permute-start(f32[16,64,256]{2,1,0:T(8,128)S(1)} %pack_z.63), channel_id=1, source_target_pairs={{0,4},{4,0},{8,12},{12,8},{16,20},{20,16},{24,28},{28,24},{1,5},{5... | collective-permute-start | bytes 3145736 | tf_op jit(solution)/shard_map/ppermute | solution.py:308
  442.5 26.2 %collective-permute-start.18 = (f32[16,64,256]{2,1,0:T(8,128)S(1)}, f32[16,64,256]{2,1,0:T(8,128)}, u32[]{:S(2)}, u32[]{:S(2)}) collective-permute-start(f32[16,64,256]{2,1,0:T(8,128)S(1)} %pack_z.59), channel_id=1, source_target_pairs={{0,24},{4,28},{8,0},{12,4},{16,8},{20,12},{24,16},{28,20},{1,25},{... | collective-permute-start | bytes 3145736 | tf_op jit(solution)/shard_map/ppermute | solution.py:308
  457.1 102.4 %collective-permute-start.28 = (f32[16,64,256]{2,1,0:T(8,128)}, f32[16,64,256]{2,1,0:T(8,128)}, u32[]{:S(2)}, u32[]{:S(2)}) collective-permute-start(f32[16,64,256]{2,1,0:T(8,128)} %pack_z.67), channel_id=1, source_target_pairs={{0,20},{4,16},{8,28},{12,24},{16,4},{20,0},{24,12},{28,8},{1,21},{... | collective-permute-start | bytes 3145736 | tf_op jit(solution)/shard_map/ppermute | solution.py:308
  460.5 110.9 %collective-permute-start.17 = (f32[4,512,256]{2,1,0:T(8,128)}, f32[4,512,256]{2,1,0:T(8,128)}, u32[]{:S(2)}, u32[]{:S(2)}) collective-permute-start(f32[4,512,256]{2,1,0:T(8,128)} %constant_dynamic-slice_fusion.20), channel_id=1, source_target_pairs={{0,2},{1,3},{2,0},{3,1},{4,6},{5,7},{6,4},{7,5},{8,10},{9,11},{10,... | collective-permute-start | bytes 6291464 | tf_op jit(solution)/shard_map/ppermute | solution.py:308
  469.9 86.0 %collective-permute-start.23 = (f32[8,64,256]{2,1,0:T(8,128)S(1)}, f32[8,64,256]{2,1,0:T(8,128)S(1)}, u32[]{:S(2)}, u32[]{:S(2)}) collective-permute-start(f32[8,64,256]{2,1,0:T(8,128)S(1)} %pack_z.62), channel_id=1, source_target_pairs={{0,16},{4,20},{8,24},{12,28},{16,0},{20,4},{24,8},{28,12},{1,17},{... | collective-permute-start | bytes 1572872 | tf_op jit(solution)/shard_map/ppermute | solution.py:308
  472.2 87.4 %collective-permute-start.19 = (f32[16,64,256]{2,1,0:T(8,128)}, f32[16,64,256]{2,1,0:T(8,128)S(1)}, u32[]{:S(2)}, u32[]{:S(2)}) collective-permute-start(f32[16,64,256]{2,1,0:T(8,128)} %pack_z.58), channel_id=1, source_target_pairs={{0,28},{4,24},{8,4},{12,0},{16,12},{20,8},{24,20},{28,16},{1,29},{... | collective-permute-start | bytes 3145736 | tf_op jit(solution)/shard_map/ppermute | solution.py:308
  474.9 88.4 %collective-permute-start.27 = (f32[16,64,256]{2,1,0:T(8,128)S(1)}, f32[16,64,256]{2,1,0:T(8,128)}, u32[]{:S(2)}, u32[]{:S(2)}) collective-permute-start(f32[16,64,256]{2,1,0:T(8,128)S(1)} %pack_z.65), channel_id=1, source_target_pairs={{0,8},{4,12},{8,16},{12,20},{16,24},{20,28},{24,0},{28,4},{1,9},{5... | collective-permute-start | bytes 3145736 | tf_op jit(solution)/shard_map/ppermute | solution.py:308
  559.5 72.1 %collective-permute-start.29 = (f32[4,512,256]{2,1,0:T(8,128)}, f32[4,512,256]{2,1,0:T(8,128)}, u32[]{:S(2)}, u32[]{:S(2)}) collective-permute-start(f32[4,512,256]{2,1,0:T(8,128)} %constant_dynamic-slice_fusion.17), channel_id=1, source_target_pairs={{0,1},{1,2},{2,3},{3,0},{4,5},{5,6},{6,7},{7,4},{8,9},{9,10},{10,1... | collective-permute-start | bytes 6291464 | tf_op jit(solution)/shard_map/ppermute | solution.py:308
  561.8 48.2 %collective-permute-start.24 = (f32[8,64,256]{2,1,0:T(8,128)S(1)}, f32[8,64,256]{2,1,0:T(8,128)}, u32[]{:S(2)}, u32[]{:S(2)}) collective-permute-start(f32[8,64,256]{2,1,0:T(8,128)S(1)} %pack_z.61), channel_id=1, source_target_pairs={{0,4},{4,0},{8,12},{12,8},{16,20},{20,16},{24,28},{28,24},{1,5},{5... | collective-permute-start | bytes 1572872 | tf_op jit(solution)/shard_map/ppermute | solution.py:308
  563.3 72.1 %collective-permute-start.36 = (f32[4,512,256]{2,1,0:T(8,128)}, f32[4,512,256]{2,1,0:T(8,128)}, u32[]{:S(2)}, u32[]{:S(2)}) collective-permute-start(f32[4,512,256]{2,1,0:T(8,128)} %constant_dynamic-slice_fusion.15), channel_id=1, source_target_pairs={{0,3},{1,0},{2,1},{3,2},{4,7},{5,4},{6,5},{7,6},{8,11},{9,8},{10,9... | collective-permute-start | bytes 6291464 | tf_op jit(solution)/shard_map/ppermute | solution.py:308
  571.4 43.2 %collective-permute-start.31 = (f32[8,64,256]{2,1,0:T(8,128)S(1)}, f32[8,64,256]{2,1,0:T(8,128)}, u32[]{:S(2)}, u32[]{:S(2)}) collective-permute-start(f32[8,64,256]{2,1,0:T(8,128)S(1)} %pack_z.70), channel_id=1, source_target_pairs={{0,12},{4,8},{8,20},{12,16},{16,28},{20,24},{24,4},{28,0},{1,13},{... | collective-permute-start | bytes 1572872 | tf_op jit(solution)/shard_map/ppermute | solution.py:308
  601.8 21.9 %collective-permute-start.20 = (f32[8,64,256]{2,1,0:T(8,128)S(1)}, f32[8,64,256]{2,1,0:T(8,128)}, u32[]{:S(2)}, u32[]{:S(2)}) collective-permute-start(f32[8,64,256]{2,1,0:T(8,128)S(1)} %pack_z.57), channel_id=1, source_target_pairs={{0,24},{4,28},{8,0},{12,4},{16,8},{20,12},{24,16},{28,20},{1,25},{... | collective-permute-start | bytes 1572872 | tf_op jit(solution)/shard_map/ppermute | solution.py:308
  623.7 69.0 %collective-permute-start.34 = (f32[8,64,256]{2,1,0:T(8,128)S(1)}, f32[8,64,256]{2,1,0:T(8,128)S(1)}, u32[]{:S(2)}, u32[]{:S(2)}) collective-permute-start(f32[8,64,256]{2,1,0:T(8,128)S(1)} %pack_z.72), channel_id=1, source_target_pairs={{0,28},{4,24},{8,4},{12,0},{16,12},{20,8},{24,20},{28,16},{1,29},{... | collective-permute-start | bytes 1572872 | tf_op jit(solution)/shard_map/ppermute | solution.py:308
  629.3 64.6 %collective-permute-start.25 = (f32[8,64,256]{2,1,0:T(8,128)S(1)}, f32[8,64,256]{2,1,0:T(8,128)}, u32[]{:S(2)}, u32[]{:S(2)}) collective-permute-start(f32[8,64,256]{2,1,0:T(8,128)S(1)} %pack_z.60), channel_id=1, source_target_pairs={{0,16},{4,20},{8,24},{12,28},{16,0},{20,4},{24,8},{28,12},{1,17},{... | collective-permute-start | bytes 1572872 | tf_op jit(solution)/shard_map/ppermute | solution.py:308
  631.6 57.8 %collective-permute-start.30 = (f32[8,64,256]{2,1,0:T(8,128)S(1)}, f32[8,64,256]{2,1,0:T(8,128)S(1)}, u32[]{:S(2)}, u32[]{:S(2)}) collective-permute-start(f32[8,64,256]{2,1,0:T(8,128)S(1)} %pack_z.66), channel_id=1, source_target_pairs={{0,20},{4,16},{8,28},{12,24},{16,4},{20,0},{24,12},{28,8},{1,21},{... | collective-permute-start | bytes 1572872 | tf_op jit(solution)/shard_map/ppermute | solution.py:308
  635.4 60.4 %collective-permute-start.37 = (f32[8,64,256]{2,1,0:T(8,128)S(1)}, f32[8,64,256]{2,1,0:T(8,128)}, u32[]{:S(2)}, u32[]{:S(2)}) collective-permute-start(f32[8,64,256]{2,1,0:T(8,128)S(1)} %pack_z.73), channel_id=1, source_target_pairs={{0,8},{4,12},{8,16},{12,20},{16,24},{20,28},{24,0},{28,4},{1,9},{5... | collective-permute-start | bytes 1572872 | tf_op jit(solution)/shard_map/ppermute | solution.py:308
  636.9 65.5 %collective-permute-start.32 = (f32[4,512,256]{2,1,0:T(8,128)}, f32[4,512,256]{2,1,0:T(8,128)}, u32[]{:S(2)}, u32[]{:S(2)}) collective-permute-start(f32[4,512,256]{2,1,0:T(8,128)} %constant_dynamic-slice_fusion.16), channel_id=1, source_target_pairs={{0,2},{1,3},{2,0},{3,1},{4,6},{5,7},{6,4},{7,5},{8,10},{9,11},{10,... | collective-permute-start | bytes 6291464 | tf_op jit(solution)/shard_map/ppermute | solution.py:308
  689.4 40.4 %collective-permute-start.38 = (f32[4,512,256]{2,1,0:T(8,128)}, f32[4,512,256]{2,1,0:T(8,128)}, u32[]{:S(2)}, u32[]{:S(2)}) collective-permute-start(f32[4,512,256]{2,1,0:T(8,128)} %constant_dynamic-slice_fusion.14), channel_id=1, source_target_pairs={{0,1},{1,2},{2,3},{3,0},{4,5},{5,6},{6,7},{7,4},{8,9},{9,10},{10,1... | collective-permute-start | bytes 6291464 | tf_op jit(solution)/shard_map/ppermute | solution.py:308
  693.9 60.7 %collective-permute-start.40 = (f32[8,64,256]{2,1,0:T(8,128)S(1)}, f32[8,64,256]{2,1,0:T(8,128)S(1)}, u32[]{:S(2)}, u32[]{:S(2)}) collective-permute-start(f32[8,64,256]{2,1,0:T(8,128)S(1)} %pack_z.75), channel_id=1, source_target_pairs={{0,4},{4,0},{8,12},{12,8},{16,20},{20,16},{24,28},{28,24},{1,5},{5... | collective-permute-start | bytes 1572872 | tf_op jit(solution)/shard_map/ppermute | solution.py:308
  695.8 45.0 %collective-permute-start.41 = (f32[4,512,256]{2,1,0:T(8,128)}, f32[4,512,256]{2,1,0:T(8,128)S(1)}, u32[]{:S(2)}, u32[]{:S(2)}) collective-permute-start(f32[4,512,256]{2,1,0:T(8,128)} %constant_dynamic-slice_fusion.13), channel_id=1, source_target_pairs={{0,3},{1,0},{2,1},{3,2},{4,7},{5,4},{6,5},{7,6},{8,11},{9,8},{10,9... | collective-permute-start | bytes 6291464 | tf_op jit(solution)/shard_map/ppermute | solution.py:308
  703.6 31.0 %collective-permute-start.35 = (f32[8,64,256]{2,1,0:T(8,128)S(1)}, f32[8,64,256]{2,1,0:T(8,128)S(1)}, u32[]{:S(2)}, u32[]{:S(2)}) collective-permute-start(f32[8,64,256]{2,1,0:T(8,128)S(1)} %pack_z.71), channel_id=1, source_target_pairs={{0,24},{4,28},{8,0},{12,4},{16,8},{20,12},{24,16},{28,20},{1,25},{... | collective-permute-start | bytes 1572872 | tf_op jit(solution)/shard_map/ppermute | solution.py:308
  703.7 28.0 %collective-permute-start.33 = (f32[8,64,256]{2,1,0:T(8,128)S(1)}, f32[8,64,256]{2,1,0:T(8,128)S(1)}, u32[]{:S(2)}, u32[]{:S(2)}) collective-permute-start(f32[8,64,256]{2,1,0:T(8,128)S(1)} %pack_z.68), channel_id=1, source_target_pairs={{0,12},{4,8},{8,20},{12,16},{16,28},{20,24},{24,4},{28,0},{1,13},{... | collective-permute-start | bytes 1572872 | tf_op jit(solution)/shard_map/ppermute | solution.py:308
  729.8 23.7 %collective-permute-start.39 = (f32[8,64,256]{2,1,0:T(8,128)S(1)}, f32[8,64,256]{2,1,0:T(8,128)}, u32[]{:S(2)}, u32[]{:S(2)}) collective-permute-start(f32[8,64,256]{2,1,0:T(8,128)S(1)} %pack_z.74), channel_id=1, source_target_pairs={{0,20},{4,16},{8,28},{12,24},{16,4},{20,0},{24,12},{28,8},{1,21},{... | collective-permute-start | bytes 1572872 | tf_op jit(solution)/shard_map/ppermute | solution.py:308
  731.6 91.6 %collective-permute-start.64 = (f32[2,512,256]{2,1,0:T(8,128)}, f32[2,512,256]{2,1,0:T(8,128)}, u32[]{:S(2)}, u32[]{:S(2)}) collective-permute-start(f32[2,512,256]{2,1,0:T(8,128)} %constant_dynamic-slice_fusion.10), channel_id=1, source_target_pairs={{0,2},{1,3},{2,0},{3,1},{4,6},{5,7},{6,4},{7,5},{8,10},{9,11},{10,... | collective-permute-start | bytes 3145736 | tf_op jit(solution)/shard_map/ppermute | solution.py:308
  734.6 35.6 %collective-permute-start.43 = (f32[8,64,256]{2,1,0:T(8,128)S(1)}, f32[8,64,256]{2,1,0:T(8,128)S(1)}, u32[]{:S(2)}, u32[]{:S(2)}) collective-permute-start(f32[8,64,256]{2,1,0:T(8,128)S(1)} %pack_z.77), channel_id=1, source_target_pairs={{0,28},{4,24},{8,4},{12,0},{16,12},{20,8},{24,20},{28,16},{1,29},{... | collective-permute-start | bytes 1572872 | tf_op jit(solution)/shard_map/ppermute | solution.py:308
  740.8 26.2 %collective-permute-start.42 = (f32[8,64,256]{2,1,0:T(8,128)S(1)}, f32[8,64,256]{2,1,0:T(8,128)S(1)}, u32[]{:S(2)}, u32[]{:S(2)}) collective-permute-start(f32[8,64,256]{2,1,0:T(8,128)S(1)} %pack_z.76), channel_id=1, source_target_pairs={{0,8},{4,12},{8,16},{12,20},{16,24},{20,28},{24,0},{28,4},{1,9},{5... | collective-permute-start | bytes 1572872 | tf_op jit(solution)/shard_map/ppermute | solution.py:308
  773.6 9.0 collective-permute-start.44
  774.6 9.5 collective-permute-start.46
  784.2 15.8 %collective-permute-start.47 = (f32[16,512]{1,0:T(8,128)S(1)}, f32[16,512]{1,0:T(8,128)S(1)}, u32[]{:S(2)}, u32[]{:S(2)}) collective-permute-start(f32[16,512]{1,0:T(8,128)S(1)} %get-tuple-element.194), channel_id=1, source_target_pairs={{0,16},{4,20},{8,24},{12,28},{16,0},{20,4},{24,8},{28,12},{1,17},{... | collective-permute-start | bytes 98312 | tf_op jit(solution)/shard_map/ppermute | solution.py:406
  820.3 76.1 %collective-permute-start.69 = (f32[2,512,256]{2,1,0:T(8,128)S(1)}, f32[2,512,256]{2,1,0:T(8,128)S(1)}, u32[]{:S(2)}, u32[]{:S(2)}) collective-permute-start(f32[2,512,256]{2,1,0:T(8,128)S(1)} %constant_dynamic-slice_fusion.6), channel_id=1, source_target_pairs={{0,3},{1,0},{2,1},{3,2},{4,7},{5,4},{6,5},{7,6},{8,11},{9,8},{10,9... | collective-permute-start | bytes 3145736 | tf_op jit(solution)/shard_map/ppermute | solution.py:308
  820.3 75.0 %collective-permute-start.68 = (f32[2,512,256]{2,1,0:T(8,128)S(1)}, f32[2,512,256]{2,1,0:T(8,128)S(1)}, u32[]{:S(2)}, u32[]{:S(2)}) collective-permute-start(f32[2,512,256]{2,1,0:T(8,128)S(1)} %constant_dynamic-slice_fusion.7), channel_id=1, source_target_pairs={{0,1},{1,2},{2,3},{3,0},{4,5},{5,6},{6,7},{7,4},{8,9},{9,10},{10,1... | collective-permute-start | bytes 3145736 | tf_op jit(solution)/shard_map/ppermute | solution.py:308
  822.4 27.0 %collective-permute-start.61 = (f32[128,512]{1,0:T(8,128)S(1)}, f32[128,512]{1,0:T(8,128)S(1)}, u32[]{:S(2)}, u32[]{:S(2)}) collective-permute-start(f32[128,512]{1,0:T(8,128)S(1)} %bitcast.351), channel_id=1, source_target_pairs={{0,2},{1,3},{2,0},{3,1},{4,6},{5,7},{6,4},{7,5},{8,10},{9,11},{10,... | collective-permute-start | bytes 786440 | tf_op jit(solution)/shard_map/ppermute | solution.py:410
  823.2 32.9 %collective-permute-start.62 = (f32[128,512]{1,0:T(8,128)S(1)}, f32[128,512]{1,0:T(8,128)S(1)}, u32[]{:S(2)}, u32[]{:S(2)}) collective-permute-start(f32[128,512]{1,0:T(8,128)S(1)} %bitcast.352), channel_id=1, source_target_pairs={{0,1},{1,2},{2,3},{3,0},{4,5},{5,6},{6,7},{7,4},{8,9},{9,10},{10,1... | collective-permute-start | bytes 786440 | tf_op jit(solution)/shard_map/ppermute | solution.py:410
  823.2 32.9 %collective-permute-start.63 = (f32[128,512]{1,0:T(8,128)S(1)}, f32[128,512]{1,0:T(8,128)S(1)}, u32[]{:S(2)}, u32[]{:S(2)}) collective-permute-start(f32[128,512]{1,0:T(8,128)S(1)} %bitcast.353), channel_id=1, source_target_pairs={{0,3},{1,0},{2,1},{3,2},{4,7},{5,4},{6,5},{7,6},{8,11},{9,8},{10,9... | collective-permute-start | bytes 786440 | tf_op jit(solution)/shard_map/ppermute | solution.py:410
  857.1 63.8 %collective-permute-start.67 = (f32[2,512,256]{2,1,0:T(8,128)}, f32[2,512,256]{2,1,0:T(8,128)}, u32[]{:S(2)}, u32[]{:S(2)}) collective-permute-start(f32[2,512,256]{2,1,0:T(8,128)} %constant_dynamic-slice_fusion.8), channel_id=1, source_target_pairs={{0,3},{1,0},{2,1},{3,2},{4,7},{5,4},{6,5},{7,6},{8,11},{9,8},{10,9... | collective-permute-start | bytes 3145736 | tf_op jit(solution)/shard_map/ppermute | solution.py:308
  859.4 60.2 %collective-permute-start.66 = (f32[2,512,256]{2,1,0:T(8,128)}, f32[2,512,256]{2,1,0:T(8,128)}, u32[]{:S(2)}, u32[]{:S(2)}) collective-permute-start(f32[2,512,256]{2,1,0:T(8,128)} %constant_dynamic-slice_fusion.9), channel_id=1, source_target_pairs={{0,1},{1,2},{2,3},{3,0},{4,5},{5,6},{6,7},{7,4},{8,9},{9,10},{10,1... | collective-permute-start | bytes 3145736 | tf_op jit(solution)/shard_map/ppermute | solution.py:308
  860.5 59.0 %collective-permute-start.65 = (f32[2,512,256]{2,1,0:T(8,128)}, f32[2,512,256]{2,1,0:T(8,128)S(1)}, u32[]{:S(2)}, u32[]{:S(2)}) collective-permute-start(f32[2,512,256]{2,1,0:T(8,128)} %constant_dynamic-slice_fusion.11), channel_id=1, source_target_pairs={{0,2},{1,3},{2,0},{3,1},{4,6},{5,7},{6,4},{7,5},{8,10},{9,11},{10,... | collective-permute-start | bytes 3145736 | tf_op jit(solution)/shard_map/ppermute | solution.py:308
  943.7 25.6 %collective-permute-start.71 = (f32[256,1024]{1,0:T(8,128)S(1)}, f32[256,1024]{1,0:T(8,128)}, u32[]{:S(2)}, u32[]{:S(2)}) collective-permute-start(f32[256,1024]{1,0:T(8,128)S(1)} %dynamic-slice_bitcast_fusion.1), channel_id=1, source_target_pairs={{0,2},{1,3},{2,0},{3,1},{4,6},{5,7},{6,4},{7,5},{8,10},{9,11},{10,... | collective-permute-start | bytes 3145736 | tf_op jit(solution)/shard_map/ppermute | solution.py:436
  970.8 12.0 %collective-permute-start.72 = (f32[256,128]{1,0:T(8,128)S(1)}, f32[256,128]{1,0:T(8,128)S(1)}, u32[]{:S(2)}, u32[]{:S(2)}) collective-permute-start(f32[256,128]{1,0:T(8,128)S(1)} %get-tuple-element.184), channel_id=1, source_target_pairs={{0,16},{4,20},{8,24},{12,28},{16,0},{20,4},{24,8},{28,12},{1,17},{... | collective-permute-start | bytes 393224 | tf_op jit(solution)/shard_map/ppermute | solution.py:444
  971.8 11.1 %collective-permute-start.73 = (f32[256,128]{1,0:T(8,128)S(1)}, f32[256,128]{1,0:T(8,128)S(1)}, u32[]{:S(2)}, u32[]{:S(2)}) collective-permute-start(f32[256,128]{1,0:T(8,128)S(1)} %get-tuple-element.190), channel_id=1, source_target_pairs={{0,12},{4,8},{8,20},{12,16},{16,28},{20,24},{24,4},{28,0},{1,13},{... | collective-permute-start | bytes 393224 | tf_op jit(solution)/shard_map/ppermute | solution.py:444
  973.2 14.1 %collective-permute-start.74 = (f32[256,128]{1,0:T(8,128)S(1)}, f32[256,128]{1,0:T(8,128)S(1)}, u32[]{:S(2)}, u32[]{:S(2)}) collective-permute-start(f32[256,128]{1,0:T(8,128)S(1)} %get-tuple-element.189), channel_id=1, source_target_pairs={{0,24},{4,28},{8,0},{12,4},{16,8},{20,12},{24,16},{28,20},{1,25},{... | collective-permute-start | bytes 393224 | tf_op jit(solution)/shard_map/ppermute | solution.py:444
  975.5 17.6 %collective-permute-start.75 = (f32[256,128]{1,0:T(8,128)S(1)}, f32[256,128]{1,0:T(8,128)S(1)}, u32[]{:S(2)}, u32[]{:S(2)}) collective-permute-start(f32[256,128]{1,0:T(8,128)S(1)} %get-tuple-element.188), channel_id=1, source_target_pairs={{0,20},{4,16},{8,28},{12,24},{16,4},{20,0},{24,12},{28,8},{1,21},{... | collective-permute-start | bytes 393224 | tf_op jit(solution)/shard_map/ppermute | solution.py:444
  976.8 16.4 %collective-permute-start.76 = (f32[256,128]{1,0:T(8,128)S(1)}, f32[256,128]{1,0:T(8,128)S(1)}, u32[]{:S(2)}, u32[]{:S(2)}) collective-permute-start(f32[256,128]{1,0:T(8,128)S(1)} %get-tuple-element.187), channel_id=1, source_target_pairs={{0,4},{4,0},{8,12},{12,8},{16,20},{20,16},{24,28},{28,24},{1,5},{5... | collective-permute-start | bytes 393224 | tf_op jit(solution)/shard_map/ppermute | solution.py:444
  982.8 10.3 %collective-permute-start.77 = (f32[256,128]{1,0:T(8,128)S(1)}, f32[256,128]{1,0:T(8,128)S(1)}, u32[]{:S(2)}, u32[]{:S(2)}) collective-permute-start(f32[256,128]{1,0:T(8,128)S(1)} %get-tuple-element.186), channel_id=1, source_target_pairs={{0,8},{4,12},{8,16},{12,20},{16,24},{20,28},{24,0},{28,4},{1,9},{5... | collective-permute-start | bytes 393224 | tf_op jit(solution)/shard_map/ppermute | solution.py:444
  982.8 13.0 %collective-permute-start.78 = (f32[256,128]{1,0:T(8,128)S(1)}, f32[256,128]{1,0:T(8,128)S(1)}, u32[]{:S(2)}, u32[]{:S(2)}) collective-permute-start(f32[256,128]{1,0:T(8,128)S(1)} %get-tuple-element.185), channel_id=1, source_target_pairs={{0,28},{4,24},{8,4},{12,0},{16,12},{20,8},{24,20},{28,16},{1,29},{... | collective-permute-start | bytes 393224 | tf_op jit(solution)/shard_map/ppermute | solution.py:444
  (35 other events, 347.2 us)

commit v10 on v8

--- a/solution.py
+++ b/solution.py
@@ -351,10 +351,12 @@
             return lax.dynamic_slice_in_dim(source, (q + d) % m * zs, zs, axis=0)
 
         got = order.send(cut, tie(whole, after), "yz", yz_perm(d))
+        crossed.append(got)
         return lax.dynamic_update_slice(cells, got[:, None], (first // m, (q - d) % m, 0, 0))
 
     gram = jnp.zeros((width_x, width_x), F32)
     first, waiting = 0, []
+    crossed = []
     group = math.lcm(m, TALL)
     for groups in chunk_depths(slab // group):
         zc = groups * group
@@ -383,12 +385,14 @@
     summed = pick(slabs, q)
     for d in turns:
         summed = summed + lax.ppermute(pick(slabs, (q + d) % m), "yz", yz_perm(d))
-    while len(waiting) >= len(turns):
-        cells = to_yz(cells, *waiting.pop(0), [summed])
+    while len(waiting) > len(turns):
+        cells = to_yz(cells, *waiting.pop(0))
+    earlier = crossed[-len(turns) :]
     strips = summed.reshape(n, rows // n, width_x)
     summed = pick(strips, g)
     for a, b in shifts:
         summed = summed + lax.ppermute(pick(strips, moved(g, a, b)), "gx", gx_perm(a, b))
+    summed = tie(summed, earlier)
     pieces = [summed] + [lax.ppermute(summed, "gx", gx_perm(a, b)) for a, b in shifts]
     places = jnp.stack([g] + [moved(g, a, b, -1) for a, b in shifts]).astype(jnp.int32)
     summed = stack(pieces, places).reshape(rows, width_x)

time: 999 us -> 1020 us (1.021)
    ppermute x50, waiting for transfers between devices: 346 us -> 371 us  [send(): got = lax.ppermute(tie(value, self.done(0)), axis, perm)]
    ppermute x3, waiting for transfers between devices: 27 us -> 6.68 us  [on_device(): pieces = [summed] + [lax.ppermute(summed, 'yz', yz_perm(d)) for d in turns]]
  transfers between devices with their start and end apart: 79 -> 79, of which waited for: 31 -> 34; matrix products, arithmetic and copies ran while one was open for 12% -> 12% of each run, Pallas kernels for 12% -> 12%
where the time goes in v10:
time: 1020 us; the launch traced here: 1010 us
  waiting for transfers between devices  438 us (43%)
  starting transfers between devices  283 us (28%)
  Pallas kernels  145 us (14%)
  local copies, waits for them, and re-layouts  131 us (13%)
    ppermute x50, waiting for transfers between devices, send(): got = lax.ppermute(tie(value, self.done(0)), axis, perm)  371 us
    ppermute x50, starting transfers between devices, send(): got = lax.ppermute(tie(value, self.done(0)), axis, perm)  242 us
    pallas_call x40, Pallas kernels, pack(): pl.pallas_call(pack_body, grid_spec=pltpu.PrefetchScalarGridSpec(num_scal...  62.9 us
    dynamic_update_slice x35, local copies, waits for them, and re-layouts, to_gx(): lax.dynamic_update_slice_in_dim(whole, got[:, None], moved(g, a, b, -1),...  40.5 us
    pallas_call x1, Pallas kernels, iterate(): pl.pallas_call(functools.partial(iterate_body, total), in_specs=[pl.Block...  34 us
    dynamic_update_slice x15, local copies, waits for them, and re-layouts, to_yz(): lax.dynamic_update_slice(cells, got[:, None], (first // m, (q - d) % m, 0...  31.1 us
    pallas_call x5, Pallas kernels, gram_of(): pl.pallas_call(functools.partial(gram_body, steps), grid=(steps,), in_spe...  26 us
    ppermute x1, waiting for transfers between devices, on_device(): lax.ppermute(pick(blocks_here, (chip + d) % chips), 'yz', perm)  24.1 us
  transfers between devices with their start and end apart: 79, of which 34 were waited for; matrix products, arithmetic and copies ran while one was open for 12% of the time, Pallas kernels for 12%

profile of v10, /device:TPU:0, one launch (start us, length us, event | category | flops | bytes accessed | tf_op | source)
XLA Modules:
  0.0 1006.0 jit_solution(13053824877233008591)
XLA Ops:
  2.9 4.0 collective-permute-start
  34.2 20.4 %collective-permute-done = f32[16,64,256]{2,1,0:T(8,128)} collective-permute-done((f32[16,64,256]{2,1,0:T(8,128)}, f32[16,64,256]{2,1,0:T(8,128)}, u32[]{:S(2)}, u32[]{:S(2)}) %collective-permute-start) | collective-permute-done | bytes 1048608 | tf_op jit(solution)/shard_map/ppermute | solution.py:299
  56.8 21.0 %collective-permute-done.1 = f32[16,64,256]{2,1,0:T(8,128)} collective-permute-done((f32[16,64,256]{2,1,0:T(8,128)}, f32[16,64,256]{2,1,0:T(8,128)}, u32[]{:S(2)}, u32[]{:S(2)}) %collective-permute-start.1) | collective-permute-done | bytes 1048608 | tf_op jit(solution)/shard_map/ppermute | solution.py:299
  77.9 42.9 %collective-permute-start.2 = (f32[16,64,256]{2,1,0:T(8,128)}, f32[16,64,256]{2,1,0:T(8,128)}, u32[]{:S(2)}, u32[]{:S(2)}) collective-permute-start(f32[16,64,256]{2,1,0:T(8,128)} %pack_z.41), channel_id=1, source_target_pairs={{0,16},{4,20},{8,24},{12,28},{16,0},{20,4},{24,8},{28,12},{1,17},{... | collective-permute-start | bytes 3145736 | tf_op jit(solution)/shard_map/ppermute | solution.py:299
  122.9 44.5 %collective-permute-done.4 = f32[16,64,256]{2,1,0:T(8,128)} collective-permute-done((f32[16,64,256]{2,1,0:T(8,128)}, f32[16,64,256]{2,1,0:T(8,128)}, u32[]{:S(2)}, u32[]{:S(2)}) %collective-permute-start.4) | collective-permute-done | bytes 1048608 | tf_op jit(solution)/shard_map/ppermute | solution.py:299
  169.6 3.4 collective-permute-start.7
  176.2 5.1 collective-permute-start.10
  188.9 51.4 %collective-permute-done.8 = f32[16,64,256]{2,1,0:T(8,128)} collective-permute-done((f32[16,64,256]{2,1,0:T(8,128)S(1)}, f32[16,64,256]{2,1,0:T(8,128)}, u32[]{:S(2)}, u32[]{:S(2)}) %collective-permute-start.8) | collective-permute-done | bytes 1048608 | tf_op jit(solution)/shard_map/ppermute | solution.py:299
  240.3 41.0 %collective-permute-start.9 = (f32[16,64,256]{2,1,0:T(8,128)S(1)}, f32[16,64,256]{2,1,0:T(8,128)}, u32[]{:S(2)}, u32[]{:S(2)}) collective-permute-start(f32[16,64,256]{2,1,0:T(8,128)S(1)} %pack_z.48), channel_id=1, source_target_pairs={{0,20},{4,16},{8,28},{12,24},{16,4},{20,0},{24,12},{28,8},{1,21},{... | collective-permute-start | bytes 3145736 | tf_op jit(solution)/shard_map/ppermute | solution.py:299
  288.1 2.9 collective-permute-start.13
  296.8 5.9 gram_x.5.before_ref
  308.0 11.6 %broadcast_in_dim.227 = f32[16,4,512,256]{3,2,1,0:T(8,128)} broadcast(f32[]{:T(128)} %constant.1232.clone.1), dimensions={} | broadcast | bytes 33554436 | tf_op jit(solution)/shard_map/broadcast_in_dim | solution.py:340
  326.3 24.3 %collective-permute-done.9 = f32[16,64,256]{2,1,0:T(8,128)} collective-permute-done((f32[16,64,256]{2,1,0:T(8,128)S(1)}, f32[16,64,256]{2,1,0:T(8,128)}, u32[]{:S(2)}, u32[]{:S(2)}) %collective-permute-start.9) | collective-permute-done | bytes 1048608 | tf_op jit(solution)/shard_map/ppermute | solution.py:299
  365.9 58.3 %collective-permute-start.16 = (f32[16,64,256]{2,1,0:T(8,128)S(1)}, f32[16,64,256]{2,1,0:T(8,128)}, u32[]{:S(2)}, u32[]{:S(2)}) collective-permute-start(f32[16,64,256]{2,1,0:T(8,128)S(1)} %pack_z.56), channel_id=1, source_target_pairs={{0,12},{4,8},{8,20},{12,16},{16,28},{20,24},{24,4},{28,0},{1,13},{... | collective-permute-start | bytes 3145736 | tf_op jit(solution)/shard_map/ppermute | solution.py:299
  425.8 13.6 %collective-permute-done.21 = f32[16,64,256]{2,1,0:T(8,128)} collective-permute-done((f32[16,64,256]{2,1,0:T(8,128)}, f32[16,64,256]{2,1,0:T(8,128)}, u32[]{:S(2)}, u32[]{:S(2)}) %collective-permute-start.21) | collective-permute-done | bytes 1048608 | tf_op jit(solution)/shard_map/ppermute | solution.py:299
  440.8 5.9 gram_x.6.before_ref
  449.2 4.4 broadcast.69.clone.2
  455.9 3.1 bitcast_dynamic-update-slice_fusion.5
  463.3 4.9 collective-permute-done.18
  468.1 5.3 collective-permute-start.19
  474.8 19.3 %collective-permute-start.27 = (f32[16,64,256]{2,1,0:T(8,128)S(1)}, f32[16,64,256]{2,1,0:T(8,128)S(1)}, u32[]{:S(2)}, u32[]{:S(2)}) collective-permute-start(f32[16,64,256]{2,1,0:T(8,128)S(1)} %pack_z.65), channel_id=1, source_target_pairs={{0,8},{4,12},{8,16},{12,20},{16,24},{20,28},{24,0},{28,4},{1,9},{5... | collective-permute-start | bytes 3145736 | tf_op jit(solution)/shard_map/ppermute | solution.py:299
  494.1 2.9 collective-permute-start.28
  501.6 3.1 bitcast_dynamic-update-slice_fusion.4
  509.0 3.1 bitcast_dynamic-update-slice_fusion.9
  512.1 42.9 %collective-permute-done.23 = f32[8,64,256]{2,1,0:T(8,128)S(1)} collective-permute-done((f32[8,64,256]{2,1,0:T(8,128)S(1)}, f32[8,64,256]{2,1,0:T(8,128)S(1)}, u32[]{:S(2)}, u32[]{:S(2)}) %collective-permute-start.23) | collective-permute-done | bytes 524320 | tf_op jit(solution)/shard_map/ppermute | solution.py:299
  559.6 17.1 %collective-permute-done.28 = f32[16,64,256]{2,1,0:T(8,128)S(1)} collective-permute-done((f32[16,64,256]{2,1,0:T(8,128)S(1)}, f32[16,64,256]{2,1,0:T(8,128)S(1)}, u32[]{:S(2)}, u32[]{:S(2)}) %collective-permute-start.28) | collective-permute-done | bytes 1048608 | tf_op jit(solution)/shard_map/ppermute | solution.py:299
  588.8 11.9 %collective-permute-start.20 = (f32[8,64,256]{2,1,0:T(8,128)S(1)}, f32[8,64,256]{2,1,0:T(8,128)S(1)}, u32[]{:S(2)}, u32[]{:S(2)}) collective-permute-start(f32[8,64,256]{2,1,0:T(8,128)S(1)} %pack_z.57), channel_id=1, source_target_pairs={{0,24},{4,28},{8,0},{12,4},{16,8},{20,12},{24,16},{28,20},{1,25},{... | collective-permute-start | bytes 1572872 | tf_op jit(solution)/shard_map/ppermute | solution.py:299
  600.7 7.7 gram_x.7.before_ref
  609.7 3.2 constant_dynamic-slice_fusion.13
  612.9 3.1 bitcast_dynamic-update-slice_fusion.3
  618.7 7.0 collective-permute-done.31
  626.9 4.2 collective-permute-start.34
  631.5 3.0 constant_dynamic-slice_fusion.16
  635.7 5.8 collective-permute-start.37
  641.5 3.1 bitcast_dynamic-update-slice_fusion.2
  644.6 3.1 constant_dynamic-slice_fusion.14
  647.6 44.3 %collective-permute-done.30 = f32[8,64,256]{2,1,0:T(8,128)S(1)} collective-permute-done((f32[8,64,256]{2,1,0:T(8,128)S(1)}, f32[8,64,256]{2,1,0:T(8,128)S(1)}, u32[]{:S(2)}, u32[]{:S(2)}) %collective-permute-start.30) | collective-permute-done | bytes 524320 | tf_op jit(solution)/shard_map/ppermute | solution.py:299
  692.0 3.3 bitcast_dynamic-update-slice_fusion.8
  709.5 4.6 collective-permute-start.35
  714.1 3.2 gram_x.8.before_ref
  717.3 17.9 %collective-permute-done.38 = f32[4,512,256]{2,1,0:T(8,128)} collective-permute-done((f32[4,512,256]{2,1,0:T(8,128)}, f32[4,512,256]{2,1,0:T(8,128)}, u32[]{:S(2)}, u32[]{:S(2)}) %collective-permute-start.38) | collective-permute-done | bytes 2097184 | tf_op jit(solution)/shard_map/ppermute | solution.py:299
  735.3 3.1 bitcast_dynamic-update-slice_fusion.1
  740.3 3.9 collective-permute-start.43
  745.3 24.4 %collective-permute-done.39 = f32[8,64,256]{2,1,0:T(8,128)} collective-permute-done((f32[8,64,256]{2,1,0:T(8,128)S(1)}, f32[8,64,256]{2,1,0:T(8,128)}, u32[]{:S(2)}, u32[]{:S(2)}) %collective-permute-start.39) | collective-permute-done | bytes 524320 | tf_op jit(solution)/shard_map/ppermute | solution.py:299
  771.9 6.4 collective-permute-done.43
  778.5 3.2 gram_x.9
  785.5 2.7 collective-permute-done.46
  790.6 5.0 collective-permute-done.44
  796.6 3.2 collective-permute-start.52
  802.7 3.1 bitcast_dynamic-update-slice_fusion
  807.9 3.3 collective-permute-start.49
  816.1 2.8 collective-permute-done.48
  820.5 18.4 %collective-permute-done.56 = f32[2,512,256]{2,1,0:T(8,128)S(1)} collective-permute-done((f32[2,512,256]{2,1,0:T(8,128)S(1)}, f32[2,512,256]{2,1,0:T(8,128)S(1)}, u32[]{:S(2)}, u32[]{:S(2)}) %collective-permute-start.56) | collective-permute-done | bytes 1048608 | tf_op jit(solution)/shard_map/ppermute | solution.py:299
  844.6 2.9 collective-permute-start.59
  861.1 5.3 collective-permute-done.64.refs_1_
  871.4 34.0 %subspace.1.basis_ref = f32[512,128]{1,0:T(8,128)} custom-call(s32[4]{0:T(128)S(1)} %pad_add_fusion.places_ref, f32[128,512]{1,0:T(8,128)S(1)} %bitcast.358, f32[128,512]{1,0:T(8,128)S(1)} %collective-permute-done.64.refs_1_, f32[128,512]{1,0:T(8,128)S(1)} %collective-permute-done.65.refs_2_, f32[128,512]{1,0:T(8,128)S(1)} %collective-permute-done.66.refs_3_, ...), custom_call_target="tpu_custom_call" | custom-call | flops 40000000000 | bytes 524288 | tf_op jit(solution)/shard_map/subspace/pallas_call | solution.py:228
  906.5 9.9 collective-permute-done.68
  919.6 21.9 %core_gram_y.1 = f32[1024,1024]{1,0:T(8,128)S(1)} custom-call(f32[16,4,512,256]{3,2,1,0:T(8,128)} %bitcast_dynamic-update-slice_fusion.40.field_ref, f32[512,128]{1,0:T(8,128)S(1)} %copy-done.11), custom_call_target="tpu_custom_call" | custom-call | flops 15032385536 | bytes 33554432 | tf_op jit(solution)/shard_map/core_gram_y/pallas_call | solution.py:117
  943.8 4.2 collective-permute-done.70
  952.1 24.1 %collective-permute-done.71 = f32[256,1024]{1,0:T(8,128)} collective-permute-done((f32[256,1024]{1,0:T(8,128)S(1)}, f32[256,1024]{1,0:T(8,128)}, u32[]{:S(2)}, u32[]{:S(2)}) %collective-permute-start.71) | collective-permute-done | bytes 1048608 | tf_op jit(solution)/shard_map/ppermute | solution.py:421
  977.7 4.1 collective-permute-start.78
  983.4 3.2 collective-permute-start.74
  991.5 8.3 collective-permute-done.75
  999.8 5.1 collective-permute-done.72
  (293 shorter events, 213.2 us)
Async XLA Ops:
  2.9 51.7 %collective-permute-start = (f32[16,64,256]{2,1,0:T(8,128)}, f32[16,64,256]{2,1,0:T(8,128)}, u32[]{:S(2)}, u32[]{:S(2)}) collective-permute-start(f32[16,64,256]{2,1,0:T(8,128)} %pack_z.40), channel_id=1, source_target_pairs={{0,16},{4,20},{8,24},{12,28},{16,0},{20,4},{24,8},{28,12},{1,17},{... | collective-permute-start | bytes 3145736 | tf_op jit(solution)/shard_map/ppermute | solution.py:299
  9.1 68.7 %collective-permute-start.1 = (f32[16,64,256]{2,1,0:T(8,128)}, f32[16,64,256]{2,1,0:T(8,128)}, u32[]{:S(2)}, u32[]{:S(2)}) collective-permute-start(f32[16,64,256]{2,1,0:T(8,128)} %pack_z.42), channel_id=1, source_target_pairs={{0,24},{4,28},{8,0},{12,4},{16,8},{20,12},{24,16},{28,20},{1,25},{... | collective-permute-start | bytes 3145736 | tf_op jit(solution)/shard_map/ppermute | solution.py:299
  12.7 108.0 %collective-permute-start.3 = (f32[16,64,256]{2,1,0:T(8,128)}, f32[16,64,256]{2,1,0:T(8,128)}, u32[]{:S(2)}, u32[]{:S(2)}) collective-permute-start(f32[16,64,256]{2,1,0:T(8,128)} %pack_z.43), channel_id=1, source_target_pairs={{0,12},{4,8},{8,20},{12,16},{16,28},{20,24},{24,4},{28,0},{1,13},{... | collective-permute-start | bytes 3145736 | tf_op jit(solution)/shard_map/ppermute | solution.py:299
  16.6 150.9 %collective-permute-start.4 = (f32[16,64,256]{2,1,0:T(8,128)}, f32[16,64,256]{2,1,0:T(8,128)}, u32[]{:S(2)}, u32[]{:S(2)}) collective-permute-start(f32[16,64,256]{2,1,0:T(8,128)} %pack_z.45), channel_id=1, source_target_pairs={{0,20},{4,16},{8,28},{12,24},{16,4},{20,0},{24,12},{28,8},{1,21},{... | collective-permute-start | bytes 3145736 | tf_op jit(solution)/shard_map/ppermute | solution.py:299
  19.8 149.8 %collective-permute-start.6 = (f32[16,64,256]{2,1,0:T(8,128)}, f32[16,64,256]{2,1,0:T(8,128)}, u32[]{:S(2)}, u32[]{:S(2)}) collective-permute-start(f32[16,64,256]{2,1,0:T(8,128)} %pack_z.47), channel_id=1, source_target_pairs={{0,4},{4,0},{8,12},{12,8},{16,20},{20,16},{24,28},{28,24},{1,5},{5... | collective-permute-start | bytes 3145736 | tf_op jit(solution)/shard_map/ppermute | solution.py:299
  77.9 208.1 %collective-permute-start.2 = (f32[16,64,256]{2,1,0:T(8,128)}, f32[16,64,256]{2,1,0:T(8,128)}, u32[]{:S(2)}, u32[]{:S(2)}) collective-permute-start(f32[16,64,256]{2,1,0:T(8,128)} %pack_z.41), channel_id=1, source_target_pairs={{0,16},{4,20},{8,24},{12,28},{16,0},{20,4},{24,8},{28,12},{1,17},{... | collective-permute-start | bytes 3145736 | tf_op jit(solution)/shard_map/ppermute | solution.py:299
  167.4 117.1 %collective-permute-start.5 = (f32[16,64,256]{2,1,0:T(8,128)}, f32[16,64,256]{2,1,0:T(8,128)}, u32[]{:S(2)}, u32[]{:S(2)}) collective-permute-start(f32[16,64,256]{2,1,0:T(8,128)} %pack_z.44), channel_id=1, source_target_pairs={{0,12},{4,8},{8,20},{12,16},{16,28},{20,24},{24,4},{28,0},{1,13},{... | collective-permute-start | bytes 3145736 | tf_op jit(solution)/shard_map/ppermute | solution.py:299
  169.6 118.5 %collective-permute-start.7 = (f32[16,64,256]{2,1,0:T(8,128)}, f32[16,64,256]{2,1,0:T(8,128)}, u32[]{:S(2)}, u32[]{:S(2)}) collective-permute-start(f32[16,64,256]{2,1,0:T(8,128)} %pack_z.46), channel_id=1, source_target_pairs={{0,24},{4,28},{8,0},{12,4},{16,8},{20,12},{24,16},{28,20},{1,25},{... | collective-permute-start | bytes 3145736 | tf_op jit(solution)/shard_map/ppermute | solution.py:299
  174.6 65.7 %collective-permute-start.8 = (f32[16,64,256]{2,1,0:T(8,128)S(1)}, f32[16,64,256]{2,1,0:T(8,128)}, u32[]{:S(2)}, u32[]{:S(2)}) collective-permute-start(f32[16,64,256]{2,1,0:T(8,128)S(1)} %copy-done.7), channel_id=1, source_target_pairs={{0,8},{4,12},{8,16},{12,20},{16,24},{20,28},{24,0},{28,4},{1,9},{5... | collective-permute-start | bytes 3145736 | tf_op jit(solution)/shard_map/ppermute | solution.py:299
  176.2 105.1 %collective-permute-start.10 = (f32[16,64,256]{2,1,0:T(8,128)S(1)}, f32[16,64,256]{2,1,0:T(8,128)S(1)}, u32[]{:S(2)}, u32[]{:S(2)}) collective-permute-start(f32[16,64,256]{2,1,0:T(8,128)S(1)} %copy-done.9), channel_id=1, source_target_pairs={{0,28},{4,24},{8,4},{12,0},{16,12},{20,8},{24,20},{28,16},{1,29},{... | collective-permute-start | bytes 3145736 | tf_op jit(solution)/shard_map/ppermute | solution.py:299
  240.3 110.4 %collective-permute-start.9 = (f32[16,64,256]{2,1,0:T(8,128)S(1)}, f32[16,64,256]{2,1,0:T(8,128)}, u32[]{:S(2)}, u32[]{:S(2)}) collective-permute-start(f32[16,64,256]{2,1,0:T(8,128)S(1)} %pack_z.48), channel_id=1, source_target_pairs={{0,20},{4,16},{8,28},{12,24},{16,4},{20,0},{24,12},{28,8},{1,21},{... | collective-permute-start | bytes 3145736 | tf_op jit(solution)/shard_map/ppermute | solution.py:299
  281.3 69.3 %collective-permute-start.11 = (f32[16,64,256]{2,1,0:T(8,128)S(1)}, f32[16,64,256]{2,1,0:T(8,128)}, u32[]{:S(2)}, u32[]{:S(2)}) collective-permute-start(f32[16,64,256]{2,1,0:T(8,128)S(1)} %pack_z.50), channel_id=1, source_target_pairs={{0,4},{4,0},{8,12},{12,8},{16,20},{20,16},{24,28},{28,24},{1,5},{5... | collective-permute-start | bytes 3145736 | tf_op jit(solution)/shard_map/ppermute | solution.py:299
  284.5 67.6 %collective-permute-start.12 = (f32[16,64,256]{2,1,0:T(8,128)}, f32[16,64,256]{2,1,0:T(8,128)S(1)}, u32[]{:S(2)}, u32[]{:S(2)}) collective-permute-start(f32[16,64,256]{2,1,0:T(8,128)} %pack_z.52), channel_id=1, source_target_pairs={{0,8},{4,12},{8,16},{12,20},{16,24},{20,28},{24,0},{28,4},{1,9},{5... | collective-permute-start | bytes 3145736 | tf_op jit(solution)/shard_map/ppermute | solution.py:299
  288.1 71.9 %collective-permute-start.13 = (f32[16,64,256]{2,1,0:T(8,128)}, f32[16,64,256]{2,1,0:T(8,128)}, u32[]{:S(2)}, u32[]{:S(2)}) collective-permute-start(f32[16,64,256]{2,1,0:T(8,128)} %pack_z.53), channel_id=1, source_target_pairs={{0,28},{4,24},{8,4},{12,0},{16,12},{20,8},{24,20},{28,16},{1,29},{... | collective-permute-start | bytes 3145736 | tf_op jit(solution)/shard_map/ppermute | solution.py:299
  295.1 70.7 %collective-permute-start.15 = (f32[4,512,256]{2,1,0:T(8,128)}, f32[4,512,256]{2,1,0:T(8,128)}, u32[]{:S(2)}, u32[]{:S(2)}) collective-permute-start(f32[4,512,256]{2,1,0:T(8,128)} %constant_dynamic-slice_fusion.19), channel_id=1, source_target_pairs={{0,2},{1,3},{2,0},{3,1},{4,6},{5,7},{6,4},{7,5},{8,10},{9,11},{10,... | collective-permute-start | bytes 6291464 | tf_op jit(solution)/shard_map/ppermute | solution.py:299
  350.6 108.3 %collective-permute-start.14 = (f32[4,512,256]{2,1,0:T(8,128)}, f32[4,512,256]{2,1,0:T(8,128)}, u32[]{:S(2)}, u32[]{:S(2)}) collective-permute-start(f32[4,512,256]{2,1,0:T(8,128)} %constant_dynamic-slice_fusion.21), channel_id=1, source_target_pairs={{0,1},{1,2},{2,3},{3,0},{4,5},{5,6},{6,7},{7,4},{8,9},{9,10},{10,1... | collective-permute-start | bytes 6291464 | tf_op jit(solution)/shard_map/ppermute | solution.py:299
  350.6 88.7 %collective-permute-start.21 = (f32[16,64,256]{2,1,0:T(8,128)}, f32[16,64,256]{2,1,0:T(8,128)}, u32[]{:S(2)}, u32[]{:S(2)}) collective-permute-start(f32[16,64,256]{2,1,0:T(8,128)} %pack_z.64), channel_id=1, source_target_pairs={{0,16},{4,20},{8,24},{12,28},{16,0},{20,4},{24,8},{28,12},{1,17},{... | collective-permute-start | bytes 3145736 | tf_op jit(solution)/shard_map/ppermute | solution.py:299
  352.1 122.6 %collective-permute-start.26 = (f32[4,512,256]{2,1,0:T(8,128)}, f32[4,512,256]{2,1,0:T(8,128)}, u32[]{:S(2)}, u32[]{:S(2)}) collective-permute-start(f32[4,512,256]{2,1,0:T(8,128)} %constant_dynamic-slice_fusion.18), channel_id=1, source_target_pairs={{0,3},{1,0},{2,1},{3,2},{4,7},{5,4},{6,5},{7,6},{8,11},{9,8},{10,9... | collective-permute-start | bytes 6291464 | tf_op jit(solution)/shard_map/ppermute | solution.py:299
  365.9 94.5 %collective-permute-start.16 = (f32[16,64,256]{2,1,0:T(8,128)S(1)}, f32[16,64,256]{2,1,0:T(8,128)}, u32[]{:S(2)}, u32[]{:S(2)}) collective-permute-start(f32[16,64,256]{2,1,0:T(8,128)S(1)} %pack_z.56), channel_id=1, source_target_pairs={{0,12},{4,8},{8,20},{12,16},{16,28},{20,24},{24,4},{28,0},{1,13},{... | collective-permute-start | bytes 3145736 | tf_op jit(solution)/shard_map/ppermute | solution.py:299
  425.7 42.5 %collective-permute-start.18 = (f32[16,64,256]{2,1,0:T(8,128)S(1)}, f32[16,64,256]{2,1,0:T(8,128)}, u32[]{:S(2)}, u32[]{:S(2)}) collective-permute-start(f32[16,64,256]{2,1,0:T(8,128)S(1)} %pack_z.59), channel_id=1, source_target_pairs={{0,24},{4,28},{8,0},{12,4},{16,8},{20,12},{24,16},{28,20},{1,25},{... | collective-permute-start | bytes 3145736 | tf_op jit(solution)/shard_map/ppermute | solution.py:299
  439.3 35.4 %collective-permute-start.22 = (f32[16,64,256]{2,1,0:T(8,128)S(1)}, f32[16,64,256]{2,1,0:T(8,128)}, u32[]{:S(2)}, u32[]{:S(2)}) collective-permute-start(f32[16,64,256]{2,1,0:T(8,128)S(1)} %pack_z.63), channel_id=1, source_target_pairs={{0,4},{4,0},{8,12},{12,8},{16,20},{20,16},{24,28},{28,24},{1,5},{5... | collective-permute-start | bytes 3145736 | tf_op jit(solution)/shard_map/ppermute | solution.py:299
  460.4 127.1 %collective-permute-start.17 = (f32[4,512,256]{2,1,0:T(8,128)}, f32[4,512,256]{2,1,0:T(8,128)}, u32[]{:S(2)}, u32[]{:S(2)}) collective-permute-start(f32[4,512,256]{2,1,0:T(8,128)} %constant_dynamic-slice_fusion.20), channel_id=1, source_target_pairs={{0,2},{1,3},{2,0},{3,1},{4,6},{5,7},{6,4},{7,5},{8,10},{9,11},{10,... | collective-permute-start | bytes 6291464 | tf_op jit(solution)/shard_map/ppermute | solution.py:299
  468.1 89.5 %collective-permute-start.19 = (f32[16,64,256]{2,1,0:T(8,128)S(1)}, f32[16,64,256]{2,1,0:T(8,128)S(1)}, u32[]{:S(2)}, u32[]{:S(2)}) collective-permute-start(f32[16,64,256]{2,1,0:T(8,128)S(1)} %pack_z.58), channel_id=1, source_target_pairs={{0,28},{4,24},{8,4},{12,0},{16,12},{20,8},{24,20},{28,16},{1,29},{... | collective-permute-start | bytes 3145736 | tf_op jit(solution)/shard_map/ppermute | solution.py:299
  474.7 80.3 %collective-permute-start.23 = (f32[8,64,256]{2,1,0:T(8,128)S(1)}, f32[8,64,256]{2,1,0:T(8,128)S(1)}, u32[]{:S(2)}, u32[]{:S(2)}) collective-permute-start(f32[8,64,256]{2,1,0:T(8,128)S(1)} %pack_z.62), channel_id=1, source_target_pairs={{0,16},{4,20},{8,24},{12,28},{16,0},{20,4},{24,8},{28,12},{1,17},{... | collective-permute-start | bytes 1572872 | tf_op jit(solution)/shard_map/ppermute | solution.py:299
  474.8 102.9 %collective-permute-start.27 = (f32[16,64,256]{2,1,0:T(8,128)S(1)}, f32[16,64,256]{2,1,0:T(8,128)S(1)}, u32[]{:S(2)}, u32[]{:S(2)}) collective-permute-start(f32[16,64,256]{2,1,0:T(8,128)S(1)} %pack_z.65), channel_id=1, source_target_pairs={{0,8},{4,12},{8,16},{12,20},{16,24},{20,28},{24,0},{28,4},{1,9},{5... | collective-permute-start | bytes 3145736 | tf_op jit(solution)/shard_map/ppermute | solution.py:299
  494.1 82.6 %collective-permute-start.28 = (f32[16,64,256]{2,1,0:T(8,128)S(1)}, f32[16,64,256]{2,1,0:T(8,128)S(1)}, u32[]{:S(2)}, u32[]{:S(2)}) collective-permute-start(f32[16,64,256]{2,1,0:T(8,128)S(1)} %pack_z.67), channel_id=1, source_target_pairs={{0,20},{4,16},{8,28},{12,24},{16,4},{20,0},{24,12},{28,8},{1,21},{... | collective-permute-start | bytes 3145736 | tf_op jit(solution)/shard_map/ppermute | solution.py:299
  559.0 50.6 %collective-permute-start.24 = (f32[8,64,256]{2,1,0:T(8,128)S(1)}, f32[8,64,256]{2,1,0:T(8,128)S(1)}, u32[]{:S(2)}, u32[]{:S(2)}) collective-permute-start(f32[8,64,256]{2,1,0:T(8,128)S(1)} %pack_z.61), channel_id=1, source_target_pairs={{0,4},{4,0},{8,12},{12,8},{16,20},{20,16},{24,28},{28,24},{1,5},{5... | collective-permute-start | bytes 1572872 | tf_op jit(solution)/shard_map/ppermute | solution.py:299
  576.7 54.5 %collective-permute-start.29 = (f32[4,512,256]{2,1,0:T(8,128)}, f32[4,512,256]{2,1,0:T(8,128)}, u32[]{:S(2)}, u32[]{:S(2)}) collective-permute-start(f32[4,512,256]{2,1,0:T(8,128)} %constant_dynamic-slice_fusion.17), channel_id=1, source_target_pairs={{0,1},{1,2},{2,3},{3,0},{4,5},{5,6},{6,7},{7,4},{8,9},{9,10},{10,1... | collective-permute-start | bytes 6291464 | tf_op jit(solution)/shard_map/ppermute | solution.py:299
  577.7 58.0 %collective-permute-start.36 = (f32[4,512,256]{2,1,0:T(8,128)S(1)}, f32[4,512,256]{2,1,0:T(8,128)S(1)}, u32[]{:S(2)}, u32[]{:S(2)}) collective-permute-start(f32[4,512,256]{2,1,0:T(8,128)S(1)} %copy-done.16), channel_id=1, source_target_pairs={{0,3},{1,0},{2,1},{3,2},{4,7},{5,4},{6,5},{7,6},{8,11},{9,8},{10,9... | collective-permute-start | bytes 6291464 | tf_op jit(solution)/shard_map/ppermute | solution.py:299
  588.8 27.1 %collective-permute-start.20 = (f32[8,64,256]{2,1,0:T(8,128)S(1)}, f32[8,64,256]{2,1,0:T(8,128)S(1)}, u32[]{:S(2)}, u32[]{:S(2)}) collective-permute-start(f32[8,64,256]{2,1,0:T(8,128)S(1)} %pack_z.57), channel_id=1, source_target_pairs={{0,24},{4,28},{8,0},{12,4},{16,8},{20,12},{24,16},{28,20},{1,25},{... | collective-permute-start | bytes 1572872 | tf_op jit(solution)/shard_map/ppermute | solution.py:299
  600.7 25.0 %collective-permute-start.31 = (f32[8,64,256]{2,1,0:T(8,128)S(1)}, f32[8,64,256]{2,1,0:T(8,128)S(1)}, u32[]{:S(2)}, u32[]{:S(2)}) collective-permute-start(f32[8,64,256]{2,1,0:T(8,128)S(1)} %pack_z.70), channel_id=1, source_target_pairs={{0,12},{4,8},{8,20},{12,16},{16,28},{20,24},{24,4},{28,0},{1,13},{... | collective-permute-start | bytes 1572872 | tf_op jit(solution)/shard_map/ppermute | solution.py:299
  617.2 82.6 %collective-permute-start.25 = (f32[8,64,256]{2,1,0:T(8,128)S(1)}, f32[8,64,256]{2,1,0:T(8,128)S(1)}, u32[]{:S(2)}, u32[]{:S(2)}) collective-permute-start(f32[8,64,256]{2,1,0:T(8,128)S(1)} %pack_z.60), channel_id=1, source_target_pairs={{0,16},{4,20},{8,24},{12,28},{16,0},{20,4},{24,8},{28,12},{1,17},{... | collective-permute-start | bytes 1572872 | tf_op jit(solution)/shard_map/ppermute | solution.py:299
  626.9 71.6 %collective-permute-start.34 = (f32[8,64,256]{2,1,0:T(8,128)S(1)}, f32[8,64,256]{2,1,0:T(8,128)S(1)}, u32[]{:S(2)}, u32[]{:S(2)}) collective-permute-start(f32[8,64,256]{2,1,0:T(8,128)S(1)} %pack_z.72), channel_id=1, source_target_pairs={{0,28},{4,24},{8,4},{12,0},{16,12},{20,8},{24,20},{28,16},{1,29},{... | collective-permute-start | bytes 1572872 | tf_op jit(solution)/shard_map/ppermute | solution.py:299
  631.2 60.7 %collective-permute-start.30 = (f32[8,64,256]{2,1,0:T(8,128)S(1)}, f32[8,64,256]{2,1,0:T(8,128)S(1)}, u32[]{:S(2)}, u32[]{:S(2)}) collective-permute-start(f32[8,64,256]{2,1,0:T(8,128)S(1)} %pack_z.66), channel_id=1, source_target_pairs={{0,20},{4,16},{8,28},{12,24},{16,4},{20,0},{24,12},{28,8},{1,21},{... | collective-permute-start | bytes 1572872 | tf_op jit(solution)/shard_map/ppermute | solution.py:299
  634.5 73.8 %collective-permute-start.32 = (f32[4,512,256]{2,1,0:T(8,128)}, f32[4,512,256]{2,1,0:T(8,128)}, u32[]{:S(2)}, u32[]{:S(2)}) collective-permute-start(f32[4,512,256]{2,1,0:T(8,128)} %constant_dynamic-slice_fusion.16), channel_id=1, source_target_pairs={{0,2},{1,3},{2,0},{3,1},{4,6},{5,7},{6,4},{7,5},{8,10},{9,11},{10,... | collective-permute-start | bytes 6291464 | tf_op jit(solution)/shard_map/ppermute | solution.py:299
  635.7 59.6 %collective-permute-start.37 = (f32[8,64,256]{2,1,0:T(8,128)S(1)}, f32[8,64,256]{2,1,0:T(8,128)S(1)}, u32[]{:S(2)}, u32[]{:S(2)}) collective-permute-start(f32[8,64,256]{2,1,0:T(8,128)S(1)} %pack_z.73), channel_id=1, source_target_pairs={{0,8},{4,12},{8,16},{12,20},{16,24},{20,28},{24,0},{28,4},{1,9},{5... | collective-permute-start | bytes 1572872 | tf_op jit(solution)/shard_map/ppermute | solution.py:299
  691.9 43.3 %collective-permute-start.38 = (f32[4,512,256]{2,1,0:T(8,128)}, f32[4,512,256]{2,1,0:T(8,128)}, u32[]{:S(2)}, u32[]{:S(2)}) collective-permute-start(f32[4,512,256]{2,1,0:T(8,128)} %constant_dynamic-slice_fusion.14), channel_id=1, source_target_pairs={{0,1},{1,2},{2,3},{3,0},{4,5},{5,6},{6,7},{7,4},{8,9},{9,10},{10,1... | collective-permute-start | bytes 6291464 | tf_op jit(solution)/shard_map/ppermute | solution.py:299
  695.2 43.8 %collective-permute-start.41 = (f32[4,512,256]{2,1,0:T(8,128)}, f32[4,512,256]{2,1,0:T(8,128)S(1)}, u32[]{:S(2)}, u32[]{:S(2)}) collective-permute-start(f32[4,512,256]{2,1,0:T(8,128)} %constant_dynamic-slice_fusion.13), channel_id=1, source_target_pairs={{0,3},{1,0},{2,1},{3,2},{4,7},{5,4},{6,5},{7,6},{8,11},{9,8},{10,9... | collective-permute-start | bytes 6291464 | tf_op jit(solution)/shard_map/ppermute | solution.py:299
  699.7 71.1 %collective-permute-start.40 = (f32[8,64,256]{2,1,0:T(8,128)S(1)}, f32[8,64,256]{2,1,0:T(8,128)S(1)}, u32[]{:S(2)}, u32[]{:S(2)}) collective-permute-start(f32[8,64,256]{2,1,0:T(8,128)S(1)} %pack_z.75), channel_id=1, source_target_pairs={{0,4},{4,0},{8,12},{12,8},{16,20},{20,16},{24,28},{28,24},{1,5},{5... | collective-permute-start | bytes 1572872 | tf_op jit(solution)/shard_map/ppermute | solution.py:299
  708.2 30.7 %collective-permute-start.33 = (f32[8,64,256]{2,1,0:T(8,128)S(1)}, f32[8,64,256]{2,1,0:T(8,128)S(1)}, u32[]{:S(2)}, u32[]{:S(2)}) collective-permute-start(f32[8,64,256]{2,1,0:T(8,128)S(1)} %pack_z.68), channel_id=1, source_target_pairs={{0,12},{4,8},{8,20},{12,16},{16,28},{20,24},{24,4},{28,0},{1,13},{... | collective-permute-start | bytes 1572872 | tf_op jit(solution)/shard_map/ppermute | solution.py:299
  709.5 30.7 %collective-permute-start.35 = (f32[8,64,256]{2,1,0:T(8,128)S(1)}, f32[8,64,256]{2,1,0:T(8,128)}, u32[]{:S(2)}, u32[]{:S(2)}) collective-permute-start(f32[8,64,256]{2,1,0:T(8,128)S(1)} %pack_z.71), channel_id=1, source_target_pairs={{0,24},{4,28},{8,0},{12,4},{16,8},{20,12},{24,16},{28,20},{1,25},{... | collective-permute-start | bytes 1572872 | tf_op jit(solution)/shard_map/ppermute | solution.py:299
  735.3 34.4 %collective-permute-start.39 = (f32[8,64,256]{2,1,0:T(8,128)S(1)}, f32[8,64,256]{2,1,0:T(8,128)}, u32[]{:S(2)}, u32[]{:S(2)}) collective-permute-start(f32[8,64,256]{2,1,0:T(8,128)S(1)} %pack_z.74), channel_id=1, source_target_pairs={{0,20},{4,16},{8,28},{12,24},{16,4},{20,0},{24,12},{28,8},{1,21},{... | collective-permute-start | bytes 1572872 | tf_op jit(solution)/shard_map/ppermute | solution.py:299
  739.0 31.9 %collective-permute-start.42 = (f32[8,64,256]{2,1,0:T(8,128)S(1)}, f32[8,64,256]{2,1,0:T(8,128)}, u32[]{:S(2)}, u32[]{:S(2)}) collective-permute-start(f32[8,64,256]{2,1,0:T(8,128)S(1)} %pack_z.76), channel_id=1, source_target_pairs={{0,8},{4,12},{8,16},{12,20},{16,24},{20,28},{24,0},{28,4},{1,9},{5... | collective-permute-start | bytes 1572872 | tf_op jit(solution)/shard_map/ppermute | solution.py:299
  740.3 38.1 %collective-permute-start.43 = (f32[8,64,256]{2,1,0:T(8,128)S(1)}, f32[8,64,256]{2,1,0:T(8,128)S(1)}, u32[]{:S(2)}, u32[]{:S(2)}) collective-permute-start(f32[8,64,256]{2,1,0:T(8,128)S(1)} %pack_z.77), channel_id=1, source_target_pairs={{0,28},{4,24},{8,4},{12,0},{16,12},{20,8},{24,20},{28,16},{1,29},{... | collective-permute-start | bytes 1572872 | tf_op jit(solution)/shard_map/ppermute | solution.py:299
  782.3 13.2 %collective-permute-start.44 = (f32[128,512]{1,0:T(8,128)S(1)}, f32[128,512]{1,0:T(8,128)S(1)}, u32[]{:S(2)}, u32[]{:S(2)}) collective-permute-start(f32[128,512]{1,0:T(8,128)S(1)} %get-tuple-element.189), channel_id=1, source_target_pairs={{0,2},{1,3},{2,0},{3,1},{4,6},{5,7},{6,4},{7,5},{8,10},{9,11},{10,... | collective-permute-start | bytes 786440 | tf_op jit(solution)/shard_map/ppermute | solution.py:387
  783.7 35.7 %collective-permute-start.54 = (f32[2,512,256]{2,1,0:T(8,128)S(1)}, f32[2,512,256]{2,1,0:T(8,128)S(1)}, u32[]{:S(2)}, u32[]{:S(2)}) collective-permute-start(f32[2,512,256]{2,1,0:T(8,128)S(1)} %constant_dynamic-slice_fusion.12), channel_id=1, source_target_pairs={{0,2},{1,3},{2,0},{3,1},{4,6},{5,7},{6,4},{7,5},{8,10},{9,11},{10,... | collective-permute-start | bytes 3145736 | tf_op jit(solution)/shard_map/ppermute | solution.py:299
  784.6 54.3 %collective-permute-start.56 = (f32[2,512,256]{2,1,0:T(8,128)S(1)}, f32[2,512,256]{2,1,0:T(8,128)S(1)}, u32[]{:S(2)}, u32[]{:S(2)}) collective-permute-start(f32[2,512,256]{2,1,0:T(8,128)S(1)} %constant_dynamic-slice_fusion.10), channel_id=1, source_target_pairs={{0,3},{1,0},{2,1},{3,2},{4,7},{5,4},{6,5},{7,6},{8,11},{9,8},{10,9... | collective-permute-start | bytes 3145736 | tf_op jit(solution)/shard_map/ppermute | solution.py:299
  795.9 45.0 %collective-permute-start.55 = (f32[2,512,256]{2,1,0:T(8,128)S(1)}, f32[2,512,256]{2,1,0:T(8,128)S(1)}, u32[]{:S(2)}, u32[]{:S(2)}) collective-permute-start(f32[2,512,256]{2,1,0:T(8,128)S(1)} %constant_dynamic-slice_fusion.11), channel_id=1, source_target_pairs={{0,1},{1,2},{2,3},{3,0},{4,5},{5,6},{6,7},{7,4},{8,9},{9,10},{10,1... | collective-permute-start | bytes 3145736 | tf_op jit(solution)/shard_map/ppermute | solution.py:299
  796.6 9.2 collective-permute-start.52
  840.8 9.2 collective-permute-start.57
  843.2 8.8 collective-permute-start.58
  844.6 10.8 %collective-permute-start.59 = (f32[16,512]{1,0:T(8,128)S(1)}, f32[16,512]{1,0:T(8,128)S(1)}, u32[]{:S(2)}, u32[]{:S(2)}) collective-permute-start(f32[16,512]{1,0:T(8,128)S(1)} %fusion.7.refs_0_), channel_id=1, source_target_pairs={{0,24},{4,28},{8,0},{12,4},{16,8},{20,12},{24,16},{28,20},{1,25},{... | collective-permute-start | bytes 98312 | tf_op jit(solution)/shard_map/ppermute | solution.py:396
  857.4 9.0 collective-permute-start.64
  858.3 9.5 collective-permute-start.66
  867.9 37.5 %collective-permute-start.67 = (f32[2,512,256]{2,1,0:T(8,128)S(1)}, f32[2,512,256]{2,1,0:T(8,128)S(1)}, u32[]{:S(2)}, u32[]{:S(2)}) collective-permute-start(f32[2,512,256]{2,1,0:T(8,128)S(1)} %constant_dynamic-slice_fusion.8), channel_id=1, source_target_pairs={{0,2},{1,3},{2,0},{3,1},{4,6},{5,7},{6,4},{7,5},{8,10},{9,11},{10,... | collective-permute-start | bytes 3145736 | tf_op jit(solution)/shard_map/ppermute | solution.py:299
  869.3 47.2 %collective-permute-start.68 = (f32[2,512,256]{2,1,0:T(8,128)S(1)}, f32[2,512,256]{2,1,0:T(8,128)S(1)}, u32[]{:S(2)}, u32[]{:S(2)}) collective-permute-start(f32[2,512,256]{2,1,0:T(8,128)S(1)} %constant_dynamic-slice_fusion.7), channel_id=1, source_target_pairs={{0,1},{1,2},{2,3},{3,0},{4,5},{5,6},{6,7},{7,4},{8,9},{9,10},{10,1... | collective-permute-start | bytes 3145736 | tf_op jit(solution)/shard_map/ppermute | solution.py:299
  870.2 47.4 %collective-permute-start.69 = (f32[2,512,256]{2,1,0:T(8,128)S(1)}, f32[2,512,256]{2,1,0:T(8,128)S(1)}, u32[]{:S(2)}, u32[]{:S(2)}) collective-permute-start(f32[2,512,256]{2,1,0:T(8,128)S(1)} %constant_dynamic-slice_fusion.6), channel_id=1, source_target_pairs={{0,3},{1,0},{2,1},{3,2},{4,7},{5,4},{6,5},{7,6},{8,11},{9,8},{10,9... | collective-permute-start | bytes 3145736 | tf_op jit(solution)/shard_map/ppermute | solution.py:299
  950.8 25.4 %collective-permute-start.71 = (f32[256,1024]{1,0:T(8,128)S(1)}, f32[256,1024]{1,0:T(8,128)}, u32[]{:S(2)}, u32[]{:S(2)}) collective-permute-start(f32[256,1024]{1,0:T(8,128)S(1)} %dynamic-slice_bitcast_fusion.1), channel_id=1, source_target_pairs={{0,2},{1,3},{2,0},{3,1},{4,6},{5,7},{6,4},{7,5},{8,10},{9,11},{10,... | collective-permute-start | bytes 3145736 | tf_op jit(solution)/shard_map/ppermute | solution.py:421
  977.7 8.9 collective-permute-start.78
  981.8 9.7 collective-permute-start.76
  982.8 17.0 %collective-permute-start.75 = (f32[256,128]{1,0:T(8,128)S(1)}, f32[256,128]{1,0:T(8,128)S(1)}, u32[]{:S(2)}, u32[]{:S(2)}) collective-permute-start(f32[256,128]{1,0:T(8,128)S(1)} %get-tuple-element.186), channel_id=1, source_target_pairs={{0,20},{4,16},{8,28},{12,24},{16,4},{20,0},{24,12},{28,8},{1,21},{... | collective-permute-start | bytes 393224 | tf_op jit(solution)/shard_map/ppermute | solution.py:429
  983.4 16.4 %collective-permute-start.74 = (f32[256,128]{1,0:T(8,128)S(1)}, f32[256,128]{1,0:T(8,128)S(1)}, u32[]{:S(2)}, u32[]{:S(2)}) collective-permute-start(f32[256,128]{1,0:T(8,128)S(1)} %get-tuple-element.187), channel_id=1, source_target_pairs={{0,24},{4,28},{8,0},{12,4},{16,8},{20,12},{24,16},{28,20},{1,25},{... | collective-permute-start | bytes 393224 | tf_op jit(solution)/shard_map/ppermute | solution.py:429
  986.6 13.2 %collective-permute-start.73 = (f32[256,128]{1,0:T(8,128)S(1)}, f32[256,128]{1,0:T(8,128)S(1)}, u32[]{:S(2)}, u32[]{:S(2)}) collective-permute-start(f32[256,128]{1,0:T(8,128)S(1)} %get-tuple-element.188), channel_id=1, source_target_pairs={{0,12},{4,8},{8,20},{12,16},{16,28},{20,24},{24,4},{28,0},{1,13},{... | collective-permute-start | bytes 393224 | tf_op jit(solution)/shard_map/ppermute | solution.py:429
  990.1 14.7 %collective-permute-start.72 = (f32[256,128]{1,0:T(8,128)S(1)}, f32[256,128]{1,0:T(8,128)S(1)}, u32[]{:S(2)}, u32[]{:S(2)}) collective-permute-start(f32[256,128]{1,0:T(8,128)S(1)} %get-tuple-element.182), channel_id=1, source_target_pairs={{0,16},{4,20},{8,24},{12,28},{16,0},{20,4},{24,8},{28,12},{1,17},{... | collective-permute-start | bytes 393224 | tf_op jit(solution)/shard_map/ppermute | solution.py:429
  (43 other events, 310.4 us)

commit v11 on v8

--- a/solution.py
+++ b/solution.py
@@ -112,7 +112,7 @@
     depth, blocks, width_x, width = cells.shape
     rank = basis.shape[1]
     width_y = blocks * width
-    block = 2 if depth % 2 == 0 else 1
+    block = 4 if depth % 4 == 0 else 1
     steps = depth // block
     return pl.pallas_call(
         functools.partial(core_body, steps, total),
@@ -130,7 +130,7 @@
             pltpu.VMEM((width_y, width_y), F32),
             pltpu.VMEM((width_y, width_y), F32),
         ],
-        compiler_params=pltpu.CompilerParams(vmem_limit_bytes=48 * MIB),
+        compiler_params=pltpu.CompilerParams(vmem_limit_bytes=56 * MIB),
         cost_estimate=pl.CostEstimate(
             flops=6 * rank * cells.size + 4 * rank * depth * width_y * width_y,
             bytes_accessed=cells.size * 4,

time: 999 us -> 1000 us (level)
  transfers between devices with their start and end apart: 79 -> 79, of which waited for: 31 -> 32; matrix products, arithmetic and copies ran while one was open for 12% -> 12% of each run, Pallas kernels for 12% -> 12%
where the time goes in v11:
time: 1000 us; the launch traced here: 991 us
  waiting for transfers between devices  425 us (42%)
  starting transfers between devices  282 us (28%)
  Pallas kernels  147 us (15%)
  local copies, waits for them, and re-layouts  129 us (13%)
    ppermute x50, waiting for transfers between devices, send(): got = lax.ppermute(tie(value, self.done(0)), axis, perm)  344 us
    ppermute x50, starting transfers between devices, send(): got = lax.ppermute(tie(value, self.done(0)), axis, perm)  242 us
    pallas_call x40, Pallas kernels, pack(): pl.pallas_call(pack_body, grid_spec=pltpu.PrefetchScalarGridSpec(num_scal...  62.9 us
    dynamic_update_slice x35, local copies, waits for them, and re-layouts, to_gx(): lax.dynamic_update_slice_in_dim(whole, got[:, None], moved(g, a, b, -1),...  40.9 us
    pallas_call x1, Pallas kernels, iterate(): pl.pallas_call(functools.partial(iterate_body, total), in_specs=[pl.Block...  34 us
    dynamic_update_slice x15, local copies, waits for them, and re-layouts, to_yz(): lax.dynamic_update_slice(cells, got[:, None], (first // m, (q - d) % m, 0...  31.2 us
    ppermute x3, waiting for transfers between devices, on_device(): pieces = [summed] + [lax.ppermute(summed, 'yz', yz_perm(d)) for d in turns]  26.1 us
    pallas_call x5, Pallas kernels, gram_of(): pl.pallas_call(functools.partial(gram_body, steps), grid=(steps,), in_spe...  25.8 us
  transfers between devices with their start and end apart: 79, of which 32 were waited for; matrix products, arithmetic and copies ran while one was open for 12% of the time, Pallas kernels for 12%

profile of v11, /device:TPU:0, one launch (start us, length us, event | category | flops | bytes accessed | tf_op | source)
XLA Modules:
  0.0 990.6 jit_solution(14453324567962683404)
XLA Ops:
  2.9 4.0 collective-permute-start
  34.3 20.4 %collective-permute-done = f32[16,64,256]{2,1,0:T(8,128)} collective-permute-done((f32[16,64,256]{2,1,0:T(8,128)}, f32[16,64,256]{2,1,0:T(8,128)}, u32[]{:S(2)}, u32[]{:S(2)}) %collective-permute-start) | collective-permute-done | bytes 1048608 | tf_op jit(solution)/shard_map/ppermute | solution.py:299
  56.8 21.0 %collective-permute-done.1 = f32[16,64,256]{2,1,0:T(8,128)} collective-permute-done((f32[16,64,256]{2,1,0:T(8,128)}, f32[16,64,256]{2,1,0:T(8,128)}, u32[]{:S(2)}, u32[]{:S(2)}) %collective-permute-start.1) | collective-permute-done | bytes 1048608 | tf_op jit(solution)/shard_map/ppermute | solution.py:299
  77.9 42.9 %collective-permute-start.2 = (f32[16,64,256]{2,1,0:T(8,128)}, f32[16,64,256]{2,1,0:T(8,128)}, u32[]{:S(2)}, u32[]{:S(2)}) collective-permute-start(f32[16,64,256]{2,1,0:T(8,128)} %pack_z.41), channel_id=1, source_target_pairs={{0,16},{4,20},{8,24},{12,28},{16,0},{20,4},{24,8},{28,12},{1,17},{... | collective-permute-start | bytes 3145736 | tf_op jit(solution)/shard_map/ppermute | solution.py:299
  122.9 44.5 %collective-permute-done.4 = f32[16,64,256]{2,1,0:T(8,128)} collective-permute-done((f32[16,64,256]{2,1,0:T(8,128)}, f32[16,64,256]{2,1,0:T(8,128)}, u32[]{:S(2)}, u32[]{:S(2)}) %collective-permute-start.4) | collective-permute-done | bytes 1048608 | tf_op jit(solution)/shard_map/ppermute | solution.py:299
  169.7 3.4 collective-permute-start.7
  176.3 5.1 collective-permute-start.10
  189.1 51.2 %collective-permute-done.8 = f32[16,64,256]{2,1,0:T(8,128)} collective-permute-done((f32[16,64,256]{2,1,0:T(8,128)S(1)}, f32[16,64,256]{2,1,0:T(8,128)}, u32[]{:S(2)}, u32[]{:S(2)}) %collective-permute-start.8) | collective-permute-done | bytes 1048608 | tf_op jit(solution)/shard_map/ppermute | solution.py:299
  240.3 41.0 %collective-permute-start.9 = (f32[16,64,256]{2,1,0:T(8,128)S(1)}, f32[16,64,256]{2,1,0:T(8,128)}, u32[]{:S(2)}, u32[]{:S(2)}) collective-permute-start(f32[16,64,256]{2,1,0:T(8,128)S(1)} %pack_z.48), channel_id=1, source_target_pairs={{0,20},{4,16},{8,28},{12,24},{16,4},{20,0},{24,12},{28,8},{1,21},{... | collective-permute-start | bytes 3145736 | tf_op jit(solution)/shard_map/ppermute | solution.py:299
  288.1 2.9 collective-permute-start.13
  296.8 5.8 gram_x.5.before_ref
  307.8 11.6 %broadcast_in_dim.227 = f32[16,4,512,256]{3,2,1,0:T(8,128)} broadcast(f32[]{:T(128)} %constant.1232.clone.1), dimensions={} | broadcast | bytes 33554436 | tf_op jit(solution)/shard_map/broadcast_in_dim | solution.py:340
  325.4 25.2 %collective-permute-done.9 = f32[16,64,256]{2,1,0:T(8,128)} collective-permute-done((f32[16,64,256]{2,1,0:T(8,128)S(1)}, f32[16,64,256]{2,1,0:T(8,128)}, u32[]{:S(2)}, u32[]{:S(2)}) %collective-permute-start.9) | collective-permute-done | bytes 1048608 | tf_op jit(solution)/shard_map/ppermute | solution.py:299
  356.4 2.3 bitcast_dynamic-update-slice_fusion.35
  367.8 57.3 %collective-permute-start.16 = (f32[16,64,256]{2,1,0:T(8,128)}, f32[16,64,256]{2,1,0:T(8,128)S(1)}, u32[]{:S(2)}, u32[]{:S(2)}) collective-permute-start(f32[16,64,256]{2,1,0:T(8,128)} %pack_z.56), channel_id=1, source_target_pairs={{0,12},{4,8},{8,20},{12,16},{16,28},{20,24},{24,4},{28,0},{1,13},{... | collective-permute-start | bytes 3145736 | tf_op jit(solution)/shard_map/ppermute | solution.py:299
  426.6 12.7 %collective-permute-done.21 = f32[16,64,256]{2,1,0:T(8,128)} collective-permute-done((f32[16,64,256]{2,1,0:T(8,128)S(1)}, f32[16,64,256]{2,1,0:T(8,128)}, u32[]{:S(2)}, u32[]{:S(2)}) %collective-permute-start.21) | collective-permute-done | bytes 1048608 | tf_op jit(solution)/shard_map/ppermute | solution.py:299
  440.8 5.9 gram_x.6.before_ref
  448.2 4.4 broadcast.69.clone.2
  454.8 3.1 bitcast_dynamic-update-slice_fusion.5
  462.2 7.0 collective-permute-done.18
  469.3 5.3 collective-permute-start.19
  475.9 19.3 %collective-permute-start.27 = (f32[16,64,256]{2,1,0:T(8,128)S(1)}, f32[16,64,256]{2,1,0:T(8,128)S(1)}, u32[]{:S(2)}, u32[]{:S(2)}) collective-permute-start(f32[16,64,256]{2,1,0:T(8,128)S(1)} %pack_z.65), channel_id=1, source_target_pairs={{0,8},{4,12},{8,16},{12,20},{16,24},{20,28},{24,0},{28,4},{1,9},{5... | collective-permute-start | bytes 3145736 | tf_op jit(solution)/shard_map/ppermute | solution.py:299
  495.2 2.9 collective-permute-start.28
  502.7 3.1 bitcast_dynamic-update-slice_fusion.4
  510.2 3.1 bitcast_dynamic-update-slice_fusion.9
  518.0 58.8 %collective-permute-done.28 = f32[16,64,256]{2,1,0:T(8,128)} collective-permute-done((f32[16,64,256]{2,1,0:T(8,128)S(1)}, f32[16,64,256]{2,1,0:T(8,128)}, u32[]{:S(2)}, u32[]{:S(2)}) %collective-permute-start.28) | collective-permute-done | bytes 1048608 | tf_op jit(solution)/shard_map/ppermute | solution.py:299
  590.1 12.5 %collective-permute-start.20 = (f32[8,64,256]{2,1,0:T(8,128)S(1)}, f32[8,64,256]{2,1,0:T(8,128)S(1)}, u32[]{:S(2)}, u32[]{:S(2)}) collective-permute-start(f32[8,64,256]{2,1,0:T(8,128)S(1)} %pack_z.57), channel_id=1, source_target_pairs={{0,24},{4,28},{8,0},{12,4},{16,8},{20,12},{24,16},{28,20},{1,25},{... | collective-permute-start | bytes 1572872 | tf_op jit(solution)/shard_map/ppermute | solution.py:299
  602.7 7.7 gram_x.7.before_ref
  611.6 3.0 constant_dynamic-slice_fusion.13
  614.6 3.1 bitcast_dynamic-update-slice_fusion.3
  620.5 7.2 collective-permute-done.31
  628.9 4.6 collective-permute-start.34
  633.7 3.0 constant_dynamic-slice_fusion.16
  638.0 5.1 collective-permute-start.37
  643.1 3.1 bitcast_dynamic-update-slice_fusion.2
  646.2 3.0 constant_dynamic-slice_fusion.14
  649.2 3.1 bitcast_dynamic-update-slice_fusion.8
  652.3 41.9 %collective-permute-done.30 = f32[8,64,256]{2,1,0:T(8,128)S(1)} collective-permute-done((f32[8,64,256]{2,1,0:T(8,128)S(1)}, f32[8,64,256]{2,1,0:T(8,128)S(1)}, u32[]{:S(2)}, u32[]{:S(2)}) %collective-permute-start.30) | collective-permute-done | bytes 524320 | tf_op jit(solution)/shard_map/ppermute | solution.py:299
  707.9 4.6 collective-permute-start.35
  712.5 3.2 gram_x.8.before_ref
  715.7 3.1 bitcast_dynamic-update-slice_fusion.1
  718.8 22.4 %collective-permute-done.38 = f32[4,512,256]{2,1,0:T(8,128)} collective-permute-done((f32[4,512,256]{2,1,0:T(8,128)}, f32[4,512,256]{2,1,0:T(8,128)}, u32[]{:S(2)}, u32[]{:S(2)}) %collective-permute-start.38) | collective-permute-done | bytes 2097184 | tf_op jit(solution)/shard_map/ppermute | solution.py:299
  743.3 3.8 collective-permute-start.43
  749.2 20.0 %collective-permute-done.39 = f32[8,64,256]{2,1,0:T(8,128)} collective-permute-done((f32[8,64,256]{2,1,0:T(8,128)S(1)}, f32[8,64,256]{2,1,0:T(8,128)}, u32[]{:S(2)}, u32[]{:S(2)}) %collective-permute-start.39) | collective-permute-done | bytes 524320 | tf_op jit(solution)/shard_map/ppermute | solution.py:299
  771.5 6.8 collective-permute-done.43
  778.4 3.2 gram_x.9
  783.8 3.1 bitcast_dynamic-update-slice_fusion
  786.9 2.8 collective-permute-done.46
  791.6 3.7 collective-permute-done.44
  807.4 2.6 collective-permute-done.48
  810.8 2.7 collective-permute-start.55
  818.0 3.6 collective-permute-start.60
  823.8 2.5 collective-permute-start.61
  829.2 4.3 collective-permute-done.61.refs_1_
  833.6 21.8 %collective-permute-done.62.refs_2_ = f32[128,512]{1,0:T(8,128)S(1)} collective-permute-done((f32[128,512]{1,0:T(8,128)S(1)}, f32[128,512]{1,0:T(8,128)S(1)}, u32[]{:S(2)}, u32[]{:S(2)}) %collective-permute-start.62) | collective-permute-done | bytes 262176 | tf_op jit(solution)/shard_map/ppermute | solution.py:395
  856.2 2.7 collective-permute-start.69
  858.9 34.0 %subspace.1.basis_ref = f32[512,128]{1,0:T(8,128)} custom-call(s32[4]{0:T(128)S(1)} %pad_add_fusion.places_ref, f32[128,512]{1,0:T(8,128)S(1)} %bitcast.356, f32[128,512]{1,0:T(8,128)S(1)} %collective-permute-done.61.refs_1_, f32[128,512]{1,0:T(8,128)S(1)} %collective-permute-done.62.refs_2_, f32[128,512]{1,0:T(8,128)S(1)} %collective-permute-done.63.refs_3_, ...), custom_call_target="tpu_custom_call" | custom-call | flops 40000000000 | bytes 524288 | tf_op jit(solution)/shard_map/subspace/pallas_call | solution.py:228
  897.2 3.1 collective-permute-done.68
  904.5 23.8 %core_gram_y.1 = f32[1024,1024]{1,0:T(8,128)} custom-call(f32[16,4,512,256]{3,2,1,0:T(8,128)} %bitcast_dynamic-update-slice_fusion.40.field_ref, f32[512,128]{1,0:T(8,128)} %subspace.1.basis_ref), custom_call_target="tpu_custom_call" | custom-call | flops 15032385536 | bytes 33554432 | tf_op jit(solution)/shard_map/core_gram_y/pallas_call | solution.py:117
  930.2 4.2 collective-permute-done.70
  934.4 2.6 bitcast_add_fusion
  939.1 23.8 %collective-permute-done.71 = f32[256,1024]{1,0:T(8,128)} collective-permute-done((f32[256,1024]{1,0:T(8,128)S(1)}, f32[256,1024]{1,0:T(8,128)}, u32[]{:S(2)}, u32[]{:S(2)}) %collective-permute-start.71) | collective-permute-done | bytes 1048608 | tf_op jit(solution)/shard_map/ppermute | solution.py:417
  973.6 5.1 collective-permute-start.72
  982.6 7.1 collective-permute-done.72
  (286 shorter events, 205.7 us)
Async XLA Ops:
  2.9 51.7 %collective-permute-start = (f32[16,64,256]{2,1,0:T(8,128)}, f32[16,64,256]{2,1,0:T(8,128)}, u32[]{:S(2)}, u32[]{:S(2)}) collective-permute-start(f32[16,64,256]{2,1,0:T(8,128)} %pack_z.40), channel_id=1, source_target_pairs={{0,16},{4,20},{8,24},{12,28},{16,0},{20,4},{24,8},{28,12},{1,17},{... | collective-permute-start | bytes 3145736 | tf_op jit(solution)/shard_map/ppermute | solution.py:299
  9.2 68.7 %collective-permute-start.1 = (f32[16,64,256]{2,1,0:T(8,128)}, f32[16,64,256]{2,1,0:T(8,128)}, u32[]{:S(2)}, u32[]{:S(2)}) collective-permute-start(f32[16,64,256]{2,1,0:T(8,128)} %pack_z.42), channel_id=1, source_target_pairs={{0,24},{4,28},{8,0},{12,4},{16,8},{20,12},{24,16},{28,20},{1,25},{... | collective-permute-start | bytes 3145736 | tf_op jit(solution)/shard_map/ppermute | solution.py:299
  12.7 108.0 %collective-permute-start.3 = (f32[16,64,256]{2,1,0:T(8,128)}, f32[16,64,256]{2,1,0:T(8,128)}, u32[]{:S(2)}, u32[]{:S(2)}) collective-permute-start(f32[16,64,256]{2,1,0:T(8,128)} %pack_z.43), channel_id=1, source_target_pairs={{0,12},{4,8},{8,20},{12,16},{16,28},{20,24},{24,4},{28,0},{1,13},{... | collective-permute-start | bytes 3145736 | tf_op jit(solution)/shard_map/ppermute | solution.py:299
  16.6 150.8 %collective-permute-start.4 = (f32[16,64,256]{2,1,0:T(8,128)}, f32[16,64,256]{2,1,0:T(8,128)}, u32[]{:S(2)}, u32[]{:S(2)}) collective-permute-start(f32[16,64,256]{2,1,0:T(8,128)} %pack_z.45), channel_id=1, source_target_pairs={{0,20},{4,16},{8,28},{12,24},{16,4},{20,0},{24,12},{28,8},{1,21},{... | collective-permute-start | bytes 3145736 | tf_op jit(solution)/shard_map/ppermute | solution.py:299
  19.8 149.9 %collective-permute-start.6 = (f32[16,64,256]{2,1,0:T(8,128)}, f32[16,64,256]{2,1,0:T(8,128)}, u32[]{:S(2)}, u32[]{:S(2)}) collective-permute-start(f32[16,64,256]{2,1,0:T(8,128)} %pack_z.47), channel_id=1, source_target_pairs={{0,4},{4,0},{8,12},{12,8},{16,20},{20,16},{24,28},{28,24},{1,5},{5... | collective-permute-start | bytes 3145736 | tf_op jit(solution)/shard_map/ppermute | solution.py:299
  77.9 208.0 %collective-permute-start.2 = (f32[16,64,256]{2,1,0:T(8,128)}, f32[16,64,256]{2,1,0:T(8,128)}, u32[]{:S(2)}, u32[]{:S(2)}) collective-permute-start(f32[16,64,256]{2,1,0:T(8,128)} %pack_z.41), channel_id=1, source_target_pairs={{0,16},{4,20},{8,24},{12,28},{16,0},{20,4},{24,8},{28,12},{1,17},{... | collective-permute-start | bytes 3145736 | tf_op jit(solution)/shard_map/ppermute | solution.py:299
  167.4 117.1 %collective-permute-start.5 = (f32[16,64,256]{2,1,0:T(8,128)}, f32[16,64,256]{2,1,0:T(8,128)}, u32[]{:S(2)}, u32[]{:S(2)}) collective-permute-start(f32[16,64,256]{2,1,0:T(8,128)} %pack_z.44), channel_id=1, source_target_pairs={{0,12},{4,8},{8,20},{12,16},{16,28},{20,24},{24,4},{28,0},{1,13},{... | collective-permute-start | bytes 3145736 | tf_op jit(solution)/shard_map/ppermute | solution.py:299
  169.7 118.4 %collective-permute-start.7 = (f32[16,64,256]{2,1,0:T(8,128)}, f32[16,64,256]{2,1,0:T(8,128)}, u32[]{:S(2)}, u32[]{:S(2)}) collective-permute-start(f32[16,64,256]{2,1,0:T(8,128)} %pack_z.46), channel_id=1, source_target_pairs={{0,24},{4,28},{8,0},{12,4},{16,8},{20,12},{24,16},{28,20},{1,25},{... | collective-permute-start | bytes 3145736 | tf_op jit(solution)/shard_map/ppermute | solution.py:299
  174.7 65.6 %collective-permute-start.8 = (f32[16,64,256]{2,1,0:T(8,128)S(1)}, f32[16,64,256]{2,1,0:T(8,128)}, u32[]{:S(2)}, u32[]{:S(2)}) collective-permute-start(f32[16,64,256]{2,1,0:T(8,128)S(1)} %copy-done.6), channel_id=1, source_target_pairs={{0,8},{4,12},{8,16},{12,20},{16,24},{20,28},{24,0},{28,4},{1,9},{5... | collective-permute-start | bytes 3145736 | tf_op jit(solution)/shard_map/ppermute | solution.py:299
  176.3 105.0 %collective-permute-start.10 = (f32[16,64,256]{2,1,0:T(8,128)S(1)}, f32[16,64,256]{2,1,0:T(8,128)S(1)}, u32[]{:S(2)}, u32[]{:S(2)}) collective-permute-start(f32[16,64,256]{2,1,0:T(8,128)S(1)} %copy-done.8), channel_id=1, source_target_pairs={{0,28},{4,24},{8,4},{12,0},{16,12},{20,8},{24,20},{28,16},{1,29},{... | collective-permute-start | bytes 3145736 | tf_op jit(solution)/shard_map/ppermute | solution.py:299
  240.3 110.4 %collective-permute-start.9 = (f32[16,64,256]{2,1,0:T(8,128)S(1)}, f32[16,64,256]{2,1,0:T(8,128)}, u32[]{:S(2)}, u32[]{:S(2)}) collective-permute-start(f32[16,64,256]{2,1,0:T(8,128)S(1)} %pack_z.48), channel_id=1, source_target_pairs={{0,20},{4,16},{8,28},{12,24},{16,4},{20,0},{24,12},{28,8},{1,21},{... | collective-permute-start | bytes 3145736 | tf_op jit(solution)/shard_map/ppermute | solution.py:299
  281.3 69.3 %collective-permute-start.11 = (f32[16,64,256]{2,1,0:T(8,128)S(1)}, f32[16,64,256]{2,1,0:T(8,128)}, u32[]{:S(2)}, u32[]{:S(2)}) collective-permute-start(f32[16,64,256]{2,1,0:T(8,128)S(1)} %pack_z.50), channel_id=1, source_target_pairs={{0,4},{4,0},{8,12},{12,8},{16,20},{20,16},{24,28},{28,24},{1,5},{5... | collective-permute-start | bytes 3145736 | tf_op jit(solution)/shard_map/ppermute | solution.py:299
  284.5 67.7 %collective-permute-start.12 = (f32[16,64,256]{2,1,0:T(8,128)}, f32[16,64,256]{2,1,0:T(8,128)}, u32[]{:S(2)}, u32[]{:S(2)}) collective-permute-start(f32[16,64,256]{2,1,0:T(8,128)} %pack_z.52), channel_id=1, source_target_pairs={{0,8},{4,12},{8,16},{12,20},{16,24},{20,28},{24,0},{28,4},{1,9},{5... | collective-permute-start | bytes 3145736 | tf_op jit(solution)/shard_map/ppermute | solution.py:299
  288.1 72.8 %collective-permute-start.13 = (f32[16,64,256]{2,1,0:T(8,128)}, f32[16,64,256]{2,1,0:T(8,128)S(1)}, u32[]{:S(2)}, u32[]{:S(2)}) collective-permute-start(f32[16,64,256]{2,1,0:T(8,128)} %pack_z.53), channel_id=1, source_target_pairs={{0,28},{4,24},{8,4},{12,0},{16,12},{20,8},{24,20},{28,16},{1,29},{... | collective-permute-start | bytes 3145736 | tf_op jit(solution)/shard_map/ppermute | solution.py:299
  295.2 72.6 %collective-permute-start.15 = (f32[4,512,256]{2,1,0:T(8,128)}, f32[4,512,256]{2,1,0:T(8,128)}, u32[]{:S(2)}, u32[]{:S(2)}) collective-permute-start(f32[4,512,256]{2,1,0:T(8,128)} %constant_dynamic-slice_fusion.19), channel_id=1, source_target_pairs={{0,2},{1,3},{2,0},{3,1},{4,6},{5,7},{6,4},{7,5},{8,10},{9,11},{10,... | collective-permute-start | bytes 6291464 | tf_op jit(solution)/shard_map/ppermute | solution.py:299
  350.6 107.2 %collective-permute-start.14 = (f32[4,512,256]{2,1,0:T(8,128)}, f32[4,512,256]{2,1,0:T(8,128)}, u32[]{:S(2)}, u32[]{:S(2)}) collective-permute-start(f32[4,512,256]{2,1,0:T(8,128)} %constant_dynamic-slice_fusion.21), channel_id=1, source_target_pairs={{0,1},{1,2},{2,3},{3,0},{4,5},{5,6},{6,7},{7,4},{8,9},{9,10},{10,1... | collective-permute-start | bytes 6291464 | tf_op jit(solution)/shard_map/ppermute | solution.py:299
  350.7 88.7 %collective-permute-start.21 = (f32[16,64,256]{2,1,0:T(8,128)S(1)}, f32[16,64,256]{2,1,0:T(8,128)}, u32[]{:S(2)}, u32[]{:S(2)}) collective-permute-start(f32[16,64,256]{2,1,0:T(8,128)S(1)} %pack_z.64), channel_id=1, source_target_pairs={{0,16},{4,20},{8,24},{12,28},{16,0},{20,4},{24,8},{28,12},{1,17},{... | collective-permute-start | bytes 3145736 | tf_op jit(solution)/shard_map/ppermute | solution.py:299
  352.2 123.7 %collective-permute-start.26 = (f32[4,512,256]{2,1,0:T(8,128)}, f32[4,512,256]{2,1,0:T(8,128)}, u32[]{:S(2)}, u32[]{:S(2)}) collective-permute-start(f32[4,512,256]{2,1,0:T(8,128)} %constant_dynamic-slice_fusion.18), channel_id=1, source_target_pairs={{0,3},{1,0},{2,1},{3,2},{4,7},{5,4},{6,5},{7,6},{8,11},{9,8},{10,9... | collective-permute-start | bytes 6291464 | tf_op jit(solution)/shard_map/ppermute | solution.py:299
  367.8 91.5 %collective-permute-start.16 = (f32[16,64,256]{2,1,0:T(8,128)}, f32[16,64,256]{2,1,0:T(8,128)S(1)}, u32[]{:S(2)}, u32[]{:S(2)}) collective-permute-start(f32[16,64,256]{2,1,0:T(8,128)} %pack_z.56), channel_id=1, source_target_pairs={{0,12},{4,8},{8,20},{12,16},{16,28},{20,24},{24,4},{28,0},{1,13},{... | collective-permute-start | bytes 3145736 | tf_op jit(solution)/shard_map/ppermute | solution.py:299
  426.6 42.7 %collective-permute-start.18 = (f32[16,64,256]{2,1,0:T(8,128)S(1)}, f32[16,64,256]{2,1,0:T(8,128)}, u32[]{:S(2)}, u32[]{:S(2)}) collective-permute-start(f32[16,64,256]{2,1,0:T(8,128)S(1)} %pack_z.59), channel_id=1, source_target_pairs={{0,24},{4,28},{8,0},{12,4},{16,8},{20,12},{24,16},{28,20},{1,25},{... | collective-permute-start | bytes 3145736 | tf_op jit(solution)/shard_map/ppermute | solution.py:299
  439.3 36.5 %collective-permute-start.22 = (f32[16,64,256]{2,1,0:T(8,128)S(1)}, f32[16,64,256]{2,1,0:T(8,128)}, u32[]{:S(2)}, u32[]{:S(2)}) collective-permute-start(f32[16,64,256]{2,1,0:T(8,128)S(1)} %pack_z.63), channel_id=1, source_target_pairs={{0,4},{4,0},{8,12},{12,8},{16,20},{20,16},{24,28},{28,24},{1,5},{5... | collective-permute-start | bytes 3145736 | tf_op jit(solution)/shard_map/ppermute | solution.py:299
  459.3 129.6 %collective-permute-start.17 = (f32[4,512,256]{2,1,0:T(8,128)}, f32[4,512,256]{2,1,0:T(8,128)}, u32[]{:S(2)}, u32[]{:S(2)}) collective-permute-start(f32[4,512,256]{2,1,0:T(8,128)} %constant_dynamic-slice_fusion.20), channel_id=1, source_target_pairs={{0,2},{1,3},{2,0},{3,1},{4,6},{5,7},{6,4},{7,5},{8,10},{9,11},{10,... | collective-permute-start | bytes 6291464 | tf_op jit(solution)/shard_map/ppermute | solution.py:299
  469.3 45.8 %collective-permute-start.19 = (f32[16,64,256]{2,1,0:T(8,128)S(1)}, f32[16,64,256]{2,1,0:T(8,128)}, u32[]{:S(2)}, u32[]{:S(2)}) collective-permute-start(f32[16,64,256]{2,1,0:T(8,128)S(1)} %pack_z.58), channel_id=1, source_target_pairs={{0,28},{4,24},{8,4},{12,0},{16,12},{20,8},{24,20},{28,16},{1,29},{... | collective-permute-start | bytes 3145736 | tf_op jit(solution)/shard_map/ppermute | solution.py:299
  475.8 37.5 %collective-permute-start.23 = (f32[8,64,256]{2,1,0:T(8,128)S(1)}, f32[8,64,256]{2,1,0:T(8,128)S(1)}, u32[]{:S(2)}, u32[]{:S(2)}) collective-permute-start(f32[8,64,256]{2,1,0:T(8,128)S(1)} %pack_z.62), channel_id=1, source_target_pairs={{0,16},{4,20},{8,24},{12,28},{16,0},{20,4},{24,8},{28,12},{1,17},{... | collective-permute-start | bytes 1572872 | tf_op jit(solution)/shard_map/ppermute | solution.py:299
  475.9 101.0 %collective-permute-start.27 = (f32[16,64,256]{2,1,0:T(8,128)S(1)}, f32[16,64,256]{2,1,0:T(8,128)S(1)}, u32[]{:S(2)}, u32[]{:S(2)}) collective-permute-start(f32[16,64,256]{2,1,0:T(8,128)S(1)} %pack_z.65), channel_id=1, source_target_pairs={{0,8},{4,12},{8,16},{12,20},{16,24},{20,28},{24,0},{28,4},{1,9},{5... | collective-permute-start | bytes 3145736 | tf_op jit(solution)/shard_map/ppermute | solution.py:299
  495.2 81.6 %collective-permute-start.28 = (f32[16,64,256]{2,1,0:T(8,128)S(1)}, f32[16,64,256]{2,1,0:T(8,128)}, u32[]{:S(2)}, u32[]{:S(2)}) collective-permute-start(f32[16,64,256]{2,1,0:T(8,128)S(1)} %pack_z.67), channel_id=1, source_target_pairs={{0,20},{4,16},{8,28},{12,24},{16,4},{20,0},{24,12},{28,8},{1,21},{... | collective-permute-start | bytes 3145736 | tf_op jit(solution)/shard_map/ppermute | solution.py:299
  516.4 95.1 %collective-permute-start.24 = (f32[8,64,256]{2,1,0:T(8,128)S(1)}, f32[8,64,256]{2,1,0:T(8,128)S(1)}, u32[]{:S(2)}, u32[]{:S(2)}) collective-permute-start(f32[8,64,256]{2,1,0:T(8,128)S(1)} %pack_z.61), channel_id=1, source_target_pairs={{0,4},{4,0},{8,12},{12,8},{16,20},{20,16},{24,28},{28,24},{1,5},{5... | collective-permute-start | bytes 1572872 | tf_op jit(solution)/shard_map/ppermute | solution.py:299
  576.9 56.7 %collective-permute-start.29 = (f32[4,512,256]{2,1,0:T(8,128)}, f32[4,512,256]{2,1,0:T(8,128)}, u32[]{:S(2)}, u32[]{:S(2)}) collective-permute-start(f32[4,512,256]{2,1,0:T(8,128)} %constant_dynamic-slice_fusion.17), channel_id=1, source_target_pairs={{0,1},{1,2},{2,3},{3,0},{4,5},{5,6},{6,7},{7,4},{8,9},{9,10},{10,1... | collective-permute-start | bytes 6291464 | tf_op jit(solution)/shard_map/ppermute | solution.py:299
  576.9 61.1 %collective-permute-start.36 = (f32[4,512,256]{2,1,0:T(8,128)S(1)}, f32[4,512,256]{2,1,0:T(8,128)S(1)}, u32[]{:S(2)}, u32[]{:S(2)}) collective-permute-start(f32[4,512,256]{2,1,0:T(8,128)S(1)} %copy-done.12), channel_id=1, source_target_pairs={{0,3},{1,0},{2,1},{3,2},{4,7},{5,4},{6,5},{7,6},{8,11},{9,8},{10,9... | collective-permute-start | bytes 6291464 | tf_op jit(solution)/shard_map/ppermute | solution.py:299
  590.1 27.6 %collective-permute-start.20 = (f32[8,64,256]{2,1,0:T(8,128)S(1)}, f32[8,64,256]{2,1,0:T(8,128)S(1)}, u32[]{:S(2)}, u32[]{:S(2)}) collective-permute-start(f32[8,64,256]{2,1,0:T(8,128)S(1)} %pack_z.57), channel_id=1, source_target_pairs={{0,24},{4,28},{8,0},{12,4},{16,8},{20,12},{24,16},{28,20},{1,25},{... | collective-permute-start | bytes 1572872 | tf_op jit(solution)/shard_map/ppermute | solution.py:299
  602.6 25.0 %collective-permute-start.31 = (f32[8,64,256]{2,1,0:T(8,128)S(1)}, f32[8,64,256]{2,1,0:T(8,128)S(1)}, u32[]{:S(2)}, u32[]{:S(2)}) collective-permute-start(f32[8,64,256]{2,1,0:T(8,128)S(1)} %pack_z.70), channel_id=1, source_target_pairs={{0,12},{4,8},{8,20},{12,16},{16,28},{20,24},{24,4},{28,0},{1,13},{... | collective-permute-start | bytes 1572872 | tf_op jit(solution)/shard_map/ppermute | solution.py:299
  618.9 80.2 %collective-permute-start.25 = (f32[8,64,256]{2,1,0:T(8,128)S(1)}, f32[8,64,256]{2,1,0:T(8,128)S(1)}, u32[]{:S(2)}, u32[]{:S(2)}) collective-permute-start(f32[8,64,256]{2,1,0:T(8,128)S(1)} %pack_z.60), channel_id=1, source_target_pairs={{0,16},{4,20},{8,24},{12,28},{16,0},{20,4},{24,8},{28,12},{1,17},{... | collective-permute-start | bytes 1572872 | tf_op jit(solution)/shard_map/ppermute | solution.py:299
  628.9 69.0 %collective-permute-start.34 = (f32[8,64,256]{2,1,0:T(8,128)S(1)}, f32[8,64,256]{2,1,0:T(8,128)S(1)}, u32[]{:S(2)}, u32[]{:S(2)}) collective-permute-start(f32[8,64,256]{2,1,0:T(8,128)S(1)} %pack_z.72), channel_id=1, source_target_pairs={{0,28},{4,24},{8,4},{12,0},{16,12},{20,8},{24,20},{28,16},{1,29},{... | collective-permute-start | bytes 1572872 | tf_op jit(solution)/shard_map/ppermute | solution.py:299
  633.6 60.6 %collective-permute-start.30 = (f32[8,64,256]{2,1,0:T(8,128)S(1)}, f32[8,64,256]{2,1,0:T(8,128)S(1)}, u32[]{:S(2)}, u32[]{:S(2)}) collective-permute-start(f32[8,64,256]{2,1,0:T(8,128)S(1)} %pack_z.66), channel_id=1, source_target_pairs={{0,20},{4,16},{8,28},{12,24},{16,4},{20,0},{24,12},{28,8},{1,21},{... | collective-permute-start | bytes 1572872 | tf_op jit(solution)/shard_map/ppermute | solution.py:299
  636.7 69.9 %collective-permute-start.32 = (f32[4,512,256]{2,1,0:T(8,128)}, f32[4,512,256]{2,1,0:T(8,128)}, u32[]{:S(2)}, u32[]{:S(2)}) collective-permute-start(f32[4,512,256]{2,1,0:T(8,128)} %constant_dynamic-slice_fusion.16), channel_id=1, source_target_pairs={{0,2},{1,3},{2,0},{3,1},{4,6},{5,7},{6,4},{7,5},{8,10},{9,11},{10,... | collective-permute-start | bytes 6291464 | tf_op jit(solution)/shard_map/ppermute | solution.py:299
  638.0 56.3 %collective-permute-start.37 = (f32[8,64,256]{2,1,0:T(8,128)S(1)}, f32[8,64,256]{2,1,0:T(8,128)S(1)}, u32[]{:S(2)}, u32[]{:S(2)}) collective-permute-start(f32[8,64,256]{2,1,0:T(8,128)S(1)} %pack_z.73), channel_id=1, source_target_pairs={{0,8},{4,12},{8,16},{12,20},{16,24},{20,28},{24,0},{28,4},{1,9},{5... | collective-permute-start | bytes 1572872 | tf_op jit(solution)/shard_map/ppermute | solution.py:299
  694.2 47.0 %collective-permute-start.38 = (f32[4,512,256]{2,1,0:T(8,128)}, f32[4,512,256]{2,1,0:T(8,128)}, u32[]{:S(2)}, u32[]{:S(2)}) collective-permute-start(f32[4,512,256]{2,1,0:T(8,128)} %constant_dynamic-slice_fusion.14), channel_id=1, source_target_pairs={{0,1},{1,2},{2,3},{3,0},{4,5},{5,6},{6,7},{7,4},{8,9},{9,10},{10,1... | collective-permute-start | bytes 6291464 | tf_op jit(solution)/shard_map/ppermute | solution.py:299
  694.2 47.0 %collective-permute-start.41 = (f32[4,512,256]{2,1,0:T(8,128)}, f32[4,512,256]{2,1,0:T(8,128)S(1)}, u32[]{:S(2)}, u32[]{:S(2)}) collective-permute-start(f32[4,512,256]{2,1,0:T(8,128)} %constant_dynamic-slice_fusion.13), channel_id=1, source_target_pairs={{0,3},{1,0},{2,1},{3,2},{4,7},{5,4},{6,5},{7,6},{8,11},{9,8},{10,9... | collective-permute-start | bytes 6291464 | tf_op jit(solution)/shard_map/ppermute | solution.py:299
  699.1 71.2 %collective-permute-start.40 = (f32[8,64,256]{2,1,0:T(8,128)S(1)}, f32[8,64,256]{2,1,0:T(8,128)S(1)}, u32[]{:S(2)}, u32[]{:S(2)}) collective-permute-start(f32[8,64,256]{2,1,0:T(8,128)S(1)} %pack_z.75), channel_id=1, source_target_pairs={{0,4},{4,0},{8,12},{12,8},{16,20},{20,16},{24,28},{28,24},{1,5},{5... | collective-permute-start | bytes 1572872 | tf_op jit(solution)/shard_map/ppermute | solution.py:299
  706.6 34.6 %collective-permute-start.33 = (f32[8,64,256]{2,1,0:T(8,128)S(1)}, f32[8,64,256]{2,1,0:T(8,128)S(1)}, u32[]{:S(2)}, u32[]{:S(2)}) collective-permute-start(f32[8,64,256]{2,1,0:T(8,128)S(1)} %pack_z.68), channel_id=1, source_target_pairs={{0,12},{4,8},{8,20},{12,16},{16,28},{20,24},{24,4},{28,0},{1,13},{... | collective-permute-start | bytes 1572872 | tf_op jit(solution)/shard_map/ppermute | solution.py:299
  707.9 35.4 %collective-permute-start.35 = (f32[8,64,256]{2,1,0:T(8,128)S(1)}, f32[8,64,256]{2,1,0:T(8,128)}, u32[]{:S(2)}, u32[]{:S(2)}) collective-permute-start(f32[8,64,256]{2,1,0:T(8,128)S(1)} %pack_z.71), channel_id=1, source_target_pairs={{0,24},{4,28},{8,0},{12,4},{16,8},{20,12},{24,16},{28,20},{1,25},{... | collective-permute-start | bytes 1572872 | tf_op jit(solution)/shard_map/ppermute | solution.py:299
  741.2 28.0 %collective-permute-start.39 = (f32[8,64,256]{2,1,0:T(8,128)S(1)}, f32[8,64,256]{2,1,0:T(8,128)}, u32[]{:S(2)}, u32[]{:S(2)}) collective-permute-start(f32[8,64,256]{2,1,0:T(8,128)S(1)} %pack_z.74), channel_id=1, source_target_pairs={{0,20},{4,16},{8,28},{12,24},{16,4},{20,0},{24,12},{28,8},{1,21},{... | collective-permute-start | bytes 1572872 | tf_op jit(solution)/shard_map/ppermute | solution.py:299
  741.2 29.2 %collective-permute-start.42 = (f32[8,64,256]{2,1,0:T(8,128)S(1)}, f32[8,64,256]{2,1,0:T(8,128)}, u32[]{:S(2)}, u32[]{:S(2)}) collective-permute-start(f32[8,64,256]{2,1,0:T(8,128)S(1)} %pack_z.76), channel_id=1, source_target_pairs={{0,8},{4,12},{8,16},{12,20},{16,24},{20,28},{24,0},{28,4},{1,9},{5... | collective-permute-start | bytes 1572872 | tf_op jit(solution)/shard_map/ppermute | solution.py:299
  743.3 35.0 %collective-permute-start.43 = (f32[8,64,256]{2,1,0:T(8,128)S(1)}, f32[8,64,256]{2,1,0:T(8,128)S(1)}, u32[]{:S(2)}, u32[]{:S(2)}) collective-permute-start(f32[8,64,256]{2,1,0:T(8,128)S(1)} %pack_z.77), channel_id=1, source_target_pairs={{0,28},{4,24},{8,4},{12,0},{16,12},{20,8},{24,20},{28,16},{1,29},{... | collective-permute-start | bytes 1572872 | tf_op jit(solution)/shard_map/ppermute | solution.py:299
  747.2 80.8 %collective-permute-start.64 = (f32[2,512,256]{2,1,0:T(8,128)S(1)}, f32[2,512,256]{2,1,0:T(8,128)S(1)}, u32[]{:S(2)}, u32[]{:S(2)}) collective-permute-start(f32[2,512,256]{2,1,0:T(8,128)S(1)} %constant_dynamic-slice_fusion.11), channel_id=1, source_target_pairs={{0,2},{1,3},{2,0},{3,1},{4,6},{5,7},{6,4},{7,5},{8,10},{9,11},{10,... | collective-permute-start | bytes 3145736 | tf_op jit(solution)/shard_map/ppermute | solution.py:299
  781.8 7.9 collective-permute-start.46
  783.0 8.6 collective-permute-start.45
  783.0 12.3 %collective-permute-start.44 = (f32[128,512]{1,0:T(8,128)S(1)}, f32[128,512]{1,0:T(8,128)S(1)}, u32[]{:S(2)}, u32[]{:S(2)}) collective-permute-start(f32[128,512]{1,0:T(8,128)S(1)} %get-tuple-element.191), channel_id=1, source_target_pairs={{0,2},{1,3},{2,0},{3,1},{4,6},{5,7},{6,4},{7,5},{8,10},{9,11},{10,... | collective-permute-start | bytes 786440 | tf_op jit(solution)/shard_map/ppermute | solution.py:385
  821.8 71.1 %collective-permute-start.65 = (f32[2,512,256]{2,1,0:T(8,128)S(1)}, f32[2,512,256]{2,1,0:T(8,128)S(1)}, u32[]{:S(2)}, u32[]{:S(2)}) collective-permute-start(f32[2,512,256]{2,1,0:T(8,128)S(1)} %constant_dynamic-slice_fusion.10), channel_id=1, source_target_pairs={{0,1},{1,2},{2,3},{3,0},{4,5},{5,6},{6,7},{7,4},{8,9},{9,10},{10,1... | collective-permute-start | bytes 3145736 | tf_op jit(solution)/shard_map/ppermute | solution.py:299
  823.8 9.7 collective-permute-start.61
  826.3 29.0 %collective-permute-start.62 = (f32[128,512]{1,0:T(8,128)S(1)}, f32[128,512]{1,0:T(8,128)S(1)}, u32[]{:S(2)}, u32[]{:S(2)}) collective-permute-start(f32[128,512]{1,0:T(8,128)S(1)} %bitcast.354), channel_id=1, source_target_pairs={{0,1},{1,2},{2,3},{3,0},{4,5},{5,6},{6,7},{7,4},{8,9},{9,10},{10,1... | collective-permute-start | bytes 786440 | tf_op jit(solution)/shard_map/ppermute | solution.py:395
  826.3 29.0 %collective-permute-start.63 = (f32[128,512]{1,0:T(8,128)S(1)}, f32[128,512]{1,0:T(8,128)S(1)}, u32[]{:S(2)}, u32[]{:S(2)}) collective-permute-start(f32[128,512]{1,0:T(8,128)S(1)} %bitcast.355), channel_id=1, source_target_pairs={{0,3},{1,0},{2,1},{3,2},{4,7},{5,4},{6,5},{7,6},{8,11},{9,8},{10,9... | collective-permute-start | bytes 786440 | tf_op jit(solution)/shard_map/ppermute | solution.py:395
  828.1 68.0 %collective-permute-start.67 = (f32[2,512,256]{2,1,0:T(8,128)S(1)}, f32[2,512,256]{2,1,0:T(8,128)S(1)}, u32[]{:S(2)}, u32[]{:S(2)}) collective-permute-start(f32[2,512,256]{2,1,0:T(8,128)S(1)} %constant_dynamic-slice_fusion.8), channel_id=1, source_target_pairs={{0,2},{1,3},{2,0},{3,1},{4,6},{5,7},{6,4},{7,5},{8,10},{9,11},{10,... | collective-permute-start | bytes 3145736 | tf_op jit(solution)/shard_map/ppermute | solution.py:299
  855.5 39.5 %collective-permute-start.66 = (f32[2,512,256]{2,1,0:T(8,128)S(1)}, f32[2,512,256]{2,1,0:T(8,128)S(1)}, u32[]{:S(2)}, u32[]{:S(2)}) collective-permute-start(f32[2,512,256]{2,1,0:T(8,128)S(1)} %get-tuple-element.175), channel_id=1, source_target_pairs={{0,3},{1,0},{2,1},{3,2},{4,7},{5,4},{6,5},{7,6},{8,11},{9,8},{10,9... | collective-permute-start | bytes 3145736 | tf_op jit(solution)/shard_map/ppermute | solution.py:299
  855.7 44.6 %collective-permute-start.68 = (f32[2,512,256]{2,1,0:T(8,128)S(1)}, f32[2,512,256]{2,1,0:T(8,128)S(1)}, u32[]{:S(2)}, u32[]{:S(2)}) collective-permute-start(f32[2,512,256]{2,1,0:T(8,128)S(1)} %constant_dynamic-slice_fusion.7), channel_id=1, source_target_pairs={{0,1},{1,2},{2,3},{3,0},{4,5},{5,6},{6,7},{7,4},{8,9},{9,10},{10,1... | collective-permute-start | bytes 3145736 | tf_op jit(solution)/shard_map/ppermute | solution.py:299
  856.2 47.2 %collective-permute-start.69 = (f32[2,512,256]{2,1,0:T(8,128)S(1)}, f32[2,512,256]{2,1,0:T(8,128)S(1)}, u32[]{:S(2)}, u32[]{:S(2)}) collective-permute-start(f32[2,512,256]{2,1,0:T(8,128)S(1)} %get-tuple-element.183), channel_id=1, source_target_pairs={{0,3},{1,0},{2,1},{3,2},{4,7},{5,4},{6,5},{7,6},{8,11},{9,8},{10,9... | collective-permute-start | bytes 3145736 | tf_op jit(solution)/shard_map/ppermute | solution.py:299
  937.1 25.8 %collective-permute-start.71 = (f32[256,1024]{1,0:T(8,128)S(1)}, f32[256,1024]{1,0:T(8,128)}, u32[]{:S(2)}, u32[]{:S(2)}) collective-permute-start(f32[256,1024]{1,0:T(8,128)S(1)} %dynamic-slice_bitcast_fusion.1), channel_id=1, source_target_pairs={{0,2},{1,3},{2,0},{3,1},{4,6},{5,7},{6,4},{7,5},{8,10},{9,11},{10,... | collective-permute-start | bytes 3145736 | tf_op jit(solution)/shard_map/ppermute | solution.py:417
  964.4 8.7 collective-permute-start.78
  965.3 8.4 collective-permute-start.77
  967.0 11.8 %collective-permute-start.76 = (f32[256,128]{1,0:T(8,128)S(1)}, f32[256,128]{1,0:T(8,128)S(1)}, u32[]{:S(2)}, u32[]{:S(2)}) collective-permute-start(f32[256,128]{1,0:T(8,128)S(1)} %get-tuple-element.187), channel_id=1, source_target_pairs={{0,4},{4,0},{8,12},{12,8},{16,20},{20,16},{24,28},{28,24},{1,5},{5... | collective-permute-start | bytes 393224 | tf_op jit(solution)/shard_map/ppermute | solution.py:425
  968.0 11.8 %collective-permute-start.75 = (f32[256,128]{1,0:T(8,128)S(1)}, f32[256,128]{1,0:T(8,128)S(1)}, u32[]{:S(2)}, u32[]{:S(2)}) collective-permute-start(f32[256,128]{1,0:T(8,128)S(1)} %get-tuple-element.188), channel_id=1, source_target_pairs={{0,20},{4,16},{8,28},{12,24},{16,4},{20,0},{24,12},{28,8},{1,21},{... | collective-permute-start | bytes 393224 | tf_op jit(solution)/shard_map/ppermute | solution.py:425
  968.8 11.8 %collective-permute-start.74 = (f32[256,128]{1,0:T(8,128)S(1)}, f32[256,128]{1,0:T(8,128)S(1)}, u32[]{:S(2)}, u32[]{:S(2)}) collective-permute-start(f32[256,128]{1,0:T(8,128)S(1)} %get-tuple-element.189), channel_id=1, source_target_pairs={{0,24},{4,28},{8,0},{12,4},{16,8},{20,12},{24,16},{28,20},{1,25},{... | collective-permute-start | bytes 393224 | tf_op jit(solution)/shard_map/ppermute | solution.py:425
  973.1 9.5 collective-permute-start.73
  973.6 16.0 %collective-permute-start.72 = (f32[256,128]{1,0:T(8,128)S(1)}, f32[256,128]{1,0:T(8,128)S(1)}, u32[]{:S(2)}, u32[]{:S(2)}) collective-permute-start(f32[256,128]{1,0:T(8,128)S(1)} %get-tuple-element.184), channel_id=1, source_target_pairs={{0,16},{4,20},{8,24},{12,28},{16,0},{20,4},{24,8},{28,12},{1,17},{... | collective-permute-start | bytes 393224 | tf_op jit(solution)/shard_map/ppermute | solution.py:425
  (40 other events, 318.1 us)
